TPU v7x, 256 devices: a whole 4x4x8 slice. The times are simulated.
256 devices in a mesh: slab: 32 (over x_hi, z, core), sub: 8 (over x_lo, y).
Axes of the slice: x: 4 (x_hi: 2, x_lo: 2; x = x_hi * 2 + x_lo), y: 4, z: 8, core: 2. Of those that a mesh axis runs over, the one named last changes fastest.
Arguments:
- velocity: float32 [3, 256, 128, 128], P(None, 'slab'), may hold values from -6 to 6
- part_vel: float32 [3, 4194304], P(None, ('slab', 'sub')), may hold values from -4 to 4
- fraction: float32 [3, 4194304], P(None, ('slab', 'sub')), may hold values from 0 to 1
- base_cell: int32 [4194304], P(('slab', 'sub')), may hold values from 0 to 438, as said below
- drag_coeff: float32 [4194304], P(('slab', 'sub')), may hold values from 2 to 20
- part_volume: float32 [4194304], P(('slab', 'sub')), may hold values from 0.005 to 0.05
- brick_of_block: int32 [32768], P(('slab', 'sub')), may hold values from 0 to 255
Outputs:
- new_velocity: float32 [3, 256, 128, 128], P(None, 'slab')
- voidfraction: float32 [256, 128, 128], P('slab')
- drag: float32 [3, 4194304], P(None, ('slab', 'sub'))
Inputs may be any that keep to these rules, and one draw needn't show every extreme that they name: `base_cell`: every particle's base plus one in each direction stays inside its brick: vertical base at most 6, horizontal bases at most 6.
All inputs are finite; a program needn't handle non-finite values.
Results may differ from a plain program's by a relative error of at most 0.0003.
Values sent between devices are 32-bit elements; how exact they have to be, the bound alone decides.
No kernel may reach another device: no remote copies, remote signals or barrier semaphores. Data moves between devices by JAX's collectives and lax.ppermute only.
A program may use at most 128 MiB of HBM per device.

v0:
```python
import math

import jax
import jax.numpy as jnp
from jax import lax
from jax.sharding import PartitionSpec as P

BLOCK = 128
ITERS = 4


EPS_MIN = 0.35
FLOW_POWER = -0.2
DRAG_POWER = -2.65
VISCOSITY = 1.2
TIME_STEP = 0.05


def padded_2(shard, sides, width):
    for axis, dim in sides:
        peers, length = (lax.axis_size(axis), shard.shape[dim])
        up = [(i, (i + 1) % peers) for i in range(peers - 1)]
        down = [(j, i) for i, j in up]
        last = lax.slice_in_dim(shard, length - width, length, axis=dim)
        initial = lax.slice_in_dim(shard, 0, width, axis=dim)
        before = lax.ppermute(last, axis, up)
        after = lax.ppermute(initial, axis, down)
        shard = jnp.concatenate([before, shard, after], axis=dim)
    return shard


def kernel_weights(base, frac, depth):
    zbase = (base // 64)[:, None, :]
    xbase = (base // 8 % 8)[:, None, :]
    ybase = (base % 8)[:, None, :]
    zrange = jnp.arange(depth, dtype=jnp.int32)[None, :, None]
    erange = jnp.arange(8, dtype=jnp.int32)[None, :, None]
    fz = frac[0][:, None, :]
    fx = frac[1][:, None, :]
    fy = frac[2][:, None, :]
    zero = jnp.float32(0.0)
    wz = jnp.where(zrange == zbase, 1.0 - fz, zero) + jnp.where(zrange == zbase + 1, fz, zero)
    wx = jnp.where(erange == xbase, 1.0 - fx, zero) + jnp.where(erange == xbase + 1, fx, zero)
    wy = jnp.where(erange == ybase, 1.0 - fy, zero) + jnp.where(erange == ybase + 1, fy, zero)
    full = wz[:, :, None, None, :] * wx[:, None, :, None, :] * wy[:, None, None, :, :]
    return full.reshape(base.shape[0], depth * 64, base.shape[1])


def particle_drag(weights, eps_rows, vel_rows, pvel, coef, pvol):
    eps_p = jnp.einsum("bcp,bc->bp", weights, eps_rows, precision=lax.Precision.HIGHEST)
    fluid = jnp.einsum("bcp,bkc->bkp", weights, vel_rows, precision=lax.Precision.HIGHEST)
    rel = fluid - pvel
    speed = jnp.sum(rel * rel, axis=1)
    factor = coef * pvol * (speed + 0.01) ** FLOW_POWER * eps_p**DRAG_POWER
    force = factor[:, None, :] * rel
    deposit = jnp.einsum("bcp,bkp->bkc", weights, force, precision=lax.Precision.HIGHEST)
    return (force, deposit)


def stencil(padded, source):
    centre = padded[:, 1:-1, 1:-1, 1:-1]
    upper = padded[:, 2:, 1:-1, 1:-1]
    lower = padded[:, :-2, 1:-1, 1:-1]
    east = padded[:, 1:-1, 2:, 1:-1]
    west = padded[:, 1:-1, :-2, 1:-1]
    north = padded[:, 1:-1, 1:-1, 2:]
    south = padded[:, 1:-1, 1:-1, :-2]
    shear = jnp.sum((upper - centre) ** 2 + (east - centre) ** 2 + (north - centre) ** 2, axis=0)
    viscous = VISCOSITY * (shear + 0.01) ** FLOW_POWER
    laplace = upper + lower + east + west + north + south - 6.0 * centre
    return centre + TIME_STEP * (viscous[None] * laplace + source)


def advance(zpad, source):
    return stencil(jnp.pad(zpad, ((0, 0), (0, 0), (1, 1), (1, 1))), source)


def to_bricks(field):
    comps, depth, width_x, width_y = field.shape
    split = field.reshape(comps, depth, width_x // 8, 8, width_y // 8, 8)
    return split.transpose(2, 4, 0, 1, 3, 5).reshape(
        width_x // 8 * (width_y // 8), comps, depth * 64
    )


def from_bricks(field, depth, width_x, width_y):
    comps = field.shape[1]
    split = field.reshape(width_x // 8, width_y // 8, comps, depth, 8, 8)
    return split.transpose(2, 3, 0, 4, 1, 5).reshape(comps, depth, width_x, width_y)


def body(velocity, part_vel, fraction, base_cell, drag_coeff, part_volume, brick_of_block):
    depth = velocity.shape[1]
    width_x = velocity.shape[2]
    width_y = velocity.shape[3]
    cells = depth * 64
    bricks = width_x // 8 * (width_y // 8)
    blocks = brick_of_block.shape[0]
    group = math.gcd(blocks, 16)
    count = blocks // group
    base = base_cell.reshape(count, group, BLOCK)
    frac = fraction.reshape(3, count, group, BLOCK).transpose(1, 0, 2, 3)
    pvel = part_vel.reshape(3, count, group, BLOCK).transpose(1, 2, 0, 3)
    coef = drag_coeff.reshape(count, group, BLOCK)
    pvol = part_volume.reshape(count, group, BLOCK)
    group_bricks = brick_of_block.reshape(count, group)
    picks = (jnp.arange(bricks, dtype=jnp.int32)[:, None] == brick_of_block[None, :]).astype(
        jnp.float32
    )

    def volume_group(items):
        weights = kernel_weights(items[0], items[1], depth)
        return jnp.einsum("bcp,bp->bc", weights, items[2], precision=lax.Precision.HIGHEST)

    volumes = lax.map(volume_group, (base, frac, pvol)).reshape(blocks, cells)
    partial_solid = jnp.dot(
        picks, volumes, precision=lax.Precision.HIGHEST, preferred_element_type=jnp.float32
    )
    solid = lax.psum(partial_solid, "sub")
    eps_brick = jnp.maximum(1.0 - solid, EPS_MIN)
    vel_bricks = to_bricks(velocity)

    def drag_group(items):
        weights = kernel_weights(items[0], items[1], depth)
        rows = items[5]
        return particle_drag(
            weights, eps_brick[rows], vel_bricks[rows], items[2], items[3], items[4]
        )

    forces, deposits = lax.map(drag_group, (base, frac, pvel, coef, pvol, group_bricks))
    partial_force = jnp.dot(
        picks,
        deposits.reshape(blocks, 3 * cells),
        precision=lax.Precision.HIGHEST,
        preferred_element_type=jnp.float32,
    )
    partial_force = partial_force.reshape(bricks, 3, cells)
    voidfraction = from_bricks(eps_brick[:, None, :], depth, width_x, width_y)[0]
    force_field = lax.psum(partial_force, "sub")
    source_brick = -force_field / eps_brick[:, None, :]
    source = from_bricks(source_brick, depth, width_x, width_y)
    current = velocity
    for step in range(ITERS):
        zpad = padded_2(current, (("slab", 1),), 1)
        current = advance(zpad, source)
    drag = forces.reshape(blocks, 3, BLOCK).transpose(1, 0, 2).reshape(3, blocks * BLOCK)
    return (current, voidfraction, drag)


def solution(mesh):
    in_specs = (
        P(None, "slab", None, None),
        P(None, ("slab", "sub")),
        P(None, ("slab", "sub")),
        P(("slab", "sub")),
        P(("slab", "sub")),
        P(("slab", "sub")),
        P(("slab", "sub")),
    )
    out_specs = (P(None, "slab", None, None), P("slab", None, None), P(None, ("slab", "sub")))
    return jax.shard_map(body, mesh=mesh, in_specs=in_specs, out_specs=out_specs, check_vma=False)
```

profile of v0, /device:TPU:225, one launch (start us, length us, event | category | flops | bytes accessed | tf_op | source)
XLA Modules:
  0.0 540.1 jit_solution(16191629649716523360)
XLA Ops:
  8.2 57.8 %while.28 = (s32[]{:T(128)}, f32[8,16,512]{2,1,0:T(8,128)S(1)}, s32[8,16,128]{2,1,0:T(8,128)}, f32[8,3,16,128]{3,2,1,0:T(8,128)S(1)}, f32[8,16,128]{2,1,0:T(8,128)}, /*index=5*/s32[]{:T(128)}, s32[]{:T(128)}, s32[]{}, s32[]{}) while((s32[]{:T(128)}, f32[8,16,512]{2,1,0:T(8,128)S(1)}, s32[8,16,128]{2,1,0:T(8,128)}, ...), condition=%wide.region_2.3_spmd, body=%wide.region_1.2_spmd.sunk | while | flops 14120964 | bytes 10207381 | solution.py:115
  11.9 3.6 fusion.111
  19.2 3.6 fusion.111
  26.4 3.6 fusion.111
  33.6 3.6 fusion.111
  40.8 3.6 fusion.111
  48.0 3.6 fusion.111
  55.2 3.6 fusion.111
  62.5 3.6 fusion.111
  67.9 16.0 %reshape.561 = f32[3,8,16,8,16,8]{5,4,3,2,1,0:T(8,128)} reshape(f32[3,8,128,128]{3,2,1,0:T(8,128)S(1)} %copy-done.2) | data formatting | bytes 3145728 | tf_op jit(solution)/shard_map/reshape | solution.py:80
  84.0 18.8 %copy.25 = f32[16,16,3,8,8,8]{1,0,5,4,3,2:T(8,128)} copy(f32[16,16,3,8,8,8]{5,1,4,0,3,2:T(8,128)} %bitcast.196) | data formatting | bytes 3145728 | tf_op jit(solution)/shard_map/transpose | solution.py:81
  102.8 8.7 %reshape.562 = f32[256,3,512]{0,2,1:T(8,128)S(1)} reshape(f32[16,16,3,8,8,8]{1,0,5,4,3,2:T(8,128)} %copy.25) | data formatting | bytes 3145728 | tf_op jit(solution)/shard_map/reshape | solution.py:81
  113.4 29.4 %all-reduce.7.cloned.1.call-done = f32[256,512]{1,0:T(8,128)} async-done(((f32[256,512]{1,0:T(8,128)}), f32[256,512]{1,0:T(8,128)}) %all-reduce.7.cloned.1.call-update) | async-done | bytes 524304 | tf_op jit(solution)/shard_map/psum | solution.py:119
  144.0 170.8 %while.29 = (s32[]{:T(128)}, f32[8,16,3,128]{3,2,1,0:T(4,128)}, f32[8,16,3,512]{3,2,1,0:T(4,128)}, f32[8,16,128]{2,1,0:T(8,128)}, f32[8,16,128]{2,1,0:T(8,128)},...) while((s32[]{:T(128)}, f32[8,16,3,128]{3,2,1,0:T(4,128)}, ...), condition=%wide.region_6.7_spmd, body=%wide.region_4.6_spmd.sunk | while | flops 89656368 | bytes 35984932 | solution.py:130
  146.3 2.5 broadcast_multiply_fusion.11
  149.4 4.0 fusion.119
  155.7 4.1 multiply_reduce_fusion.2
  160.5 4.2 fusion.121
  167.6 2.5 broadcast_multiply_fusion.11
  170.8 4.0 fusion.119
  177.0 4.1 multiply_reduce_fusion.2
  181.8 4.2 fusion.121
  189.0 2.5 broadcast_multiply_fusion.11
  192.1 4.0 fusion.119
  198.4 4.1 multiply_reduce_fusion.2
  203.2 4.2 fusion.121
  210.3 2.5 broadcast_multiply_fusion.11
  213.5 4.0 fusion.119
  219.7 4.1 multiply_reduce_fusion.2
  224.5 4.2 fusion.121
  234.8 4.0 fusion.119
  241.1 4.1 multiply_reduce_fusion.2
  245.9 4.2 fusion.121
  256.1 4.0 fusion.119
  262.4 4.1 multiply_reduce_fusion.2
  267.2 4.2 fusion.121
  277.5 4.0 fusion.119
  283.8 4.1 multiply_reduce_fusion.2
  288.6 4.2 fusion.121
  295.7 2.5 broadcast_multiply_fusion.11
  298.8 4.0 fusion.119
  305.1 4.1 multiply_reduce_fusion.2
  309.9 4.2 fusion.121
  317.6 3.1 fusion.75
  320.8 7.6 %collective-permute-start = (f32[3,1,128,128]{3,2,1,0:T(8,128)S(1)}, f32[3,1,128,128]{3,2,1,0:T(8,128)S(1)}, u32[]{:S(2)}, u32[]{:S(2)}) collective-permute-start(f32[3,1,128,128]{3,2,1,0:T(8,128)S(1)} %get-tuple-element.390), channel_id=1, source_target_pairs={{8,0},{16,8},{24,16},{32,24},{40,32},{48,40},{56,48},{64,56},{72,6... | collective-permute-start | bytes 589832 | tf_op jit(solution)/shard_map/ppermute | solution.py:27
  328.3 3.7 collective-permute-start.1
  334.5 2.6 select_maximum_fusion.6
  340.1 65.7 %all-reduce.9.cloned.1.call-done = f32[256,3,512]{2,0,1:T(8,128)} async-done(((f32[256,3,512]{2,0,1:T(8,128)}), f32[256,3,512]{2,0,1:T(8,128)}) %all-reduce.9.cloned.1.call-update) | async-done | bytes 1572880 | tf_op jit(solution)/shard_map/psum | solution.py:139
  405.8 2.8 negate_divide_fusion
  410.5 6.7 %reshape.568 = f32[16,16,3,8,8,8]{1,0,5,4,3,2:T(8,128)} reshape(f32[256,3,512]{0,2,1:T(8,128)S(1)} %copy.30) | data formatting | bytes 3145728 | tf_op jit(solution)/shard_map/reshape | solution.py:88
  417.2 17.8 %copy.31 = f32[3,8,16,8,16,8]{5,4,3,2,1,0:T(8,128)} copy(f32[3,8,16,8,16,8]{4,2,5,3,1,0:T(8,128)} %bitcast.197) | data formatting | bytes 3145728 | tf_op jit(solution)/shard_map/transpose | solution.py:89
  435.0 17.1 %reshape.569 = f32[3,8,128,128]{3,2,1,0:T(8,128)S(1)} reshape(f32[3,8,16,8,16,8]{5,4,3,2,1,0:T(8,128)} %copy.31) | data formatting | bytes 3145728 | tf_op jit(solution)/shard_map/reshape | solution.py:89
  452.1 5.9 %fusion.64 = f32[3,8,128,128]{3,2,1,0:T(8,128)S(1)} fusion(f32[3,8,128,128]{3,2,1,0:T(8,128)S(1)} %copy-done.2, f32[3,8,128,128]{3,2,1,0:T(8,128)S(1)} %reshape.569, f32[3,10,130,130]{3,2,1,0:T(8,128)} %copy-done.1, f32[3,1,128,128]{3,2,1,0:T(8,128)S(1)} %collective-permute-done.1, f32[3,1,128,128]{3,2,1,0:T(8,128)S(1)} %collective-permute-done, ...), kind=kLoop, calls=%fused_computation.167 | loop fusion | flops 5111808 | bytes 11927552 | tf_op jit(solution)/shard_map/add | solution.py:71
  458.1 7.1 %collective-permute-start.2 = (f32[3,1,128,128]{3,2,1,0:T(8,128)S(1)}, f32[3,1,128,128]{3,2,1,0:T(8,128)S(1)}, u32[]{:S(2)}, u32[]{:S(2)}) collective-permute-start(f32[3,1,128,128]{3,2,1,0:T(8,128)S(1)} %get-tuple-element.388), channel_id=1, source_target_pairs={{8,0},{16,8},{24,16},{32,24},{40,32},{48,40},{56,48},{64,56},{72,6... | collective-permute-start | bytes 589832 | tf_op jit(solution)/shard_map/ppermute | solution.py:27
  465.2 3.6 collective-permute-start.3
  471.3 2.6 select_maximum_fusion.4
  476.6 2.7 collective-permute-start.4
  479.3 7.4 %collective-permute-start.5 = (f32[3,1,128,128]{3,2,1,0:T(8,128)S(1)}, f32[3,1,128,128]{3,2,1,0:T(8,128)S(1)}, u32[]{:S(2)}, u32[]{:S(2)}) collective-permute-start(f32[3,1,128,128]{3,2,1,0:T(8,128)S(1)} %get-tuple-element.385), channel_id=1, source_target_pairs={{0,8},{8,16},{16,24},{24,32},{32,40},{40,48},{48,56},{56,64},{64,7... | collective-permute-start | bytes 589832 | tf_op jit(solution)/shard_map/ppermute | solution.py:26
  489.1 2.6 select_maximum_fusion.2
  497.0 8.0 %collective-permute-start.7 = (f32[3,1,128,128]{3,2,1,0:T(8,128)}, f32[3,1,128,128]{3,2,1,0:T(8,128)S(1)}, u32[]{:S(2)}, u32[]{:S(2)}) collective-permute-start(f32[3,1,128,128]{3,2,1,0:T(8,128)} %get-tuple-element.383), channel_id=1, source_target_pairs={{0,8},{8,16},{16,24},{24,32},{32,40},{40,48},{48,56},{56,64},{64,7... | collective-permute-start | bytes 589832 | tf_op jit(solution)/shard_map/ppermute | solution.py:26
  508.9 3.7 reshape_broadcast_in_dim.3
  512.6 7.0 %copy.33 = f32[1,8,16,8,16,8]{5,4,3,2,1,0:T(8,128)} copy(f32[1,8,16,8,16,8]{4,2,5,3,1,0:T(8,128)} %bitcast.198) | data formatting | bytes 1048576 | tf_op jit(solution)/shard_map/transpose | solution.py:89
  519.6 7.1 %squeeze_reshape.3 = f32[8,128,128]{2,1,0:T(8,128)} reshape(f32[1,8,16,8,16,8]{5,4,3,2,1,0:T(8,128)} %copy.33) | data formatting | bytes 1048576 | tf_op jit(solution)/shard_map/squeeze;reshape | solution.py:138
  526.6 2.6 select_maximum_fusion
  (254 shorter events, 124.3 us)
Async XLA Ops:
  7.2 135.7 %all-reduce.7.cloned.1.call-start = ((), (), s32[]{:S(2)}) async-start(), calls=%async_computation | async-start | bytes 1048576 | tf_op jit(solution)/shard_map/psum | solution.py:119
  8.2 57.9 %copy-start.4 = (s32[128]{0:T(128)S(1)}, s32[128]{0:T(128)}, u32[]{:S(2)}) copy-start(s32[128]{0:T(128)} %param.17) | copy-start | bytes 1540
  8.2 59.7 %copy-start.2 = (f32[3,8,128,128]{3,2,1,0:T(8,128)S(1)}, f32[3,8,128,128]{3,2,1,0:T(8,128)}, u32[]{:S(2)}) copy-start(f32[3,8,128,128]{3,2,1,0:T(8,128)} %param.11) | copy-start | bytes 4718596
  67.3 338.5 %all-reduce.9.cloned.1.call-start = ((), (), s32[]{:S(2)}) async-start(), calls=%async_computation.1 | async-start | bytes 3145728 | tf_op jit(solution)/shard_map/psum | solution.py:139
  155.7 4.8 copy-start
  177.0 4.8 copy-start
  198.4 4.8 copy-start
  219.7 4.8 copy-start
  241.1 4.8 copy-start
  262.4 4.8 copy-start
  283.7 4.8 copy-start
  305.1 4.8 copy-start
  314.8 91.0 %copy-start.3 = (f32[256,512]{1,0:T(8,128)}, f32[256,512]{1,0:T(8,128)S(1)}, u32[]{:S(2)}) copy-start(f32[256,512]{1,0:T(8,128)S(1)} %get-tuple-element.631) | copy-start | bytes 1572868
  320.8 12.6 %collective-permute-start = (f32[3,1,128,128]{3,2,1,0:T(8,128)S(1)}, f32[3,1,128,128]{3,2,1,0:T(8,128)S(1)}, u32[]{:S(2)}, u32[]{:S(2)}) collective-permute-start(f32[3,1,128,128]{3,2,1,0:T(8,128)S(1)} %get-tuple-element.390), channel_id=1, source_target_pairs={{8,0},{16,8},{24,16},{32,24},{40,32},{48,40},{56,48},{64,56},{72,6... | collective-permute-start | bytes 589832 | tf_op jit(solution)/shard_map/ppermute | solution.py:27
  328.3 6.2 %collective-permute-start.1 = (f32[3,1,128,128]{3,2,1,0:T(8,128)S(1)}, f32[3,1,128,128]{3,2,1,0:T(8,128)S(1)}, u32[]{:S(2)}, u32[]{:S(2)}) collective-permute-start(f32[3,1,128,128]{3,2,1,0:T(8,128)S(1)} %get-tuple-element.389), channel_id=1, source_target_pairs={{0,8},{8,16},{16,24},{24,32},{32,40},{40,48},{48,56},{56,64},{64,7... | collective-permute-start | bytes 589832 | tf_op jit(solution)/shard_map/ppermute | solution.py:26
  337.1 1.9 copy-start.1
  458.1 12.1 %collective-permute-start.2 = (f32[3,1,128,128]{3,2,1,0:T(8,128)S(1)}, f32[3,1,128,128]{3,2,1,0:T(8,128)S(1)}, u32[]{:S(2)}, u32[]{:S(2)}) collective-permute-start(f32[3,1,128,128]{3,2,1,0:T(8,128)S(1)} %get-tuple-element.388), channel_id=1, source_target_pairs={{8,0},{16,8},{24,16},{32,24},{40,32},{48,40},{56,48},{64,56},{72,6... | collective-permute-start | bytes 589832 | tf_op jit(solution)/shard_map/ppermute | solution.py:27
  465.2 6.2 %collective-permute-start.3 = (f32[3,1,128,128]{3,2,1,0:T(8,128)S(1)}, f32[3,1,128,128]{3,2,1,0:T(8,128)S(1)}, u32[]{:S(2)}, u32[]{:S(2)}) collective-permute-start(f32[3,1,128,128]{3,2,1,0:T(8,128)S(1)} %get-tuple-element.387), channel_id=1, source_target_pairs={{0,8},{8,16},{16,24},{24,32},{32,40},{40,48},{48,56},{56,64},{64,7... | collective-permute-start | bytes 589832 | tf_op jit(solution)/shard_map/ppermute | solution.py:26
  476.6 11.3 %collective-permute-start.4 = (f32[3,1,128,128]{3,2,1,0:T(8,128)S(1)}, f32[3,1,128,128]{3,2,1,0:T(8,128)S(1)}, u32[]{:S(2)}, u32[]{:S(2)}) collective-permute-start(f32[3,1,128,128]{3,2,1,0:T(8,128)S(1)} %get-tuple-element.386), channel_id=1, source_target_pairs={{8,0},{16,8},{24,16},{32,24},{40,32},{48,40},{56,48},{64,56},{72,6... | collective-permute-start | bytes 589832 | tf_op jit(solution)/shard_map/ppermute | solution.py:27
  479.3 9.8 %collective-permute-start.5 = (f32[3,1,128,128]{3,2,1,0:T(8,128)S(1)}, f32[3,1,128,128]{3,2,1,0:T(8,128)S(1)}, u32[]{:S(2)}, u32[]{:S(2)}) collective-permute-start(f32[3,1,128,128]{3,2,1,0:T(8,128)S(1)} %get-tuple-element.385), channel_id=1, source_target_pairs={{0,8},{8,16},{16,24},{24,32},{32,40},{40,48},{48,56},{56,64},{64,7... | collective-permute-start | bytes 589832 | tf_op jit(solution)/shard_map/ppermute | solution.py:26
  495.1 31.5 %collective-permute-start.6 = (f32[3,1,128,128]{3,2,1,0:T(8,128)}, f32[3,1,128,128]{3,2,1,0:T(8,128)S(1)}, u32[]{:S(2)}, u32[]{:S(2)}) collective-permute-start(f32[3,1,128,128]{3,2,1,0:T(8,128)} %get-tuple-element.384), channel_id=1, source_target_pairs={{8,0},{16,8},{24,16},{32,24},{40,32},{48,40},{56,48},{64,56},{72,6... | collective-permute-start | bytes 589832 | tf_op jit(solution)/shard_map/ppermute | solution.py:27
  497.0 29.6 %collective-permute-start.7 = (f32[3,1,128,128]{3,2,1,0:T(8,128)}, f32[3,1,128,128]{3,2,1,0:T(8,128)S(1)}, u32[]{:S(2)}, u32[]{:S(2)}) collective-permute-start(f32[3,1,128,128]{3,2,1,0:T(8,128)} %get-tuple-element.383), channel_id=1, source_target_pairs={{0,8},{8,16},{16,24},{24,32},{32,40},{40,48},{48,56},{56,64},{64,7... | collective-permute-start | bytes 589832 | tf_op jit(solution)/shard_map/ppermute | solution.py:26
Sparse Core Ops, SparseCore 0:
  67.4 75.3 all-reduce.6
  320.8 84.9 all-reduce.8
where the time goes:
time: 549 us; the launch traced here: 540 us
  local copies, waits for them, and re-layouts  144 us (26%)
  matrix products  131 us (24%)
  other arithmetic  104 us (19%)
  waiting for transfers between devices  103 us (19%)
  starting transfers between devices  42.5 us (8%)
  between operations  14.6 us (3%)
    psum x1, waiting for transfers between devices, body(): force_field = lax.psum(partial_force, 'sub')  65.7 us
    dot_general x8, matrix products, particle_drag(): jnp.einsum('bcp,bkp->bkc', weights, force, precision=lax.Precision.HIGHEST)  33.7 us
    dot_general x8, matrix products, particle_drag(): jnp.einsum('bcp,bkc->bkp', weights, vel_rows, precision=lax.Precision.HIG...  32.5 us
    dot_general x8, matrix products, particle_drag(): jnp.einsum('bcp,bc->bp', weights, eps_rows, precision=lax.Precision.HIGHEST)  32.2 us
    psum x1, waiting for transfers between devices, body(): solid = lax.psum(partial_solid, 'sub')  29.4 us
    dot_general x8, matrix products, volume_group(): jnp.einsum('bcp,bp->bc', weights, items[2], precision=lax.Precision.HIGHEST)  28.8 us
    mul x32, other arithmetic, kernel_weights(): wz[:, :, None, None, :] * wx[:, None, :, None, :] * wy[:, None, None, :, :]  25.7 us
    transpose x2, local copies, waits for them, and re-layouts, from_bricks(): split.transpose(2, 3, 0, 4, 1, 5).reshape(comps, depth, width_x, width_y)  24.7 us
  transfers between devices with their start and end apart: 10, of which 8 were waited for; matrix products, arithmetic and copies ran while one was open for 13% of the time, Pallas kernels for 0%

commit v1 on v0

v1 whole, which is shorter than its diff:
```python
import functools

import jax
import jax.numpy as jnp
from jax import lax
from jax.experimental import pallas as pl
from jax.experimental.pallas import tpu as pltpu
from jax.sharding import PartitionSpec as P

BLOCK = 128
LANES = 128
EPS_MIN = 0.35
FLOW_POWER = -0.2
DRAG_POWER = -2.65
VISCOSITY = 1.2
TIME_STEP = 0.05
ITERS = 4
UNROLL = 8
F32 = jnp.float32
PARAMS = pltpu.CompilerParams(vmem_limit_bytes=32 * 1024 * 1024)
FULL = pltpu.CompilerParams(vmem_limit_bytes=60 * 1024 * 1024)
VMEM = pl.BlockSpec(memory_space=pltpu.VMEM)
SMEM = pl.BlockSpec(memory_space=pltpu.SMEM)
HBM = pl.BlockSpec(memory_space=pltpu.HBM)
ANY = pl.BlockSpec(memory_space=pl.ANY)


def transpose_granules(tiles, lane):
    for bit in (1, 2, 4):
        shift = 8 * bit
        high = (lane & shift) != 0
        new = list(tiles)
        for a in range(8):
            if a & bit:
                continue
            b = a | bit
            va, vb = tiles[a], tiles[b]
            new[a] = jnp.where(high, pltpu.roll(vb, shift, 1), va)
            new[b] = jnp.where(high, vb, pltpu.roll(va, LANES - shift, 1))
        tiles = new
    return tiles


def fetch(pairs, sems):
    copies = [pltpu.make_async_copy(a, b, sems.at[i]) for i, (a, b) in enumerate(pairs)]
    for copy in copies:
        copy.start()
    return copies


def lanes_iota():
    return lax.broadcasted_iota(jnp.int32, (8, LANES), 1)


def rows_iota():
    return lax.broadcasted_iota(jnp.int32, (8, LANES), 0)


def spread(row):
    return jnp.broadcast_to(row, (8, LANES))


def particles(base_ref, frac_ref, block):
    at = pl.ds(pl.multiple_of(block * BLOCK, BLOCK), BLOCK)
    base = spread(base_ref[pl.ds(block, 1), :])
    fz = spread(frac_ref[0:1, at])
    fx = spread(frac_ref[1:2, at])
    fy = spread(frac_ref[2:3, at])
    return at, base >> 6, (base >> 3) & 7, base & 7, fz, fx, fy


def axis_weights(rows, first, frac):
    zero = jnp.zeros_like(frac)
    return jnp.where(rows == first, 1.0 - frac, jnp.where(rows == first + 1, frac, zero))


def plane_weights(rows, zb, yb, fz, fy):
    ky = axis_weights(rows, yb, fy)
    parts = []
    for z in range(8):
        kz = jnp.where(zb == z, 1.0 - fz, jnp.where(zb == z - 1, fz, jnp.zeros_like(fz)))
        parts.append(kz * ky)
    full = jnp.concatenate(parts, axis=0)
    high = full.astype(jnp.bfloat16)
    low = (full - high.astype(F32)).astype(jnp.bfloat16)
    return jnp.concatenate([high, low], axis=0)


def split_rows(parts):
    full = jnp.concatenate(parts, axis=0)
    high = full.astype(jnp.bfloat16).astype(F32)
    return jnp.concatenate([high, full - high], axis=0).astype(jnp.bfloat16)


def deposit(parts, weights):
    left = split_rows(parts)
    both = lax.dot_general(
        left, weights, (((1,), (1,)), ((), ())), preferred_element_type=F32
    )
    half = both.shape[0] // 2
    both = both[:half] + both[half:]
    return both + pltpu.roll(both, 64, 1)


def corner_terms(zb, yb, fz, fy, offset):
    index = (zb << 3) + yb + offset
    gz, gy = 1.0 - fz, 1.0 - fy
    return (
        (index, gz * gy),
        (index + 1, gz * fy),
        (index + 8, fz * gy),
        (index + 9, fz * fy),
    )


def interpolate(tile, kx, corners):
    total = None
    for index, weight in corners:
        term = weight * jnp.take_along_axis(tile, index, axis=1, mode="promise_in_bounds")
        total = term if total is None else total + term
    return jnp.sum(kx * total, axis=0, keepdims=True)


def brick_place(brick):
    return brick >> 4, brick & 7, (brick >> 3) & 1


def solid_kernel(
    brick_hbm, base_hbm, frac_hbm, pvol_hbm, out_ref, brick_ref, base_ref, frac_ref, pvol_ref, sems
):
    copies = fetch(
        [(brick_hbm, brick_ref), (base_hbm, base_ref), (frac_hbm, frac_ref), (pvol_hbm, pvol_ref)],
        sems,
    )
    out_ref[...] = jnp.zeros_like(out_ref)
    for copy in copies:
        copy.wait()
    rows, lane = rows_iota(), lanes_iota()

    def step(number, carry):
        found = []
        for k in range(UNROLL):
            block = number * UNROLL + k
            _, zb, xb, yb, fz, fx, fy = particles(base_ref, frac_ref, block)
            kx = axis_weights(rows, xb, fx) * spread(pvol_ref[pl.ds(block, 1), :])
            found.append(deposit([kx], plane_weights(rows, zb, yb, fz, fy)))
        for k in range(UNROLL):
            tx, t3, t1 = brick_place(brick_ref[number * UNROLL + k])
            tile = tx * 8 + t3
            out_ref[tile] += jnp.where((lane >> 6) == t1, found[k], 0.0)
        return carry

    lax.fori_loop(0, base_ref.shape[0] // UNROLL, step, 0)


def eps_kernel(parts_ref, out_ref, copies_ref):
    total = parts_ref[0]
    for j in range(1, parts_ref.shape[0]):
        total = total + parts_ref[j]
    total = jnp.maximum(1.0 - total, EPS_MIN)
    out_ref[...] = total
    for j in range(copies_ref.shape[0]):
        copies_ref[j] = total


def slip_kernel(
    solid_any, sub_ref, brick_hbm, base_hbm, frac_hbm, pvel_hbm, coef_hbm, pvol_hbm, velocity_hbm,
    out_ref, window_ref,
    brick_ref, base_ref, frac_ref, pvel_ref, coef_ref, pvol_ref, velocity_ref, table, sems,
):
    copies = fetch(
        [(velocity_hbm.at[c], velocity_ref.at[c]) for c in range(3)]
        + [
            (brick_hbm, brick_ref),
            (base_hbm, base_ref),
            (frac_hbm, frac_ref),
            (pvel_hbm, pvel_ref),
            (coef_hbm, coef_ref),
            (pvol_hbm, pvol_ref),
        ],
        sems,
    )
    rows, lane = rows_iota(), lanes_iota()
    tiles_x = velocity_ref.shape[2] // 8

    for c in range(3):
        copies[c].wait()

        def convert(tx, carry, c=c):
            at = pl.ds(pl.multiple_of(tx * 8, 8), 8)
            tiles = transpose_granules([velocity_ref[c, z, at, :] for z in range(8)], lane)
            for t3 in range(8):
                table[(tx * 3 + c) * 8 + t3] = tiles[t3]
            return carry

        lax.fori_loop(0, tiles_x, convert, 0)
    for copy in copies[3:]:
        copy.wait()

    for r in range(4):
        want = sub_ref[0] * 2 + r - 1
        inside = jnp.logical_and(want >= 0, want < tiles_x)
        at = pl.ds(pl.multiple_of(jnp.clip(want, 0, tiles_x - 1) * 8, 8), 8)
        window_ref[:, :, 8 * r : 8 * r + 8, :] = jnp.where(inside, velocity_ref[:, :, at, :], 0.0)

    def step(number, carry):
        for k in range(UNROLL):
            block = number * UNROLL + k
            at, zb, xb, yb, fz, fx, fy = particles(base_ref, frac_ref, block)
            tx, t3, t1 = brick_place(brick_ref[block])
            kx = axis_weights(rows, xb, fx)
            corners = corner_terms(zb, yb, fz, fy, t1 * 64)
            rel = [
                interpolate(table[(tx * 3 + c) * 8 + t3], kx, corners) - pvel_ref[c : c + 1, at]
                for c in range(3)
            ]
            speed = rel[0] * rel[0] + rel[1] * rel[1] + rel[2] * rel[2]
            factor = coef_ref[pl.ds(block, 1), :] * pvol_ref[pl.ds(block, 1), :]
            factor = factor * jnp.exp(FLOW_POWER * jnp.log(speed + 0.01))
            for c in range(3):
                out_ref[c : c + 1, at] = factor * rel[c]
        return carry

    lax.fori_loop(0, base_ref.shape[0] // UNROLL, step, 0)


def drag_kernel(
    brick_ref, base_ref, frac_ref, slip_ref, eps_ref, below_any, above_any, drag_ref, out_ref
):
    out_ref[...] = jnp.zeros_like(out_ref)
    rows, lane = rows_iota(), lanes_iota()

    def step(number, carry):
        found = []
        for k in range(UNROLL):
            block = number * UNROLL + k
            at, zb, xb, yb, fz, fx, fy = particles(base_ref, frac_ref, block)
            tx, t3, t1 = brick_place(brick_ref[block])
            kx = axis_weights(rows, xb, fx)
            eps = interpolate(eps_ref[tx * 8 + t3], kx, corner_terms(zb, yb, fz, fy, t1 * 64))
            factor = jnp.exp(DRAG_POWER * jnp.log(eps))
            parts = []
            for c in range(3):
                force = factor * slip_ref[c : c + 1, at]
                drag_ref[c : c + 1, at] = force
                parts.append(kx * spread(force))
            found.append(deposit(parts, plane_weights(rows, zb, yb, fz, fy)))
        for k in range(UNROLL):
            tx, t3, t1 = brick_place(brick_ref[number * UNROLL + k])
            mine = (lane >> 6) == t1
            for c in range(3):
                tile = (tx * 3 + c) * 8 + t3
                out_ref[tile] += jnp.where(mine, found[k][8 * c : 8 * c + 8], 0.0)
        return carry

    lax.fori_loop(0, base_ref.shape[0] // UNROLL, step, 0)


def source_kernel(parts_ref, eps_ref, own_ref, low_ref, high_ref):
    lane = lanes_iota()
    for t in range(2):
        for c in range(3):
            tiles = []
            for t3 in range(8):
                at = (t * 3 + c) * 8 + t3
                total = parts_ref[0, at]
                for j in range(1, parts_ref.shape[0]):
                    total = total + parts_ref[j, at]
                tiles.append(-total / eps_ref[t * 8 + t3])
            tiles = transpose_granules(tiles, lane)
            for z in range(8):
                own_ref[c, z, 8 * t : 8 * t + 8, :] = tiles[z]
                if z < 3:
                    low_ref[c, z, 8 * t : 8 * t + 8, :] = tiles[z]
                if z >= 5:
                    high_ref[c, z - 5, 8 * t : 8 * t + 8, :] = tiles[z]


def void_kernel(eps_ref, out_ref):
    lane = lanes_iota()

    def convert(tx, carry):
        tiles = transpose_granules([eps_ref[tx * 8 + t3] for t3 in range(8)], lane)
        for z in range(8):
            out_ref[z, pl.ds(pl.multiple_of(tx * 8, 8), 8), :] = tiles[z]
        return carry

    lax.fori_loop(0, out_ref.shape[1] // 8, convert, 0)


def stencil_kernel(
    place_ref, window_ref, below_ref, above_ref, own_ref, low_ref, high_ref, left_ref, right_ref, out_ref, first, second, source
):
    slab, sub, planes, width = place_ref[0], place_ref[1], place_ref[2], place_ref[3]
    first[:, 0:4] = below_ref[...]
    first[:, 4:12] = window_ref[...]
    first[:, 12:16] = above_ref[...]
    source[:, 0:3, 8:24, :] = low_ref[...]
    source[:, 3:11, 8:24, :] = own_ref[...]
    source[:, 11:14, 8:24, :] = high_ref[...]
    source[:, :, 0:8, :] = left_ref[...]
    source[:, :, 24:32, :] = right_ref[...]
    lane = lax.broadcasted_iota(jnp.int32, (32, LANES), 1)
    row = lax.broadcasted_iota(jnp.int32, (32, LANES), 0) + sub * 16 - 8
    inside_x = jnp.logical_and(row >= 0, row < width)
    buffers = (first, second)
    for number in range(ITERS):
        old, new = buffers[number % 2], buffers[(number + 1) % 2]

        def plane(z, carry, old=old, new=new):
            shear = None
            centres, laps = [], []
            for c in range(3):
                centre = old[c, z]
                upper = old[c, z + 1]
                lower = old[c, z - 1]
                east = pltpu.roll(centre, 31, 0)
                west = pltpu.roll(centre, 1, 0)
                north = jnp.where(lane == LANES - 1, 0.0, pltpu.roll(centre, LANES - 1, 1))
                south = jnp.where(lane == 0, 0.0, pltpu.roll(centre, 1, 1))
                term = (upper - centre) ** 2 + (east - centre) ** 2 + (north - centre) ** 2
                shear = term if shear is None else shear + term
                centres.append(centre)
                laps.append(upper + lower + east + west + north + south - 6.0 * centre)
            viscous = VISCOSITY * jnp.exp(FLOW_POWER * jnp.log(shear + 0.01))
            height = slab * 8 - 4 + z
            keep = jnp.logical_and(inside_x, jnp.logical_and(height >= 0, height < planes))
            for c in range(3):
                moved = centres[c] + TIME_STEP * (viscous * laps[c] + source[c, z - 1])
                new[c, z] = jnp.where(keep, moved, 0.0)
            return carry

        lax.fori_loop(number + 1, 15 - number, plane, 0)
    last = buffers[ITERS % 2]
    for j in range(out_ref.shape[0]):
        out_ref[j] = last[:, 4:12, 8:24, :]


def place_kernel(parts_ref, out_ref, sems):
    rows = parts_ref.shape[3]
    copies = fetch(
        [
            (parts_ref.at[j], out_ref.at[:, :, pl.ds(j * rows, rows), :])
            for j in range(parts_ref.shape[0])
        ],
        sems,
    )
    for copy in copies:
        copy.wait()


def call(kernel, out_shapes, ins, scratch=(), outs=None, us=1.0, params=PARAMS):
    return pl.pallas_call(
        kernel,
        out_shape=[jax.ShapeDtypeStruct(s, F32) for s in out_shapes],
        in_specs=ins,
        out_specs=outs or [VMEM] * len(out_shapes),
        scratch_shapes=list(scratch),
        compiler_params=params,
        cost_estimate=pl.CostEstimate(flops=int(us * 1e9), bytes_accessed=int(us * 3.6e6), transcendentals=0),
    )


def shift(x, axis, up):
    peers = lax.axis_size(axis)
    pairs = [(i, i + 1) if up else (i + 1, i) for i in range(peers - 1)]
    return lax.ppermute(x, axis, pairs)


def body(velocity, part_vel, fraction, base_cell, drag_coeff, part_volume, brick_of_block):
    depth, width_x = velocity.shape[1], velocity.shape[2]
    blocks = brick_of_block.shape[0]
    subs = lax.axis_size("sub")
    slab = lax.axis_index("slab").astype(jnp.int32)
    sub = lax.axis_index("sub").astype(jnp.int32)
    tiles_x = width_x // 8
    tiles = tiles_x * 8
    share = tiles // subs
    base = base_cell.reshape(blocks, BLOCK)
    coef = drag_coeff.reshape(blocks, BLOCK)
    pvol = part_volume.reshape(blocks, BLOCK)

    particles_vmem = [
        pltpu.SMEM((blocks,), jnp.int32),
        pltpu.VMEM((blocks, BLOCK), jnp.int32),
        pltpu.VMEM((3, blocks * BLOCK), F32),
    ]
    row_vmem = pltpu.VMEM((blocks, BLOCK), F32)
    (solid,) = call(
        solid_kernel,
        [(tiles, 8, LANES)],
        [HBM] * 4,
        particles_vmem + [row_vmem, pltpu.SemaphoreType.DMA((4,))],
        us=6.0,
        params=FULL,
    )(brick_of_block, base, fraction, pvol)
    solid_parts = lax.all_to_all(solid.reshape(subs, share, 8, LANES), "sub", 0, 0)
    slip, window = call(
        slip_kernel,
        [(3, blocks * BLOCK), (3, depth, 32, LANES)],
        [ANY, SMEM] + [HBM] * 7,
        particles_vmem
        + [
            pltpu.VMEM((3, blocks * BLOCK), F32),
            row_vmem,
            row_vmem,
            pltpu.VMEM(velocity.shape, F32),
            pltpu.VMEM((3 * tiles, 8, LANES), F32),
            pltpu.SemaphoreType.DMA((9,)),
        ],
        us=9.0,
        params=FULL,
    )(solid, sub.reshape(1), brick_of_block, base, fraction, part_vel, coef, pvol, velocity)
    below = shift(window[:, depth - 4 :], "slab", True)
    above = shift(window[:, :4], "slab", False)

    eps_own, eps_copies = call(
        eps_kernel, [(share, 8, LANES), (subs, share, 8, LANES)], [VMEM], us=0.5
    )(solid_parts)
    eps = lax.all_to_all(eps_copies, "sub", 0, 0).reshape(tiles, 8, LANES)
    drag, force = call(
        drag_kernel,
        [(3, blocks * BLOCK), (3 * tiles, 8, LANES)],
        [SMEM] + [VMEM] * 4 + [ANY] * 2,
        us=8.0,
    )(brick_of_block, base, fraction, slip, eps, below, above)
    force_parts = lax.all_to_all(force.reshape(subs, 3 * share, 8, LANES), "sub", 0, 0)
    (voidfraction,) = call(void_kernel, [(depth, width_x, LANES)], [VMEM], us=3.0)(eps)

    rows = width_x // subs
    own, first, last = call(
        source_kernel,
        [(3, depth, rows, LANES), (3, 3, rows, LANES), (3, 3, rows, LANES)],
        [VMEM, VMEM],
    )(force_parts, eps_own)
    low = shift(last, "slab", True)
    high = shift(first, "slab", False)
    whole = jnp.concatenate([low, own, high], axis=1)
    left = shift(whole[:, :, 8:16], "sub", True)
    right = shift(whole[:, :, 0:8], "sub", False)
    planes = depth * lax.axis_size("slab")
    place = jnp.stack([slab, sub, jnp.int32(planes), jnp.int32(width_x)])
    (moved,) = call(
        stencil_kernel,
        [(subs, 3, depth, rows, LANES)],
        [SMEM] + [VMEM] * 8,
        [
            pltpu.VMEM((3, 16, 32, LANES), F32),
            pltpu.VMEM((3, 16, 32, LANES), F32),
            pltpu.VMEM((3, 14, 32, LANES), F32),
        ],
        us=6.0,
    )(place, window, below, above, own, low, high, left, right)
    moved = lax.all_to_all(moved, "sub", 0, 0)
    (new_velocity,) = call(
        place_kernel,
        [velocity.shape],
        [ANY],
        [pltpu.SemaphoreType.DMA((subs,))],
        outs=[ANY],
    )(moved)
    return new_velocity, voidfraction, drag


def solution(mesh):
    in_specs = (
        P(None, "slab", None, None),
        P(None, ("slab", "sub")),
        P(None, ("slab", "sub")),
        P(("slab", "sub")),
        P(("slab", "sub")),
        P(("slab", "sub")),
        P(("slab", "sub")),
    )
    out_specs = (P(None, "slab", None, None), P("slab", None, None), P(None, ("slab", "sub")))
    return jax.shard_map(body, mesh=mesh, in_specs=in_specs, out_specs=out_specs, check_vma=False)
```

time: 549 us -> 146 us (0.27); the launches traced: 540 us -> 144 us
  local copies, waits for them, and re-layouts: 144 us -> 2.07 us
  matrix products: 131 us -> 0 us
  other arithmetic: 104 us -> 0.08 us
  waiting for transfers between devices: 103 us -> 33.9 us
  Pallas kernels: 0 us -> 46.8 us
  blocking collectives: 0 us -> 25.5 us
  between operations: 14.6 us -> 0.78 us
  starting transfers between devices: 42.5 us -> 34.8 us
    dot_general x34 -> x0, matrix products: 131 us -> none  [the longest x8 33.7 us: particle_drag(): jnp.einsum('bcp,bkp->bkc', weights, force, precision=lax.Precision.HIGHEST)]
    psum x2 -> x0, waiting for transfers between devices: 95.1 us -> none  [the longest x1 65.7 us: body(): force_field = lax.psum(partial_force, 'sub')]
    reshape x6 -> x0, local copies, waits for them, and re-layouts: 49.7 us -> none  [the longest x1 17.1 us: from_bricks(): split.transpose(2, 3, 0, 4, 1, 5).reshape(comps, depth, width_x, width_y)]
    pallas_call x0 -> x8, Pallas kernels: none -> 46.8 us  [the longest x1 18.2 us: body(): call(slip_kernel, [(3, blocks * BLOCK), (3, depth, 32, LANES)], [ANY, SME...]
    add x84 -> x0, other arithmetic: 46.5 us -> none  [the longest x16 11.5 us: kernel_weights(): xbase + 1]
    transpose x3 -> x0, local copies, waits for them, and re-layouts: 43.5 us -> none  [the longest x2 24.7 us: from_bricks(): split.transpose(2, 3, 0, 4, 1, 5).reshape(comps, depth, width_x, width_y)]
    mul x44 -> x0, other arithmetic: 33.5 us -> none  [the longest x32 25.7 us: kernel_weights(): wz[:, :, None, None, :] * wx[:, None, :, None, :] * wy[:, None, None, :, :]]
    all_to_all x0 -> x1, blocking collectives: none -> 25.5 us  [body(): lax.all_to_all(force.reshape(subs, 3 * share, 8, LANES), 'sub', 0, 0)]
  transfers between devices with their start and end apart: 10 -> 9, of which waited for: 8 -> 7; matrix products, arithmetic and copies ran while one was open for 13% -> 1% of each run, Pallas kernels for 0% -> 16%
where the time goes in v1:
time: 146 us; the launch traced here: 144 us
  Pallas kernels  46.8 us (32%)
  starting transfers between devices  34.8 us (24%)
  waiting for transfers between devices  33.9 us (23%)
  blocking collectives  25.5 us (17%)
  local copies, waits for them, and re-layouts  2.07 us (1%)
    all_to_all x1, blocking collectives, body(): lax.all_to_all(force.reshape(subs, 3 * share, 8, LANES), 'sub', 0, 0)  25.5 us
    ppermute x6, starting transfers between devices, shift(): return lax.ppermute(x, axis, pairs)  18.9 us
    pallas_call x1, Pallas kernels, body(): call(slip_kernel, [(3, blocks * BLOCK), (3, depth, 32, LANES)], [ANY, SME...  18.2 us
    all_to_all x1, waiting for transfers between devices, body(): moved = lax.all_to_all(moved, 'sub', 0, 0)  14 us
    ppermute x6, waiting for transfers between devices, shift(): return lax.ppermute(x, axis, pairs)  12.1 us
    pallas_call x1, Pallas kernels, body(): call(drag_kernel, [(3, blocks * BLOCK), (3 * tiles, 8, LANES)], [SMEM] +...  8.11 us
    all_to_all x1, waiting for transfers between devices, body(): lax.all_to_all(solid.reshape(subs, share, 8, LANES), 'sub', 0, 0)  7.81 us
    pallas_call x1, Pallas kernels, body(): call(solid_kernel, [(tiles, 8, LANES)], [HBM] * 4, particles_vmem + [row_...  7.12 us
  transfers between devices with their start and end apart: 9, of which 7 were waited for; matrix products, arithmetic and copies ran while one was open for 1% of the time, Pallas kernels for 16%

profile of v1, /device:TPU:225, one launch (start us, length us, event | category | flops | bytes accessed | tf_op | source)
XLA Modules:
  0.0 143.9 jit_solution(8797639863899030198)
XLA Ops:
  0.6 7.1 %shard_map.94.solid_any = f32[128,8,128]{2,1,0:T(8,128)} custom-call(s32[128]{0:T(128)} %brick_ref.1, s32[128,128]{1,0:T(8,128)} %bitcast.11, f32[3,16384]{1,0:T(4,128)} %frac_ref.1, f32[128,128]{1,0:T(8,128)} %bitcast.15), custom_call_target="tpu_custom_call" | custom-call | flops 6000000000 | bytes 21600000 | tf_op jit(solution)/shard_map/pallas_call | solution.py:389
  7.8 5.1 %all-to-all-start = ((f32[8,16,8,128]{3,2,1,0:T(8,128)}), f32[8,16,8,128]{3,2,1,0:T(8,128)S(1)}, u32[]{:S(2)}, u32[]{:S(2)}) async-start(f32[8,16,8,128]{3,2,1,0:T(8,128)} %bitcast.14), calls=%async_computation | async-start | bytes 1048576 | tf_op jit(solution)/shard_map/all_to_all | solution.py:397
  12.9 7.8 %all-to-all-done.parts_ref = f32[8,16,8,128]{3,2,1,0:T(8,128)S(1)} async-done(((f32[8,16,8,128]{3,2,1,0:T(8,128)}), f32[8,16,8,128]{3,2,1,0:T(8,128)S(1)}, u32[]{:S(2)}, u32[]{:S(2)}) %all-to-all-start) | async-done | bytes 524320 | tf_op jit(solution)/shard_map/all_to_all | solution.py:397
  20.7 0.8 shard_map.96
  21.5 5.2 %all-to-all-start.1 = ((f32[8,16,8,128]{3,2,1,0:T(8,128)}), f32[8,16,8,128]{3,2,1,0:T(8,128)S(1)}, u32[]{:S(2)}, u32[]{:S(2)}) async-start(f32[8,16,8,128]{3,2,1,0:T(8,128)} %get-tuple-element.14), calls=%async_computation.1 | async-start | bytes 1048576 | tf_op jit(solution)/shard_map/all_to_all | solution.py:420
  26.7 0.0 copy-start.1
  26.7 0.0 copy-start.2
  26.7 0.0 copy-start.3
  26.8 18.2 %shard_map.95 = (f32[3,16384]{1,0:T(4,128)}, f32[3,8,32,128]{3,2,1,0:T(8,128)}) custom-call(f32[128,8,128]{2,1,0:T(8,128)} %shard_map.94.solid_any, s32[1]{0:T(128)} %bitcast.1.sub_ref, s32[128]{0:T(128)} %brick_ref.1, s32[128,128]{1,0:T(8,128)} %bitcast.12, f32[3,16384]{1,0:T(4,128)} %frac_ref.1, f32[3,16384]{1,0:T(4,128)} %pvel_hbm.1, ...), custom_call_target="tpu_custom_call" | custom-call | flops 8999999488 | bytes 32400000 | tf_op jit(solution)/shard_map/pallas_call | solution.py:398
  45.0 1.1 fusion
  46.0 3.0 %collective-permute-start.1 = (f32[3,4,32,128]{3,2,1,0:T(8,128)S(1)}, f32[3,4,32,128]{3,2,1,0:T(8,128)S(1)}, u32[]{:S(2)}, u32[]{:S(2)}) collective-permute-start(f32[3,4,32,128]{3,2,1,0:T(8,128)S(1)} %get-tuple-element.21), channel_id=1, source_target_pairs={{8,0},{16,8},{24,16},{32,24},{40,32},{48,40},{56,48},{64,56},{72,6... | collective-permute-start | bytes 589832 | tf_op jit(solution)/shard_map/ppermute | solution.py:367
  49.0 6.2 %collective-permute-start = (f32[3,4,32,128]{3,2,1,0:T(8,128)S(1)}, f32[3,4,32,128]{3,2,1,0:T(8,128)S(1)}, u32[]{:S(2)}, u32[]{:S(2)}) collective-permute-start(f32[3,4,32,128]{3,2,1,0:T(8,128)S(1)} %get-tuple-element.22), channel_id=1, source_target_pairs={{0,8},{8,16},{16,24},{24,32},{32,40},{40,48},{48,56},{56,64},{64,7... | collective-permute-start | bytes 589832 | tf_op jit(solution)/shard_map/ppermute | solution.py:367
  55.2 1.4 collective-permute-done.1.above_any.above_ref
  56.6 1.2 collective-permute-done.below_any.below_ref
  57.8 0.0 all-to-all-done.1
  57.8 0.0 copy-done.1
  57.8 0.0 copy-done.2
  57.8 0.0 copy-done.3
  57.8 0.0 copy-start.4
  57.8 0.9 copy-done.4
  58.8 8.1 %shard_map.97 = (f32[3,16384]{1,0:T(4,128)}, f32[384,8,128]{2,1,0:T(8,128)S(1)}) custom-call(s32[128]{0:T(128)S(1)} %copy-done.3, s32[128,128]{1,0:T(8,128)S(1)} %bitcast.13, f32[3,16384]{1,0:T(4,128)S(1)} %copy-done.1, f32[3,16384]{1,0:T(4,128)S(1)} %copy-done.4, f32[128,8,128]{2,1,0:T(8,128)S(1)} %bitcast.9, ...), custom_call_target="tpu_custom_call" | custom-call | flops 8000000000 | bytes 28800000 | tf_op jit(solution)/shard_map/pallas_call | solution.py:421
  66.9 25.5 %all_to_all.20.parts_ref = f32[8,48,8,128]{3,2,1,0:T(8,128)S(1)} all-to-all(f32[8,48,8,128]{3,2,1,0:T(8,128)S(1)} %bitcast.8), channel_id=1, replica_groups=mesh['slab'=32,'sub'=8] {'sub'}, dimensions={0} | all-to-all | bytes 3145728 | tf_op jit(solution)/shard_map/all_to_all | solution.py:427
  92.4 0.0 copy-start
  92.4 0.3 shard_map.98
  92.7 2.6 %collective-permute-start.2 = (f32[3,3,16,128]{3,2,1,0:T(8,128)S(1)}, f32[3,3,16,128]{3,2,1,0:T(8,128)S(1)}, u32[]{:S(2)}, u32[]{:S(2)}) collective-permute-start(f32[3,3,16,128]{3,2,1,0:T(8,128)S(1)} %get-tuple-element.18), channel_id=1, source_target_pairs={{0,8},{8,16},{16,24},{24,32},{32,40},{40,48},{48,56},{56,64},{64,7... | collective-permute-start | bytes 221192 | tf_op jit(solution)/shard_map/ppermute | solution.py:367
  95.3 1.9 %collective-permute-start.3 = (f32[3,3,16,128]{3,2,1,0:T(8,128)S(1)}, f32[3,3,16,128]{3,2,1,0:T(8,128)S(1)}, u32[]{:S(2)}, u32[]{:S(2)}) collective-permute-start(f32[3,3,16,128]{3,2,1,0:T(8,128)S(1)} %get-tuple-element.19), channel_id=1, source_target_pairs={{8,0},{16,8},{24,16},{32,24},{40,32},{48,40},{56,48},{64,56},{72,6... | collective-permute-start | bytes 221192 | tf_op jit(solution)/shard_map/ppermute | solution.py:367
  97.2 0.0 collective-permute-done.2.low_ref
  97.2 7.3 %collective-permute-done.3.high_ref = f32[3,3,16,128]{3,2,1,0:T(8,128)S(1)} collective-permute-done((f32[3,3,16,128]{3,2,1,0:T(8,128)S(1)}, f32[3,3,16,128]{3,2,1,0:T(8,128)S(1)}, u32[]{:S(2)}, u32[]{:S(2)}) %collective-permute-start.3) | collective-permute-done | bytes 73760 | tf_op jit(solution)/shard_map/ppermute | solution.py:367
  104.6 1.3 collective-permute-start.5
  105.9 4.0 %collective-permute-start.4 = (f32[3,14,8,128]{3,2,1,0:T(8,128)S(1)}, f32[3,14,8,128]{3,2,1,0:T(8,128)S(1)}, u32[]{:S(2)}, u32[]{:S(2)}) collective-permute-start(f32[3,14,8,128]{3,2,1,0:T(8,128)S(1)} %get-tuple-element.24), channel_id=1, source_target_pairs={{0,1},{1,2},{2,3},{3,4},{4,5},{5,6},{6,7},{8,9},{9,10},{10,11},{11... | collective-permute-start | bytes 516104 | tf_op jit(solution)/shard_map/ppermute | solution.py:367
  109.9 0.1 pad_add_fusion.place_ref
  110.0 0.8 collective-permute-done.5.right_ref
  110.7 1.5 %collective-permute-done.4.left_ref = f32[3,14,8,128]{3,2,1,0:T(8,128)S(1)} collective-permute-done((f32[3,14,8,128]{3,2,1,0:T(8,128)S(1)}, f32[3,14,8,128]{3,2,1,0:T(8,128)S(1)}, u32[]{:S(2)}, u32[]{:S(2)}) %collective-permute-start.4) | collective-permute-done | bytes 172064 | tf_op jit(solution)/shard_map/ppermute | solution.py:367
  112.2 0.0 copy-done
  112.2 6.7 %shard_map.99 = f32[8,3,8,16,128]{4,3,2,1,0:T(8,128)} custom-call(s32[4]{0:T(128)S(1)} %pad_add_fusion.place_ref, f32[3,8,32,128]{3,2,1,0:T(8,128)S(1)} %copy-done, f32[3,4,32,128]{3,2,1,0:T(8,128)S(1)} %collective-permute-done.below_any.below_ref, f32[3,4,32,128]{3,2,1,0:T(8,128)S(1)} %collective-permute-done.1.above_any.above_ref, ...), custom_call_target="tpu_custom_call" | custom-call | flops 6000000000 | bytes 21600000 | tf_op jit(solution)/shard_map/pallas_call | solution.py:443
  118.9 5.5 %all-to-all-start.3 = ((f32[8,3,8,16,128]{4,3,2,1,0:T(8,128)}), f32[8,3,8,16,128]{4,3,2,1,0:T(8,128)S(1)}, u32[]{:S(2)}, u32[]{:S(2)}) async-start(f32[8,3,8,16,128]{4,3,2,1,0:T(8,128)} %shard_map.99), calls=%async_computation.3 | async-start | bytes 3145728 | tf_op jit(solution)/shard_map/all_to_all | solution.py:454
  124.5 4.3 %shard_map.101 = f32[8,128,128]{2,1,0:T(8,128)} custom-call(f32[128,8,128]{2,1,0:T(8,128)S(1)} %bitcast.10), custom_call_target="tpu_custom_call" | custom-call | flops 3000000000 | bytes 10800000 | tf_op jit(solution)/shard_map/pallas_call | solution.py:428
  128.7 14.0 %all-to-all-done.3.parts_ref = f32[8,3,8,16,128]{4,3,2,1,0:T(8,128)S(1)} async-done(((f32[8,3,8,16,128]{4,3,2,1,0:T(8,128)}), f32[8,3,8,16,128]{4,3,2,1,0:T(8,128)S(1)}, u32[]{:S(2)}, u32[]{:S(2)}) %all-to-all-start.3) | async-done | bytes 1572896 | tf_op jit(solution)/shard_map/all_to_all | solution.py:454
  142.7 1.2 shard_map.100
  (4 shorter events, 0.1 us)
Async XLA Ops:
  7.8 12.9 %all-to-all-start = ((f32[8,16,8,128]{3,2,1,0:T(8,128)}), f32[8,16,8,128]{3,2,1,0:T(8,128)S(1)}, u32[]{:S(2)}, u32[]{:S(2)}) async-start(f32[8,16,8,128]{3,2,1,0:T(8,128)} %bitcast.14), calls=%async_computation | async-start | bytes 1048576 | tf_op jit(solution)/shard_map/all_to_all | solution.py:397
  21.5 36.3 %all-to-all-start.1 = ((f32[8,16,8,128]{3,2,1,0:T(8,128)}), f32[8,16,8,128]{3,2,1,0:T(8,128)S(1)}, u32[]{:S(2)}, u32[]{:S(2)}) async-start(f32[8,16,8,128]{3,2,1,0:T(8,128)} %get-tuple-element.14), calls=%async_computation.1 | async-start | bytes 1048576 | tf_op jit(solution)/shard_map/all_to_all | solution.py:420
  26.7 31.1 %copy-start.1 = (f32[3,16384]{1,0:T(4,128)S(1)}, f32[3,16384]{1,0:T(4,128)}, u32[]{:S(2)}) copy-start(f32[3,16384]{1,0:T(4,128)} %frac_ref.1) | copy-start | bytes 589828
  26.7 31.1 %copy-start.2 = (s32[16384]{0:T(1024)S(1)}, s32[16384]{0:T(1024)}, u32[]{:S(2)}) copy-start(s32[16384]{0:T(1024)} %param.10) | copy-start | bytes 196612
  26.7 31.1 %copy-start.3 = (s32[128]{0:T(128)S(1)}, s32[128]{0:T(128)}, u32[]{:S(2)}) copy-start(s32[128]{0:T(128)} %brick_ref.1) | copy-start | bytes 1540
  46.0 10.6 %collective-permute-start.1 = (f32[3,4,32,128]{3,2,1,0:T(8,128)S(1)}, f32[3,4,32,128]{3,2,1,0:T(8,128)S(1)}, u32[]{:S(2)}, u32[]{:S(2)}) collective-permute-start(f32[3,4,32,128]{3,2,1,0:T(8,128)S(1)} %get-tuple-element.21), channel_id=1, source_target_pairs={{8,0},{16,8},{24,16},{32,24},{40,32},{48,40},{56,48},{64,56},{72,6... | collective-permute-start | bytes 589832 | tf_op jit(solution)/shard_map/ppermute | solution.py:367
  49.0 8.8 %collective-permute-start = (f32[3,4,32,128]{3,2,1,0:T(8,128)S(1)}, f32[3,4,32,128]{3,2,1,0:T(8,128)S(1)}, u32[]{:S(2)}, u32[]{:S(2)}) collective-permute-start(f32[3,4,32,128]{3,2,1,0:T(8,128)S(1)} %get-tuple-element.22), channel_id=1, source_target_pairs={{0,8},{8,16},{16,24},{24,32},{32,40},{40,48},{48,56},{56,64},{64,7... | collective-permute-start | bytes 589832 | tf_op jit(solution)/shard_map/ppermute | solution.py:367
  57.8 1.0 copy-start.4
  92.4 19.8 %copy-start = (f32[3,8,32,128]{3,2,1,0:T(8,128)S(1)}, f32[3,8,32,128]{3,2,1,0:T(8,128)}, u32[]{:S(2)}) copy-start(f32[3,8,32,128]{3,2,1,0:T(8,128)} %get-tuple-element.12.window_ref) | copy-start | bytes 1179652
  92.7 4.5 %collective-permute-start.2 = (f32[3,3,16,128]{3,2,1,0:T(8,128)S(1)}, f32[3,3,16,128]{3,2,1,0:T(8,128)S(1)}, u32[]{:S(2)}, u32[]{:S(2)}) collective-permute-start(f32[3,3,16,128]{3,2,1,0:T(8,128)S(1)} %get-tuple-element.18), channel_id=1, source_target_pairs={{0,8},{8,16},{16,24},{24,32},{32,40},{40,48},{48,56},{56,64},{64,7... | collective-permute-start | bytes 221192 | tf_op jit(solution)/shard_map/ppermute | solution.py:367
  95.3 9.3 %collective-permute-start.3 = (f32[3,3,16,128]{3,2,1,0:T(8,128)S(1)}, f32[3,3,16,128]{3,2,1,0:T(8,128)S(1)}, u32[]{:S(2)}, u32[]{:S(2)}) collective-permute-start(f32[3,3,16,128]{3,2,1,0:T(8,128)S(1)} %get-tuple-element.19), channel_id=1, source_target_pairs={{8,0},{16,8},{24,16},{32,24},{40,32},{48,40},{56,48},{64,56},{72,6... | collective-permute-start | bytes 221192 | tf_op jit(solution)/shard_map/ppermute | solution.py:367
  104.6 6.2 %collective-permute-start.5 = (f32[3,14,8,128]{3,2,1,0:T(8,128)S(1)}, f32[3,14,8,128]{3,2,1,0:T(8,128)S(1)}, u32[]{:S(2)}, u32[]{:S(2)}) collective-permute-start(f32[3,14,8,128]{3,2,1,0:T(8,128)S(1)} %get-tuple-element.23), channel_id=1, source_target_pairs={{1,0},{2,1},{3,2},{4,3},{5,4},{6,5},{7,6},{9,8},{10,9},{11,10},{12... | collective-permute-start | bytes 516104 | tf_op jit(solution)/shard_map/ppermute | solution.py:367
  105.9 6.3 %collective-permute-start.4 = (f32[3,14,8,128]{3,2,1,0:T(8,128)S(1)}, f32[3,14,8,128]{3,2,1,0:T(8,128)S(1)}, u32[]{:S(2)}, u32[]{:S(2)}) collective-permute-start(f32[3,14,8,128]{3,2,1,0:T(8,128)S(1)} %get-tuple-element.24), channel_id=1, source_target_pairs={{0,1},{1,2},{2,3},{3,4},{4,5},{5,6},{6,7},{8,9},{9,10},{10,11},{11... | collective-permute-start | bytes 516104 | tf_op jit(solution)/shard_map/ppermute | solution.py:367
  118.9 23.8 %all-to-all-start.3 = ((f32[8,3,8,16,128]{4,3,2,1,0:T(8,128)}), f32[8,3,8,16,128]{4,3,2,1,0:T(8,128)S(1)}, u32[]{:S(2)}, u32[]{:S(2)}) async-start(f32[8,3,8,16,128]{4,3,2,1,0:T(8,128)} %shard_map.99), calls=%async_computation.3 | async-start | bytes 3145728 | tf_op jit(solution)/shard_map/all_to_all | solution.py:454

commit v2 on v1

v2 whole, which is shorter than its diff:
```python
import functools

import jax
import jax.numpy as jnp
from jax import lax
from jax.experimental import pallas as pl
from jax.experimental.pallas import tpu as pltpu
from jax.sharding import PartitionSpec as P

BLOCK = 128
LANES = 128
EPS_MIN = 0.35
FLOW_POWER = -0.2
DRAG_POWER = -2.65
VISCOSITY = 1.2
TIME_STEP = 0.05
ITERS = 4
UNROLL = 16
F32 = jnp.float32
PARAMS = pltpu.CompilerParams(vmem_limit_bytes=16 * 1024 * 1024)
FULL = pltpu.CompilerParams(vmem_limit_bytes=60 * 1024 * 1024)
VMEM = pl.BlockSpec(memory_space=pltpu.VMEM)
SMEM = pl.BlockSpec(memory_space=pltpu.SMEM)
HBM = pl.BlockSpec(memory_space=pltpu.HBM)
ANY = pl.BlockSpec(memory_space=pl.ANY)


def transpose_granules(tiles, lane):
    for bit in (1, 2, 4):
        shift = 8 * bit
        high = (lane & shift) != 0
        new = list(tiles)
        for a in range(8):
            if a & bit:
                continue
            b = a | bit
            va, vb = tiles[a], tiles[b]
            new[a] = jnp.where(high, pltpu.roll(vb, shift, 1), va)
            new[b] = jnp.where(high, vb, pltpu.roll(va, LANES - shift, 1))
        tiles = new
    return tiles


def fetch(pairs, sems):
    copies = [pltpu.make_async_copy(a, b, sems.at[i]) for i, (a, b) in enumerate(pairs)]
    for copy in copies:
        copy.start()
    return copies


def lanes_iota():
    return lax.broadcasted_iota(jnp.int32, (8, LANES), 1)


def rows_iota():
    return lax.broadcasted_iota(jnp.int32, (8, LANES), 0)


def spread(row):
    return jnp.broadcast_to(row, (8, LANES))


def particles(base_ref, frac_ref, block):
    at = pl.ds(pl.multiple_of(block * BLOCK, BLOCK), BLOCK)
    base = spread(base_ref[pl.ds(block, 1), :])
    fz = spread(frac_ref[0:1, at])
    fx = spread(frac_ref[1:2, at])
    fy = spread(frac_ref[2:3, at])
    return at, base >> 6, (base >> 3) & 7, base & 7, fz, fx, fy


def axis_weights(rows, first, frac):
    zero = jnp.zeros_like(frac)
    return jnp.where(rows == first, 1.0 - frac, jnp.where(rows == first + 1, frac, zero))


def halves(value):
    high = value.astype(jnp.bfloat16).astype(F32)
    return high, value - high


def plane_weights(rows, zb, yb, fz, fy):
    ky = axis_weights(rows, yb, fy)
    zero = jnp.zeros_like(fz)
    at = [zb == z for z in range(7)]
    parts = []
    for here, above in zip(halves((1.0 - fz) * ky), halves(fz * ky)):
        for z in range(8):
            part = zero if z == 0 else jnp.where(at[z - 1], above, zero)
            parts.append(part if z == 7 else jnp.where(at[z], here, part))
    return jnp.concatenate(parts, axis=0).astype(jnp.bfloat16)


def split_rows(parts):
    full = jnp.concatenate(parts, axis=0)
    high = full.astype(jnp.bfloat16).astype(F32)
    return jnp.concatenate([high, full - high], axis=0).astype(jnp.bfloat16)


def deposit(parts, weights):
    left = split_rows(parts)
    both = lax.dot_general(
        left, weights, (((1,), (1,)), ((), ())), preferred_element_type=F32
    )
    half = both.shape[0] // 2
    both = both[:half] + both[half:]
    return both + pltpu.roll(both, 64, 1)


def corner_terms(zb, yb, fz, fy, offset):
    index = (zb << 3) + yb + offset
    gz, gy = 1.0 - fz, 1.0 - fy
    return (
        (index, gz * gy),
        (index + 1, gz * fy),
        (index + 8, fz * gy),
        (index + 9, fz * fy),
    )


def interpolate(tile, kx, corners):
    total = None
    for index, weight in corners:
        term = weight * jnp.take_along_axis(tile, index, axis=1, mode="promise_in_bounds")
        total = term if total is None else total + term
    return jnp.sum(kx * total, axis=0, keepdims=True)


def brick_place(brick):
    return brick >> 4, brick & 7, (brick >> 3) & 1


def solid_kernel(
    brick_hbm, base_hbm, frac_hbm, pvol_hbm, out_ref, brick_ref, base_ref, frac_ref, pvol_ref, sems
):
    copies = fetch(
        [(brick_hbm, brick_ref), (base_hbm, base_ref), (frac_hbm, frac_ref), (pvol_hbm, pvol_ref)],
        sems,
    )
    out_ref[...] = jnp.zeros_like(out_ref)
    for copy in copies:
        copy.wait()
    rows, lane = rows_iota(), lanes_iota()

    def step(number, carry):
        found = []
        for k in range(UNROLL):
            block = number * UNROLL + k
            _, zb, xb, yb, fz, fx, fy = particles(base_ref, frac_ref, block)
            kx = axis_weights(rows, xb, fx) * spread(pvol_ref[pl.ds(block, 1), :])
            found.append(deposit([kx], plane_weights(rows, zb, yb, fz, fy)))
        for k in range(UNROLL):
            tx, t3, t1 = brick_place(brick_ref[number * UNROLL + k])
            tile = tx * 8 + t3
            out_ref[tile] += jnp.where((lane >> 6) == t1, found[k], 0.0)
        return carry

    lax.fori_loop(0, base_ref.shape[0] // UNROLL, step, 0)


def eps_kernel(parts_ref, out_ref, copies_ref):
    total = parts_ref[0]
    for j in range(1, parts_ref.shape[0]):
        total = total + parts_ref[j]
    total = jnp.maximum(1.0 - total, EPS_MIN)
    out_ref[...] = total
    for j in range(copies_ref.shape[0]):
        copies_ref[j] = total


def slip_kernel(
    first, count,
    after_any, brick_hbm, base_hbm, frac_hbm, pvel_hbm, coef_hbm, pvol_hbm, velocity_hbm,
    out_ref,
    brick_ref, base_ref, frac_ref, pvel_ref, coef_ref, pvol_ref, velocity_ref, table_ref, sems,
):
    some = pl.ds(first, count)
    wide = pl.ds(first * BLOCK, count * BLOCK)
    copies = fetch(
        [
            (velocity_hbm, velocity_ref),
            (brick_hbm, brick_ref),
            (base_hbm.at[some], base_ref),
            (frac_hbm.at[:, wide], frac_ref),
            (pvel_hbm.at[:, wide], pvel_ref),
            (coef_hbm.at[some], coef_ref),
            (pvol_hbm.at[some], pvol_ref),
        ],
        sems,
    )
    rows, lane = rows_iota(), lanes_iota()
    tiles_x = velocity_ref.shape[2] // 8

    def convert(number, carry):
        for k in range(2):
            tx = number * 2 + k
            at = pl.ds(pl.multiple_of(tx * 8, 8), 8)
            for c in range(3):
                tiles = transpose_granules([velocity_ref[c, z, at, :] for z in range(8)], lane)
                for t3 in range(8):
                    table_ref[(tx * 3 + c) * 8 + t3] = tiles[t3]
        return carry

    copies[0].wait()
    lax.fori_loop(0, tiles_x // 2, convert, 0)
    for copy in copies[1:]:
        copy.wait()

    def step(number, carry):
        for k in range(UNROLL):
            block = number * UNROLL + k
            at, zb, xb, yb, fz, fx, fy = particles(base_ref, frac_ref, block)
            tx, t3, t1 = brick_place(brick_ref[first + block])
            kx = axis_weights(rows, xb, fx)
            corners = corner_terms(zb, yb, fz, fy, t1 * 64)
            rel = [
                interpolate(table_ref[(tx * 3 + c) * 8 + t3], kx, corners) - pvel_ref[c : c + 1, at]
                for c in range(3)
            ]
            speed = rel[0] * rel[0] + rel[1] * rel[1] + rel[2] * rel[2]
            factor = coef_ref[pl.ds(block, 1), :] * pvol_ref[pl.ds(block, 1), :]
            factor = factor * jnp.exp(FLOW_POWER * jnp.log(speed + 0.01))
            for c in range(3):
                out_ref[c : c + 1, at] = factor * rel[c]
        return carry

    lax.fori_loop(0, count // UNROLL, step, 0)


def pack_halo(rows, tiles):
    a, b, c, d = tiles
    middle = jnp.logical_or(rows == 3, rows == 4)
    first = jnp.where(middle, pltpu.roll(d, 3, 0), a)
    second = jnp.where(rows == 3, pltpu.roll(d, 1, 0), jnp.where(rows == 4, pltpu.roll(d, 7, 0), b))
    third = jnp.where(middle, pltpu.roll(d, 5, 0), c)
    return first, second, third


def unpack_halo(rows, tiles):
    a, b, c = tiles
    inner = jnp.where(rows == 2, pltpu.roll(b, 7, 0), pltpu.roll(b, 1, 0))
    d = jnp.where(rows < 2, pltpu.roll(a, 5, 0), jnp.where(rows > 5, pltpu.roll(c, 3, 0), inner))
    return a, b, c, d


def drag_kernel(
    brick_ref, base_ref, frac_ref, slip_a_hbm, slip_b_hbm, eps_ref,
    drag_ref, out_hbm, tick_ref,
    force_ref, slip_a_ref, slip_b_ref, sems,
):
    subs = force_ref.shape[0]
    rows, lane = rows_iota(), lanes_iota()
    slips = fetch([(slip_a_hbm, slip_a_ref), (slip_b_hbm, slip_b_ref)], sems)
    for j in range(subs):
        force_ref[j, 0:48] = jnp.zeros((48, 8, LANES), F32)
    halves_of = ((slip_a_ref, 0), (slip_b_ref, slip_a_ref.shape[1] // BLOCK))
    for copy in slips:
        copy.wait()

    for slip_ref, start in halves_of:

        def step(number, carry, slip_ref=slip_ref, start=start):
            found = []
            for k in range(UNROLL):
                inner = number * UNROLL + k
                block = inner + start
                at, zb, xb, yb, fz, fx, fy = particles(base_ref, frac_ref, block)
                inner_at = pl.ds(pl.multiple_of(inner * BLOCK, BLOCK), BLOCK)
                tx, t3, t1 = brick_place(brick_ref[block])
                kx = axis_weights(rows, xb, fx)
                eps = interpolate(eps_ref[tx * 8 + t3], kx, corner_terms(zb, yb, fz, fy, t1 * 64))
                factor = jnp.exp(DRAG_POWER * jnp.log(eps))
                parts = []
                for c in range(3):
                    force = factor * slip_ref[c : c + 1, inner_at]
                    drag_ref[c : c + 1, at] = force
                    parts.append(kx * spread(force))
                found.append(deposit(parts, plane_weights(rows, zb, yb, fz, fy)))
            for k in range(UNROLL):
                tx, t3, t1 = brick_place(brick_ref[number * UNROLL + k + start])
                mine = (lane >> 6) == t1
                for c in range(3):
                    tile = (tx & 1) * 24 + c * 8 + t3
                    force_ref[tx >> 1, tile] += jnp.where(mine, found[k][8 * c : 8 * c + 8], 0.0)
            return carry

        lax.fori_loop(0, slip_ref.shape[1] // BLOCK // UNROLL, step, 0)
    copies = fetch([(force_ref.at[j, 0:48], out_hbm.at[j, 0:48]) for j in range(subs)], sems)
    zero = jnp.zeros((8, LANES), F32)
    more = []
    for j in range(subs):
        for quad in range(6):
            tiles = []
            for k in range(4):
                at = quad * 4 + k
                after = force_ref[j + 1, at] if j + 1 < subs else zero
                before = force_ref[j - 1, 24 + at] if j > 0 else zero
                tiles.append(jnp.where(rows < 4, after, before))
            for k, tile in enumerate(pack_halo(rows, tiles)):
                force_ref[j, 48 + quad * 3 + k] = tile
        copy = pltpu.make_async_copy(
            force_ref.at[j, 48:66], out_hbm.at[j, 48:66], sems.at[subs + j]
        )
        copy.start()
        more.append(copy)
    tick_ref[...] = zero
    for copy in copies + more:
        copy.wait()


def source_kernel(sub_ref, parts_ref, eps_ref, first_any, void_any, own_ref, low_ref, high_ref):
    lane, rows = lanes_iota(), rows_iota()
    sub = sub_ref[0]
    tiles_x = eps_ref.shape[0] // 8
    after = jnp.minimum(sub * 2 + 2, tiles_x - 1) * 8
    before = jnp.maximum(sub * 2 - 1, 0) * 8

    def summed(at):
        total = parts_ref[0, at]
        for j in range(1, parts_ref.shape[0]):
            total = total + parts_ref[j, at]
        return total

    for t in range(3):
        for c in range(3):
            if t < 2:
                forces = [summed(t * 24 + c * 8 + t3) for t3 in range(8)]
            else:
                forces = []
                for quad in (2 * c, 2 * c + 1):
                    forces += unpack_halo(rows, [summed(48 + quad * 3 + k) for k in range(3)])
            tiles = []
            for t3 in range(8):
                if t < 2:
                    eps = eps_ref[(sub * 2 + t) * 8 + t3]
                else:
                    eps = jnp.where(rows < 4, eps_ref[after + t3], eps_ref[before + t3])
                tiles.append(-forces[t3] / eps)
            tiles = transpose_granules(tiles, lane)
            first = 8 * (t + 1) % 24
            for z in range(8):
                own_ref[c, z, first : first + 8, :] = tiles[z]
                if z < 3:
                    low_ref[c, z, first : first + 8, :] = tiles[z]
                if z >= 5:
                    high_ref[c, z - 5, first : first + 8, :] = tiles[z]


def window_kernel(sub_ref, after_any, velocity_hbm, out_ref, top_ref, bottom_ref, sems):
    depth = velocity_hbm.shape[1]
    tiles_x = velocity_hbm.shape[2] // 8
    pairs, inside = [], []
    for r in range(4):
        want = sub_ref[0] * 2 + r - 1
        inside.append(jnp.logical_and(want >= 0, want < tiles_x))
        at = pl.ds(pl.multiple_of(jnp.clip(want, 0, tiles_x - 1) * 8, 8), 8)
        pairs.append((velocity_hbm.at[:, :, at, :], out_ref.at[:, :, 8 * r : 8 * r + 8, :]))
    for copy in fetch(pairs, sems):
        copy.wait()
    for r in range(4):
        at = slice(8 * r, 8 * r + 8)
        rows = jnp.where(inside[r], out_ref[:, :, at, :], 0.0)
        out_ref[:, :, at, :] = rows
        top_ref[:, :, at, :] = rows[:, depth - 4 :]
        bottom_ref[:, :, at, :] = rows[:, :4]


def void_kernel(after_any, eps_ref, out_ref, tick_ref):
    tick_ref[...] = jnp.zeros_like(tick_ref)
    lane = lanes_iota()

    def convert(number, carry):
        for k in range(4):
            tx = number * 4 + k
            tiles = transpose_granules([eps_ref[tx * 8 + t3] for t3 in range(8)], lane)
            for z in range(8):
                out_ref[z, pl.ds(pl.multiple_of(tx * 8, 8), 8), :] = tiles[z]
        return carry

    lax.fori_loop(0, out_ref.shape[1] // 32, convert, 0)


def edges(slab, sub, planes, width):
    row = lax.broadcasted_iota(jnp.int32, (32, LANES), 0) + sub * 16 - 8
    inside_x = jnp.logical_and(row >= 0, row < width)

    def keep(z):
        height = slab * 8 - 4 + z
        return jnp.logical_and(inside_x, jnp.logical_and(height >= 0, height < planes))

    return keep


def unforced(old, z, lane):
    shear = None
    centres, laps = [], []
    for c in range(3):
        centre = old[c, z]
        upper = old[c, z + 1]
        lower = old[c, z - 1]
        east = pltpu.roll(centre, 31, 0)
        west = pltpu.roll(centre, 1, 0)
        north = jnp.where(lane == LANES - 1, 0.0, pltpu.roll(centre, LANES - 1, 1))
        south = jnp.where(lane == 0, 0.0, pltpu.roll(centre, 1, 1))
        term = (upper - centre) ** 2 + (east - centre) ** 2 + (north - centre) ** 2
        shear = term if shear is None else shear + term
        centres.append(centre)
        laps.append(upper + lower + east + west + north + south - 6.0 * centre)
    viscous = (TIME_STEP * VISCOSITY) * jnp.exp(FLOW_POWER * jnp.log(shear + 0.01))
    return [centres[c] + viscous * laps[c] for c in range(3)]


def first_kernel(window_ref, below_ref, above_ref, out_ref, tick_ref, old):
    tick_ref[...] = jnp.zeros_like(tick_ref)
    old[:, 0:4] = below_ref[...]
    old[:, 4:12] = window_ref[...]
    old[:, 12:16] = above_ref[...]
    lane = lax.broadcasted_iota(jnp.int32, (32, LANES), 1)

    def plane(number, carry):
        for k in range(2):
            z = number * 2 + k
            moved = unforced(old, z + 1, lane)
            for c in range(3):
                out_ref[c, z] = moved[c]
        return carry

    lax.fori_loop(0, 7, plane, 0)


def stencil_kernel(
    place_ref, first_ref, own_ref, low_ref, high_ref, out_ref, even, odd, source
):
    keep = edges(place_ref[0], place_ref[1], place_ref[2], place_ref[3])
    lane = lax.broadcasted_iota(jnp.int32, (32, LANES), 1)
    for part, planes in ((low_ref, slice(0, 3)), (own_ref, slice(3, 11)), (high_ref, slice(11, 14))):
        source[:, planes, 0:24, :] = part[...]
        source[:, planes, 24:32, :] = part[:, :, 0:8, :]

    def first(number, carry):
        for k in range(2):
            z = number * 2 + k
            inside = keep(z + 1)
            for c in range(3):
                moved = first_ref[c, z] + TIME_STEP * source[c, z]
                odd[c, z + 1] = jnp.where(inside, moved, 0.0)
        return carry

    lax.fori_loop(0, 7, first, 0)
    buffers = (even, odd)
    for step in range(1, ITERS):
        old, new = buffers[step % 2], buffers[(step + 1) % 2]

        def plane(number, carry, old=old, new=new, step=step):
            for k in range(2):
                z = number * 2 + k + step + 1
                moved = unforced(old, z, lane)
                inside = keep(z)
                for c in range(3):
                    forced = moved[c] + TIME_STEP * source[c, z - 1]
                    new[c, z] = jnp.where(inside, forced, 0.0)
            return carry

        lax.fori_loop(0, 7 - step, plane, 0)
    for j in range(out_ref.shape[0]):
        out_ref[j] = even[:, 4:12, 8:24, :]


def place_kernel(parts_ref, out_ref, sems):
    rows = parts_ref.shape[3]
    copies = fetch(
        [
            (parts_ref.at[j], out_ref.at[:, :, pl.ds(j * rows, rows), :])
            for j in range(parts_ref.shape[0])
        ],
        sems,
    )
    for copy in copies:
        copy.wait()


def call(kernel, out_shapes, ins, scratch=(), outs=None, us=1.0, params=PARAMS):
    return pl.pallas_call(
        kernel,
        out_shape=[jax.ShapeDtypeStruct(s, F32) for s in out_shapes],
        in_specs=ins,
        out_specs=outs or [VMEM] * len(out_shapes),
        scratch_shapes=list(scratch),
        compiler_params=params,
        cost_estimate=pl.CostEstimate(flops=int(us * 1e9), bytes_accessed=int(us * 3.6e6), transcendentals=0),
    )


def shift(x, axis, up):
    peers = lax.axis_size(axis)
    pairs = [(i, i + 1) if up else (i + 1, i) for i in range(peers - 1)]
    return lax.ppermute(x, axis, pairs)


def body(velocity, part_vel, fraction, base_cell, drag_coeff, part_volume, brick_of_block):
    depth, width_x = velocity.shape[1], velocity.shape[2]
    blocks = brick_of_block.shape[0]
    subs = lax.axis_size("sub")
    slab = lax.axis_index("slab").astype(jnp.int32)
    sub = lax.axis_index("sub").astype(jnp.int32)
    tiles_x = width_x // 8
    tiles = tiles_x * 8
    share = tiles // subs
    base = base_cell.reshape(blocks, BLOCK)
    coef = drag_coeff.reshape(blocks, BLOCK)
    pvol = part_volume.reshape(blocks, BLOCK)

    particles_vmem = [
        pltpu.SMEM((blocks,), jnp.int32),
        pltpu.VMEM((blocks, BLOCK), jnp.int32),
        pltpu.VMEM((3, blocks * BLOCK), F32),
    ]
    row_vmem = pltpu.VMEM((blocks, BLOCK), F32)
    (solid,) = call(
        solid_kernel,
        [(tiles, 8, LANES)],
        [HBM] * 4,
        particles_vmem + [row_vmem, pltpu.SemaphoreType.DMA((4,))],
        us=5.0,
        params=FULL,
    )(brick_of_block, base, fraction, pvol)
    solid_parts = lax.all_to_all(solid.reshape(subs, share, 8, LANES), "sub", 0, 0)
    sub_at = sub.reshape(1)
    half = blocks // 2

    def slip_of(first, after):
        (slip,) = call(
            functools.partial(slip_kernel, first, half),
            [(3, half * BLOCK)],
            [ANY] + [HBM] * 7,
            [
                pltpu.SMEM((blocks,), jnp.int32),
                pltpu.VMEM((half, BLOCK), jnp.int32),
                pltpu.VMEM((3, half * BLOCK), F32),
                pltpu.VMEM((3, half * BLOCK), F32),
                pltpu.VMEM((half, BLOCK), F32),
                pltpu.VMEM((half, BLOCK), F32),
                pltpu.VMEM(velocity.shape, F32),
                pltpu.VMEM((3 * tiles, 8, LANES), F32),
                pltpu.SemaphoreType.DMA((7,)),
            ],
            us=5.0,
            params=FULL,
        )(after, brick_of_block, base, fraction, part_vel, coef, pvol, velocity)
        return slip

    slip_a = slip_of(0, solid)
    eps_own, eps_copies = call(
        eps_kernel, [(share, 8, LANES), (subs, share, 8, LANES)], [VMEM], us=0.5
    )(solid_parts)
    slip_b = slip_of(half, eps_own)
    eps = lax.all_to_all(eps_copies, "sub", 0, 0).reshape(tiles, 8, LANES)
    drag, force, drag_tick = call(
        drag_kernel,
        [(3, blocks * BLOCK), (subs, 66, 8, LANES), (8, LANES)],
        [SMEM, VMEM, VMEM, HBM, HBM, VMEM],
        [
            pltpu.VMEM((subs, 66, 8, LANES), F32),
            pltpu.VMEM((3, half * BLOCK), F32),
            pltpu.VMEM((3, half * BLOCK), F32),
            pltpu.SemaphoreType.DMA((2 * subs,)),
        ],
        outs=[VMEM, HBM, VMEM],
        us=6.0,
        params=FULL,
    )(brick_of_block, base, fraction, slip_a, slip_b, eps)
    force_parts = lax.all_to_all(force, "sub", 0, 0)
    window, top, bottom = call(
        window_kernel,
        [(3, depth, 32, LANES), (3, 4, 32, LANES), (3, 4, 32, LANES)],
        [SMEM, ANY, HBM],
        [pltpu.SemaphoreType.DMA((4,))],
    )(sub_at, drag_tick, velocity)
    below = shift(top, "slab", True)
    above = shift(bottom, "slab", False)
    voidfraction, void_tick = call(
        void_kernel, [(depth, width_x, LANES), (8, LANES)], [ANY, VMEM], us=2.0
    )(drag_tick, eps)
    first, first_tick = call(
        first_kernel,
        [(3, 14, 32, LANES), (8, LANES)],
        [VMEM] * 3,
        [pltpu.VMEM((3, 16, 32, LANES), F32)],
        us=1.0,
    )(window, below, above)

    rows = width_x // subs
    own, low_own, high_own = call(
        source_kernel,
        [(3, depth, 24, LANES), (3, 3, 24, LANES), (3, 3, 24, LANES)],
        [SMEM, VMEM, VMEM, ANY, ANY],
    )(sub_at, force_parts, eps, first_tick, void_tick)
    low = shift(high_own, "slab", True)
    high = shift(low_own, "slab", False)
    planes = depth * lax.axis_size("slab")
    place = jnp.stack([slab, sub, jnp.int32(planes), jnp.int32(width_x)])
    (moved,) = call(
        stencil_kernel,
        [(subs, 3, depth, rows, LANES)],
        [SMEM] + [VMEM] * 4,
        [
            pltpu.VMEM((3, 16, 32, LANES), F32),
            pltpu.VMEM((3, 16, 32, LANES), F32),
            pltpu.VMEM((3, 14, 32, LANES), F32),
        ],
        us=4.0,
    )(place, first, own, low, high)
    moved = lax.all_to_all(moved, "sub", 0, 0)
    (new_velocity,) = call(
        place_kernel,
        [velocity.shape],
        [ANY],
        [pltpu.SemaphoreType.DMA((subs,))],
        outs=[ANY],
    )(moved)
    return new_velocity, voidfraction, drag


def solution(mesh):
    in_specs = (
        P(None, "slab", None, None),
        P(None, ("slab", "sub")),
        P(None, ("slab", "sub")),
        P(("slab", "sub")),
        P(("slab", "sub")),
        P(("slab", "sub")),
        P(("slab", "sub")),
    )
    out_specs = (P(None, "slab", None, None), P("slab", None, None), P(None, ("slab", "sub")))
    return jax.shard_map(body, mesh=mesh, in_specs=in_specs, out_specs=out_specs, check_vma=False)
```

time: 146 us -> 116 us (0.79)
  Pallas kernels: 46.8 us -> 36.1 us
  starting transfers between devices: 34.8 us -> 25.2 us
  waiting for transfers between devices: 33.9 us -> 24.8 us
  blocking collectives: 25.5 us -> 22.5 us
  local copies, waits for them, and re-layouts: 2.07 us -> 4.42 us
    ppermute x6 -> x4, starting transfers between devices: 18.9 us -> 9.67 us  [shift(): return lax.ppermute(x, axis, pairs)]
    pallas_call x5 -> x8, Pallas kernels: 37.6 us -> 28.5 us  [the longest x2 13.5 us: slip_of(): call(functools.partial(slip_kernel, first, half), [(3, half * BLOCK)], [A...]
    all_to_all x1, waiting for transfers between devices: 7.81 us -> 1.03 us  [body(): lax.all_to_all(solid.reshape(subs, share, 8, LANES), 'sub', 0, 0)]
    all_to_all x1, waiting for transfers between devices: 14 us -> 9.8 us  [body(): force_parts = lax.all_to_all(force, 'sub', 0, 0)]
    unnamed x12 -> x18, local copies, waits for them, and re-layouts: 0.99 us -> 4.42 us
    all_to_all x1, blocking collectives: 25.5 us -> 22.5 us  [body(): moved = lax.all_to_all(moved, 'sub', 0, 0)]
    pallas_call x1, Pallas kernels: 7.12 us -> 5.58 us  [body(): call(solid_kernel, [(tiles, 8, LANES)], [HBM] * 4, particles_vmem + [row_...]
    ppermute x6 -> x4, waiting for transfers between devices: 12.1 us -> 13 us  [shift(): return lax.ppermute(x, axis, pairs)]
  transfers between devices with their start and end apart: 9 -> 7, of which waited for: 7 -> 5; matrix products, arithmetic and copies ran while one was open for 1% -> 0% of each run, Pallas kernels for 16% -> 14%
where the time goes in v2:
time: 116 us; the launch traced here: 114 us
  Pallas kernels  36.1 us (31%)
  starting transfers between devices  25.2 us (22%)
  waiting for transfers between devices  24.8 us (21%)
  blocking collectives  22.5 us (19%)
  local copies, waits for them, and re-layouts  4.42 us (4%)
    all_to_all x1, blocking collectives, body(): moved = lax.all_to_all(moved, 'sub', 0, 0)  22.5 us
    pallas_call x2, Pallas kernels, slip_of(): call(functools.partial(slip_kernel, first, half), [(3, half * BLOCK)], [A...  13.5 us
    ppermute x4, waiting for transfers between devices, shift(): return lax.ppermute(x, axis, pairs)  13 us
    all_to_all x1, waiting for transfers between devices, body(): force_parts = lax.all_to_all(force, 'sub', 0, 0)  9.8 us
    ppermute x4, starting transfers between devices, shift(): return lax.ppermute(x, axis, pairs)  9.67 us
    pallas_call x1, Pallas kernels, body(): call(drag_kernel, [(3, blocks * BLOCK), (subs, 66, 8, LANES), (8, LANES)]...  8.97 us
    pallas_call x1, Pallas kernels, body(): call(solid_kernel, [(tiles, 8, LANES)], [HBM] * 4, particles_vmem + [row_...  5.58 us
    all_to_all x1, starting transfers between devices, body(): eps = lax.all_to_all(eps_copies, 'sub', 0, 0).reshape(tiles, 8, LANES)  5.21 us
  transfers between devices with their start and end apart: 7, of which 5 were waited for; matrix products, arithmetic and copies ran while one was open for 0% of the time, Pallas kernels for 14%

profile of v2, /device:TPU:225, one launch (start us, length us, event | category | flops | bytes accessed | tf_op | source)
XLA Modules:
  0.0 114.1 jit_solution(16957960489235361094)
XLA Ops:
  0.6 5.6 %shard_map.94.after_any = f32[128,8,128]{2,1,0:T(8,128)} custom-call(s32[128]{0:T(128)} %brick_ref.1, s32[128,128]{1,0:T(8,128)} %bitcast.16, f32[3,16384]{1,0:T(4,128)} %frac_ref.1, f32[128,128]{1,0:T(8,128)} %bitcast.11), custom_call_target="tpu_custom_call" | custom-call | flops 5000000000 | bytes 18000000 | tf_op jit(solution)/shard_map/pallas_call | solution.py:519
  6.2 5.1 %all-to-all-start = ((f32[8,16,8,128]{3,2,1,0:T(8,128)}), f32[8,16,8,128]{3,2,1,0:T(8,128)S(1)}, u32[]{:S(2)}, u32[]{:S(2)}) async-start(f32[8,16,8,128]{3,2,1,0:T(8,128)} %bitcast.10), calls=%async_computation | async-start | bytes 1048576 | tf_op jit(solution)/shard_map/all_to_all | solution.py:527
  11.4 6.8 %shard_map.95.slip_a_hbm = f32[3,8192]{1,0:T(4,128)} custom-call(f32[128,8,128]{2,1,0:T(8,128)} %shard_map.94.after_any, s32[128]{0:T(128)} %brick_ref.1, s32[128,128]{1,0:T(8,128)} %bitcast.17, f32[3,16384]{1,0:T(4,128)} %frac_ref.1, f32[3,16384]{1,0:T(4,128)} %pvel_hbm.3, f32[128,128]{1,0:T(8,128)} %bitcast.14, f32[128,128]{1,0:T(8,128)} %bitcast.12, ...), custom_call_target="tpu_custom_call" | custom-call | flops 5000000000 | bytes 18000000 | tf_op jit(solution)/shard_map/pallas_call | solution.py:532
  18.1 1.0 all-to-all-done.parts_ref
  19.1 0.8 shard_map.96
  20.0 0.0 copy-start.7
  20.0 0.6 copy-done.7
  20.6 5.2 %all-to-all-start.1 = ((f32[8,16,8,128]{3,2,1,0:T(8,128)}), f32[8,16,8,128]{3,2,1,0:T(8,128)S(1)}, u32[]{:S(2)}, u32[]{:S(2)}) async-start(f32[8,16,8,128]{3,2,1,0:T(8,128)} %get-tuple-element.19), calls=%async_computation.1 | async-start | bytes 1048576 | tf_op jit(solution)/shard_map/all_to_all | solution.py:557
  25.8 6.7 %shard_map.97.slip_b_hbm = f32[3,8192]{1,0:T(4,128)} custom-call(f32[16,8,128]{2,1,0:T(8,128)} %copy-done.7, s32[128]{0:T(128)} %brick_ref.1, s32[128,128]{1,0:T(8,128)} %bitcast.18, f32[3,16384]{1,0:T(4,128)} %frac_ref.1, f32[3,16384]{1,0:T(4,128)} %pvel_hbm.3, f32[128,128]{1,0:T(8,128)} %bitcast.15, f32[128,128]{1,0:T(8,128)} %bitcast.13, ...), custom_call_target="tpu_custom_call" | custom-call | flops 5000000000 | bytes 18000000 | tf_op jit(solution)/shard_map/pallas_call | solution.py:532
  32.6 1.1 all-to-all-done.1
  33.6 0.0 copy-start
  33.6 0.8 copy-done
  34.4 9.0 %shard_map.98 = (f32[3,16384]{1,0:T(4,128)}, f32[8,66,8,128]{3,2,1,0:T(8,128)}, f32[8,128]{1,0:T(8,128)}) custom-call(s32[128]{0:T(128)} %brick_ref.1, s32[128,128]{1,0:T(8,128)} %bitcast.19, f32[3,16384]{1,0:T(4,128)} %frac_ref.1, f32[3,8192]{1,0:T(4,128)} %shard_map.95.slip_a_hbm, f32[3,8192]{1,0:T(4,128)} %shard_map.97.slip_b_hbm, f32[128,8,128]{2,1,0:T(8,128)} %bitcast.7), custom_call_target="tpu_custom_call" | custom-call | flops 6000000000 | bytes 21600000 | tf_op jit(solution)/shard_map/pallas_call | solution.py:558
  43.4 0.0 copy-start.8
  43.4 5.2 %all-to-all-start.2 = ((f32[8,66,8,128]{3,2,1,0:T(8,128)}), f32[8,66,8,128]{3,2,1,0:T(8,128)S(1)}, u32[]{:S(2)}, u32[]{:S(2)}) async-start(f32[8,66,8,128]{3,2,1,0:T(8,128)} %get-tuple-element.25), calls=%async_computation.2 | async-start | bytes 4325376 | tf_op jit(solution)/shard_map/all_to_all | solution.py:572
  48.6 0.0 copy-done.8
  48.6 0.0 copy-start.2
  48.6 1.4 %copy-done.2 = f32[3,8,128,128]{3,2,1,0:T(8,128)S(1)} copy-done((f32[3,8,128,128]{3,2,1,0:T(8,128)S(1)}, f32[3,8,128,128]{3,2,1,0:T(8,128)}, u32[]{:S(2)}) %copy-start.2) | copy-done | bytes 1572888
  50.0 0.0 copy-start.1
  50.0 0.2 shard_map.99
  50.2 0.0 copy-start.3
  50.2 0.7 copy-done.3
  51.0 2.2 %collective-permute-start = (f32[3,4,32,128]{3,2,1,0:T(8,128)S(1)}, f32[3,4,32,128]{3,2,1,0:T(8,128)S(1)}, u32[]{:S(2)}, u32[]{:S(2)}) collective-permute-start(f32[3,4,32,128]{3,2,1,0:T(8,128)S(1)} %get-tuple-element.22), channel_id=1, source_target_pairs={{0,8},{8,16},{16,24},{24,32},{32,40},{40,48},{48,56},{56,64},{64,7... | collective-permute-start | bytes 589832 | tf_op jit(solution)/shard_map/ppermute | solution.py:497
  53.2 2.8 %collective-permute-start.1 = (f32[3,4,32,128]{3,2,1,0:T(8,128)S(1)}, f32[3,4,32,128]{3,2,1,0:T(8,128)S(1)}, u32[]{:S(2)}, u32[]{:S(2)}) collective-permute-start(f32[3,4,32,128]{3,2,1,0:T(8,128)S(1)} %get-tuple-element.23), channel_id=1, source_target_pairs={{8,0},{16,8},{24,16},{32,24},{40,32},{48,40},{56,48},{64,56},{72,6... | collective-permute-start | bytes 589832 | tf_op jit(solution)/shard_map/ppermute | solution.py:497
  56.0 0.0 copy-done.1
  56.0 0.0 copy-start.4
  56.0 1.8 %shard_map.101 = (f32[8,128,128]{2,1,0:T(8,128)}, f32[8,128]{1,0:T(8,128)S(1)}) custom-call(f32[8,128]{1,0:T(8,128)S(1)} %copy-done.8, f32[128,8,128]{2,1,0:T(8,128)S(1)} %bitcast.8), custom_call_target="tpu_custom_call" | custom-call | flops 2000000000 | bytes 7200000 | tf_op jit(solution)/shard_map/pallas_call | solution.py:581
  57.8 0.0 collective-permute-done.below_ref
  57.8 6.1 %collective-permute-done.1.above_ref = f32[3,4,32,128]{3,2,1,0:T(8,128)S(1)} collective-permute-done((f32[3,4,32,128]{3,2,1,0:T(8,128)S(1)}, f32[3,4,32,128]{3,2,1,0:T(8,128)S(1)}, u32[]{:S(2)}, u32[]{:S(2)}) %collective-permute-start.1) | collective-permute-done | bytes 196640 | tf_op jit(solution)/shard_map/ppermute | solution.py:497
  63.9 0.0 copy-done.4
  63.9 0.9 shard_map.100
  64.8 0.0 copy-start.5
  64.8 0.8 copy-done.5
  65.7 9.8 %all-to-all-done.2.parts_ref = f32[8,66,8,128]{3,2,1,0:T(8,128)S(1)} async-done(((f32[8,66,8,128]{3,2,1,0:T(8,128)}), f32[8,66,8,128]{3,2,1,0:T(8,128)S(1)}, u32[]{:S(2)}, u32[]{:S(2)}) %all-to-all-start.2) | async-done | bytes 2162720 | tf_op jit(solution)/shard_map/all_to_all | solution.py:572
  75.5 0.0 copy-start.6
  75.5 0.4 shard_map.102
  75.9 1.9 %collective-permute-start.2 = (f32[3,3,24,128]{3,2,1,0:T(8,128)S(1)}, f32[3,3,24,128]{3,2,1,0:T(8,128)S(1)}, u32[]{:S(2)}, u32[]{:S(2)}) collective-permute-start(f32[3,3,24,128]{3,2,1,0:T(8,128)S(1)} %get-tuple-element.29), channel_id=1, source_target_pairs={{0,8},{8,16},{16,24},{24,32},{32,40},{40,48},{48,56},{56,64},{64,7... | collective-permute-start | bytes 331784 | tf_op jit(solution)/shard_map/ppermute | solution.py:497
  77.8 2.8 %collective-permute-start.3 = (f32[3,3,24,128]{3,2,1,0:T(8,128)S(1)}, f32[3,3,24,128]{3,2,1,0:T(8,128)S(1)}, u32[]{:S(2)}, u32[]{:S(2)}) collective-permute-start(f32[3,3,24,128]{3,2,1,0:T(8,128)S(1)} %get-tuple-element.30), channel_id=1, source_target_pairs={{8,0},{16,8},{24,16},{32,24},{40,32},{48,40},{56,48},{64,56},{72,6... | collective-permute-start | bytes 331784 | tf_op jit(solution)/shard_map/ppermute | solution.py:497
  80.6 0.1 pad_add_fusion.place_ref
  80.7 0.0 collective-permute-done.2.low_ref
  80.7 6.8 %collective-permute-done.3.high_ref = f32[3,3,24,128]{3,2,1,0:T(8,128)S(1)} collective-permute-done((f32[3,3,24,128]{3,2,1,0:T(8,128)S(1)}, f32[3,3,24,128]{3,2,1,0:T(8,128)S(1)}, u32[]{:S(2)}, u32[]{:S(2)}) %collective-permute-start.3) | collective-permute-done | bytes 110624 | tf_op jit(solution)/shard_map/ppermute | solution.py:497
  87.5 0.0 copy-done.6
  87.5 2.8 %shard_map.103 = f32[8,3,8,16,128]{4,3,2,1,0:T(8,128)S(1)} custom-call(s32[4]{0:T(128)S(1)} %pad_add_fusion.place_ref, f32[3,14,32,128]{3,2,1,0:T(8,128)S(1)} %copy-done.6, f32[3,8,24,128]{3,2,1,0:T(8,128)S(1)} %get-tuple-element.28.own_ref, f32[3,3,24,128]{3,2,1,0:T(8,128)S(1)} %collective-permute-done.2.low_ref, ...), custom_call_target="tpu_custom_call" | custom-call | flops 4000000000 | bytes 14400000 | tf_op jit(solution)/shard_map/pallas_call | solution.py:602
  90.3 22.5 %all_to_all.20.parts_ref = f32[8,3,8,16,128]{4,3,2,1,0:T(8,128)S(1)} all-to-all(f32[8,3,8,16,128]{4,3,2,1,0:T(8,128)S(1)} %shard_map.103), channel_id=1, replica_groups=mesh['slab'=32,'sub'=8] {'sub'}, dimensions={0} | all-to-all | bytes 3145728 | tf_op jit(solution)/shard_map/all_to_all | solution.py:613
  112.9 1.2 %shard_map.104 = f32[3,8,128,128]{3,2,1,0:T(8,128)} custom-call(f32[8,3,8,16,128]{4,3,2,1,0:T(8,128)S(1)} %all_to_all.20.parts_ref), custom_call_target="tpu_custom_call" | custom-call | flops 1000000000 | bytes 3600000 | tf_op jit(solution)/shard_map/pallas_call | solution.py:614
Async XLA Ops:
  6.2 12.9 %all-to-all-start = ((f32[8,16,8,128]{3,2,1,0:T(8,128)}), f32[8,16,8,128]{3,2,1,0:T(8,128)S(1)}, u32[]{:S(2)}, u32[]{:S(2)}) async-start(f32[8,16,8,128]{3,2,1,0:T(8,128)} %bitcast.10), calls=%async_computation | async-start | bytes 1048576 | tf_op jit(solution)/shard_map/all_to_all | solution.py:527
  20.0 0.6 copy-start.7
  20.6 13.0 %all-to-all-start.1 = ((f32[8,16,8,128]{3,2,1,0:T(8,128)}), f32[8,16,8,128]{3,2,1,0:T(8,128)S(1)}, u32[]{:S(2)}, u32[]{:S(2)}) async-start(f32[8,16,8,128]{3,2,1,0:T(8,128)} %get-tuple-element.19), calls=%async_computation.1 | async-start | bytes 1048576 | tf_op jit(solution)/shard_map/all_to_all | solution.py:557
  33.6 0.8 copy-start
  43.4 5.2 %copy-start.8 = (f32[8,128]{1,0:T(8,128)S(1)}, f32[8,128]{1,0:T(8,128)}, u32[]{:S(2)}) copy-start(f32[8,128]{1,0:T(8,128)} %get-tuple-element.20.after_any) | copy-start | bytes 12292
  43.4 32.0 %all-to-all-start.2 = ((f32[8,66,8,128]{3,2,1,0:T(8,128)}), f32[8,66,8,128]{3,2,1,0:T(8,128)S(1)}, u32[]{:S(2)}, u32[]{:S(2)}) async-start(f32[8,66,8,128]{3,2,1,0:T(8,128)} %get-tuple-element.25), calls=%async_computation.2 | async-start | bytes 4325376 | tf_op jit(solution)/shard_map/all_to_all | solution.py:572
  48.6 1.4 %copy-start.2 = (f32[3,8,128,128]{3,2,1,0:T(8,128)S(1)}, f32[3,8,128,128]{3,2,1,0:T(8,128)}, u32[]{:S(2)}) copy-start(f32[3,8,128,128]{3,2,1,0:T(8,128)} %velocity_hbm.5) | copy-start | bytes 4718596
  50.0 5.9 %copy-start.1 = (f32[8,16,8,128]{3,2,1,0:T(8,128)S(1)}, f32[8,16,8,128]{3,2,1,0:T(8,128)}, u32[]{:S(2)}) copy-start(f32[8,16,8,128]{3,2,1,0:T(8,128)} %copy-done) | copy-start | bytes 1572868
  50.2 0.7 copy-start.3
  51.0 6.8 %collective-permute-start = (f32[3,4,32,128]{3,2,1,0:T(8,128)S(1)}, f32[3,4,32,128]{3,2,1,0:T(8,128)S(1)}, u32[]{:S(2)}, u32[]{:S(2)}) collective-permute-start(f32[3,4,32,128]{3,2,1,0:T(8,128)S(1)} %get-tuple-element.22), channel_id=1, source_target_pairs={{0,8},{8,16},{16,24},{24,32},{32,40},{40,48},{48,56},{56,64},{64,7... | collective-permute-start | bytes 589832 | tf_op jit(solution)/shard_map/ppermute | solution.py:497
  53.2 10.7 %collective-permute-start.1 = (f32[3,4,32,128]{3,2,1,0:T(8,128)S(1)}, f32[3,4,32,128]{3,2,1,0:T(8,128)S(1)}, u32[]{:S(2)}, u32[]{:S(2)}) collective-permute-start(f32[3,4,32,128]{3,2,1,0:T(8,128)S(1)} %get-tuple-element.23), channel_id=1, source_target_pairs={{8,0},{16,8},{24,16},{32,24},{40,32},{48,40},{56,48},{64,56},{72,6... | collective-permute-start | bytes 589832 | tf_op jit(solution)/shard_map/ppermute | solution.py:497
  56.0 7.9 %copy-start.4 = (f32[3,8,32,128]{3,2,1,0:T(8,128)S(1)}, f32[3,8,32,128]{3,2,1,0:T(8,128)}, u32[]{:S(2)}) copy-start(f32[3,8,32,128]{3,2,1,0:T(8,128)} %copy-done.3) | copy-start | bytes 1179652
  64.8 0.8 copy-start.5
  75.5 12.0 %copy-start.6 = (f32[3,14,32,128]{3,2,1,0:T(8,128)S(1)}, f32[3,14,32,128]{3,2,1,0:T(8,128)}, u32[]{:S(2)}) copy-start(f32[3,14,32,128]{3,2,1,0:T(8,128)} %copy-done.5) | copy-start | bytes 2064388
  75.9 4.8 %collective-permute-start.2 = (f32[3,3,24,128]{3,2,1,0:T(8,128)S(1)}, f32[3,3,24,128]{3,2,1,0:T(8,128)S(1)}, u32[]{:S(2)}, u32[]{:S(2)}) collective-permute-start(f32[3,3,24,128]{3,2,1,0:T(8,128)S(1)} %get-tuple-element.29), channel_id=1, source_target_pairs={{0,8},{8,16},{16,24},{24,32},{32,40},{40,48},{48,56},{56,64},{64,7... | collective-permute-start | bytes 331784 | tf_op jit(solution)/shard_map/ppermute | solution.py:497
  77.8 9.7 %collective-permute-start.3 = (f32[3,3,24,128]{3,2,1,0:T(8,128)S(1)}, f32[3,3,24,128]{3,2,1,0:T(8,128)S(1)}, u32[]{:S(2)}, u32[]{:S(2)}) collective-permute-start(f32[3,3,24,128]{3,2,1,0:T(8,128)S(1)} %get-tuple-element.30), channel_id=1, source_target_pairs={{8,0},{16,8},{24,16},{32,24},{40,32},{48,40},{56,48},{64,56},{72,6... | collective-permute-start | bytes 331784 | tf_op jit(solution)/shard_map/ppermute | solution.py:497

commit v3 on v2

--- a/solution.py
+++ b/solution.py
@@ -15,10 +15,11 @@
 VISCOSITY = 1.2
 TIME_STEP = 0.05
 ITERS = 4
+OUTER = (0, 1, 2, 5, 6, 7)
+INNER = (3, 4)
 UNROLL = 16
 F32 = jnp.float32
 PARAMS = pltpu.CompilerParams(vmem_limit_bytes=16 * 1024 * 1024)
-FULL = pltpu.CompilerParams(vmem_limit_bytes=60 * 1024 * 1024)
 VMEM = pl.BlockSpec(memory_space=pltpu.VMEM)
 SMEM = pl.BlockSpec(memory_space=pltpu.SMEM)
 HBM = pl.BlockSpec(memory_space=pltpu.HBM)
@@ -131,7 +132,8 @@
 
 
 def solid_kernel(
-    brick_hbm, base_hbm, frac_hbm, pvol_hbm, out_ref, brick_ref, base_ref, frac_ref, pvol_ref, sems
+    brick_hbm, base_hbm, frac_hbm, pvol_hbm, out_hbm,
+    out_ref, brick_ref, base_ref, frac_ref, pvol_ref, sems,
 ):
     copies = fetch(
         [(brick_hbm, brick_ref), (base_hbm, base_ref), (frac_hbm, frac_ref), (pvol_hbm, pvol_ref)],
@@ -156,23 +158,25 @@
         return carry
 
     lax.fori_loop(0, base_ref.shape[0] // UNROLL, step, 0)
-
-
-def eps_kernel(parts_ref, out_ref, copies_ref):
+    (copy,) = fetch([(out_ref, out_hbm)], sems)
+    copy.wait()
+
+
+def eps_kernel(parts_ref, copies_hbm, out_ref, sems):
     total = parts_ref[0]
     for j in range(1, parts_ref.shape[0]):
         total = total + parts_ref[j]
     total = jnp.maximum(1.0 - total, EPS_MIN)
     out_ref[...] = total
-    for j in range(copies_ref.shape[0]):
-        copies_ref[j] = total
+    for copy in fetch([(out_ref, copies_hbm.at[j]) for j in range(copies_hbm.shape[0])], sems):
+        copy.wait()
 
 
 def slip_kernel(
     first, count,
     after_any, brick_hbm, base_hbm, frac_hbm, pvel_hbm, coef_hbm, pvol_hbm, velocity_hbm,
-    out_ref,
-    brick_ref, base_ref, frac_ref, pvel_ref, coef_ref, pvol_ref, velocity_ref, table_ref, sems,
+    out_any,
+    out_ref, brick_ref, base_ref, frac_ref, pvel_ref, coef_ref, pvol_ref, velocity_ref, table_ref, sems,
 ):
     some = pl.ds(first, count)
     wide = pl.ds(first * BLOCK, count * BLOCK)
@@ -225,6 +229,8 @@
         return carry
 
     lax.fori_loop(0, count // UNROLL, step, 0)
+    (copy,) = fetch([(out_ref, out_any)], sems)
+    copy.wait()
 
 
 def pack_halo(rows, tiles):
@@ -243,21 +249,33 @@
     return a, b, c, d
 
 
+def pack_all(rows, tiles):
+    packed = []
+    for quad in range(len(tiles) // 4):
+        packed += pack_halo(rows, tiles[quad * 4 : quad * 4 + 4])
+    return packed + tiles[len(tiles) // 4 * 4 :]
+
+
+def unpack_all(rows, packed, count):
+    tiles = []
+    for quad in range(count // 4):
+        tiles += unpack_halo(rows, packed[quad * 3 : quad * 3 + 3])
+    return tiles + packed[count // 4 * 3 :]
+
+
 def drag_kernel(
-    brick_ref, base_ref, frac_ref, slip_a_hbm, slip_b_hbm, eps_ref,
-    drag_ref, out_hbm, tick_ref,
-    force_ref, slip_a_ref, slip_b_ref, sems,
+    brick_ref, base_ref, frac_ref, slip_a_hbm, slip_b_ref, eps_ref,
+    drag_ref, outer_hbm, inner_hbm, tick_ref,
+    force_ref, outer_ref, inner_ref, slip_a_ref, sems,
 ):
     subs = force_ref.shape[0]
     rows, lane = rows_iota(), lanes_iota()
-    slips = fetch([(slip_a_hbm, slip_a_ref), (slip_b_hbm, slip_b_ref)], sems)
+    (copy,) = fetch([(slip_a_hbm, slip_a_ref)], sems)
     for j in range(subs):
-        force_ref[j, 0:48] = jnp.zeros((48, 8, LANES), F32)
-    halves_of = ((slip_a_ref, 0), (slip_b_ref, slip_a_ref.shape[1] // BLOCK))
-    for copy in slips:
-        copy.wait()
-
-    for slip_ref, start in halves_of:
+        force_ref[j] = jnp.zeros(force_ref.shape[1:], F32)
+    copy.wait()
+
+    for slip_ref, start in ((slip_a_ref, 0), (slip_b_ref, slip_a_ref.shape[1] // BLOCK)):
 
         def step(number, carry, slip_ref=slip_ref, start=start):
             found = []
@@ -285,35 +303,42 @@
             return carry
 
         lax.fori_loop(0, slip_ref.shape[1] // BLOCK // UNROLL, step, 0)
-    copies = fetch([(force_ref.at[j, 0:48], out_hbm.at[j, 0:48]) for j in range(subs)], sems)
+
+    def convert(j, carry):
+        for c in range(3):
+            for t in range(2):
+                tiles = [force_ref[j, t * 24 + c * 8 + t3] for t3 in range(8)]
+                tiles = transpose_granules(tiles, lane)
+                for ref, planes in ((outer_ref, OUTER), (inner_ref, INNER)):
+                    for n, z in enumerate(planes):
+                        ref[j, (c * 2 + t) * len(planes) + n] = tiles[z]
+        return carry
+
+    lax.fori_loop(0, subs, convert, 0)
+    copies = []
     zero = jnp.zeros((8, LANES), F32)
-    more = []
     for j in range(subs):
-        for quad in range(6):
+        for ref, out_hbm, planes in ((outer_ref, outer_hbm, OUTER), (inner_ref, inner_hbm, INNER)):
+            size = len(planes)
             tiles = []
-            for k in range(4):
-                at = quad * 4 + k
-                after = force_ref[j + 1, at] if j + 1 < subs else zero
-                before = force_ref[j - 1, 24 + at] if j > 0 else zero
-                tiles.append(jnp.where(rows < 4, after, before))
-            for k, tile in enumerate(pack_halo(rows, tiles)):
-                force_ref[j, 48 + quad * 3 + k] = tile
-        copy = pltpu.make_async_copy(
-            force_ref.at[j, 48:66], out_hbm.at[j, 48:66], sems.at[subs + j]
-        )
-        copy.start()
-        more.append(copy)
+            for c in range(3):
+                for n in range(size):
+                    after = ref[j + 1, c * 2 * size + n] if j + 1 < subs else zero
+                    before = ref[j - 1, (c * 2 + 1) * size + n] if j > 0 else zero
+                    tiles.append(jnp.where(rows < 4, after, before))
+            for n, tile in enumerate(pack_all(rows, tiles)):
+                ref[j, 6 * size + n] = tile
+            copy = pltpu.make_async_copy(ref.at[j], out_hbm.at[j], sems.at[len(copies)])
+            copy.start()
+            copies.append(copy)
     tick_ref[...] = zero
-    for copy in copies + more:
+    for copy in copies:
         copy.wait()
 
 
-def source_kernel(sub_ref, parts_ref, eps_ref, first_any, void_any, own_ref, low_ref, high_ref):
-    lane, rows = lanes_iota(), rows_iota()
-    sub = sub_ref[0]
-    tiles_x = eps_ref.shape[0] // 8
-    after = jnp.minimum(sub * 2 + 2, tiles_x - 1) * 8
-    before = jnp.maximum(sub * 2 - 1, 0) * 8
+def source_kernel(planes, void_ref, first_any, parts_ref, *out_refs):
+    rows = rows_iota()
+    size = len(planes)
 
     def summed(at):
         total = parts_ref[0, at]
@@ -321,29 +346,15 @@
             total = total + parts_ref[j, at]
         return total
 
-    for t in range(3):
+    packed = [summed(at) for at in range(6 * size, parts_ref.shape[1])]
+    halo = unpack_all(rows, packed, 3 * size)
+    for n, z in enumerate(planes):
+        out_ref, at = out_refs[n // 3], n % 3
         for c in range(3):
-            if t < 2:
-                forces = [summed(t * 24 + c * 8 + t3) for t3 in range(8)]
-            else:
-                forces = []
-                for quad in (2 * c, 2 * c + 1):
-                    forces += unpack_halo(rows, [summed(48 + quad * 3 + k) for k in range(3)])
-            tiles = []
-            for t3 in range(8):
-                if t < 2:
-                    eps = eps_ref[(sub * 2 + t) * 8 + t3]
-                else:
-                    eps = jnp.where(rows < 4, eps_ref[after + t3], eps_ref[before + t3])
-                tiles.append(-forces[t3] / eps)
-            tiles = transpose_granules(tiles, lane)
-            first = 8 * (t + 1) % 24
-            for z in range(8):
-                own_ref[c, z, first : first + 8, :] = tiles[z]
-                if z < 3:
-                    low_ref[c, z, first : first + 8, :] = tiles[z]
-                if z >= 5:
-                    high_ref[c, z - 5, first : first + 8, :] = tiles[z]
+            forces = [halo[c * size + n]] + [summed((c * 2 + t) * size + n) for t in range(2)]
+            for t, force in enumerate(forces):
+                part = slice(8 * t, 8 * t + 8)
+                out_ref[c, at, part, :] = -force / void_ref[z, part, :]
 
 
 def window_kernel(sub_ref, after_any, velocity_hbm, out_ref, top_ref, bottom_ref, sems):
@@ -365,9 +376,9 @@
         bottom_ref[:, :, at, :] = rows[:, :4]
 
 
-def void_kernel(after_any, eps_ref, out_ref, tick_ref):
-    tick_ref[...] = jnp.zeros_like(tick_ref)
-    lane = lanes_iota()
+def void_kernel(sub_ref, after_any, eps_ref, out_ref, window_ref):
+    lane, rows = lanes_iota(), rows_iota()
+    tiles_x = out_ref.shape[1] // 8
 
     def convert(number, carry):
         for k in range(4):
@@ -377,7 +388,16 @@
                 out_ref[z, pl.ds(pl.multiple_of(tx * 8, 8), 8), :] = tiles[z]
         return carry
 
-    lax.fori_loop(0, out_ref.shape[1] // 32, convert, 0)
+    lax.fori_loop(0, tiles_x // 4, convert, 0)
+    own = sub_ref[0] * 2
+
+    def tile(tx):
+        return out_ref[:, pl.ds(pl.multiple_of(tx * 8, 8), 8), :]
+
+    after, before = tile(jnp.minimum(own + 2, tiles_x - 1)), tile(jnp.maximum(own - 1, 0))
+    window_ref[:, 0:8, :] = jnp.where(rows[None] < 4, after, before)
+    window_ref[:, 8:16, :] = tile(own)
+    window_ref[:, 16:24, :] = tile(own + 1)
 
 
 def edges(slab, sub, planes, width):
@@ -429,13 +449,16 @@
 
 
 def stencil_kernel(
-    place_ref, first_ref, own_ref, low_ref, high_ref, out_ref, even, odd, source
+    place_ref, first_ref, below_ref, low_ref, inner_ref, high_ref, above_ref, out_ref, even, odd, source
 ):
     keep = edges(place_ref[0], place_ref[1], place_ref[2], place_ref[3])
     lane = lax.broadcasted_iota(jnp.int32, (32, LANES), 1)
-    for part, planes in ((low_ref, slice(0, 3)), (own_ref, slice(3, 11)), (high_ref, slice(11, 14))):
+    start = 0
+    for part in (below_ref, low_ref, inner_ref, high_ref, above_ref):
+        planes = slice(start, start + part.shape[1])
         source[:, planes, 0:24, :] = part[...]
         source[:, planes, 24:32, :] = part[:, :, 0:8, :]
+        start += part.shape[1]
 
     def first(number, carry):
         for k in range(2):
@@ -468,25 +491,29 @@
 
 def place_kernel(parts_ref, out_ref, sems):
     rows = parts_ref.shape[3]
-    copies = fetch(
-        [
-            (parts_ref.at[j], out_ref.at[:, :, pl.ds(j * rows, rows), :])
-            for j in range(parts_ref.shape[0])
-        ],
-        sems,
-    )
-    for copy in copies:
+    pairs = []
+    for j in range(parts_ref.shape[0]):
+        pairs.append((parts_ref.at[j], out_ref.at[:, :, j * rows : (j + 1) * rows, :]))
+    for copy in fetch(pairs, sems):
         copy.wait()
 
 
-def call(kernel, out_shapes, ins, scratch=(), outs=None, us=1.0, params=PARAMS):
+def pinned(*arrays):
+    return [pltpu.with_memory_space_constraint(x, pltpu.HBM) for x in arrays]
+
+
+def call(kernel, out_shapes, ins, scratch=(), outs=None, us=1.0):
+    outs = outs or [VMEM] * len(out_shapes)
     return pl.pallas_call(
         kernel,
-        out_shape=[jax.ShapeDtypeStruct(s, F32) for s in out_shapes],
+        out_shape=[
+            pltpu.HBM(s, F32) if spec is HBM else jax.ShapeDtypeStruct(s, F32)
+            for s, spec in zip(out_shapes, outs)
+        ],
         in_specs=ins,
-        out_specs=outs or [VMEM] * len(out_shapes),
+        out_specs=outs,
         scratch_shapes=list(scratch),
-        compiler_params=params,
+        compiler_params=PARAMS,
         cost_estimate=pl.CostEstimate(flops=int(us * 1e9), bytes_accessed=int(us * 3.6e6), transcendentals=0),
     )
 
@@ -520,20 +547,23 @@
         solid_kernel,
         [(tiles, 8, LANES)],
         [HBM] * 4,
-        particles_vmem + [row_vmem, pltpu.SemaphoreType.DMA((4,))],
+        [pltpu.VMEM((tiles, 8, LANES), F32)]
+        + particles_vmem
+        + [row_vmem, pltpu.SemaphoreType.DMA((4,))],
+        outs=[HBM],
         us=5.0,
-        params=FULL,
-    )(brick_of_block, base, fraction, pvol)
+    )(*pinned(brick_of_block, base, fraction, pvol))
     solid_parts = lax.all_to_all(solid.reshape(subs, share, 8, LANES), "sub", 0, 0)
     sub_at = sub.reshape(1)
     half = blocks // 2
 
-    def slip_of(first, after):
+    def slip_of(first, after, out):
         (slip,) = call(
             functools.partial(slip_kernel, first, half),
             [(3, half * BLOCK)],
-            [ANY] + [HBM] * 7,
+            [HBM] * 8,
             [
+                pltpu.VMEM((3, half * BLOCK), F32),
                 pltpu.SMEM((blocks,), jnp.int32),
                 pltpu.VMEM((half, BLOCK), jnp.int32),
                 pltpu.VMEM((3, half * BLOCK), F32),
@@ -545,42 +575,54 @@
                 pltpu.SemaphoreType.DMA((7,)),
             ],
             us=5.0,
-            params=FULL,
-        )(after, brick_of_block, base, fraction, part_vel, coef, pvol, velocity)
+            )(after, brick_of_block, base, fraction, part_vel, coef, pvol, velocity)
         return slip
 
-    slip_a = slip_of(0, solid)
-    eps_own, eps_copies = call(
-        eps_kernel, [(share, 8, LANES), (subs, share, 8, LANES)], [VMEM], us=0.5
+    slip_a = slip_of(0, solid, HBM)
+    (eps_copies,) = call(
+        eps_kernel,
+        [(subs, share, 8, LANES)],
+        [VMEM],
+        [pltpu.VMEM((share, 8, LANES), F32), pltpu.SemaphoreType.DMA((subs,))],
+        outs=[HBM],
+        us=0.5,
     )(solid_parts)
-    slip_b = slip_of(half, eps_own)
+    slip_b = slip_of(half, eps_copies, ANY)
     eps = lax.all_to_all(eps_copies, "sub", 0, 0).reshape(tiles, 8, LANES)
-    drag, force, drag_tick = call(
+    outer_tiles = 6 * len(OUTER) + 14
+    inner_tiles = 6 * len(INNER) + 5
+    drag, outer, inner, tick = call(
         drag_kernel,
-        [(3, blocks * BLOCK), (subs, 66, 8, LANES), (8, LANES)],
-        [SMEM, VMEM, VMEM, HBM, HBM, VMEM],
         [
-            pltpu.VMEM((subs, 66, 8, LANES), F32),
-            pltpu.VMEM((3, half * BLOCK), F32),
+            (3, blocks * BLOCK),
+            (subs, outer_tiles, 8, LANES),
+            (subs, inner_tiles, 8, LANES),
+            (8, LANES),
+        ],
+        [SMEM, VMEM, VMEM, HBM, VMEM, VMEM],
+        [
+            pltpu.VMEM((subs, 48, 8, LANES), F32),
+            pltpu.VMEM((subs, outer_tiles, 8, LANES), F32),
+            pltpu.VMEM((subs, inner_tiles, 8, LANES), F32),
             pltpu.VMEM((3, half * BLOCK), F32),
             pltpu.SemaphoreType.DMA((2 * subs,)),
         ],
-        outs=[VMEM, HBM, VMEM],
-        us=6.0,
-        params=FULL,
-    )(brick_of_block, base, fraction, slip_a, slip_b, eps)
-    force_parts = lax.all_to_all(force, "sub", 0, 0)
+        outs=[VMEM, HBM, HBM, VMEM],
+        us=7.0,
+    )(brick_of_block, base, fraction, *pinned(slip_a), slip_b, eps)
+    outer = lax.all_to_all(outer, "sub", 0, 0)
+    inner = lax.all_to_all(inner, "sub", 0, 0)
     window, top, bottom = call(
         window_kernel,
         [(3, depth, 32, LANES), (3, 4, 32, LANES), (3, 4, 32, LANES)],
         [SMEM, ANY, HBM],
         [pltpu.SemaphoreType.DMA((4,))],
-    )(sub_at, drag_tick, velocity)
+    )(sub_at, tick, *pinned(velocity))
     below = shift(top, "slab", True)
     above = shift(bottom, "slab", False)
-    voidfraction, void_tick = call(
-        void_kernel, [(depth, width_x, LANES), (8, LANES)], [ANY, VMEM], us=2.0
-    )(drag_tick, eps)
+    voidfraction, void_window = call(
+        void_kernel, [(depth, width_x, LANES), (depth, 24, LANES)], [SMEM, ANY, VMEM], us=2.0
+    )(sub_at, tick, eps)
     first, first_tick = call(
         first_kernel,
         [(3, 14, 32, LANES), (8, LANES)],
@@ -590,33 +632,34 @@
     )(window, below, above)
 
     rows = width_x // subs
-    own, low_own, high_own = call(
-        source_kernel,
-        [(3, depth, 24, LANES), (3, 3, 24, LANES), (3, 3, 24, LANES)],
-        [SMEM, VMEM, VMEM, ANY, ANY],
-    )(sub_at, force_parts, eps, first_tick, void_tick)
-    low = shift(high_own, "slab", True)
-    high = shift(low_own, "slab", False)
+    low_own, high_own = call(
+        functools.partial(source_kernel, OUTER), [(3, 3, 24, LANES)] * 2, [VMEM, ANY, VMEM]
+    )(void_window, first_tick, outer)
+    below = shift(high_own, "slab", True)
+    above = shift(low_own, "slab", False)
+    (inner_own,) = call(
+        functools.partial(source_kernel, INNER), [(3, 2, 24, LANES)], [VMEM, ANY, VMEM]
+    )(void_window, low_own, inner)
     planes = depth * lax.axis_size("slab")
     place = jnp.stack([slab, sub, jnp.int32(planes), jnp.int32(width_x)])
     (moved,) = call(
         stencil_kernel,
         [(subs, 3, depth, rows, LANES)],
-        [SMEM] + [VMEM] * 4,
+        [SMEM] + [VMEM] * 6,
         [
             pltpu.VMEM((3, 16, 32, LANES), F32),
             pltpu.VMEM((3, 16, 32, LANES), F32),
             pltpu.VMEM((3, 14, 32, LANES), F32),
         ],
         us=4.0,
-    )(place, first, own, low, high)
+    )(place, first, below, low_own, inner_own, high_own, above)
     moved = lax.all_to_all(moved, "sub", 0, 0)
     (new_velocity,) = call(
         place_kernel,
         [velocity.shape],
         [ANY],
         [pltpu.SemaphoreType.DMA((subs,))],
-        outs=[ANY],
+        outs=[HBM],
     )(moved)
     return new_velocity, voidfraction, drag
 

time: 116 us -> 119 us (1.026)
  starting transfers between devices: 25.2 us -> 28.8 us
  waiting for transfers between devices: 24.8 us -> 22.1 us
  blocking collectives: 22.5 us -> 24.5 us
    ppermute x4, waiting for transfers between devices: 13 us -> 5.9 us  [shift(): return lax.ppermute(x, axis, pairs)]
    all_to_all x1 -> x2, waiting for transfers between devices: 9.8 us -> 14.3 us  [the longest x1 14.3 us: body(): outer = lax.all_to_all(outer, 'sub', 0, 0)]
    all_to_all x1 -> x2, starting transfers between devices: 5.2 us -> 8.92 us  [the longest x1 5.21 us: body(): outer = lax.all_to_all(outer, 'sub', 0, 0)]
    all_to_all x1, blocking collectives: 22.5 us -> 24.5 us  [body(): moved = lax.all_to_all(moved, 'sub', 0, 0)]
    pallas_call x8 -> x9, Pallas kernels: 33.9 us -> 32.5 us  [the longest x2 10.8 us: slip_of(): call(functools.partial(slip_kernel, first, half), [(3, half * BLOCK)], [H...]
    unnamed x18 -> x32, local copies, waits for them, and re-layouts: 4.42 us -> 5.35 us
  transfers between devices with their start and end apart: 7 -> 8, of which waited for: 5 -> 4; matrix products, arithmetic and copies ran while one was open for 0% -> 0% of each run, Pallas kernels for 14% -> 13%
where the time goes in v3:
time: 119 us; the launch traced here: 118 us
  Pallas kernels  35.8 us (30%)
  starting transfers between devices  28.8 us (24%)
  blocking collectives  24.5 us (21%)
  waiting for transfers between devices  22.1 us (19%)
  local copies, waits for them, and re-layouts  5.35 us (4%)
    all_to_all x1, blocking collectives, body(): moved = lax.all_to_all(moved, 'sub', 0, 0)  24.5 us
    all_to_all x1, waiting for transfers between devices, body(): outer = lax.all_to_all(outer, 'sub', 0, 0)  14.3 us
    pallas_call x2, Pallas kernels, slip_of(): call(functools.partial(slip_kernel, first, half), [(3, half * BLOCK)], [H...  10.8 us
    pallas_call x1, Pallas kernels, body(): call(drag_kernel, [(3, blocks * BLOCK), (subs, outer_tiles, 8, LANES), (s...  10.4 us
    ppermute x4, starting transfers between devices, shift(): return lax.ppermute(x, axis, pairs)  9.57 us
    ppermute x4, waiting for transfers between devices, shift(): return lax.ppermute(x, axis, pairs)  5.9 us
    pallas_call x1, Pallas kernels, body(): call(solid_kernel, [(tiles, 8, LANES)], [HBM] * 4, [pltpu.VMEM((tiles, 8,...  5.71 us
    unnamed x32, local copies, waits for them, and re-layouts  5.35 us
  transfers between devices with their start and end apart: 8, of which 4 were waited for; matrix products, arithmetic and copies ran while one was open for 0% of the time, Pallas kernels for 13%

profile of v3, /device:TPU:225, one launch (start us, length us, event | category | flops | bytes accessed | tf_op | source)
XLA Modules:
  0.0 117.6 jit_solution(14628800986894996636)
XLA Ops:
  0.6 0.0 copy-start.2
  0.6 0.0 copy-start.3
  0.7 0.0 copy-start.4
  0.7 0.0 copy-start.5
  0.7 0.0 copy-start.6
  0.7 0.0 copy-start.7
  0.7 0.0 copy-start.8
  0.7 5.7 %shard_map.94.after_any = f32[128,8,128]{2,1,0:T(8,128)} custom-call(s32[128]{0:T(128)} %brick_ref.1, s32[128,128]{1,0:T(8,128)} %bitcast.15, f32[3,16384]{1,0:T(4,128)} %frac_ref.1, f32[128,128]{1,0:T(8,128)} %bitcast.10), custom_call_target="tpu_custom_call" | custom-call | flops 5000000000 | bytes 18000000 | tf_op jit(solution)/shard_map/pallas_call | solution.py:546
  6.4 5.1 %all-to-all-start = ((f32[8,16,8,128]{3,2,1,0:T(8,128)}), f32[8,16,8,128]{3,2,1,0:T(8,128)S(1)}, u32[]{:S(2)}, u32[]{:S(2)}) async-start(f32[8,16,8,128]{3,2,1,0:T(8,128)} %bitcast.9), calls=%async_computation | async-start | bytes 1048576 | tf_op jit(solution)/shard_map/all_to_all | solution.py:556
  11.6 0.0 copy-done.2
  11.6 0.0 copy-done.3
  11.6 0.0 copy-done.4
  11.6 0.0 copy-done.5
  11.6 0.0 copy-done.6
  11.6 0.0 copy-done.7
  11.6 0.0 copy-done.8
  11.6 0.0 copy-start.1
  11.6 1.0 copy-done.1
  12.7 5.4 %shard_map.95.slip_a_hbm = f32[3,8192]{1,0:T(4,128)S(1)} custom-call(f32[128,8,128]{2,1,0:T(8,128)S(1)} %copy-done.1, s32[128]{0:T(128)S(1)} %copy-done.8, s32[128,128]{1,0:T(8,128)S(1)} %bitcast.16, f32[3,16384]{1,0:T(4,128)S(1)} %copy-done.4, f32[3,16384]{1,0:T(4,128)S(1)} %copy-done.3, f32[128,128]{1,0:T(8,128)S(1)} %bitcast.13, f32[128,128]{1,0:T(8,128)S(1)} %bitcast.11, ...), custom_call_target="tpu_custom_call" | custom-call | flops 5000000000 | bytes 18000000 | tf_op jit(solution)/shard_map/pallas_call | solution.py:561
  18.1 0.0 copy-start.15
  18.1 0.6 copy-done.15
  18.8 0.6 all-to-all-done.parts_ref
  19.4 0.9 shard_map.96.after_any
  20.2 5.2 %all-to-all-start.1 = ((f32[8,16,8,128]{3,2,1,0:T(8,128)}), f32[8,16,8,128]{3,2,1,0:T(8,128)S(1)}, u32[]{:S(2)}, u32[]{:S(2)}) async-start(f32[8,16,8,128]{3,2,1,0:T(8,128)} %shard_map.96.after_any), calls=%async_computation.1 | async-start | bytes 1048576 | tf_op jit(solution)/shard_map/all_to_all | solution.py:591
  25.5 0.0 copy-start
  25.5 1.1 copy-done
  26.5 5.4 %shard_map.97.slip_b_ref = f32[3,8192]{1,0:T(4,128)S(1)} custom-call(f32[8,16,8,128]{3,2,1,0:T(8,128)S(1)} %copy-done, s32[128]{0:T(128)S(1)} %copy-done.8, s32[128,128]{1,0:T(8,128)S(1)} %bitcast.17, f32[3,16384]{1,0:T(4,128)S(1)} %copy-done.4, f32[3,16384]{1,0:T(4,128)S(1)} %copy-done.3, f32[128,128]{1,0:T(8,128)S(1)} %bitcast.14, ...), custom_call_target="tpu_custom_call" | custom-call | flops 5000000000 | bytes 18000000 | tf_op jit(solution)/shard_map/pallas_call | solution.py:561
  32.0 1.3 %all-to-all-done.1 = f32[8,16,8,128]{3,2,1,0:T(8,128)S(1)} async-done(((f32[8,16,8,128]{3,2,1,0:T(8,128)}), f32[8,16,8,128]{3,2,1,0:T(8,128)S(1)}, u32[]{:S(2)}, u32[]{:S(2)}) %all-to-all-start.1) | async-done | bytes 524320 | tf_op jit(solution)/shard_map/all_to_all | solution.py:591
  33.3 10.4 %shard_map.98 = (f32[3,16384]{1,0:T(4,128)}, f32[8,50,8,128]{3,2,1,0:T(8,128)}, f32[8,17,8,128]{3,2,1,0:T(8,128)}, f32[8,128]{1,0:T(8,128)S(1)}) custom-call(s32[128]{0:T(128)S(1)} %copy-done.8, s32[128,128]{1,0:T(8,128)S(1)} %bitcast.18, f32[3,16384]{1,0:T(4,128)S(1)} %copy-done.4, f32[3,8192]{1,0:T(4,128)} %copy-done.15, ...), custom_call_target="tpu_custom_call" | custom-call | flops 7000000000 | bytes 25200000 | tf_op jit(solution)/shard_map/pallas_call | solution.py:594
  43.7 5.2 %all-to-all-start.2 = ((f32[8,50,8,128]{3,2,1,0:T(8,128)}), f32[8,50,8,128]{3,2,1,0:T(8,128)S(1)}, u32[]{:S(2)}, u32[]{:S(2)}) async-start(f32[8,50,8,128]{3,2,1,0:T(8,128)} %get-tuple-element.23), calls=%async_computation.2 | async-start | bytes 3276800 | tf_op jit(solution)/shard_map/all_to_all | solution.py:613
  48.9 1.2 %shard_map.99 = (f32[3,8,32,128]{3,2,1,0:T(8,128)S(1)}, f32[3,4,32,128]{3,2,1,0:T(8,128)S(1)}, f32[3,4,32,128]{3,2,1,0:T(8,128)S(1)}) custom-call(s32[1]{0:T(128)} %bitcast.1.sub_ref, f32[8,128]{1,0:T(8,128)S(1)} %get-tuple-element.16.after_any, f32[3,8,128,128]{3,2,1,0:T(8,128)} %velocity_hbm.5), custom_call_target="tpu_custom_call" | custom-call | flops 1000000000 | bytes 3600000 | tf_op jit(solution)/shard_map/pallas_call | solution.py:615
  50.1 0.0 copy-start.9
  50.1 0.7 copy-done.9
  50.8 2.2 %collective-permute-start = (f32[3,4,32,128]{3,2,1,0:T(8,128)S(1)}, f32[3,4,32,128]{3,2,1,0:T(8,128)S(1)}, u32[]{:S(2)}, u32[]{:S(2)}) collective-permute-start(f32[3,4,32,128]{3,2,1,0:T(8,128)S(1)} %get-tuple-element.18), channel_id=1, source_target_pairs={{0,8},{8,16},{16,24},{24,32},{32,40},{40,48},{48,56},{56,64},{64,7... | collective-permute-start | bytes 589832 | tf_op jit(solution)/shard_map/ppermute | solution.py:524
  53.0 2.8 %collective-permute-start.1 = (f32[3,4,32,128]{3,2,1,0:T(8,128)S(1)}, f32[3,4,32,128]{3,2,1,0:T(8,128)S(1)}, u32[]{:S(2)}, u32[]{:S(2)}) collective-permute-start(f32[3,4,32,128]{3,2,1,0:T(8,128)S(1)} %get-tuple-element.19), channel_id=1, source_target_pairs={{8,0},{16,8},{24,16},{32,24},{40,32},{48,40},{56,48},{64,56},{72,6... | collective-permute-start | bytes 589832 | tf_op jit(solution)/shard_map/ppermute | solution.py:524
  55.8 14.3 %all-to-all-done.2.parts_ref = f32[8,50,8,128]{3,2,1,0:T(8,128)S(1)} async-done(((f32[8,50,8,128]{3,2,1,0:T(8,128)}), f32[8,50,8,128]{3,2,1,0:T(8,128)S(1)}, u32[]{:S(2)}, u32[]{:S(2)}) %all-to-all-start.2) | async-done | bytes 1638432 | tf_op jit(solution)/shard_map/all_to_all | solution.py:613
  70.1 3.7 %all-to-all-start.3 = ((f32[8,17,8,128]{3,2,1,0:T(8,128)}), f32[8,17,8,128]{3,2,1,0:T(8,128)S(1)}, u32[]{:S(2)}, u32[]{:S(2)}) async-start(f32[8,17,8,128]{3,2,1,0:T(8,128)} %get-tuple-element.26), calls=%async_computation.3 | async-start | bytes 1114112 | tf_op jit(solution)/shard_map/all_to_all | solution.py:614
  73.8 0.0 copy-start.10
  73.8 1.8 %shard_map.101 = (f32[8,128,128]{2,1,0:T(8,128)}, f32[8,24,128]{2,1,0:T(8,128)S(1)}) custom-call(s32[1]{0:T(128)} %bitcast.1.sub_ref, f32[8,128]{1,0:T(8,128)S(1)} %get-tuple-element.16.after_any, f32[128,8,128]{2,1,0:T(8,128)S(1)} %bitcast.8), custom_call_target="tpu_custom_call" | custom-call | flops 2000000000 | bytes 7200000 | tf_op jit(solution)/shard_map/pallas_call | solution.py:623
  75.6 0.0 copy-start.13
  75.6 0.0 collective-permute-done.below_ref
  75.6 0.0 collective-permute-done.1.above_ref
  75.6 0.0 copy-done.10
  75.6 0.9 shard_map.100
  76.6 0.0 copy-start.11
  76.6 0.8 copy-done.11
  77.4 0.0 copy-done.13
  77.4 0.1 shard_map.102
  77.5 1.9 %collective-permute-start.2 = (f32[3,3,24,128]{3,2,1,0:T(8,128)S(1)}, f32[3,3,24,128]{3,2,1,0:T(8,128)S(1)}, u32[]{:S(2)}, u32[]{:S(2)}) collective-permute-start(f32[3,3,24,128]{3,2,1,0:T(8,128)S(1)} %get-tuple-element.24.high_ref), channel_id=1, source_target_pairs={{0,8},{8,16},{16,24},{24,32},{32,40},{40,48},{48,56},{56,64},{64,7... | collective-permute-start | bytes 331784 | tf_op jit(solution)/shard_map/ppermute | solution.py:524
  79.4 2.7 %collective-permute-start.3 = (f32[3,3,24,128]{3,2,1,0:T(8,128)S(1)}, f32[3,3,24,128]{3,2,1,0:T(8,128)S(1)}, u32[]{:S(2)}, u32[]{:S(2)}) collective-permute-start(f32[3,3,24,128]{3,2,1,0:T(8,128)S(1)} %get-tuple-element.25.first_any.low_ref), channel_id=1, source_target_pairs={{8,0},{16,8},{24,16},{32,24},{40,32},{48,40},{56,48},{64,56},{72,6... | collective-permute-start | bytes 331784 | tf_op jit(solution)/shard_map/ppermute | solution.py:524
  82.1 0.1 pad_add_fusion.place_ref
  82.2 0.0 copy-start.12
  82.2 0.0 all-to-all-done.3.parts_ref
  82.2 0.0 copy-start.14
  82.2 1.0 copy-done.14
  83.2 0.0 collective-permute-done.2.below_ref
  83.2 5.9 %collective-permute-done.3.above_ref = f32[3,3,24,128]{3,2,1,0:T(8,128)S(1)} collective-permute-done((f32[3,3,24,128]{3,2,1,0:T(8,128)S(1)}, f32[3,3,24,128]{3,2,1,0:T(8,128)S(1)}, u32[]{:S(2)}, u32[]{:S(2)}) %collective-permute-start.3) | collective-permute-done | bytes 110624 | tf_op jit(solution)/shard_map/ppermute | solution.py:524
  89.1 0.0 copy-done.12
  89.1 2.8 %shard_map.104 = f32[8,3,8,16,128]{4,3,2,1,0:T(8,128)S(1)} custom-call(s32[4]{0:T(128)S(1)} %pad_add_fusion.place_ref, f32[3,14,32,128]{3,2,1,0:T(8,128)S(1)} %copy-done.12, f32[3,3,24,128]{3,2,1,0:T(8,128)S(1)} %collective-permute-done.2.below_ref, f32[3,3,24,128]{3,2,1,0:T(8,128)S(1)} %get-tuple-element.25.first_any.low_ref, ...), custom_call_target="tpu_custom_call" | custom-call | flops 4000000000 | bytes 14400000 | tf_op jit(solution)/shard_map/pallas_call | solution.py:645
  91.9 24.5 %all_to_all.25.parts_ref = f32[8,3,8,16,128]{4,3,2,1,0:T(8,128)S(1)} all-to-all(f32[8,3,8,16,128]{4,3,2,1,0:T(8,128)S(1)} %shard_map.104), channel_id=1, replica_groups=mesh['slab'=32,'sub'=8] {'sub'}, dimensions={0} | all-to-all | bytes 3145728 | tf_op jit(solution)/shard_map/all_to_all | solution.py:656
  116.4 1.2 %shard_map.105 = f32[3,8,128,128]{3,2,1,0:T(8,128)} custom-call(f32[8,3,8,16,128]{4,3,2,1,0:T(8,128)S(1)} %all_to_all.25.parts_ref), custom_call_target="tpu_custom_call" | custom-call | flops 1000000000 | bytes 3600000 | tf_op jit(solution)/shard_map/pallas_call | solution.py:657
  (1 shorter events, 0.0 us)
Async XLA Ops:
  0.6 10.9 %copy-start.2 = (f32[3,8,128,128]{3,2,1,0:T(8,128)S(1)}, f32[3,8,128,128]{3,2,1,0:T(8,128)}, u32[]{:S(2)}) copy-start(f32[3,8,128,128]{3,2,1,0:T(8,128)} %velocity_hbm.5) | copy-start | bytes 4718596
  0.6 10.9 %copy-start.3 = (f32[3,16384]{1,0:T(4,128)S(1)}, f32[3,16384]{1,0:T(4,128)}, u32[]{:S(2)}) copy-start(f32[3,16384]{1,0:T(4,128)} %pvel_hbm.3) | copy-start | bytes 589828
  0.7 10.9 %copy-start.4 = (f32[3,16384]{1,0:T(4,128)S(1)}, f32[3,16384]{1,0:T(4,128)}, u32[]{:S(2)}) copy-start(f32[3,16384]{1,0:T(4,128)} %frac_ref.1) | copy-start | bytes 589828
  0.7 10.9 %copy-start.5 = (f32[16384]{0:T(1024)S(1)}, f32[16384]{0:T(1024)}, u32[]{:S(2)}) copy-start(f32[16384]{0:T(1024)} %param.12) | copy-start | bytes 196612
  0.7 10.9 %copy-start.6 = (f32[16384]{0:T(1024)S(1)}, f32[16384]{0:T(1024)}, u32[]{:S(2)}) copy-start(f32[16384]{0:T(1024)} %param.11) | copy-start | bytes 196612
  0.7 10.9 %copy-start.7 = (s32[16384]{0:T(1024)S(1)}, s32[16384]{0:T(1024)}, u32[]{:S(2)}) copy-start(s32[16384]{0:T(1024)} %param.10) | copy-start | bytes 196612
  0.7 10.9 %copy-start.8 = (s32[128]{0:T(128)S(1)}, s32[128]{0:T(128)}, u32[]{:S(2)}) copy-start(s32[128]{0:T(128)} %brick_ref.1) | copy-start | bytes 1540
  6.4 12.9 %all-to-all-start = ((f32[8,16,8,128]{3,2,1,0:T(8,128)}), f32[8,16,8,128]{3,2,1,0:T(8,128)S(1)}, u32[]{:S(2)}, u32[]{:S(2)}) async-start(f32[8,16,8,128]{3,2,1,0:T(8,128)} %bitcast.9), calls=%async_computation | async-start | bytes 1048576 | tf_op jit(solution)/shard_map/all_to_all | solution.py:556
  11.6 1.0 copy-start.1
  18.1 0.7 copy-start.15
  20.2 13.0 %all-to-all-start.1 = ((f32[8,16,8,128]{3,2,1,0:T(8,128)}), f32[8,16,8,128]{3,2,1,0:T(8,128)S(1)}, u32[]{:S(2)}, u32[]{:S(2)}) async-start(f32[8,16,8,128]{3,2,1,0:T(8,128)} %shard_map.96.after_any), calls=%async_computation.1 | async-start | bytes 1048576 | tf_op jit(solution)/shard_map/all_to_all | solution.py:591
  25.5 1.1 copy-start
  43.7 26.4 %all-to-all-start.2 = ((f32[8,50,8,128]{3,2,1,0:T(8,128)}), f32[8,50,8,128]{3,2,1,0:T(8,128)S(1)}, u32[]{:S(2)}, u32[]{:S(2)}) async-start(f32[8,50,8,128]{3,2,1,0:T(8,128)} %get-tuple-element.23), calls=%async_computation.2 | async-start | bytes 3276800 | tf_op jit(solution)/shard_map/all_to_all | solution.py:613
  50.1 0.7 copy-start.9
  50.8 24.8 %collective-permute-start = (f32[3,4,32,128]{3,2,1,0:T(8,128)S(1)}, f32[3,4,32,128]{3,2,1,0:T(8,128)S(1)}, u32[]{:S(2)}, u32[]{:S(2)}) collective-permute-start(f32[3,4,32,128]{3,2,1,0:T(8,128)S(1)} %get-tuple-element.18), channel_id=1, source_target_pairs={{0,8},{8,16},{16,24},{24,32},{32,40},{40,48},{48,56},{56,64},{64,7... | collective-permute-start | bytes 589832 | tf_op jit(solution)/shard_map/ppermute | solution.py:524
  53.0 22.6 %collective-permute-start.1 = (f32[3,4,32,128]{3,2,1,0:T(8,128)S(1)}, f32[3,4,32,128]{3,2,1,0:T(8,128)S(1)}, u32[]{:S(2)}, u32[]{:S(2)}) collective-permute-start(f32[3,4,32,128]{3,2,1,0:T(8,128)S(1)} %get-tuple-element.19), channel_id=1, source_target_pairs={{8,0},{16,8},{24,16},{32,24},{40,32},{48,40},{56,48},{64,56},{72,6... | collective-permute-start | bytes 589832 | tf_op jit(solution)/shard_map/ppermute | solution.py:524
  70.1 12.1 %all-to-all-start.3 = ((f32[8,17,8,128]{3,2,1,0:T(8,128)}), f32[8,17,8,128]{3,2,1,0:T(8,128)S(1)}, u32[]{:S(2)}, u32[]{:S(2)}) async-start(f32[8,17,8,128]{3,2,1,0:T(8,128)} %get-tuple-element.26), calls=%async_computation.3 | async-start | bytes 1114112 | tf_op jit(solution)/shard_map/all_to_all | solution.py:614
  73.8 1.8 %copy-start.10 = (f32[3,8,32,128]{3,2,1,0:T(8,128)S(1)}, f32[3,8,32,128]{3,2,1,0:T(8,128)}, u32[]{:S(2)}) copy-start(f32[3,8,32,128]{3,2,1,0:T(8,128)} %copy-done.9) | copy-start | bytes 1179652
  75.6 1.8 %copy-start.13 = (f32[8,24,128]{2,1,0:T(8,128)}, f32[8,24,128]{2,1,0:T(8,128)S(1)}, u32[]{:S(2)}) copy-start(f32[8,24,128]{2,1,0:T(8,128)S(1)} %get-tuple-element.21.void_ref) | copy-start | bytes 294916
  76.6 0.8 copy-start.11
  77.5 5.7 %collective-permute-start.2 = (f32[3,3,24,128]{3,2,1,0:T(8,128)S(1)}, f32[3,3,24,128]{3,2,1,0:T(8,128)S(1)}, u32[]{:S(2)}, u32[]{:S(2)}) collective-permute-start(f32[3,3,24,128]{3,2,1,0:T(8,128)S(1)} %get-tuple-element.24.high_ref), channel_id=1, source_target_pairs={{0,8},{8,16},{16,24},{24,32},{32,40},{40,48},{48,56},{56,64},{64,7... | collective-permute-start | bytes 331784 | tf_op jit(solution)/shard_map/ppermute | solution.py:524
  79.4 9.7 %collective-permute-start.3 = (f32[3,3,24,128]{3,2,1,0:T(8,128)S(1)}, f32[3,3,24,128]{3,2,1,0:T(8,128)S(1)}, u32[]{:S(2)}, u32[]{:S(2)}) collective-permute-start(f32[3,3,24,128]{3,2,1,0:T(8,128)S(1)} %get-tuple-element.25.first_any.low_ref), channel_id=1, source_target_pairs={{8,0},{16,8},{24,16},{32,24},{40,32},{48,40},{56,48},{64,56},{72,6... | collective-permute-start | bytes 331784 | tf_op jit(solution)/shard_map/ppermute | solution.py:524
  82.2 6.9 %copy-start.12 = (f32[3,14,32,128]{3,2,1,0:T(8,128)S(1)}, f32[3,14,32,128]{3,2,1,0:T(8,128)}, u32[]{:S(2)}) copy-start(f32[3,14,32,128]{3,2,1,0:T(8,128)} %copy-done.11) | copy-start | bytes 2064388
  82.2 1.0 copy-start.14

commit v4 on v2

--- a/solution.py
+++ b/solution.py
@@ -18,7 +18,6 @@
 UNROLL = 16
 F32 = jnp.float32
 PARAMS = pltpu.CompilerParams(vmem_limit_bytes=16 * 1024 * 1024)
-FULL = pltpu.CompilerParams(vmem_limit_bytes=60 * 1024 * 1024)
 VMEM = pl.BlockSpec(memory_space=pltpu.VMEM)
 SMEM = pl.BlockSpec(memory_space=pltpu.SMEM)
 HBM = pl.BlockSpec(memory_space=pltpu.HBM)
@@ -97,14 +96,24 @@
     return jnp.concatenate([high, full - high], axis=0).astype(jnp.bfloat16)
 
 
-def deposit(parts, weights):
-    left = split_rows(parts)
+def deposit(blocks):
+    left = []
+    for n, (parts, _) in enumerate(blocks):
+        rows = split_rows(parts)
+        pair = [rows, jnp.zeros_like(rows)]
+        left.append(jnp.concatenate(pair if n == 0 else pair[::-1], axis=1))
     both = lax.dot_general(
-        left, weights, (((1,), (1,)), ((), ())), preferred_element_type=F32
+        jnp.concatenate(left, axis=0),
+        jnp.concatenate([weights for _, weights in blocks], axis=1),
+        (((1,), (1,)), ((), ())),
+        preferred_element_type=F32,
     )
-    half = both.shape[0] // 2
-    both = both[:half] + both[half:]
-    return both + pltpu.roll(both, 64, 1)
+    half = both.shape[0] // 4
+    found = []
+    for n in range(2):
+        total = both[2 * n * half : (2 * n + 1) * half] + both[(2 * n + 1) * half : (2 * n + 2) * half]
+        found.append(total + pltpu.roll(total, 64, 1))
+    return found
 
 
 def corner_terms(zb, yb, fz, fy, offset):
@@ -131,7 +140,8 @@
 
 
 def solid_kernel(
-    brick_hbm, base_hbm, frac_hbm, pvol_hbm, out_ref, brick_ref, base_ref, frac_ref, pvol_ref, sems
+    brick_hbm, base_hbm, frac_hbm, pvol_hbm, out_hbm,
+    out_ref, brick_ref, base_ref, frac_ref, pvol_ref, sems,
 ):
     copies = fetch(
         [(brick_hbm, brick_ref), (base_hbm, base_ref), (frac_hbm, frac_ref), (pvol_hbm, pvol_ref)],
@@ -148,7 +158,8 @@
             block = number * UNROLL + k
             _, zb, xb, yb, fz, fx, fy = particles(base_ref, frac_ref, block)
             kx = axis_weights(rows, xb, fx) * spread(pvol_ref[pl.ds(block, 1), :])
-            found.append(deposit([kx], plane_weights(rows, zb, yb, fz, fy)))
+            found.append(([kx], plane_weights(rows, zb, yb, fz, fy)))
+        found = sum((deposit(found[k : k + 2]) for k in range(0, UNROLL, 2)), [])
         for k in range(UNROLL):
             tx, t3, t1 = brick_place(brick_ref[number * UNROLL + k])
             tile = tx * 8 + t3
@@ -156,23 +167,25 @@
         return carry
 
     lax.fori_loop(0, base_ref.shape[0] // UNROLL, step, 0)
-
-
-def eps_kernel(parts_ref, out_ref, copies_ref):
+    (copy,) = fetch([(out_ref, out_hbm)], sems)
+    copy.wait()
+
+
+def eps_kernel(parts_ref, copies_hbm, out_ref, sems):
     total = parts_ref[0]
     for j in range(1, parts_ref.shape[0]):
         total = total + parts_ref[j]
     total = jnp.maximum(1.0 - total, EPS_MIN)
     out_ref[...] = total
-    for j in range(copies_ref.shape[0]):
-        copies_ref[j] = total
+    for copy in fetch([(out_ref, copies_hbm.at[j]) for j in range(copies_hbm.shape[0])], sems):
+        copy.wait()
 
 
 def slip_kernel(
     first, count,
     after_any, brick_hbm, base_hbm, frac_hbm, pvel_hbm, coef_hbm, pvol_hbm, velocity_hbm,
-    out_ref,
-    brick_ref, base_ref, frac_ref, pvel_ref, coef_ref, pvol_ref, velocity_ref, table_ref, sems,
+    out_any,
+    out_ref, brick_ref, base_ref, frac_ref, pvel_ref, coef_ref, pvol_ref, velocity_ref, table_ref, sems,
 ):
     some = pl.ds(first, count)
     wide = pl.ds(first * BLOCK, count * BLOCK)
@@ -225,6 +238,8 @@
         return carry
 
     lax.fori_loop(0, count // UNROLL, step, 0)
+    (copy,) = fetch([(out_ref, out_any)], sems)
+    copy.wait()
 
 
 def pack_halo(rows, tiles):
@@ -244,20 +259,18 @@
 
 
 def drag_kernel(
-    brick_ref, base_ref, frac_ref, slip_a_hbm, slip_b_hbm, eps_ref,
+    brick_ref, base_ref, frac_ref, slip_a_hbm, slip_b_ref, eps_ref,
     drag_ref, out_hbm, tick_ref,
-    force_ref, slip_a_ref, slip_b_ref, sems,
+    force_ref, slip_a_ref, sems,
 ):
     subs = force_ref.shape[0]
     rows, lane = rows_iota(), lanes_iota()
-    slips = fetch([(slip_a_hbm, slip_a_ref), (slip_b_hbm, slip_b_ref)], sems)
+    (copy,) = fetch([(slip_a_hbm, slip_a_ref)], sems)
     for j in range(subs):
         force_ref[j, 0:48] = jnp.zeros((48, 8, LANES), F32)
-    halves_of = ((slip_a_ref, 0), (slip_b_ref, slip_a_ref.shape[1] // BLOCK))
-    for copy in slips:
-        copy.wait()
-
-    for slip_ref, start in halves_of:
+    copy.wait()
+
+    for slip_ref, start in ((slip_a_ref, 0), (slip_b_ref, slip_a_ref.shape[1] // BLOCK)):
 
         def step(number, carry, slip_ref=slip_ref, start=start):
             found = []
@@ -275,7 +288,8 @@
                     force = factor * slip_ref[c : c + 1, inner_at]
                     drag_ref[c : c + 1, at] = force
                     parts.append(kx * spread(force))
-                found.append(deposit(parts, plane_weights(rows, zb, yb, fz, fy)))
+                found.append((parts, plane_weights(rows, zb, yb, fz, fy)))
+            found = sum((deposit(found[k : k + 2]) for k in range(0, UNROLL, 2)), [])
             for k in range(UNROLL):
                 tx, t3, t1 = brick_place(brick_ref[number * UNROLL + k + start])
                 mine = (lane >> 6) == t1
@@ -287,30 +301,28 @@
         lax.fori_loop(0, slip_ref.shape[1] // BLOCK // UNROLL, step, 0)
     copies = fetch([(force_ref.at[j, 0:48], out_hbm.at[j, 0:48]) for j in range(subs)], sems)
     zero = jnp.zeros((8, LANES), F32)
-    more = []
+    tick_ref[...] = zero
     for j in range(subs):
         for quad in range(6):
             tiles = []
-            for k in range(4):
-                at = quad * 4 + k
+            for at in range(quad * 4, quad * 4 + 4):
                 after = force_ref[j + 1, at] if j + 1 < subs else zero
                 before = force_ref[j - 1, 24 + at] if j > 0 else zero
                 tiles.append(jnp.where(rows < 4, after, before))
-            for k, tile in enumerate(pack_halo(rows, tiles)):
-                force_ref[j, 48 + quad * 3 + k] = tile
+            for n, tile in enumerate(pack_halo(rows, tiles)):
+                force_ref[j, 48 + quad * 3 + n] = tile
         copy = pltpu.make_async_copy(
             force_ref.at[j, 48:66], out_hbm.at[j, 48:66], sems.at[subs + j]
         )
         copy.start()
-        more.append(copy)
-    tick_ref[...] = zero
-    for copy in copies + more:
+        copies.append(copy)
+    for copy in copies:
         copy.wait()
 
 
-def source_kernel(sub_ref, parts_ref, eps_ref, first_any, void_any, own_ref, low_ref, high_ref):
+def source_kernel(place_ref, parts_ref, eps_ref, first_any, void_any, own_ref, even_ref, odd_ref):
     lane, rows = lanes_iota(), rows_iota()
-    sub = sub_ref[0]
+    even, sub = place_ref[0] % 2 == 0, place_ref[1]
     tiles_x = eps_ref.shape[0] // 8
     after = jnp.minimum(sub * 2 + 2, tiles_x - 1) * 8
     before = jnp.maximum(sub * 2 - 1, 0) * 8
@@ -340,18 +352,19 @@
             first = 8 * (t + 1) % 24
             for z in range(8):
                 own_ref[c, z, first : first + 8, :] = tiles[z]
-                if z < 3:
-                    low_ref[c, z, first : first + 8, :] = tiles[z]
-                if z >= 5:
-                    high_ref[c, z - 5, first : first + 8, :] = tiles[z]
-
-
-def window_kernel(sub_ref, after_any, velocity_hbm, out_ref, top_ref, bottom_ref, sems):
+            for n in range(3):
+                at = slice(first, first + 8)
+                even_ref[c, n, at, :] = jnp.where(even, tiles[5 + n], tiles[n])
+                odd_ref[c, n, at, :] = jnp.where(even, tiles[n], tiles[5 + n])
+
+
+def window_kernel(place_ref, after_any, velocity_hbm, out_ref, even_ref, odd_ref, sems):
+    even = place_ref[0] % 2 == 0
     depth = velocity_hbm.shape[1]
     tiles_x = velocity_hbm.shape[2] // 8
     pairs, inside = [], []
     for r in range(4):
-        want = sub_ref[0] * 2 + r - 1
+        want = place_ref[1] * 2 + r - 1
         inside.append(jnp.logical_and(want >= 0, want < tiles_x))
         at = pl.ds(pl.multiple_of(jnp.clip(want, 0, tiles_x - 1) * 8, 8), 8)
         pairs.append((velocity_hbm.at[:, :, at, :], out_ref.at[:, :, 8 * r : 8 * r + 8, :]))
@@ -361,8 +374,8 @@
         at = slice(8 * r, 8 * r + 8)
         rows = jnp.where(inside[r], out_ref[:, :, at, :], 0.0)
         out_ref[:, :, at, :] = rows
-        top_ref[:, :, at, :] = rows[:, depth - 4 :]
-        bottom_ref[:, :, at, :] = rows[:, :4]
+        even_ref[:, :, at, :] = jnp.where(even, rows[:, depth - 4 :], rows[:, :4])
+        odd_ref[:, :, at, :] = jnp.where(even, rows[:, :4], rows[:, depth - 4 :])
 
 
 def void_kernel(after_any, eps_ref, out_ref, tick_ref):
@@ -410,11 +423,12 @@
     return [centres[c] + viscous * laps[c] for c in range(3)]
 
 
-def first_kernel(window_ref, below_ref, above_ref, out_ref, tick_ref, old):
+def first_kernel(place_ref, window_ref, even_ref, odd_ref, out_ref, tick_ref, old):
     tick_ref[...] = jnp.zeros_like(tick_ref)
-    old[:, 0:4] = below_ref[...]
+    side = place_ref[0] % 2
+    old[:, pl.ds(12 - 12 * side, 4)] = even_ref[...]
+    old[:, pl.ds(12 * side, 4)] = odd_ref[...]
     old[:, 4:12] = window_ref[...]
-    old[:, 12:16] = above_ref[...]
     lane = lax.broadcasted_iota(jnp.int32, (32, LANES), 1)
 
     def plane(number, carry):
@@ -429,11 +443,13 @@
 
 
 def stencil_kernel(
-    place_ref, first_ref, own_ref, low_ref, high_ref, out_ref, even, odd, source
+    place_ref, first_ref, own_ref, even_ref, odd_ref, out_ref, even, odd, source
 ):
     keep = edges(place_ref[0], place_ref[1], place_ref[2], place_ref[3])
     lane = lax.broadcasted_iota(jnp.int32, (32, LANES), 1)
-    for part, planes in ((low_ref, slice(0, 3)), (own_ref, slice(3, 11)), (high_ref, slice(11, 14))):
+    side = place_ref[0] % 2
+    parts = ((even_ref, pl.ds(11 - 11 * side, 3)), (own_ref, slice(3, 11)), (odd_ref, pl.ds(11 * side, 3)))
+    for part, planes in parts:
         source[:, planes, 0:24, :] = part[...]
         source[:, planes, 24:32, :] = part[:, :, 0:8, :]
 
@@ -468,33 +484,36 @@
 
 def place_kernel(parts_ref, out_ref, sems):
     rows = parts_ref.shape[3]
-    copies = fetch(
-        [
-            (parts_ref.at[j], out_ref.at[:, :, pl.ds(j * rows, rows), :])
-            for j in range(parts_ref.shape[0])
-        ],
-        sems,
-    )
-    for copy in copies:
+    pairs = []
+    for j in range(parts_ref.shape[0]):
+        pairs.append((parts_ref.at[j], out_ref.at[:, :, j * rows : (j + 1) * rows, :]))
+    for copy in fetch(pairs, sems):
         copy.wait()
 
 
-def call(kernel, out_shapes, ins, scratch=(), outs=None, us=1.0, params=PARAMS):
+def pinned(*arrays):
+    return [pltpu.with_memory_space_constraint(x, pltpu.HBM) for x in arrays]
+
+
+def call(kernel, out_shapes, ins, scratch=(), outs=None, us=1.0):
+    outs = outs or [VMEM] * len(out_shapes)
     return pl.pallas_call(
         kernel,
-        out_shape=[jax.ShapeDtypeStruct(s, F32) for s in out_shapes],
+        out_shape=[
+            pltpu.HBM(s, F32) if spec is HBM else jax.ShapeDtypeStruct(s, F32)
+            for s, spec in zip(out_shapes, outs)
+        ],
         in_specs=ins,
-        out_specs=outs or [VMEM] * len(out_shapes),
+        out_specs=outs,
         scratch_shapes=list(scratch),
-        compiler_params=params,
+        compiler_params=PARAMS,
         cost_estimate=pl.CostEstimate(flops=int(us * 1e9), bytes_accessed=int(us * 3.6e6), transcendentals=0),
     )
 
 
-def shift(x, axis, up):
-    peers = lax.axis_size(axis)
-    pairs = [(i, i + 1) if up else (i + 1, i) for i in range(peers - 1)]
-    return lax.ppermute(x, axis, pairs)
+def pair_up(x, first):
+    pairs = [(i, i + 1) for i in range(first, lax.axis_size("slab") - 1, 2)]
+    return lax.ppermute(x, "slab", pairs + [(j, i) for i, j in pairs])
 
 
 def body(velocity, part_vel, fraction, base_cell, drag_coeff, part_volume, brick_of_block):
@@ -520,20 +539,22 @@
         solid_kernel,
         [(tiles, 8, LANES)],
         [HBM] * 4,
-        particles_vmem + [row_vmem, pltpu.SemaphoreType.DMA((4,))],
+        [pltpu.VMEM((tiles, 8, LANES), F32)]
+        + particles_vmem
+        + [row_vmem, pltpu.SemaphoreType.DMA((4,))],
+        outs=[HBM],
         us=5.0,
-        params=FULL,
-    )(brick_of_block, base, fraction, pvol)
+    )(*pinned(brick_of_block, base, fraction, pvol))
     solid_parts = lax.all_to_all(solid.reshape(subs, share, 8, LANES), "sub", 0, 0)
-    sub_at = sub.reshape(1)
     half = blocks // 2
 
-    def slip_of(first, after):
+    def slip_of(first, after, out):
         (slip,) = call(
             functools.partial(slip_kernel, first, half),
             [(3, half * BLOCK)],
-            [ANY] + [HBM] * 7,
+            [HBM] * 8,
             [
+                pltpu.VMEM((3, half * BLOCK), F32),
                 pltpu.SMEM((blocks,), jnp.int32),
                 pltpu.VMEM((half, BLOCK), jnp.int32),
                 pltpu.VMEM((3, half * BLOCK), F32),
@@ -545,60 +566,60 @@
                 pltpu.SemaphoreType.DMA((7,)),
             ],
             us=5.0,
-            params=FULL,
-        )(after, brick_of_block, base, fraction, part_vel, coef, pvol, velocity)
+            )(after, brick_of_block, base, fraction, part_vel, coef, pvol, velocity)
         return slip
 
-    slip_a = slip_of(0, solid)
-    eps_own, eps_copies = call(
-        eps_kernel, [(share, 8, LANES), (subs, share, 8, LANES)], [VMEM], us=0.5
+    slip_a = slip_of(0, solid, HBM)
+    (eps_copies,) = call(
+        eps_kernel,
+        [(subs, share, 8, LANES)],
+        [VMEM],
+        [pltpu.VMEM((share, 8, LANES), F32), pltpu.SemaphoreType.DMA((subs,))],
+        outs=[HBM],
+        us=0.5,
     )(solid_parts)
-    slip_b = slip_of(half, eps_own)
+    slip_b = slip_of(half, eps_copies, ANY)
     eps = lax.all_to_all(eps_copies, "sub", 0, 0).reshape(tiles, 8, LANES)
-    drag, force, drag_tick = call(
+    drag, force, tick = call(
         drag_kernel,
         [(3, blocks * BLOCK), (subs, 66, 8, LANES), (8, LANES)],
-        [SMEM, VMEM, VMEM, HBM, HBM, VMEM],
+        [SMEM, VMEM, VMEM, HBM, VMEM, VMEM],
         [
             pltpu.VMEM((subs, 66, 8, LANES), F32),
-            pltpu.VMEM((3, half * BLOCK), F32),
             pltpu.VMEM((3, half * BLOCK), F32),
             pltpu.SemaphoreType.DMA((2 * subs,)),
         ],
         outs=[VMEM, HBM, VMEM],
         us=6.0,
-        params=FULL,
-    )(brick_of_block, base, fraction, slip_a, slip_b, eps)
-    force_parts = lax.all_to_all(force, "sub", 0, 0)
-    window, top, bottom = call(
+    )(brick_of_block, base, fraction, *pinned(slip_a), slip_b, eps)
+    forces = lax.all_to_all(force, "sub", 0, 0)
+    planes = depth * lax.axis_size("slab")
+    place = jnp.stack([slab, sub, jnp.int32(planes), jnp.int32(width_x)])
+    window, even, odd = call(
         window_kernel,
         [(3, depth, 32, LANES), (3, 4, 32, LANES), (3, 4, 32, LANES)],
         [SMEM, ANY, HBM],
         [pltpu.SemaphoreType.DMA((4,))],
-    )(sub_at, drag_tick, velocity)
-    below = shift(top, "slab", True)
-    above = shift(bottom, "slab", False)
+    )(place, tick, *pinned(velocity))
+    even, odd = pair_up(even, 0), pair_up(odd, 1)
     voidfraction, void_tick = call(
         void_kernel, [(depth, width_x, LANES), (8, LANES)], [ANY, VMEM], us=2.0
-    )(drag_tick, eps)
+    )(tick, eps)
     first, first_tick = call(
         first_kernel,
         [(3, 14, 32, LANES), (8, LANES)],
-        [VMEM] * 3,
+        [SMEM] + [VMEM] * 3,
         [pltpu.VMEM((3, 16, 32, LANES), F32)],
         us=1.0,
-    )(window, below, above)
+    )(place, window, even, odd)
 
     rows = width_x // subs
-    own, low_own, high_own = call(
+    own, even, odd = call(
         source_kernel,
         [(3, depth, 24, LANES), (3, 3, 24, LANES), (3, 3, 24, LANES)],
         [SMEM, VMEM, VMEM, ANY, ANY],
-    )(sub_at, force_parts, eps, first_tick, void_tick)
-    low = shift(high_own, "slab", True)
-    high = shift(low_own, "slab", False)
-    planes = depth * lax.axis_size("slab")
-    place = jnp.stack([slab, sub, jnp.int32(planes), jnp.int32(width_x)])
+    )(place, forces, eps, first_tick, void_tick)
+    even, odd = pair_up(even, 0), pair_up(odd, 1)
     (moved,) = call(
         stencil_kernel,
         [(subs, 3, depth, rows, LANES)],
@@ -609,14 +630,14 @@
             pltpu.VMEM((3, 14, 32, LANES), F32),
         ],
         us=4.0,
-    )(place, first, own, low, high)
+    )(place, first, own, even, odd)
     moved = lax.all_to_all(moved, "sub", 0, 0)
     (new_velocity,) = call(
         place_kernel,
         [velocity.shape],
         [ANY],
         [pltpu.SemaphoreType.DMA((subs,))],
-        outs=[ANY],
+        outs=[HBM],
     )(moved)
     return new_velocity, voidfraction, drag
 

time: 116 us -> 110 us (0.948); the launches traced: 114 us -> 110 us
  starting transfers between devices: 25.2 us -> 21.5 us
  waiting for transfers between devices: 24.8 us -> 28.3 us
  Pallas kernels: 36.1 us -> 34.1 us
  local copies, waits for them, and re-layouts: 4.42 us -> 2.79 us
    ppermute x4, starting transfers between devices: 9.67 us -> 6.02 us  [pair_up(): return lax.ppermute(x, 'slab', pairs + [(j, i) for i, j in pairs])]
    pallas_call x5, Pallas kernels: 20.8 us -> 18.1 us  [the longest x2 10.8 us: slip_of(): call(functools.partial(slip_kernel, first, half), [(3, half * BLOCK)], [H...]
    all_to_all x1, waiting for transfers between devices: 9.8 us -> 11.6 us  [body(): forces = lax.all_to_all(force, 'sub', 0, 0)]
    ppermute x4, waiting for transfers between devices: 13 us -> 14.7 us  [pair_up(): return lax.ppermute(x, 'slab', pairs + [(j, i) for i, j in pairs])]
    unnamed x18 -> x20, local copies, waits for them, and re-layouts: 4.42 us -> 2.79 us
    pallas_call x1, Pallas kernels: 0.15 us -> 1.7 us  [body(): call(window_kernel, [(3, depth, 32, LANES), (3, 4, 32, LANES), (3, 4, 32,...]
    pallas_call x1, Pallas kernels: 8.97 us -> 7.63 us  [body(): call(drag_kernel, [(3, blocks * BLOCK), (subs, 66, 8, LANES), (8, LANES)]...]
where the time goes in v4:
time: 110 us
  Pallas kernels  34.1 us (31%)
  waiting for transfers between devices  28.3 us (26%)
  blocking collectives  22 us (20%)
  starting transfers between devices  21.5 us (20%)
  local copies, waits for them, and re-layouts  2.79 us (3%)
    all_to_all x1, blocking collectives, body(): moved = lax.all_to_all(moved, 'sub', 0, 0)  22 us
    ppermute x4, waiting for transfers between devices, pair_up(): return lax.ppermute(x, 'slab', pairs + [(j, i) for i, j in pairs])  14.7 us
    all_to_all x1, waiting for transfers between devices, body(): forces = lax.all_to_all(force, 'sub', 0, 0)  11.6 us
    pallas_call x2, Pallas kernels, slip_of(): call(functools.partial(slip_kernel, first, half), [(3, half * BLOCK)], [H...  10.8 us
    pallas_call x1, Pallas kernels, body(): call(drag_kernel, [(3, blocks * BLOCK), (subs, 66, 8, LANES), (8, LANES)]...  7.63 us
    ppermute x4, starting transfers between devices, pair_up(): return lax.ppermute(x, 'slab', pairs + [(j, i) for i, j in pairs])  6.02 us
    all_to_all x1, starting transfers between devices, body(): forces = lax.all_to_all(force, 'sub', 0, 0)  5.19 us
    all_to_all x1, starting transfers between devices, body(): eps = lax.all_to_all(eps_copies, 'sub', 0, 0).reshape(tiles, 8, LANES)  5.19 us
  transfers between devices with their start and end apart: 7, of which 5 were waited for; matrix products, arithmetic and copies ran while one was open for 0% of the time, Pallas kernels for 14%

profile of v4, /device:TPU:225, one launch (start us, length us, event | category | flops | bytes accessed | tf_op | source)
XLA Modules:
  0.0 109.7 jit_solution(15343851965824899612)
XLA Ops:
  0.6 0.0 copy-start.2
  0.6 0.0 copy-start.3
  0.7 0.0 copy-start.4
  0.7 0.0 copy-start.5
  0.7 0.0 copy-start.6
  0.7 0.0 copy-start.7
  0.7 0.0 copy-start.8
  0.7 4.9 %shard_map.94.after_any = f32[128,8,128]{2,1,0:T(8,128)} custom-call(s32[128]{0:T(128)} %brick_ref.1, s32[128,128]{1,0:T(8,128)} %bitcast.16, f32[3,16384]{1,0:T(4,128)} %frac_ref.1, f32[128,128]{1,0:T(8,128)} %bitcast.11), custom_call_target="tpu_custom_call" | custom-call | flops 5000000000 | bytes 18000000 | tf_op jit(solution)/shard_map/pallas_call | solution.py:538
  5.6 5.1 %all-to-all-start = ((f32[8,16,8,128]{3,2,1,0:T(8,128)}), f32[8,16,8,128]{3,2,1,0:T(8,128)S(1)}, u32[]{:S(2)}, u32[]{:S(2)}) async-start(f32[8,16,8,128]{3,2,1,0:T(8,128)} %bitcast.10), calls=%async_computation | async-start | bytes 1048576 | tf_op jit(solution)/shard_map/all_to_all | solution.py:548
  10.8 0.0 copy-done.2
  10.8 0.0 copy-done.3
  10.8 0.0 copy-done.4
  10.8 0.0 copy-done.5
  10.8 0.0 copy-done.6
  10.8 0.0 copy-done.7
  10.8 0.0 copy-done.8
  10.8 0.0 copy-start.1
  10.8 1.0 copy-done.1
  11.9 5.4 %shard_map.95.slip_a_hbm = f32[3,8192]{1,0:T(4,128)S(1)} custom-call(f32[128,8,128]{2,1,0:T(8,128)S(1)} %copy-done.1, s32[128]{0:T(128)S(1)} %copy-done.8, s32[128,128]{1,0:T(8,128)S(1)} %bitcast.17, f32[3,16384]{1,0:T(4,128)S(1)} %copy-done.4, f32[3,16384]{1,0:T(4,128)S(1)} %copy-done.3, f32[128,128]{1,0:T(8,128)S(1)} %bitcast.14, f32[128,128]{1,0:T(8,128)S(1)} %bitcast.12, ...), custom_call_target="tpu_custom_call" | custom-call | flops 5000000000 | bytes 18000000 | tf_op jit(solution)/shard_map/pallas_call | solution.py:552
  17.3 0.0 copy-start.9
  17.3 0.6 copy-done.9
  17.9 0.6 all-to-all-done.parts_ref
  18.6 0.9 shard_map.96.after_any
  19.5 5.2 %all-to-all-start.1 = ((f32[8,16,8,128]{3,2,1,0:T(8,128)}), f32[8,16,8,128]{3,2,1,0:T(8,128)S(1)}, u32[]{:S(2)}, u32[]{:S(2)}) async-start(f32[8,16,8,128]{3,2,1,0:T(8,128)} %shard_map.96.after_any), calls=%async_computation.1 | async-start | bytes 1048576 | tf_op jit(solution)/shard_map/all_to_all | solution.py:582
  24.7 0.0 copy-start
  24.7 1.1 copy-done
  25.7 5.4 %shard_map.97.slip_b_ref = f32[3,8192]{1,0:T(4,128)S(1)} custom-call(f32[8,16,8,128]{3,2,1,0:T(8,128)S(1)} %copy-done, s32[128]{0:T(128)S(1)} %copy-done.8, s32[128,128]{1,0:T(8,128)S(1)} %bitcast.18, f32[3,16384]{1,0:T(4,128)S(1)} %copy-done.4, f32[3,16384]{1,0:T(4,128)S(1)} %copy-done.3, f32[128,128]{1,0:T(8,128)S(1)} %bitcast.15, ...), custom_call_target="tpu_custom_call" | custom-call | flops 5000000000 | bytes 18000000 | tf_op jit(solution)/shard_map/pallas_call | solution.py:552
  31.2 1.3 %all-to-all-done.1 = f32[8,16,8,128]{3,2,1,0:T(8,128)S(1)} async-done(((f32[8,16,8,128]{3,2,1,0:T(8,128)}), f32[8,16,8,128]{3,2,1,0:T(8,128)S(1)}, u32[]{:S(2)}, u32[]{:S(2)}) %all-to-all-start.1) | async-done | bytes 524320 | tf_op jit(solution)/shard_map/all_to_all | solution.py:582
  32.5 7.6 %shard_map.98 = (f32[3,16384]{1,0:T(4,128)}, f32[8,66,8,128]{3,2,1,0:T(8,128)}, f32[8,128]{1,0:T(8,128)S(1)}) custom-call(s32[128]{0:T(128)S(1)} %copy-done.8, s32[128,128]{1,0:T(8,128)S(1)} %bitcast.19, f32[3,16384]{1,0:T(4,128)S(1)} %copy-done.4, f32[3,8192]{1,0:T(4,128)} %copy-done.9, f32[3,8192]{1,0:T(4,128)S(1)} %shard_map.97.slip_b_ref, ...), custom_call_target="tpu_custom_call" | custom-call | flops 6000000000 | bytes 21600000 | tf_op jit(solution)/shard_map/pallas_call | solution.py:583
  40.1 5.2 %all-to-all-start.2 = ((f32[8,66,8,128]{3,2,1,0:T(8,128)}), f32[8,66,8,128]{3,2,1,0:T(8,128)S(1)}, u32[]{:S(2)}, u32[]{:S(2)}) async-start(f32[8,66,8,128]{3,2,1,0:T(8,128)} %get-tuple-element.21), calls=%async_computation.2 | async-start | bytes 4325376 | tf_op jit(solution)/shard_map/all_to_all | solution.py:595
  45.3 0.1 pad_add_fusion.place_ref
  45.4 1.7 %shard_map.99 = (f32[3,8,32,128]{3,2,1,0:T(8,128)S(1)}, f32[3,4,32,128]{3,2,1,0:T(8,128)S(1)}, f32[3,4,32,128]{3,2,1,0:T(8,128)S(1)}) custom-call(s32[4]{0:T(128)S(1)} %pad_add_fusion.place_ref, f32[8,128]{1,0:T(8,128)S(1)} %get-tuple-element.16.after_any, f32[3,8,128,128]{3,2,1,0:T(8,128)} %velocity_hbm.5), custom_call_target="tpu_custom_call" | custom-call | flops 1000000000 | bytes 3600000 | tf_op jit(solution)/shard_map/pallas_call | solution.py:598
  47.1 1.3 %collective-permute-start = (f32[3,4,32,128]{3,2,1,0:T(8,128)S(1)}, f32[3,4,32,128]{3,2,1,0:T(8,128)S(1)}, u32[]{:S(2)}, u32[]{:S(2)}) collective-permute-start(f32[3,4,32,128]{3,2,1,0:T(8,128)S(1)} %get-tuple-element.18), channel_id=1, source_target_pairs={{0,8},{16,24},{32,40},{48,56},{64,72},{80,88},{96,104},{112,120},{... | collective-permute-start | bytes 589832 | tf_op jit(solution)/shard_map/ppermute | solution.py:516
  48.3 1.9 %collective-permute-start.1 = (f32[3,4,32,128]{3,2,1,0:T(8,128)S(1)}, f32[3,4,32,128]{3,2,1,0:T(8,128)S(1)}, u32[]{:S(2)}, u32[]{:S(2)}) collective-permute-start(f32[3,4,32,128]{3,2,1,0:T(8,128)S(1)} %get-tuple-element.19), channel_id=1, source_target_pairs={{8,16},{24,32},{40,48},{56,64},{72,80},{88,96},{104,112},{120,128}... | collective-permute-start | bytes 589832 | tf_op jit(solution)/shard_map/ppermute | solution.py:516
  50.3 1.8 %shard_map.101 = (f32[8,128,128]{2,1,0:T(8,128)}, f32[8,128]{1,0:T(8,128)S(1)}) custom-call(f32[8,128]{1,0:T(8,128)S(1)} %get-tuple-element.16.after_any, f32[128,8,128]{2,1,0:T(8,128)S(1)} %bitcast.8), custom_call_target="tpu_custom_call" | custom-call | flops 2000000000 | bytes 7200000 | tf_op jit(solution)/shard_map/pallas_call | solution.py:605
  52.0 0.0 collective-permute-done.even_ref
  52.0 7.0 %collective-permute-done.1.odd_ref = f32[3,4,32,128]{3,2,1,0:T(8,128)S(1)} collective-permute-done((f32[3,4,32,128]{3,2,1,0:T(8,128)S(1)}, f32[3,4,32,128]{3,2,1,0:T(8,128)S(1)}, u32[]{:S(2)}, u32[]{:S(2)}) %collective-permute-start.1) | collective-permute-done | bytes 196640 | tf_op jit(solution)/shard_map/ppermute | solution.py:516
  59.0 1.5 %shard_map.100 = (f32[3,14,32,128]{3,2,1,0:T(8,128)S(1)}, f32[8,128]{1,0:T(8,128)S(1)}) custom-call(s32[4]{0:T(128)S(1)} %pad_add_fusion.place_ref, f32[3,8,32,128]{3,2,1,0:T(8,128)S(1)} %get-tuple-element.17.window_ref, f32[3,4,32,128]{3,2,1,0:T(8,128)S(1)} %collective-permute-done.even_ref, f32[3,4,32,128]{3,2,1,0:T(8,128)S(1)} %collective-permute-done.1.odd_ref), custom_call_target="tpu_custom_call" | custom-call | flops 1000000000 | bytes 3600000 | tf_op jit(solution)/shard_map/pallas_call | solution.py:608
  60.5 11.6 %all-to-all-done.2.parts_ref = f32[8,66,8,128]{3,2,1,0:T(8,128)S(1)} async-done(((f32[8,66,8,128]{3,2,1,0:T(8,128)}), f32[8,66,8,128]{3,2,1,0:T(8,128)S(1)}, u32[]{:S(2)}, u32[]{:S(2)}) %all-to-all-start.2) | async-done | bytes 2162720 | tf_op jit(solution)/shard_map/all_to_all | solution.py:595
  72.1 1.0 shard_map.102
  73.1 0.9 collective-permute-start.2
  74.0 1.9 %collective-permute-start.3 = (f32[3,3,24,128]{3,2,1,0:T(8,128)S(1)}, f32[3,3,24,128]{3,2,1,0:T(8,128)S(1)}, u32[]{:S(2)}, u32[]{:S(2)}) collective-permute-start(f32[3,3,24,128]{3,2,1,0:T(8,128)S(1)} %get-tuple-element.26), channel_id=1, source_target_pairs={{8,16},{24,32},{40,48},{56,64},{72,80},{88,96},{104,112},{120,128}... | collective-permute-start | bytes 331784 | tf_op jit(solution)/shard_map/ppermute | solution.py:516
  76.0 0.0 collective-permute-done.2.even_ref
  76.0 7.7 %collective-permute-done.3.odd_ref = f32[3,3,24,128]{3,2,1,0:T(8,128)S(1)} collective-permute-done((f32[3,3,24,128]{3,2,1,0:T(8,128)S(1)}, f32[3,3,24,128]{3,2,1,0:T(8,128)S(1)}, u32[]{:S(2)}, u32[]{:S(2)}) %collective-permute-start.3) | collective-permute-done | bytes 110624 | tf_op jit(solution)/shard_map/ppermute | solution.py:516
  83.7 2.8 %shard_map.103 = f32[8,3,8,16,128]{4,3,2,1,0:T(8,128)S(1)} custom-call(s32[4]{0:T(128)S(1)} %pad_add_fusion.place_ref, f32[3,14,32,128]{3,2,1,0:T(8,128)S(1)} %get-tuple-element.20.first_ref, f32[3,8,24,128]{3,2,1,0:T(8,128)S(1)} %get-tuple-element.24.own_ref, f32[3,3,24,128]{3,2,1,0:T(8,128)S(1)} %collective-permute-done.2.even_ref, ...), custom_call_target="tpu_custom_call" | custom-call | flops 4000000000 | bytes 14400000 | tf_op jit(solution)/shard_map/pallas_call | solution.py:623
  86.5 22.0 %all_to_all.20.parts_ref = f32[8,3,8,16,128]{4,3,2,1,0:T(8,128)S(1)} all-to-all(f32[8,3,8,16,128]{4,3,2,1,0:T(8,128)S(1)} %shard_map.103), channel_id=1, replica_groups=mesh['slab'=32,'sub'=8] {'sub'}, dimensions={0} | all-to-all | bytes 3145728 | tf_op jit(solution)/shard_map/all_to_all | solution.py:634
  108.5 1.2 %shard_map.104 = f32[3,8,128,128]{3,2,1,0:T(8,128)} custom-call(f32[8,3,8,16,128]{4,3,2,1,0:T(8,128)S(1)} %all_to_all.20.parts_ref), custom_call_target="tpu_custom_call" | custom-call | flops 1000000000 | bytes 3600000 | tf_op jit(solution)/shard_map/pallas_call | solution.py:635
Async XLA Ops:
  0.6 10.1 %copy-start.2 = (f32[3,8,128,128]{3,2,1,0:T(8,128)S(1)}, f32[3,8,128,128]{3,2,1,0:T(8,128)}, u32[]{:S(2)}) copy-start(f32[3,8,128,128]{3,2,1,0:T(8,128)} %velocity_hbm.5) | copy-start | bytes 4718596
  0.6 10.1 %copy-start.3 = (f32[3,16384]{1,0:T(4,128)S(1)}, f32[3,16384]{1,0:T(4,128)}, u32[]{:S(2)}) copy-start(f32[3,16384]{1,0:T(4,128)} %pvel_hbm.3) | copy-start | bytes 589828
  0.7 10.1 %copy-start.4 = (f32[3,16384]{1,0:T(4,128)S(1)}, f32[3,16384]{1,0:T(4,128)}, u32[]{:S(2)}) copy-start(f32[3,16384]{1,0:T(4,128)} %frac_ref.1) | copy-start | bytes 589828
  0.7 10.1 %copy-start.5 = (f32[16384]{0:T(1024)S(1)}, f32[16384]{0:T(1024)}, u32[]{:S(2)}) copy-start(f32[16384]{0:T(1024)} %param.12) | copy-start | bytes 196612
  0.7 10.1 %copy-start.6 = (f32[16384]{0:T(1024)S(1)}, f32[16384]{0:T(1024)}, u32[]{:S(2)}) copy-start(f32[16384]{0:T(1024)} %param.11) | copy-start | bytes 196612
  0.7 10.1 %copy-start.7 = (s32[16384]{0:T(1024)S(1)}, s32[16384]{0:T(1024)}, u32[]{:S(2)}) copy-start(s32[16384]{0:T(1024)} %param.10) | copy-start | bytes 196612
  0.7 10.1 %copy-start.8 = (s32[128]{0:T(128)S(1)}, s32[128]{0:T(128)}, u32[]{:S(2)}) copy-start(s32[128]{0:T(128)} %brick_ref.1) | copy-start | bytes 1540
  5.6 13.0 %all-to-all-start = ((f32[8,16,8,128]{3,2,1,0:T(8,128)}), f32[8,16,8,128]{3,2,1,0:T(8,128)S(1)}, u32[]{:S(2)}, u32[]{:S(2)}) async-start(f32[8,16,8,128]{3,2,1,0:T(8,128)} %bitcast.10), calls=%async_computation | async-start | bytes 1048576 | tf_op jit(solution)/shard_map/all_to_all | solution.py:548
  10.8 1.0 copy-start.1
  17.3 0.7 copy-start.9
  19.5 13.0 %all-to-all-start.1 = ((f32[8,16,8,128]{3,2,1,0:T(8,128)}), f32[8,16,8,128]{3,2,1,0:T(8,128)S(1)}, u32[]{:S(2)}, u32[]{:S(2)}) async-start(f32[8,16,8,128]{3,2,1,0:T(8,128)} %shard_map.96.after_any), calls=%async_computation.1 | async-start | bytes 1048576 | tf_op jit(solution)/shard_map/all_to_all | solution.py:582
  24.7 1.1 copy-start
  40.1 32.0 %all-to-all-start.2 = ((f32[8,66,8,128]{3,2,1,0:T(8,128)}), f32[8,66,8,128]{3,2,1,0:T(8,128)S(1)}, u32[]{:S(2)}, u32[]{:S(2)}) async-start(f32[8,66,8,128]{3,2,1,0:T(8,128)} %get-tuple-element.21), calls=%async_computation.2 | async-start | bytes 4325376 | tf_op jit(solution)/shard_map/all_to_all | solution.py:595
  47.1 4.9 %collective-permute-start = (f32[3,4,32,128]{3,2,1,0:T(8,128)S(1)}, f32[3,4,32,128]{3,2,1,0:T(8,128)S(1)}, u32[]{:S(2)}, u32[]{:S(2)}) collective-permute-start(f32[3,4,32,128]{3,2,1,0:T(8,128)S(1)} %get-tuple-element.18), channel_id=1, source_target_pairs={{0,8},{16,24},{32,40},{48,56},{64,72},{80,88},{96,104},{112,120},{... | collective-permute-start | bytes 589832 | tf_op jit(solution)/shard_map/ppermute | solution.py:516
  48.3 10.7 %collective-permute-start.1 = (f32[3,4,32,128]{3,2,1,0:T(8,128)S(1)}, f32[3,4,32,128]{3,2,1,0:T(8,128)S(1)}, u32[]{:S(2)}, u32[]{:S(2)}) collective-permute-start(f32[3,4,32,128]{3,2,1,0:T(8,128)S(1)} %get-tuple-element.19), channel_id=1, source_target_pairs={{8,16},{24,32},{40,48},{56,64},{72,80},{88,96},{104,112},{120,128}... | collective-permute-start | bytes 589832 | tf_op jit(solution)/shard_map/ppermute | solution.py:516
  73.1 2.9 %collective-permute-start.2 = (f32[3,3,24,128]{3,2,1,0:T(8,128)S(1)}, f32[3,3,24,128]{3,2,1,0:T(8,128)S(1)}, u32[]{:S(2)}, u32[]{:S(2)}) collective-permute-start(f32[3,3,24,128]{3,2,1,0:T(8,128)S(1)} %get-tuple-element.25), channel_id=1, source_target_pairs={{0,8},{16,24},{32,40},{48,56},{64,72},{80,88},{96,104},{112,120},{... | collective-permute-start | bytes 331784 | tf_op jit(solution)/shard_map/ppermute | solution.py:516
  74.0 9.7 %collective-permute-start.3 = (f32[3,3,24,128]{3,2,1,0:T(8,128)S(1)}, f32[3,3,24,128]{3,2,1,0:T(8,128)S(1)}, u32[]{:S(2)}, u32[]{:S(2)}) collective-permute-start(f32[3,3,24,128]{3,2,1,0:T(8,128)S(1)} %get-tuple-element.26), channel_id=1, source_target_pairs={{8,16},{24,32},{40,48},{56,64},{72,80},{88,96},{104,112},{120,128}... | collective-permute-start | bytes 331784 | tf_op jit(solution)/shard_map/ppermute | solution.py:516

commit v5 on v4

--- a/solution.py
+++ b/solution.py
@@ -242,22 +242,6 @@
     copy.wait()
 
 
-def pack_halo(rows, tiles):
-    a, b, c, d = tiles
-    middle = jnp.logical_or(rows == 3, rows == 4)
-    first = jnp.where(middle, pltpu.roll(d, 3, 0), a)
-    second = jnp.where(rows == 3, pltpu.roll(d, 1, 0), jnp.where(rows == 4, pltpu.roll(d, 7, 0), b))
-    third = jnp.where(middle, pltpu.roll(d, 5, 0), c)
-    return first, second, third
-
-
-def unpack_halo(rows, tiles):
-    a, b, c = tiles
-    inner = jnp.where(rows == 2, pltpu.roll(b, 7, 0), pltpu.roll(b, 1, 0))
-    d = jnp.where(rows < 2, pltpu.roll(a, 5, 0), jnp.where(rows > 5, pltpu.roll(c, 3, 0), inner))
-    return a, b, c, d
-
-
 def drag_kernel(
     brick_ref, base_ref, frac_ref, slip_a_hbm, slip_b_ref, eps_ref,
     drag_ref, out_hbm, tick_ref,
@@ -267,7 +251,7 @@
     rows, lane = rows_iota(), lanes_iota()
     (copy,) = fetch([(slip_a_hbm, slip_a_ref)], sems)
     for j in range(subs):
-        force_ref[j, 0:48] = jnp.zeros((48, 8, LANES), F32)
+        force_ref[j] = jnp.zeros(force_ref.shape[1:], F32)
     copy.wait()
 
     for slip_ref, start in ((slip_a_ref, 0), (slip_b_ref, slip_a_ref.shape[1] // BLOCK)):
@@ -299,63 +283,53 @@
             return carry
 
         lax.fori_loop(0, slip_ref.shape[1] // BLOCK // UNROLL, step, 0)
-    copies = fetch([(force_ref.at[j, 0:48], out_hbm.at[j, 0:48]) for j in range(subs)], sems)
-    zero = jnp.zeros((8, LANES), F32)
-    tick_ref[...] = zero
-    for j in range(subs):
-        for quad in range(6):
-            tiles = []
-            for at in range(quad * 4, quad * 4 + 4):
-                after = force_ref[j + 1, at] if j + 1 < subs else zero
-                before = force_ref[j - 1, 24 + at] if j > 0 else zero
-                tiles.append(jnp.where(rows < 4, after, before))
-            for n, tile in enumerate(pack_halo(rows, tiles)):
-                force_ref[j, 48 + quad * 3 + n] = tile
-        copy = pltpu.make_async_copy(
-            force_ref.at[j, 48:66], out_hbm.at[j, 48:66], sems.at[subs + j]
-        )
-        copy.start()
-        copies.append(copy)
-    for copy in copies:
+    tick_ref[...] = jnp.zeros_like(tick_ref)
+    for copy in fetch([(force_ref.at[j], out_hbm.at[j]) for j in range(subs)], sems):
         copy.wait()
 
 
-def source_kernel(place_ref, parts_ref, eps_ref, first_any, void_any, own_ref, even_ref, odd_ref):
+def source_kernel(place_ref, parts_ref, eps_ref, first_any, own_ref, even_ref, odd_ref):
     lane, rows = lanes_iota(), rows_iota()
-    even, sub = place_ref[0] % 2 == 0, place_ref[1]
-    tiles_x = eps_ref.shape[0] // 8
-    after = jnp.minimum(sub * 2 + 2, tiles_x - 1) * 8
-    before = jnp.maximum(sub * 2 - 1, 0) * 8
-
-    def summed(at):
-        total = parts_ref[0, at]
-        for j in range(1, parts_ref.shape[0]):
-            total = total + parts_ref[j, at]
-        return total
-
-    for t in range(3):
-        for c in range(3):
-            if t < 2:
-                forces = [summed(t * 24 + c * 8 + t3) for t3 in range(8)]
-            else:
-                forces = []
-                for quad in (2 * c, 2 * c + 1):
-                    forces += unpack_halo(rows, [summed(48 + quad * 3 + k) for k in range(3)])
+    even = place_ref[1] % 2 == 0
+    for c in range(3):
+        grid = []
+        for t in range(2):
             tiles = []
             for t3 in range(8):
-                if t < 2:
-                    eps = eps_ref[(sub * 2 + t) * 8 + t3]
-                else:
-                    eps = jnp.where(rows < 4, eps_ref[after + t3], eps_ref[before + t3])
-                tiles.append(-forces[t3] / eps)
+                at = (t * 3 + c) * 8 + t3
+                total = parts_ref[0, at]
+                for j in range(1, parts_ref.shape[0]):
+                    total = total + parts_ref[j, at]
+                tiles.append(-total / eps_ref[t * 8 + t3])
             tiles = transpose_granules(tiles, lane)
-            first = 8 * (t + 1) % 24
             for z in range(8):
-                own_ref[c, z, first : first + 8, :] = tiles[z]
-            for n in range(3):
-                at = slice(first, first + 8)
-                even_ref[c, n, at, :] = jnp.where(even, tiles[5 + n], tiles[n])
-                odd_ref[c, n, at, :] = jnp.where(even, tiles[n], tiles[5 + n])
+                own_ref[c, z, 8 * t : 8 * t + 8, :] = tiles[z]
+            grid.append(tiles)
+        for q in range(4):
+            first = jnp.where(rows < 4, grid[0][2 * q], pltpu.roll(grid[0][2 * q + 1], 4, 0))
+            last = jnp.where(rows < 4, pltpu.roll(grid[1][2 * q], 4, 0), grid[1][2 * q + 1])
+            even_ref[c, q] = jnp.where(even, last, first)
+            odd_ref[c, q] = jnp.where(even, first, last)
+
+
+def halo_kernel(place_ref, own_ref, even_ref, odd_ref, halo_ref, up_ref, down_ref):
+    rows = rows_iota()
+    slab_even, sub_even = place_ref[0] % 2 == 0, place_ref[1] % 2 == 0
+    for c in range(3):
+        tiles = []
+        for q in range(4):
+            after = jnp.where(sub_even, even_ref[c, q], odd_ref[c, q])
+            before = jnp.where(sub_even, odd_ref[c, q], even_ref[c, q])
+            tiles.append(jnp.where(rows < 4, after, pltpu.roll(before, 4, 0)))
+            tiles.append(jnp.where(rows < 4, pltpu.roll(after, 4, 0), before))
+        for z in range(8):
+            halo_ref[c, z] = tiles[z]
+        for n in range(3):
+            low, high = own_ref[c, n], own_ref[c, 5 + n]
+            up_ref[c, n, 0:8, :] = jnp.where(slab_even, tiles[5 + n], tiles[n])
+            up_ref[c, n, 8:24, :] = jnp.where(slab_even, high, low)
+            down_ref[c, n, 0:8, :] = jnp.where(slab_even, tiles[n], tiles[5 + n])
+            down_ref[c, n, 8:24, :] = jnp.where(slab_even, low, high)
 
 
 def window_kernel(place_ref, after_any, velocity_hbm, out_ref, even_ref, odd_ref, sems):
@@ -378,8 +352,7 @@
         odd_ref[:, :, at, :] = jnp.where(even, rows[:, :4], rows[:, depth - 4 :])
 
 
-def void_kernel(after_any, eps_ref, out_ref, tick_ref):
-    tick_ref[...] = jnp.zeros_like(tick_ref)
+def void_kernel(place_ref, after_any, eps_ref, out_ref, own_ref):
     lane = lanes_iota()
 
     def convert(number, carry):
@@ -391,6 +364,7 @@
         return carry
 
     lax.fori_loop(0, out_ref.shape[1] // 32, convert, 0)
+    own_ref[...] = eps_ref[pl.ds(place_ref[1] * own_ref.shape[0], own_ref.shape[0])]
 
 
 def edges(slab, sub, planes, width):
@@ -443,13 +417,16 @@
 
 
 def stencil_kernel(
-    place_ref, first_ref, own_ref, even_ref, odd_ref, out_ref, even, odd, source
+    place_ref, first_ref, own_ref, halo_ref, even_ref, odd_ref, out_ref, even, odd, source
 ):
     keep = edges(place_ref[0], place_ref[1], place_ref[2], place_ref[3])
     lane = lax.broadcasted_iota(jnp.int32, (32, LANES), 1)
     side = place_ref[0] % 2
-    parts = ((even_ref, pl.ds(11 - 11 * side, 3)), (own_ref, slice(3, 11)), (odd_ref, pl.ds(11 * side, 3)))
-    for part, planes in parts:
+    source[:, 3:11, 0:8, :] = halo_ref[...]
+    source[:, 3:11, 8:24, :] = own_ref[...]
+    source[:, 3:11, 24:32, :] = halo_ref[...]
+    for part, start in ((even_ref, 11 - 11 * side), (odd_ref, 11 * side)):
+        planes = pl.ds(start, 3)
         source[:, planes, 0:24, :] = part[...]
         source[:, planes, 24:32, :] = part[:, :, 0:8, :]
 
@@ -511,9 +488,9 @@
     )
 
 
-def pair_up(x, first):
-    pairs = [(i, i + 1) for i in range(first, lax.axis_size("slab") - 1, 2)]
-    return lax.ppermute(x, "slab", pairs + [(j, i) for i, j in pairs])
+def pair_up(x, first, axis="slab"):
+    pairs = [(i, i + 1) for i in range(first, lax.axis_size(axis) - 1, 2)]
+    return lax.ppermute(x, axis, pairs + [(j, i) for i, j in pairs])
 
 
 def body(velocity, part_vel, fraction, base_cell, drag_coeff, part_volume, brick_of_block):
@@ -582,12 +559,12 @@
     eps = lax.all_to_all(eps_copies, "sub", 0, 0).reshape(tiles, 8, LANES)
     drag, force, tick = call(
         drag_kernel,
-        [(3, blocks * BLOCK), (subs, 66, 8, LANES), (8, LANES)],
+        [(3, blocks * BLOCK), (subs, 48, 8, LANES), (8, LANES)],
         [SMEM, VMEM, VMEM, HBM, VMEM, VMEM],
         [
-            pltpu.VMEM((subs, 66, 8, LANES), F32),
+            pltpu.VMEM((subs, 48, 8, LANES), F32),
             pltpu.VMEM((3, half * BLOCK), F32),
-            pltpu.SemaphoreType.DMA((2 * subs,)),
+            pltpu.SemaphoreType.DMA((subs,)),
         ],
         outs=[VMEM, HBM, VMEM],
         us=6.0,
@@ -602,9 +579,9 @@
         [pltpu.SemaphoreType.DMA((4,))],
     )(place, tick, *pinned(velocity))
     even, odd = pair_up(even, 0), pair_up(odd, 1)
-    voidfraction, void_tick = call(
-        void_kernel, [(depth, width_x, LANES), (8, LANES)], [ANY, VMEM], us=2.0
-    )(tick, eps)
+    voidfraction, eps_own = call(
+        void_kernel, [(depth, width_x, LANES), (share, 8, LANES)], [SMEM, ANY, VMEM], us=2.0
+    )(place, tick, eps)
     first, first_tick = call(
         first_kernel,
         [(3, 14, 32, LANES), (8, LANES)],
@@ -616,21 +593,27 @@
     rows = width_x // subs
     own, even, odd = call(
         source_kernel,
-        [(3, depth, 24, LANES), (3, 3, 24, LANES), (3, 3, 24, LANES)],
-        [SMEM, VMEM, VMEM, ANY, ANY],
-    )(place, forces, eps, first_tick, void_tick)
+        [(3, depth, rows, LANES), (3, 4, 8, LANES), (3, 4, 8, LANES)],
+        [SMEM, VMEM, VMEM, ANY],
+    )(place, forces, eps_own, first_tick)
+    even, odd = pair_up(even, 0, "sub"), pair_up(odd, 1, "sub")
+    halo, even, odd = call(
+        halo_kernel,
+        [(3, depth, 8, LANES), (3, 3, 24, LANES), (3, 3, 24, LANES)],
+        [SMEM] + [VMEM] * 3,
+    )(place, own, even, odd)
     even, odd = pair_up(even, 0), pair_up(odd, 1)
     (moved,) = call(
         stencil_kernel,
         [(subs, 3, depth, rows, LANES)],
-        [SMEM] + [VMEM] * 4,
+        [SMEM] + [VMEM] * 5,
         [
             pltpu.VMEM((3, 16, 32, LANES), F32),
             pltpu.VMEM((3, 16, 32, LANES), F32),
             pltpu.VMEM((3, 14, 32, LANES), F32),
         ],
         us=4.0,
-    )(place, first, own, even, odd)
+    )(place, first, own, halo, even, odd)
     moved = lax.all_to_all(moved, "sub", 0, 0)
     (new_velocity,) = call(
         place_kernel,

time: 110 us -> 112 us (1.018)
  waiting for transfers between devices: 28.3 us -> 22 us
  blocking collectives: 22 us -> 26.1 us
  starting transfers between devices: 21.5 us -> 23.8 us
  local copies, waits for them, and re-layouts: 2.79 us -> 4.21 us
    all_to_all x1, waiting for transfers between devices: 11.6 us -> 4.91 us  [body(): forces = lax.all_to_all(force, 'sub', 0, 0)]
    all_to_all x1, blocking collectives: 22 us -> 26.1 us  [body(): moved = lax.all_to_all(moved, 'sub', 0, 0)]
    ppermute x4 -> x6, starting transfers between devices: 6.02 us -> 8.28 us  [pair_up(): return lax.ppermute(x, axis, pairs + [(j, i) for i, j in pairs])]
    ppermute x4 -> x6, waiting for transfers between devices: 14.7 us -> 16.5 us  [pair_up(): return lax.ppermute(x, axis, pairs + [(j, i) for i, j in pairs])]
    unnamed x20 -> x22, local copies, waits for them, and re-layouts: 2.79 us -> 4.21 us
    all_to_all x1, waiting for transfers between devices: 1.32 us -> 0.01 us  [body(): eps = lax.all_to_all(eps_copies, 'sub', 0, 0).reshape(tiles, 8, LANES)]
    pallas_call x4 -> x5, Pallas kernels: 13.2 us -> 13.8 us  [the longest x1 7.33 us: body(): call(drag_kernel, [(3, blocks * BLOCK), (subs, 48, 8, LANES), (8, LANES)]...]
  transfers between devices with their start and end apart: 7 -> 9, of which waited for: 5 -> 5; matrix products, arithmetic and copies ran while one was open for 0% -> 0% of each run, Pallas kernels for 14% -> 15%
where the time goes in v5:
time: 112 us
  Pallas kernels  34.9 us (31%)
  blocking collectives  26.1 us (23%)
  starting transfers between devices  23.8 us (21%)
  waiting for transfers between devices  22 us (20%)
  local copies, waits for them, and re-layouts  4.21 us (4%)
    all_to_all x1, blocking collectives, body(): moved = lax.all_to_all(moved, 'sub', 0, 0)  26.1 us
    ppermute x6, waiting for transfers between devices, pair_up(): return lax.ppermute(x, axis, pairs + [(j, i) for i, j in pairs])  16.5 us
    pallas_call x2, Pallas kernels, slip_of(): call(functools.partial(slip_kernel, first, half), [(3, half * BLOCK)], [H...  10.8 us
    ppermute x6, starting transfers between devices, pair_up(): return lax.ppermute(x, axis, pairs + [(j, i) for i, j in pairs])  8.28 us
    pallas_call x1, Pallas kernels, body(): call(drag_kernel, [(3, blocks * BLOCK), (subs, 48, 8, LANES), (8, LANES)]...  7.33 us
    all_to_all x1, starting transfers between devices, body(): eps = lax.all_to_all(eps_copies, 'sub', 0, 0).reshape(tiles, 8, LANES)  5.2 us
    all_to_all x1, starting transfers between devices, body(): forces = lax.all_to_all(force, 'sub', 0, 0)  5.15 us
    all_to_all x1, starting transfers between devices, body(): lax.all_to_all(solid.reshape(subs, share, 8, LANES), 'sub', 0, 0)  5.12 us
  transfers between devices with their start and end apart: 9, of which 5 were waited for; matrix products, arithmetic and copies ran while one was open for 0% of the time, Pallas kernels for 15%

profile of v5, /device:TPU:225, one launch (start us, length us, event | category | flops | bytes accessed | tf_op | source)
XLA Modules:
  0.0 111.8 jit_solution(8698243185860159958)
XLA Ops:
  0.6 0.0 copy-start.2
  0.6 0.0 copy-start.4
  0.7 0.0 copy-start.5
  0.7 0.0 copy-start.6
  0.7 0.0 copy-start.7
  0.7 0.0 copy-start.8
  0.7 0.0 copy-start.9
  0.7 4.9 %shard_map.94.after_any = f32[128,8,128]{2,1,0:T(8,128)} custom-call(s32[128]{0:T(128)} %brick_ref.1, s32[128,128]{1,0:T(8,128)} %bitcast.15, f32[3,16384]{1,0:T(4,128)} %frac_ref.1, f32[128,128]{1,0:T(8,128)} %bitcast.10), custom_call_target="tpu_custom_call" | custom-call | flops 5000000000 | bytes 18000000 | tf_op jit(solution)/shard_map/pallas_call | solution.py:515
  5.6 5.1 %all-to-all-start = ((f32[8,16,8,128]{3,2,1,0:T(8,128)}), f32[8,16,8,128]{3,2,1,0:T(8,128)S(1)}, u32[]{:S(2)}, u32[]{:S(2)}) async-start(f32[8,16,8,128]{3,2,1,0:T(8,128)} %bitcast.9), calls=%async_computation | async-start | bytes 1048576 | tf_op jit(solution)/shard_map/all_to_all | solution.py:525
  10.8 0.0 copy-done.2
  10.8 0.0 copy-done.4
  10.8 0.0 copy-done.5
  10.8 0.0 copy-done.6
  10.8 0.0 copy-done.7
  10.8 0.0 copy-done.8
  10.8 0.0 copy-done.9
  10.8 0.0 copy-start.1
  10.8 1.0 copy-done.1
  11.9 5.4 %shard_map.95.slip_a_hbm = f32[3,8192]{1,0:T(4,128)S(1)} custom-call(f32[128,8,128]{2,1,0:T(8,128)S(1)} %copy-done.1, s32[128]{0:T(128)S(1)} %copy-done.9, s32[128,128]{1,0:T(8,128)S(1)} %bitcast.16, f32[3,16384]{1,0:T(4,128)S(1)} %copy-done.5, f32[3,16384]{1,0:T(4,128)S(1)} %copy-done.4, f32[128,128]{1,0:T(8,128)S(1)} %bitcast.13, f32[128,128]{1,0:T(8,128)S(1)} %bitcast.11, ...), custom_call_target="tpu_custom_call" | custom-call | flops 5000000000 | bytes 18000000 | tf_op jit(solution)/shard_map/pallas_call | solution.py:529
  17.3 0.0 copy-start.10
  17.3 0.7 copy-done.10
  18.0 0.6 all-to-all-done.parts_ref
  18.6 0.9 shard_map.96.after_any
  19.5 5.2 %all-to-all-start.1 = ((f32[8,16,8,128]{3,2,1,0:T(8,128)}), f32[8,16,8,128]{3,2,1,0:T(8,128)S(1)}, u32[]{:S(2)}, u32[]{:S(2)}) async-start(f32[8,16,8,128]{3,2,1,0:T(8,128)} %shard_map.96.after_any), calls=%async_computation.1 | async-start | bytes 1048576 | tf_op jit(solution)/shard_map/all_to_all | solution.py:559
  24.6 0.0 copy-start
  24.7 1.1 copy-done
  25.7 0.0 copy-start.3
  25.7 1.4 %copy-done.3 = f32[3,8,128,128]{3,2,1,0:T(8,128)S(1)} copy-done((f32[3,8,128,128]{3,2,1,0:T(8,128)S(1)}, f32[3,8,128,128]{3,2,1,0:T(8,128)}, u32[]{:S(2)}) %copy-start.3) | copy-done | bytes 1572888
  27.1 5.4 %shard_map.97.slip_b_ref = f32[3,8192]{1,0:T(4,128)S(1)} custom-call(f32[8,16,8,128]{3,2,1,0:T(8,128)S(1)} %copy-done, s32[128]{0:T(128)S(1)} %copy-done.9, s32[128,128]{1,0:T(8,128)S(1)} %bitcast.17, f32[3,16384]{1,0:T(4,128)S(1)} %copy-done.5, f32[3,16384]{1,0:T(4,128)S(1)} %copy-done.4, f32[128,128]{1,0:T(8,128)S(1)} %bitcast.14, ...), custom_call_target="tpu_custom_call" | custom-call | flops 5000000000 | bytes 18000000 | tf_op jit(solution)/shard_map/pallas_call | solution.py:529
  32.6 0.0 all-to-all-done.1
  32.6 7.3 %shard_map.98 = (f32[3,16384]{1,0:T(4,128)}, f32[8,48,8,128]{3,2,1,0:T(8,128)}, f32[8,128]{1,0:T(8,128)S(1)}) custom-call(s32[128]{0:T(128)S(1)} %copy-done.9, s32[128,128]{1,0:T(8,128)S(1)} %bitcast.18, f32[3,16384]{1,0:T(4,128)S(1)} %copy-done.5, f32[3,8192]{1,0:T(4,128)} %copy-done.10, f32[3,8192]{1,0:T(4,128)S(1)} %shard_map.97.slip_b_ref, ...), custom_call_target="tpu_custom_call" | custom-call | flops 6000000000 | bytes 21600000 | tf_op jit(solution)/shard_map/pallas_call | solution.py:560
  39.9 5.2 %all-to-all-start.2 = ((f32[8,48,8,128]{3,2,1,0:T(8,128)}), f32[8,48,8,128]{3,2,1,0:T(8,128)S(1)}, u32[]{:S(2)}, u32[]{:S(2)}) async-start(f32[8,48,8,128]{3,2,1,0:T(8,128)} %get-tuple-element.24), calls=%async_computation.2 | async-start | bytes 3145728 | tf_op jit(solution)/shard_map/all_to_all | solution.py:572
  45.1 0.1 pad_add_fusion.place_ref
  45.1 1.7 %shard_map.99 = (f32[3,8,32,128]{3,2,1,0:T(8,128)S(1)}, f32[3,4,32,128]{3,2,1,0:T(8,128)S(1)}, f32[3,4,32,128]{3,2,1,0:T(8,128)S(1)}) custom-call(s32[4]{0:T(128)S(1)} %pad_add_fusion.place_ref, f32[8,128]{1,0:T(8,128)S(1)} %get-tuple-element.19.after_any, f32[3,8,128,128]{3,2,1,0:T(8,128)} %velocity_hbm.5), custom_call_target="tpu_custom_call" | custom-call | flops 1000000000 | bytes 3600000 | tf_op jit(solution)/shard_map/pallas_call | solution.py:575
  46.9 1.6 %collective-permute-start = (f32[3,4,32,128]{3,2,1,0:T(8,128)S(1)}, f32[3,4,32,128]{3,2,1,0:T(8,128)S(1)}, u32[]{:S(2)}, u32[]{:S(2)}) collective-permute-start(f32[3,4,32,128]{3,2,1,0:T(8,128)S(1)} %get-tuple-element.21), channel_id=1, source_target_pairs={{0,8},{16,24},{32,40},{48,56},{64,72},{80,88},{96,104},{112,120},{... | collective-permute-start | bytes 589832 | tf_op jit(solution)/shard_map/ppermute | solution.py:493
  48.5 1.9 %collective-permute-start.1 = (f32[3,4,32,128]{3,2,1,0:T(8,128)S(1)}, f32[3,4,32,128]{3,2,1,0:T(8,128)S(1)}, u32[]{:S(2)}, u32[]{:S(2)}) collective-permute-start(f32[3,4,32,128]{3,2,1,0:T(8,128)S(1)} %get-tuple-element.22), channel_id=1, source_target_pairs={{8,16},{24,32},{40,48},{56,64},{72,80},{88,96},{104,112},{120,128}... | collective-permute-start | bytes 589832 | tf_op jit(solution)/shard_map/ppermute | solution.py:493
  50.4 2.3 %shard_map.101 = (f32[8,128,128]{2,1,0:T(8,128)}, f32[16,8,128]{2,1,0:T(8,128)S(1)}) custom-call(s32[4]{0:T(128)S(1)} %pad_add_fusion.place_ref, f32[8,128]{1,0:T(8,128)S(1)} %get-tuple-element.19.after_any, f32[128,8,128]{2,1,0:T(8,128)S(1)} %bitcast.8), custom_call_target="tpu_custom_call" | custom-call | flops 2000000000 | bytes 7200000 | tf_op jit(solution)/shard_map/pallas_call | solution.py:582
  52.7 0.0 collective-permute-done.even_ref
  52.7 6.5 %collective-permute-done.1.odd_ref = f32[3,4,32,128]{3,2,1,0:T(8,128)S(1)} collective-permute-done((f32[3,4,32,128]{3,2,1,0:T(8,128)S(1)}, f32[3,4,32,128]{3,2,1,0:T(8,128)S(1)}, u32[]{:S(2)}, u32[]{:S(2)}) %collective-permute-start.1) | collective-permute-done | bytes 196640 | tf_op jit(solution)/shard_map/ppermute | solution.py:493
  59.2 1.5 %shard_map.100 = (f32[3,14,32,128]{3,2,1,0:T(8,128)S(1)}, f32[8,128]{1,0:T(8,128)S(1)}) custom-call(s32[4]{0:T(128)S(1)} %pad_add_fusion.place_ref, f32[3,8,32,128]{3,2,1,0:T(8,128)S(1)} %get-tuple-element.20.window_ref, f32[3,4,32,128]{3,2,1,0:T(8,128)S(1)} %collective-permute-done.even_ref, f32[3,4,32,128]{3,2,1,0:T(8,128)S(1)} %collective-permute-done.1.odd_ref), custom_call_target="tpu_custom_call" | custom-call | flops 1000000000 | bytes 3600000 | tf_op jit(solution)/shard_map/pallas_call | solution.py:585
  60.7 4.9 %all-to-all-done.2.parts_ref = f32[8,48,8,128]{3,2,1,0:T(8,128)S(1)} async-done(((f32[8,48,8,128]{3,2,1,0:T(8,128)}), f32[8,48,8,128]{3,2,1,0:T(8,128)S(1)}, u32[]{:S(2)}, u32[]{:S(2)}) %all-to-all-start.2) | async-done | bytes 1572896 | tf_op jit(solution)/shard_map/all_to_all | solution.py:572
  65.6 0.8 shard_map.102
  66.4 0.1 collective-permute-start.2
  66.5 0.7 collective-permute-start.3
  67.2 2.3 %collective-permute-done.2.even_ref = f32[3,4,8,128]{3,2,1,0:T(8,128)S(1)} collective-permute-done((f32[3,4,8,128]{3,2,1,0:T(8,128)S(1)}, f32[3,4,8,128]{3,2,1,0:T(8,128)S(1)}, u32[]{:S(2)}, u32[]{:S(2)}) %collective-permute-start.2) | collective-permute-done | bytes 49184 | tf_op jit(solution)/shard_map/ppermute | solution.py:493
  69.4 0.0 collective-permute-done.3.odd_ref
  69.4 0.6 shard_map.103
  70.0 2.1 %collective-permute-start.4 = (f32[3,3,24,128]{3,2,1,0:T(8,128)S(1)}, f32[3,3,24,128]{3,2,1,0:T(8,128)S(1)}, u32[]{:S(2)}, u32[]{:S(2)}) collective-permute-start(f32[3,3,24,128]{3,2,1,0:T(8,128)S(1)} %get-tuple-element.31), channel_id=1, source_target_pairs={{0,8},{16,24},{32,40},{48,56},{64,72},{80,88},{96,104},{112,120},{... | collective-permute-start | bytes 331784 | tf_op jit(solution)/shard_map/ppermute | solution.py:493
  72.1 1.9 %collective-permute-start.5 = (f32[3,3,24,128]{3,2,1,0:T(8,128)S(1)}, f32[3,3,24,128]{3,2,1,0:T(8,128)S(1)}, u32[]{:S(2)}, u32[]{:S(2)}) collective-permute-start(f32[3,3,24,128]{3,2,1,0:T(8,128)S(1)} %get-tuple-element.32), channel_id=1, source_target_pairs={{8,16},{24,32},{40,48},{56,64},{72,80},{88,96},{104,112},{120,128}... | collective-permute-start | bytes 331784 | tf_op jit(solution)/shard_map/ppermute | solution.py:493
  74.0 0.0 collective-permute-done.4.even_ref
  74.0 7.7 %collective-permute-done.5.odd_ref = f32[3,3,24,128]{3,2,1,0:T(8,128)S(1)} collective-permute-done((f32[3,3,24,128]{3,2,1,0:T(8,128)S(1)}, f32[3,3,24,128]{3,2,1,0:T(8,128)S(1)}, u32[]{:S(2)}, u32[]{:S(2)}) %collective-permute-start.5) | collective-permute-done | bytes 110624 | tf_op jit(solution)/shard_map/ppermute | solution.py:493
  81.8 2.8 %shard_map.104 = f32[8,3,8,16,128]{4,3,2,1,0:T(8,128)S(1)} custom-call(s32[4]{0:T(128)S(1)} %pad_add_fusion.place_ref, f32[3,14,32,128]{3,2,1,0:T(8,128)S(1)} %get-tuple-element.23.first_ref, f32[3,8,16,128]{3,2,1,0:T(8,128)S(1)} %get-tuple-element.27.own_ref, f32[3,8,8,128]{3,2,1,0:T(8,128)S(1)} %get-tuple-element.30.halo_ref, ...), custom_call_target="tpu_custom_call" | custom-call | flops 4000000000 | bytes 14400000 | tf_op jit(solution)/shard_map/pallas_call | solution.py:606
  84.6 26.1 %all_to_all.20.parts_ref = f32[8,3,8,16,128]{4,3,2,1,0:T(8,128)S(1)} all-to-all(f32[8,3,8,16,128]{4,3,2,1,0:T(8,128)S(1)} %shard_map.104), channel_id=1, replica_groups=mesh['slab'=32,'sub'=8] {'sub'}, dimensions={0} | all-to-all | bytes 3145728 | tf_op jit(solution)/shard_map/all_to_all | solution.py:617
  110.6 1.2 %shard_map.105 = f32[3,8,128,128]{3,2,1,0:T(8,128)} custom-call(f32[8,3,8,16,128]{4,3,2,1,0:T(8,128)S(1)} %all_to_all.20.parts_ref), custom_call_target="tpu_custom_call" | custom-call | flops 1000000000 | bytes 3600000 | tf_op jit(solution)/shard_map/pallas_call | solution.py:618
Async XLA Ops:
  0.6 10.1 %copy-start.2 = (f32[3,8,128,128]{3,2,1,0:T(8,128)S(1)}, f32[3,8,128,128]{3,2,1,0:T(8,128)}, u32[]{:S(2)}) copy-start(f32[3,8,128,128]{3,2,1,0:T(8,128)} %velocity_hbm.5) | copy-start | bytes 4718596
  0.6 10.1 %copy-start.4 = (f32[3,16384]{1,0:T(4,128)S(1)}, f32[3,16384]{1,0:T(4,128)}, u32[]{:S(2)}) copy-start(f32[3,16384]{1,0:T(4,128)} %pvel_hbm.3) | copy-start | bytes 589828
  0.7 10.1 %copy-start.5 = (f32[3,16384]{1,0:T(4,128)S(1)}, f32[3,16384]{1,0:T(4,128)}, u32[]{:S(2)}) copy-start(f32[3,16384]{1,0:T(4,128)} %frac_ref.1) | copy-start | bytes 589828
  0.7 10.1 %copy-start.6 = (f32[16384]{0:T(1024)S(1)}, f32[16384]{0:T(1024)}, u32[]{:S(2)}) copy-start(f32[16384]{0:T(1024)} %param.12) | copy-start | bytes 196612
  0.7 10.1 %copy-start.7 = (f32[16384]{0:T(1024)S(1)}, f32[16384]{0:T(1024)}, u32[]{:S(2)}) copy-start(f32[16384]{0:T(1024)} %param.11) | copy-start | bytes 196612
  0.7 10.1 %copy-start.8 = (s32[16384]{0:T(1024)S(1)}, s32[16384]{0:T(1024)}, u32[]{:S(2)}) copy-start(s32[16384]{0:T(1024)} %param.10) | copy-start | bytes 196612
  0.7 10.1 %copy-start.9 = (s32[128]{0:T(128)S(1)}, s32[128]{0:T(128)}, u32[]{:S(2)}) copy-start(s32[128]{0:T(128)} %brick_ref.1) | copy-start | bytes 1540
  5.6 12.9 %all-to-all-start = ((f32[8,16,8,128]{3,2,1,0:T(8,128)}), f32[8,16,8,128]{3,2,1,0:T(8,128)S(1)}, u32[]{:S(2)}, u32[]{:S(2)}) async-start(f32[8,16,8,128]{3,2,1,0:T(8,128)} %bitcast.9), calls=%async_computation | async-start | bytes 1048576 | tf_op jit(solution)/shard_map/all_to_all | solution.py:525
  10.8 1.0 copy-start.1
  17.3 0.7 copy-start.10
  19.5 13.1 %all-to-all-start.1 = ((f32[8,16,8,128]{3,2,1,0:T(8,128)}), f32[8,16,8,128]{3,2,1,0:T(8,128)S(1)}, u32[]{:S(2)}, u32[]{:S(2)}) async-start(f32[8,16,8,128]{3,2,1,0:T(8,128)} %shard_map.96.after_any), calls=%async_computation.1 | async-start | bytes 1048576 | tf_op jit(solution)/shard_map/all_to_all | solution.py:559
  24.6 1.1 copy-start
  25.7 1.4 %copy-start.3 = (f32[3,8,128,128]{3,2,1,0:T(8,128)S(1)}, f32[3,8,128,128]{3,2,1,0:T(8,128)}, u32[]{:S(2)}) copy-start(f32[3,8,128,128]{3,2,1,0:T(8,128)} %velocity_hbm.5) | copy-start | bytes 4718596
  39.9 25.7 %all-to-all-start.2 = ((f32[8,48,8,128]{3,2,1,0:T(8,128)}), f32[8,48,8,128]{3,2,1,0:T(8,128)S(1)}, u32[]{:S(2)}, u32[]{:S(2)}) async-start(f32[8,48,8,128]{3,2,1,0:T(8,128)} %get-tuple-element.24), calls=%async_computation.2 | async-start | bytes 3145728 | tf_op jit(solution)/shard_map/all_to_all | solution.py:572
  46.9 5.8 %collective-permute-start = (f32[3,4,32,128]{3,2,1,0:T(8,128)S(1)}, f32[3,4,32,128]{3,2,1,0:T(8,128)S(1)}, u32[]{:S(2)}, u32[]{:S(2)}) collective-permute-start(f32[3,4,32,128]{3,2,1,0:T(8,128)S(1)} %get-tuple-element.21), channel_id=1, source_target_pairs={{0,8},{16,24},{32,40},{48,56},{64,72},{80,88},{96,104},{112,120},{... | collective-permute-start | bytes 589832 | tf_op jit(solution)/shard_map/ppermute | solution.py:493
  48.5 10.7 %collective-permute-start.1 = (f32[3,4,32,128]{3,2,1,0:T(8,128)S(1)}, f32[3,4,32,128]{3,2,1,0:T(8,128)S(1)}, u32[]{:S(2)}, u32[]{:S(2)}) collective-permute-start(f32[3,4,32,128]{3,2,1,0:T(8,128)S(1)} %get-tuple-element.22), channel_id=1, source_target_pairs={{8,16},{24,32},{40,48},{56,64},{72,80},{88,96},{104,112},{120,128}... | collective-permute-start | bytes 589832 | tf_op jit(solution)/shard_map/ppermute | solution.py:493
  66.4 3.0 %collective-permute-start.2 = (f32[3,4,8,128]{3,2,1,0:T(8,128)S(1)}, f32[3,4,8,128]{3,2,1,0:T(8,128)S(1)}, u32[]{:S(2)}, u32[]{:S(2)}) collective-permute-start(f32[3,4,8,128]{3,2,1,0:T(8,128)S(1)} %get-tuple-element.28), channel_id=1, source_target_pairs={{0,1},{2,3},{4,5},{6,7},{1,0},{3,2},{5,4},{7,6},{8,9},{10,11},{12,... | collective-permute-start | bytes 147464 | tf_op jit(solution)/shard_map/ppermute | solution.py:493
  66.5 2.9 %collective-permute-start.3 = (f32[3,4,8,128]{3,2,1,0:T(8,128)S(1)}, f32[3,4,8,128]{3,2,1,0:T(8,128)S(1)}, u32[]{:S(2)}, u32[]{:S(2)}) collective-permute-start(f32[3,4,8,128]{3,2,1,0:T(8,128)S(1)} %get-tuple-element.29), channel_id=1, source_target_pairs={{1,2},{3,4},{5,6},{2,1},{4,3},{6,5},{9,10},{11,12},{13,14},{10,9},... | collective-permute-start | bytes 147464 | tf_op jit(solution)/shard_map/ppermute | solution.py:493
  70.0 4.0 %collective-permute-start.4 = (f32[3,3,24,128]{3,2,1,0:T(8,128)S(1)}, f32[3,3,24,128]{3,2,1,0:T(8,128)S(1)}, u32[]{:S(2)}, u32[]{:S(2)}) collective-permute-start(f32[3,3,24,128]{3,2,1,0:T(8,128)S(1)} %get-tuple-element.31), channel_id=1, source_target_pairs={{0,8},{16,24},{32,40},{48,56},{64,72},{80,88},{96,104},{112,120},{... | collective-permute-start | bytes 331784 | tf_op jit(solution)/shard_map/ppermute | solution.py:493
  72.1 9.7 %collective-permute-start.5 = (f32[3,3,24,128]{3,2,1,0:T(8,128)S(1)}, f32[3,3,24,128]{3,2,1,0:T(8,128)S(1)}, u32[]{:S(2)}, u32[]{:S(2)}) collective-permute-start(f32[3,3,24,128]{3,2,1,0:T(8,128)S(1)} %get-tuple-element.32), channel_id=1, source_target_pairs={{8,16},{24,32},{40,48},{56,64},{72,80},{88,96},{104,112},{120,128}... | collective-permute-start | bytes 331784 | tf_op jit(solution)/shard_map/ppermute | solution.py:493

commit v6 on v5

--- a/solution.py
+++ b/solution.py
@@ -140,7 +140,7 @@
 
 
 def solid_kernel(
-    brick_hbm, base_hbm, frac_hbm, pvol_hbm, out_hbm,
+    brick_hbm, base_hbm, frac_hbm, pvol_hbm, out_hbm, tick_ref,
     out_ref, brick_ref, base_ref, frac_ref, pvol_ref, sems,
 ):
     copies = fetch(
@@ -168,10 +168,12 @@
 
     lax.fori_loop(0, base_ref.shape[0] // UNROLL, step, 0)
     (copy,) = fetch([(out_ref, out_hbm)], sems)
+    tick_ref[...] = jnp.zeros_like(tick_ref)
     copy.wait()
 
 
-def eps_kernel(parts_ref, copies_hbm, out_ref, sems):
+def eps_kernel(parts_ref, copies_hbm, tick_ref, out_ref, sems):
+    tick_ref[...] = jnp.zeros_like(tick_ref)
     total = parts_ref[0]
     for j in range(1, parts_ref.shape[0]):
         total = total + parts_ref[j]
@@ -184,8 +186,8 @@
 def slip_kernel(
     first, count,
     after_any, brick_hbm, base_hbm, frac_hbm, pvel_hbm, coef_hbm, pvol_hbm, velocity_hbm,
-    out_any,
-    out_ref, brick_ref, base_ref, frac_ref, pvel_ref, coef_ref, pvol_ref, velocity_ref, table_ref, sems,
+    out_ref,
+    brick_ref, base_ref, frac_ref, pvel_ref, coef_ref, pvol_ref, velocity_ref, table_ref, sems,
 ):
     some = pl.ds(first, count)
     wide = pl.ds(first * BLOCK, count * BLOCK)
@@ -238,21 +240,17 @@
         return carry
 
     lax.fori_loop(0, count // UNROLL, step, 0)
-    (copy,) = fetch([(out_ref, out_any)], sems)
-    copy.wait()
 
 
 def drag_kernel(
-    brick_ref, base_ref, frac_ref, slip_a_hbm, slip_b_ref, eps_ref,
+    brick_ref, base_ref, frac_ref, slip_a_ref, slip_b_ref, eps_ref,
     drag_ref, out_hbm, tick_ref,
-    force_ref, slip_a_ref, sems,
+    force_ref, sems,
 ):
     subs = force_ref.shape[0]
     rows, lane = rows_iota(), lanes_iota()
-    (copy,) = fetch([(slip_a_hbm, slip_a_ref)], sems)
     for j in range(subs):
         force_ref[j] = jnp.zeros(force_ref.shape[1:], F32)
-    copy.wait()
 
     for slip_ref, start in ((slip_a_ref, 0), (slip_b_ref, slip_a_ref.shape[1] // BLOCK)):
 
@@ -288,9 +286,14 @@
         copy.wait()
 
 
-def source_kernel(place_ref, parts_ref, eps_ref, first_any, own_ref, even_ref, odd_ref):
+def source_kernel(place_ref, parts_ref, eps_ref, first_any, own_ref, *out_refs):
+    sub_refs, slab_refs, both_refs = out_refs[:2], out_refs[2:4], out_refs[4:]
     lane, rows = lanes_iota(), rows_iota()
-    even = place_ref[1] % 2 == 0
+    slab_even, sub_even = place_ref[0] % 2 == 0, place_ref[1] % 2 == 0
+
+    def swapped(flag, one, two):
+        return jnp.where(flag, one, two), jnp.where(flag, two, one)
+
     for c in range(3):
         grid = []
         for t in range(2):
@@ -305,31 +308,26 @@
             for z in range(8):
                 own_ref[c, z, 8 * t : 8 * t + 8, :] = tiles[z]
             grid.append(tiles)
+
+        def packed(z, y):
+            first = jnp.where(rows < 4, grid[0][z], pltpu.roll(grid[0][y], 4, 0))
+            last = jnp.where(rows < 4, pltpu.roll(grid[1][z], 4, 0), grid[1][y])
+            return swapped(sub_even, last, first)
+
         for q in range(4):
-            first = jnp.where(rows < 4, grid[0][2 * q], pltpu.roll(grid[0][2 * q + 1], 4, 0))
-            last = jnp.where(rows < 4, pltpu.roll(grid[1][2 * q], 4, 0), grid[1][2 * q + 1])
-            even_ref[c, q] = jnp.where(even, last, first)
-            odd_ref[c, q] = jnp.where(even, first, last)
-
-
-def halo_kernel(place_ref, own_ref, even_ref, odd_ref, halo_ref, up_ref, down_ref):
-    rows = rows_iota()
-    slab_even, sub_even = place_ref[0] % 2 == 0, place_ref[1] % 2 == 0
-    for c in range(3):
-        tiles = []
-        for q in range(4):
-            after = jnp.where(sub_even, even_ref[c, q], odd_ref[c, q])
-            before = jnp.where(sub_even, odd_ref[c, q], even_ref[c, q])
-            tiles.append(jnp.where(rows < 4, after, pltpu.roll(before, 4, 0)))
-            tiles.append(jnp.where(rows < 4, pltpu.roll(after, 4, 0), before))
-        for z in range(8):
-            halo_ref[c, z] = tiles[z]
+            for ref, tile in zip(sub_refs, packed(2 * q, 2 * q + 1)):
+                ref[c, q] = tile
         for n in range(3):
-            low, high = own_ref[c, n], own_ref[c, 5 + n]
-            up_ref[c, n, 0:8, :] = jnp.where(slab_even, tiles[5 + n], tiles[n])
-            up_ref[c, n, 8:24, :] = jnp.where(slab_even, high, low)
-            down_ref[c, n, 0:8, :] = jnp.where(slab_even, tiles[n], tiles[5 + n])
-            down_ref[c, n, 8:24, :] = jnp.where(slab_even, low, high)
+            for t in range(2):
+                pair = swapped(slab_even, grid[t][5 + n], grid[t][n])
+                for ref, tile in zip(slab_refs, pair):
+                    ref[c, n, 8 * t : 8 * t + 8, :] = tile
+        for q in range(2):
+            high, low = packed(5 + 2 * q, 6 + q), packed(2 * q, 1 + q)
+            for m in range(2):
+                pair = swapped(slab_even, high[m], low[m])
+                for p in range(2):
+                    both_refs[2 * p + m][c, q] = pair[p]
 
 
 def window_kernel(place_ref, after_any, velocity_hbm, out_ref, even_ref, odd_ref, sems):
@@ -417,18 +415,33 @@
 
 
 def stencil_kernel(
-    place_ref, first_ref, own_ref, halo_ref, even_ref, odd_ref, out_ref, even, odd, source
+    place_ref, first_ref, own_ref, *refs
 ):
+    sub_refs, slab_refs, both_refs = refs[:2], refs[2:4], refs[4:8]
+    out_ref, even, odd, source = refs[8:]
     keep = edges(place_ref[0], place_ref[1], place_ref[2], place_ref[3])
     lane = lax.broadcasted_iota(jnp.int32, (32, LANES), 1)
-    side = place_ref[0] % 2
-    source[:, 3:11, 0:8, :] = halo_ref[...]
+    above, after = place_ref[0] % 2 == 0, place_ref[1] % 2 == 0
+    top = jnp.where(above, 11, 0)
+    right = pl.multiple_of(jnp.where(after, 24, 0), 8)
     source[:, 3:11, 8:24, :] = own_ref[...]
-    source[:, 3:11, 24:32, :] = halo_ref[...]
-    for part, start in ((even_ref, 11 - 11 * side), (odd_ref, 11 * side)):
-        planes = pl.ds(start, 3)
-        source[:, planes, 0:24, :] = part[...]
-        source[:, planes, 24:32, :] = part[:, :, 0:8, :]
+    planes = (pl.ds(top, 3), pl.ds(11 - top, 3))
+    for p in range(2):
+        source[:, planes[p], 8:24, :] = slab_refs[p][...]
+    for m in range(2):
+        row = pl.ds(pl.multiple_of(24 * m + (1 - 2 * m) * right, 8), 8)
+        front = after if m == 0 else jnp.logical_not(after)
+        for c in range(3):
+            for ref, start, count in (
+                (sub_refs[m], 3, 8),
+                (both_refs[m], top, 3),
+                (both_refs[2 + m], 11 - top, 3),
+            ):
+                for n in range(count):
+                    tile = ref[c, n // 2]
+                    moved = pltpu.roll(tile, 4, 0)
+                    straight = front if n % 2 == 0 else jnp.logical_not(front)
+                    source[c, start + n, row, :] = jnp.where(straight, tile, moved)
 
     def first(number, carry):
         for k in range(2):
@@ -488,9 +501,18 @@
     )
 
 
-def pair_up(x, first, axis="slab"):
-    pairs = [(i, i + 1) for i in range(first, lax.axis_size(axis) - 1, 2)]
-    return lax.ppermute(x, axis, pairs + [(j, i) for i, j in pairs])
+def pair_up(x, slab_first, sub_first):
+    partners = []
+    for axis, first in (("slab", slab_first), ("sub", sub_first)):
+        size = lax.axis_size(axis)
+        if first is None:
+            partners.append({i: i for i in range(size)})
+        else:
+            pairs = [(i, i + 1) for i in range(first, size - 1, 2)]
+            partners.append(dict(pairs + [(j, i) for i, j in pairs]))
+    subs = lax.axis_size("sub")
+    moves = [(i * subs + j, k * subs + n) for i, k in partners[0].items() for j, n in partners[1].items()]
+    return lax.ppermute(x, ("slab", "sub"), moves)
 
 
 def body(velocity, part_vel, fraction, base_cell, drag_coeff, part_volume, brick_of_block):
@@ -512,26 +534,25 @@
         pltpu.VMEM((3, blocks * BLOCK), F32),
     ]
     row_vmem = pltpu.VMEM((blocks, BLOCK), F32)
-    (solid,) = call(
+    solid, solid_tick = call(
         solid_kernel,
-        [(tiles, 8, LANES)],
+        [(tiles, 8, LANES), (8, LANES)],
         [HBM] * 4,
         [pltpu.VMEM((tiles, 8, LANES), F32)]
         + particles_vmem
         + [row_vmem, pltpu.SemaphoreType.DMA((4,))],
-        outs=[HBM],
+        outs=[HBM, VMEM],
         us=5.0,
     )(*pinned(brick_of_block, base, fraction, pvol))
     solid_parts = lax.all_to_all(solid.reshape(subs, share, 8, LANES), "sub", 0, 0)
     half = blocks // 2
 
-    def slip_of(first, after, out):
+    def slip_of(first, after):
         (slip,) = call(
             functools.partial(slip_kernel, first, half),
             [(3, half * BLOCK)],
-            [HBM] * 8,
+            [ANY] + [HBM] * 7,
             [
-                pltpu.VMEM((3, half * BLOCK), F32),
                 pltpu.SMEM((blocks,), jnp.int32),
                 pltpu.VMEM((half, BLOCK), jnp.int32),
                 pltpu.VMEM((3, half * BLOCK), F32),
@@ -546,29 +567,28 @@
             )(after, brick_of_block, base, fraction, part_vel, coef, pvol, velocity)
         return slip
 
-    slip_a = slip_of(0, solid, HBM)
-    (eps_copies,) = call(
+    slip_a = slip_of(0, solid_tick)
+    eps_copies, eps_tick = call(
         eps_kernel,
-        [(subs, share, 8, LANES)],
+        [(subs, share, 8, LANES), (8, LANES)],
         [VMEM],
         [pltpu.VMEM((share, 8, LANES), F32), pltpu.SemaphoreType.DMA((subs,))],
-        outs=[HBM],
+        outs=[HBM, VMEM],
         us=0.5,
     )(solid_parts)
-    slip_b = slip_of(half, eps_copies, ANY)
+    slip_b = slip_of(half, eps_tick)
     eps = lax.all_to_all(eps_copies, "sub", 0, 0).reshape(tiles, 8, LANES)
     drag, force, tick = call(
         drag_kernel,
         [(3, blocks * BLOCK), (subs, 48, 8, LANES), (8, LANES)],
-        [SMEM, VMEM, VMEM, HBM, VMEM, VMEM],
+        [SMEM] + [VMEM] * 5,
         [
             pltpu.VMEM((subs, 48, 8, LANES), F32),
-            pltpu.VMEM((3, half * BLOCK), F32),
             pltpu.SemaphoreType.DMA((subs,)),
         ],
         outs=[VMEM, HBM, VMEM],
         us=6.0,
-    )(brick_of_block, base, fraction, *pinned(slip_a), slip_b, eps)
+    )(brick_of_block, base, fraction, slip_a, slip_b, eps)
     forces = lax.all_to_all(force, "sub", 0, 0)
     planes = depth * lax.axis_size("slab")
     place = jnp.stack([slab, sub, jnp.int32(planes), jnp.int32(width_x)])
@@ -578,7 +598,7 @@
         [SMEM, ANY, HBM],
         [pltpu.SemaphoreType.DMA((4,))],
     )(place, tick, *pinned(velocity))
-    even, odd = pair_up(even, 0), pair_up(odd, 1)
+    even, odd = pair_up(even, 0, None), pair_up(odd, 1, None)
     voidfraction, eps_own = call(
         void_kernel, [(depth, width_x, LANES), (share, 8, LANES)], [SMEM, ANY, VMEM], us=2.0
     )(place, tick, eps)
@@ -591,29 +611,27 @@
     )(place, window, even, odd)
 
     rows = width_x // subs
-    own, even, odd = call(
+    own, *sent = call(
         source_kernel,
-        [(3, depth, rows, LANES), (3, 4, 8, LANES), (3, 4, 8, LANES)],
+        [(3, depth, rows, LANES)]
+        + [(3, 4, 8, LANES)] * 2
+        + [(3, 3, rows, LANES)] * 2
+        + [(3, 2, 8, LANES)] * 4,
         [SMEM, VMEM, VMEM, ANY],
     )(place, forces, eps_own, first_tick)
-    even, odd = pair_up(even, 0, "sub"), pair_up(odd, 1, "sub")
-    halo, even, odd = call(
-        halo_kernel,
-        [(3, depth, 8, LANES), (3, 3, 24, LANES), (3, 3, 24, LANES)],
-        [SMEM] + [VMEM] * 3,
-    )(place, own, even, odd)
-    even, odd = pair_up(even, 0), pair_up(odd, 1)
+    pairings = [(None, 0), (None, 1), (0, None), (1, None), (0, 0), (0, 1), (1, 0), (1, 1)]
+    halos = [pair_up(x, *pairing) for x, pairing in zip(sent, pairings)]
     (moved,) = call(
         stencil_kernel,
         [(subs, 3, depth, rows, LANES)],
-        [SMEM] + [VMEM] * 5,
+        [SMEM] + [VMEM] * 10,
         [
             pltpu.VMEM((3, 16, 32, LANES), F32),
             pltpu.VMEM((3, 16, 32, LANES), F32),
             pltpu.VMEM((3, 14, 32, LANES), F32),
         ],
         us=4.0,
-    )(place, first, own, halo, even, odd)
+    )(place, first, own, *halos)
     moved = lax.all_to_all(moved, "sub", 0, 0)
     (new_velocity,) = call(
         place_kernel,

time: 112 us -> 120 us (1.071)
  starting transfers between devices: 23.8 us -> 34.5 us
  blocking collectives: 26.1 us -> 32 us
  waiting for transfers between devices: 22 us -> 17 us
  local copies, waits for them, and re-layouts: 4.21 us -> 1.44 us
  Pallas kernels: 34.9 us -> 33.2 us
    ppermute x6 -> x10, starting transfers between devices: 8.28 us -> 19 us  [pair_up(): return lax.ppermute(x, ('slab', 'sub'), moves)]
    ppermute x6 -> x10, waiting for transfers between devices: 16.5 us -> 8.05 us  [pair_up(): return lax.ppermute(x, ('slab', 'sub'), moves)]
    all_to_all x1, blocking collectives: 26.1 us -> 32 us  [body(): moved = lax.all_to_all(moved, 'sub', 0, 0)]
    unnamed x22 -> x16, local copies, waits for them, and re-layouts: 4.21 us -> 1.44 us
    all_to_all x1, waiting for transfers between devices: 0.61 us -> 2.47 us  [body(): lax.all_to_all(solid.reshape(subs, share, 8, LANES), 'sub', 0, 0)]
    pallas_call x7 -> x6, Pallas kernels: 20.8 us -> 20 us  [the longest x2 10.5 us: slip_of(): call(functools.partial(slip_kernel, first, half), [(3, half * BLOCK)], [A...]
  transfers between devices with their start and end apart: 9 -> 13, of which waited for: 5 -> 6; matrix products, arithmetic and copies ran while one was open for 0% -> 0% of each run, Pallas kernels for 15% -> 13%
where the time goes in v6:
time: 120 us; the launch traced here: 119 us
  starting transfers between devices  34.5 us (29%)
  Pallas kernels  33.2 us (28%)
  blocking collectives  32 us (27%)
  waiting for transfers between devices  17 us (14%)
  local copies, waits for them, and re-layouts  1.44 us (1%)
    all_to_all x1, blocking collectives, body(): moved = lax.all_to_all(moved, 'sub', 0, 0)  32 us
    ppermute x10, starting transfers between devices, pair_up(): return lax.ppermute(x, ('slab', 'sub'), moves)  19 us
    pallas_call x2, Pallas kernels, slip_of(): call(functools.partial(slip_kernel, first, half), [(3, half * BLOCK)], [A...  10.5 us
    ppermute x10, waiting for transfers between devices, pair_up(): return lax.ppermute(x, ('slab', 'sub'), moves)  8.05 us
    pallas_call x1, Pallas kernels, body(): call(drag_kernel, [(3, blocks * BLOCK), (subs, 48, 8, LANES), (8, LANES)]...  6.53 us
    all_to_all x1, waiting for transfers between devices, body(): forces = lax.all_to_all(force, 'sub', 0, 0)  5.3 us
    all_to_all x1, starting transfers between devices, body(): forces = lax.all_to_all(force, 'sub', 0, 0)  5.21 us
    all_to_all x1, starting transfers between devices, body(): eps = lax.all_to_all(eps_copies, 'sub', 0, 0).reshape(tiles, 8, LANES)  5.2 us
  transfers between devices with their start and end apart: 13, of which 6 were waited for; matrix products, arithmetic and copies ran while one was open for 0% of the time, Pallas kernels for 13%

profile of v6, /device:TPU:225, one launch (start us, length us, event | category | flops | bytes accessed | tf_op | source)
XLA Modules:
  0.0 119.1 jit_solution(5617550599617275044)
XLA Ops:
  0.6 0.0 copy-start
  0.6 0.0 copy-start.2
  0.7 0.0 copy-start.3
  0.7 0.0 copy-start.4
  0.7 0.0 copy-start.5
  0.7 0.0 copy-start.6
  0.7 0.0 copy-start.7
  0.7 4.9 %shard_map.94 = (f32[128,8,128]{2,1,0:T(8,128)}, f32[8,128]{1,0:T(8,128)S(1)}) custom-call(s32[128]{0:T(128)} %brick_ref.1, s32[128,128]{1,0:T(8,128)} %bitcast.14, f32[3,16384]{1,0:T(4,128)} %frac_ref.1, f32[128,128]{1,0:T(8,128)} %bitcast.9), custom_call_target="tpu_custom_call" | custom-call | flops 5000000000 | bytes 18000000 | tf_op jit(solution)/shard_map/pallas_call | solution.py:537
  5.6 5.1 %all-to-all-start = ((f32[8,16,8,128]{3,2,1,0:T(8,128)}), f32[8,16,8,128]{3,2,1,0:T(8,128)S(1)}, u32[]{:S(2)}, u32[]{:S(2)}) async-start(f32[8,16,8,128]{3,2,1,0:T(8,128)} %bitcast.18), calls=%async_computation | async-start | bytes 1048576 | tf_op jit(solution)/shard_map/all_to_all | solution.py:547
  10.8 0.0 copy-done
  10.8 0.0 copy-done.2
  10.8 0.0 copy-done.3
  10.8 0.0 copy-done.4
  10.8 0.0 copy-done.5
  10.8 0.0 copy-done.6
  10.8 0.0 copy-done.7
  10.8 5.3 %shard_map.95.slip_a_ref = f32[3,8192]{1,0:T(4,128)S(1)} custom-call(f32[8,128]{1,0:T(8,128)S(1)} %get-tuple-element.26.after_any, s32[128]{0:T(128)S(1)} %copy-done.7, s32[128,128]{1,0:T(8,128)S(1)} %bitcast.15, f32[3,16384]{1,0:T(4,128)S(1)} %copy-done.3, f32[3,16384]{1,0:T(4,128)S(1)} %copy-done.2, f32[128,128]{1,0:T(8,128)S(1)} %bitcast.12, ...), custom_call_target="tpu_custom_call" | custom-call | flops 5000000000 | bytes 18000000 | tf_op jit(solution)/shard_map/pallas_call | solution.py:551
  16.1 2.5 %all-to-all-done.parts_ref = f32[8,16,8,128]{3,2,1,0:T(8,128)S(1)} async-done(((f32[8,16,8,128]{3,2,1,0:T(8,128)}), f32[8,16,8,128]{3,2,1,0:T(8,128)S(1)}, u32[]{:S(2)}, u32[]{:S(2)}) %all-to-all-start) | async-done | bytes 524320 | tf_op jit(solution)/shard_map/all_to_all | solution.py:547
  18.6 0.9 shard_map.96
  19.4 5.2 %all-to-all-start.1 = ((f32[8,16,8,128]{3,2,1,0:T(8,128)}), f32[8,16,8,128]{3,2,1,0:T(8,128)S(1)}, u32[]{:S(2)}, u32[]{:S(2)}) async-start(f32[8,16,8,128]{3,2,1,0:T(8,128)} %get-tuple-element.29), calls=%async_computation.1 | async-start | bytes 1048576 | tf_op jit(solution)/shard_map/all_to_all | solution.py:580
  24.7 0.0 copy-start.1
  24.7 1.4 %copy-done.1 = f32[3,8,128,128]{3,2,1,0:T(8,128)S(1)} copy-done((f32[3,8,128,128]{3,2,1,0:T(8,128)S(1)}, f32[3,8,128,128]{3,2,1,0:T(8,128)}, u32[]{:S(2)}) %copy-start.1) | copy-done | bytes 1572888
  26.1 5.3 %shard_map.97.slip_b_ref = f32[3,8192]{1,0:T(4,128)S(1)} custom-call(f32[8,128]{1,0:T(8,128)S(1)} %get-tuple-element.28.after_any, s32[128]{0:T(128)S(1)} %copy-done.7, s32[128,128]{1,0:T(8,128)S(1)} %bitcast.16, f32[3,16384]{1,0:T(4,128)S(1)} %copy-done.3, f32[3,16384]{1,0:T(4,128)S(1)} %copy-done.2, f32[128,128]{1,0:T(8,128)S(1)} %bitcast.13, ...), custom_call_target="tpu_custom_call" | custom-call | flops 5000000000 | bytes 18000000 | tf_op jit(solution)/shard_map/pallas_call | solution.py:551
  31.3 1.1 all-to-all-done.1
  32.5 6.5 %shard_map.98 = (f32[3,16384]{1,0:T(4,128)}, f32[8,48,8,128]{3,2,1,0:T(8,128)}, f32[8,128]{1,0:T(8,128)S(1)}) custom-call(s32[128]{0:T(128)S(1)} %copy-done.7, s32[128,128]{1,0:T(8,128)S(1)} %bitcast.17, f32[3,16384]{1,0:T(4,128)S(1)} %copy-done.3, f32[3,8192]{1,0:T(4,128)S(1)} %shard_map.95.slip_a_ref, f32[3,8192]{1,0:T(4,128)S(1)} %shard_map.97.slip_b_ref, ...), custom_call_target="tpu_custom_call" | custom-call | flops 6000000000 | bytes 21600000 | tf_op jit(solution)/shard_map/pallas_call | solution.py:581
  39.0 5.2 %all-to-all-start.2 = ((f32[8,48,8,128]{3,2,1,0:T(8,128)}), f32[8,48,8,128]{3,2,1,0:T(8,128)S(1)}, u32[]{:S(2)}, u32[]{:S(2)}) async-start(f32[8,48,8,128]{3,2,1,0:T(8,128)} %get-tuple-element.35), calls=%async_computation.2 | async-start | bytes 3145728 | tf_op jit(solution)/shard_map/all_to_all | solution.py:592
  44.2 0.1 pad_add_fusion.place_ref
  44.3 1.7 %shard_map.99 = (f32[3,8,32,128]{3,2,1,0:T(8,128)S(1)}, f32[3,4,32,128]{3,2,1,0:T(8,128)S(1)}, f32[3,4,32,128]{3,2,1,0:T(8,128)S(1)}) custom-call(s32[4]{0:T(128)S(1)} %pad_add_fusion.place_ref, f32[8,128]{1,0:T(8,128)S(1)} %get-tuple-element.30.after_any, f32[3,8,128,128]{3,2,1,0:T(8,128)} %velocity_hbm.5), custom_call_target="tpu_custom_call" | custom-call | flops 1000000000 | bytes 3600000 | tf_op jit(solution)/shard_map/pallas_call | solution.py:595
  46.0 1.2 %collective-permute-start = (f32[3,4,32,128]{3,2,1,0:T(8,128)S(1)}, f32[3,4,32,128]{3,2,1,0:T(8,128)S(1)}, u32[]{:S(2)}, u32[]{:S(2)}) collective-permute-start(f32[3,4,32,128]{3,2,1,0:T(8,128)S(1)} %get-tuple-element.32), channel_id=1, source_target_pairs={{0,8},{1,9},{2,10},{3,11},{4,12},{5,13},{6,14},{7,15},{16,24},{17,... | collective-permute-start | bytes 589832 | tf_op jit(solution)/shard_map/ppermute | solution.py:515
  47.3 1.9 %collective-permute-start.1 = (f32[3,4,32,128]{3,2,1,0:T(8,128)S(1)}, f32[3,4,32,128]{3,2,1,0:T(8,128)S(1)}, u32[]{:S(2)}, u32[]{:S(2)}) collective-permute-start(f32[3,4,32,128]{3,2,1,0:T(8,128)S(1)} %get-tuple-element.33), channel_id=1, source_target_pairs={{8,16},{9,17},{10,18},{11,19},{12,20},{13,21},{14,22},{15,23},{24,... | collective-permute-start | bytes 589832 | tf_op jit(solution)/shard_map/ppermute | solution.py:515
  49.2 2.3 %shard_map.101 = (f32[8,128,128]{2,1,0:T(8,128)}, f32[16,8,128]{2,1,0:T(8,128)S(1)}) custom-call(s32[4]{0:T(128)S(1)} %pad_add_fusion.place_ref, f32[8,128]{1,0:T(8,128)S(1)} %get-tuple-element.30.after_any, f32[128,8,128]{2,1,0:T(8,128)S(1)} %bitcast.8), custom_call_target="tpu_custom_call" | custom-call | flops 2000000000 | bytes 7200000 | tf_op jit(solution)/shard_map/pallas_call | solution.py:602
  51.5 0.0 collective-permute-done.even_ref
  51.5 6.5 %collective-permute-done.1.odd_ref = f32[3,4,32,128]{3,2,1,0:T(8,128)S(1)} collective-permute-done((f32[3,4,32,128]{3,2,1,0:T(8,128)S(1)}, f32[3,4,32,128]{3,2,1,0:T(8,128)S(1)}, u32[]{:S(2)}, u32[]{:S(2)}) %collective-permute-start.1) | collective-permute-done | bytes 196640 | tf_op jit(solution)/shard_map/ppermute | solution.py:515
  57.9 1.5 %shard_map.100 = (f32[3,14,32,128]{3,2,1,0:T(8,128)S(1)}, f32[8,128]{1,0:T(8,128)S(1)}) custom-call(s32[4]{0:T(128)S(1)} %pad_add_fusion.place_ref, f32[3,8,32,128]{3,2,1,0:T(8,128)S(1)} %get-tuple-element.31.window_ref, f32[3,4,32,128]{3,2,1,0:T(8,128)S(1)} %collective-permute-done.even_ref, f32[3,4,32,128]{3,2,1,0:T(8,128)S(1)} %collective-permute-done.1.odd_ref), custom_call_target="tpu_custom_call" | custom-call | flops 1000000000 | bytes 3600000 | tf_op jit(solution)/shard_map/pallas_call | solution.py:605
  59.4 5.3 %all-to-all-done.2.parts_ref = f32[8,48,8,128]{3,2,1,0:T(8,128)S(1)} async-done(((f32[8,48,8,128]{3,2,1,0:T(8,128)}), f32[8,48,8,128]{3,2,1,0:T(8,128)S(1)}, u32[]{:S(2)}, u32[]{:S(2)}) %all-to-all-start.2) | async-done | bytes 1572896 | tf_op jit(solution)/shard_map/all_to_all | solution.py:592
  64.7 0.8 shard_map.102
  65.6 1.4 %collective-permute-start.6 = (f32[3,2,8,128]{3,2,1,0:T(8,128)S(1)}, f32[3,2,8,128]{3,2,1,0:T(8,128)S(1)}, u32[]{:S(2)}, u32[]{:S(2)}) collective-permute-start(f32[3,2,8,128]{3,2,1,0:T(8,128)S(1)} %get-tuple-element.43), channel_id=1, source_target_pairs={{0,9},{2,11},{4,13},{6,15},{1,8},{3,10},{5,12},{7,14},{16,25},{18,... | collective-permute-start | bytes 73736 | tf_op jit(solution)/shard_map/ppermute | solution.py:515
  67.0 0.7 collective-permute-start.7
  67.6 0.1 collective-permute-start.4
  67.7 1.9 %collective-permute-start.5 = (f32[3,3,16,128]{3,2,1,0:T(8,128)S(1)}, f32[3,3,16,128]{3,2,1,0:T(8,128)S(1)}, u32[]{:S(2)}, u32[]{:S(2)}) collective-permute-start(f32[3,3,16,128]{3,2,1,0:T(8,128)S(1)} %get-tuple-element.42), channel_id=1, source_target_pairs={{8,16},{9,17},{10,18},{11,19},{12,20},{13,21},{14,22},{15,23},{24,... | collective-permute-start | bytes 221192 | tf_op jit(solution)/shard_map/ppermute | solution.py:515
  69.7 10.4 %collective-permute-start.8 = (f32[3,2,8,128]{3,2,1,0:T(8,128)S(1)}, f32[3,2,8,128]{3,2,1,0:T(8,128)S(1)}, u32[]{:S(2)}, u32[]{:S(2)}) collective-permute-start(f32[3,2,8,128]{3,2,1,0:T(8,128)S(1)} %get-tuple-element.45), channel_id=1, source_target_pairs={{8,17},{10,19},{12,21},{14,23},{9,16},{11,18},{13,20},{15,22},{24,... | collective-permute-start | bytes 73736 | tf_op jit(solution)/shard_map/ppermute | solution.py:515
  80.0 0.0 collective-permute-done.6.refs_4_
  80.1 0.1 collective-permute-start.2
  80.2 0.0 collective-permute-done.7.refs_5_
  80.2 0.7 collective-permute-start.3
  80.8 0.7 collective-permute-done.8.refs_6_
  81.5 0.7 collective-permute-start.9
  82.2 0.0 collective-permute-done.9.refs_7_
  82.2 0.9 collective-permute-done.2.refs_0_
  83.1 0.0 collective-permute-done.3.refs_1_
  83.1 0.0 collective-permute-done.4.refs_2_
  83.1 0.0 collective-permute-done.5.refs_3_
  83.1 2.8 %shard_map.103 = f32[8,3,8,16,128]{4,3,2,1,0:T(8,128)S(1)} custom-call(s32[4]{0:T(128)S(1)} %pad_add_fusion.place_ref, f32[3,14,32,128]{3,2,1,0:T(8,128)S(1)} %get-tuple-element.34.first_ref, f32[3,8,16,128]{3,2,1,0:T(8,128)S(1)} %get-tuple-element.38.own_ref, f32[3,4,8,128]{3,2,1,0:T(8,128)S(1)} %collective-permute-done.2.refs_0_, ...), custom_call_target="tpu_custom_call" | custom-call | flops 4000000000 | bytes 14400000 | tf_op jit(solution)/shard_map/pallas_call | solution.py:624
  85.9 32.0 %all_to_all.20.parts_ref = f32[8,3,8,16,128]{4,3,2,1,0:T(8,128)S(1)} all-to-all(f32[8,3,8,16,128]{4,3,2,1,0:T(8,128)S(1)} %shard_map.103), channel_id=1, replica_groups=mesh['slab'=32,'sub'=8] {'sub'}, dimensions={0} | all-to-all | bytes 3145728 | tf_op jit(solution)/shard_map/all_to_all | solution.py:635
  117.9 1.2 %shard_map.104 = f32[3,8,128,128]{3,2,1,0:T(8,128)} custom-call(f32[8,3,8,16,128]{4,3,2,1,0:T(8,128)S(1)} %all_to_all.20.parts_ref), custom_call_target="tpu_custom_call" | custom-call | flops 1000000000 | bytes 3600000 | tf_op jit(solution)/shard_map/pallas_call | solution.py:636
Async XLA Ops:
  0.6 10.1 %copy-start = (f32[3,8,128,128]{3,2,1,0:T(8,128)S(1)}, f32[3,8,128,128]{3,2,1,0:T(8,128)}, u32[]{:S(2)}) copy-start(f32[3,8,128,128]{3,2,1,0:T(8,128)} %velocity_hbm.5) | copy-start | bytes 4718596
  0.6 10.1 %copy-start.2 = (f32[3,16384]{1,0:T(4,128)S(1)}, f32[3,16384]{1,0:T(4,128)}, u32[]{:S(2)}) copy-start(f32[3,16384]{1,0:T(4,128)} %pvel_hbm.3) | copy-start | bytes 589828
  0.7 10.1 %copy-start.3 = (f32[3,16384]{1,0:T(4,128)S(1)}, f32[3,16384]{1,0:T(4,128)}, u32[]{:S(2)}) copy-start(f32[3,16384]{1,0:T(4,128)} %frac_ref.1) | copy-start | bytes 589828
  0.7 10.1 %copy-start.4 = (f32[16384]{0:T(1024)S(1)}, f32[16384]{0:T(1024)}, u32[]{:S(2)}) copy-start(f32[16384]{0:T(1024)} %param.12) | copy-start | bytes 196612
  0.7 10.1 %copy-start.5 = (f32[16384]{0:T(1024)S(1)}, f32[16384]{0:T(1024)}, u32[]{:S(2)}) copy-start(f32[16384]{0:T(1024)} %param.11) | copy-start | bytes 196612
  0.7 10.1 %copy-start.6 = (s32[16384]{0:T(1024)S(1)}, s32[16384]{0:T(1024)}, u32[]{:S(2)}) copy-start(s32[16384]{0:T(1024)} %param.10) | copy-start | bytes 196612
  0.7 10.1 %copy-start.7 = (s32[128]{0:T(128)S(1)}, s32[128]{0:T(128)}, u32[]{:S(2)}) copy-start(s32[128]{0:T(128)} %brick_ref.1) | copy-start | bytes 1540
  5.6 12.9 %all-to-all-start = ((f32[8,16,8,128]{3,2,1,0:T(8,128)}), f32[8,16,8,128]{3,2,1,0:T(8,128)S(1)}, u32[]{:S(2)}, u32[]{:S(2)}) async-start(f32[8,16,8,128]{3,2,1,0:T(8,128)} %bitcast.18), calls=%async_computation | async-start | bytes 1048576 | tf_op jit(solution)/shard_map/all_to_all | solution.py:547
  19.4 13.0 %all-to-all-start.1 = ((f32[8,16,8,128]{3,2,1,0:T(8,128)}), f32[8,16,8,128]{3,2,1,0:T(8,128)S(1)}, u32[]{:S(2)}, u32[]{:S(2)}) async-start(f32[8,16,8,128]{3,2,1,0:T(8,128)} %get-tuple-element.29), calls=%async_computation.1 | async-start | bytes 1048576 | tf_op jit(solution)/shard_map/all_to_all | solution.py:580
  24.7 1.4 %copy-start.1 = (f32[3,8,128,128]{3,2,1,0:T(8,128)S(1)}, f32[3,8,128,128]{3,2,1,0:T(8,128)}, u32[]{:S(2)}) copy-start(f32[3,8,128,128]{3,2,1,0:T(8,128)} %velocity_hbm.5) | copy-start | bytes 4718596
  39.0 25.7 %all-to-all-start.2 = ((f32[8,48,8,128]{3,2,1,0:T(8,128)}), f32[8,48,8,128]{3,2,1,0:T(8,128)S(1)}, u32[]{:S(2)}, u32[]{:S(2)}) async-start(f32[8,48,8,128]{3,2,1,0:T(8,128)} %get-tuple-element.35), calls=%async_computation.2 | async-start | bytes 3145728 | tf_op jit(solution)/shard_map/all_to_all | solution.py:592
  46.0 5.5 %collective-permute-start = (f32[3,4,32,128]{3,2,1,0:T(8,128)S(1)}, f32[3,4,32,128]{3,2,1,0:T(8,128)S(1)}, u32[]{:S(2)}, u32[]{:S(2)}) collective-permute-start(f32[3,4,32,128]{3,2,1,0:T(8,128)S(1)} %get-tuple-element.32), channel_id=1, source_target_pairs={{0,8},{1,9},{2,10},{3,11},{4,12},{5,13},{6,14},{7,15},{16,24},{17,... | collective-permute-start | bytes 589832 | tf_op jit(solution)/shard_map/ppermute | solution.py:515
  47.3 10.7 %collective-permute-start.1 = (f32[3,4,32,128]{3,2,1,0:T(8,128)S(1)}, f32[3,4,32,128]{3,2,1,0:T(8,128)S(1)}, u32[]{:S(2)}, u32[]{:S(2)}) collective-permute-start(f32[3,4,32,128]{3,2,1,0:T(8,128)S(1)} %get-tuple-element.33), channel_id=1, source_target_pairs={{8,16},{9,17},{10,18},{11,19},{12,20},{13,21},{14,22},{15,23},{24,... | collective-permute-start | bytes 589832 | tf_op jit(solution)/shard_map/ppermute | solution.py:515
  65.6 14.5 %collective-permute-start.6 = (f32[3,2,8,128]{3,2,1,0:T(8,128)S(1)}, f32[3,2,8,128]{3,2,1,0:T(8,128)S(1)}, u32[]{:S(2)}, u32[]{:S(2)}) collective-permute-start(f32[3,2,8,128]{3,2,1,0:T(8,128)S(1)} %get-tuple-element.43), channel_id=1, source_target_pairs={{0,9},{2,11},{4,13},{6,15},{1,8},{3,10},{5,12},{7,14},{16,25},{18,... | collective-permute-start | bytes 73736 | tf_op jit(solution)/shard_map/ppermute | solution.py:515
  67.0 13.2 %collective-permute-start.7 = (f32[3,2,8,128]{3,2,1,0:T(8,128)S(1)}, f32[3,2,8,128]{3,2,1,0:T(8,128)S(1)}, u32[]{:S(2)}, u32[]{:S(2)}) collective-permute-start(f32[3,2,8,128]{3,2,1,0:T(8,128)S(1)} %get-tuple-element.44), channel_id=1, source_target_pairs={{1,10},{3,12},{5,14},{2,9},{4,11},{6,13},{17,26},{19,28},{21,30},{... | collective-permute-start | bytes 73736 | tf_op jit(solution)/shard_map/ppermute | solution.py:515
  67.6 15.5 %collective-permute-start.4 = (f32[3,3,16,128]{3,2,1,0:T(8,128)S(1)}, f32[3,3,16,128]{3,2,1,0:T(8,128)S(1)}, u32[]{:S(2)}, u32[]{:S(2)}) collective-permute-start(f32[3,3,16,128]{3,2,1,0:T(8,128)S(1)} %get-tuple-element.41), channel_id=1, source_target_pairs={{0,8},{1,9},{2,10},{3,11},{4,12},{5,13},{6,14},{7,15},{16,24},{17,... | collective-permute-start | bytes 221192 | tf_op jit(solution)/shard_map/ppermute | solution.py:515
  67.7 15.4 %collective-permute-start.5 = (f32[3,3,16,128]{3,2,1,0:T(8,128)S(1)}, f32[3,3,16,128]{3,2,1,0:T(8,128)S(1)}, u32[]{:S(2)}, u32[]{:S(2)}) collective-permute-start(f32[3,3,16,128]{3,2,1,0:T(8,128)S(1)} %get-tuple-element.42), channel_id=1, source_target_pairs={{8,16},{9,17},{10,18},{11,19},{12,20},{13,21},{14,22},{15,23},{24,... | collective-permute-start | bytes 221192 | tf_op jit(solution)/shard_map/ppermute | solution.py:515
  69.7 11.9 %collective-permute-start.8 = (f32[3,2,8,128]{3,2,1,0:T(8,128)S(1)}, f32[3,2,8,128]{3,2,1,0:T(8,128)S(1)}, u32[]{:S(2)}, u32[]{:S(2)}) collective-permute-start(f32[3,2,8,128]{3,2,1,0:T(8,128)S(1)} %get-tuple-element.45), channel_id=1, source_target_pairs={{8,17},{10,19},{12,21},{14,23},{9,16},{11,18},{13,20},{15,22},{24,... | collective-permute-start | bytes 73736 | tf_op jit(solution)/shard_map/ppermute | solution.py:515
  80.1 3.0 %collective-permute-start.2 = (f32[3,4,8,128]{3,2,1,0:T(8,128)S(1)}, f32[3,4,8,128]{3,2,1,0:T(8,128)S(1)}, u32[]{:S(2)}, u32[]{:S(2)}) collective-permute-start(f32[3,4,8,128]{3,2,1,0:T(8,128)S(1)} %get-tuple-element.39), channel_id=1, source_target_pairs={{0,1},{2,3},{4,5},{6,7},{1,0},{3,2},{5,4},{7,6},{8,9},{10,11},{12,... | collective-permute-start | bytes 147464 | tf_op jit(solution)/shard_map/ppermute | solution.py:515
  80.2 2.9 %collective-permute-start.3 = (f32[3,4,8,128]{3,2,1,0:T(8,128)S(1)}, f32[3,4,8,128]{3,2,1,0:T(8,128)S(1)}, u32[]{:S(2)}, u32[]{:S(2)}) collective-permute-start(f32[3,4,8,128]{3,2,1,0:T(8,128)S(1)} %get-tuple-element.40), channel_id=1, source_target_pairs={{1,2},{3,4},{5,6},{2,1},{4,3},{6,5},{9,10},{11,12},{13,14},{10,9},... | collective-permute-start | bytes 147464 | tf_op jit(solution)/shard_map/ppermute | solution.py:515
  81.5 0.7 collective-permute-start.9

commit v7 on v4

--- a/solution.py
+++ b/solution.py
@@ -135,12 +135,32 @@
     return jnp.sum(kx * total, axis=0, keepdims=True)
 
 
+def interpolate_pair(blocks):
+    lane = lanes_iota()
+    left = []
+    for n, (tile, t1, _, _) in enumerate(blocks):
+        brick = jnp.where((lane >> 6) == t1, tile, 0.0)
+        rows = split_rows([brick + pltpu.roll(brick, 64, 1)])
+        pair = [rows, jnp.zeros_like(rows)]
+        left.append(jnp.concatenate(pair if n == 0 else pair[::-1], axis=1))
+    both = jnp.dot(
+        jnp.concatenate(left, axis=0),
+        jnp.concatenate([weights for _, _, _, weights in blocks], axis=0),
+        preferred_element_type=F32,
+    )
+    found = []
+    for n, (_, _, kx, _) in enumerate(blocks):
+        total = both[16 * n : 16 * n + 8] + both[16 * n + 8 : 16 * n + 16]
+        found.append(jnp.sum(kx * total, axis=0, keepdims=True))
+    return found
+
+
 def brick_place(brick):
     return brick >> 4, brick & 7, (brick >> 3) & 1
 
 
 def solid_kernel(
-    brick_hbm, base_hbm, frac_hbm, pvol_hbm, out_hbm,
+    brick_hbm, base_hbm, frac_hbm, pvol_hbm, out_hbm, tick_ref,
     out_ref, brick_ref, base_ref, frac_ref, pvol_ref, sems,
 ):
     copies = fetch(
@@ -168,10 +188,12 @@
 
     lax.fori_loop(0, base_ref.shape[0] // UNROLL, step, 0)
     (copy,) = fetch([(out_ref, out_hbm)], sems)
+    tick_ref[...] = jnp.zeros_like(tick_ref)
     copy.wait()
 
 
-def eps_kernel(parts_ref, copies_hbm, out_ref, sems):
+def eps_kernel(parts_ref, copies_hbm, tick_ref, out_ref, sems):
+    tick_ref[...] = jnp.zeros_like(tick_ref)
     total = parts_ref[0]
     for j in range(1, parts_ref.shape[0]):
         total = total + parts_ref[j]
@@ -184,8 +206,8 @@
 def slip_kernel(
     first, count,
     after_any, brick_hbm, base_hbm, frac_hbm, pvel_hbm, coef_hbm, pvol_hbm, velocity_hbm,
-    out_any,
-    out_ref, brick_ref, base_ref, frac_ref, pvel_ref, coef_ref, pvol_ref, velocity_ref, table_ref, sems,
+    out_ref,
+    brick_ref, base_ref, frac_ref, pvel_ref, coef_ref, pvol_ref, velocity_ref, table_ref, sems,
 ):
     some = pl.ds(first, count)
     wide = pl.ds(first * BLOCK, count * BLOCK)
@@ -238,8 +260,6 @@
         return carry
 
     lax.fori_loop(0, count // UNROLL, step, 0)
-    (copy,) = fetch([(out_ref, out_any)], sems)
-    copy.wait()
 
 
 def pack_halo(rows, tiles):
@@ -259,36 +279,39 @@
 
 
 def drag_kernel(
-    brick_ref, base_ref, frac_ref, slip_a_hbm, slip_b_ref, eps_ref,
+    brick_ref, base_ref, frac_ref, slip_a_ref, slip_b_ref, eps_ref,
     drag_ref, out_hbm, tick_ref,
-    force_ref, slip_a_ref, sems,
+    force_ref, sems,
 ):
     subs = force_ref.shape[0]
     rows, lane = rows_iota(), lanes_iota()
-    (copy,) = fetch([(slip_a_hbm, slip_a_ref)], sems)
     for j in range(subs):
         force_ref[j, 0:48] = jnp.zeros((48, 8, LANES), F32)
-    copy.wait()
 
     for slip_ref, start in ((slip_a_ref, 0), (slip_b_ref, slip_a_ref.shape[1] // BLOCK)):
 
         def step(number, carry, slip_ref=slip_ref, start=start):
+            known = []
+            for k in range(UNROLL):
+                block = number * UNROLL + k + start
+                _, zb, xb, yb, fz, fx, fy = particles(base_ref, frac_ref, block)
+                tx, t3, t1 = brick_place(brick_ref[block])
+                kx = axis_weights(rows, xb, fx)
+                known.append((eps_ref[tx * 8 + t3], t1, kx, plane_weights(rows, zb, yb, fz, fy)))
+            at_particles = sum((interpolate_pair(known[k : k + 2]) for k in range(0, UNROLL, 2)), [])
             found = []
             for k in range(UNROLL):
                 inner = number * UNROLL + k
-                block = inner + start
-                at, zb, xb, yb, fz, fx, fy = particles(base_ref, frac_ref, block)
                 inner_at = pl.ds(pl.multiple_of(inner * BLOCK, BLOCK), BLOCK)
-                tx, t3, t1 = brick_place(brick_ref[block])
-                kx = axis_weights(rows, xb, fx)
-                eps = interpolate(eps_ref[tx * 8 + t3], kx, corner_terms(zb, yb, fz, fy, t1 * 64))
-                factor = jnp.exp(DRAG_POWER * jnp.log(eps))
+                at = pl.ds(pl.multiple_of((inner + start) * BLOCK, BLOCK), BLOCK)
+                _, _, kx, weights = known[k]
+                factor = jnp.exp(DRAG_POWER * jnp.log(at_particles[k]))
                 parts = []
                 for c in range(3):
                     force = factor * slip_ref[c : c + 1, inner_at]
                     drag_ref[c : c + 1, at] = force
                     parts.append(kx * spread(force))
-                found.append((parts, plane_weights(rows, zb, yb, fz, fy)))
+                found.append((parts, weights))
             found = sum((deposit(found[k : k + 2]) for k in range(0, UNROLL, 2)), [])
             for k in range(UNROLL):
                 tx, t3, t1 = brick_place(brick_ref[number * UNROLL + k + start])
@@ -320,12 +343,9 @@
         copy.wait()
 
 
-def source_kernel(place_ref, parts_ref, eps_ref, first_any, void_any, own_ref, even_ref, odd_ref):
+def source_kernel(place_ref, parts_ref, eps_ref, first_any, own_ref, even_ref, odd_ref):
     lane, rows = lanes_iota(), rows_iota()
-    even, sub = place_ref[0] % 2 == 0, place_ref[1]
-    tiles_x = eps_ref.shape[0] // 8
-    after = jnp.minimum(sub * 2 + 2, tiles_x - 1) * 8
-    before = jnp.maximum(sub * 2 - 1, 0) * 8
+    even = place_ref[0] % 2 == 0
 
     def summed(at):
         total = parts_ref[0, at]
@@ -343,11 +363,7 @@
                     forces += unpack_halo(rows, [summed(48 + quad * 3 + k) for k in range(3)])
             tiles = []
             for t3 in range(8):
-                if t < 2:
-                    eps = eps_ref[(sub * 2 + t) * 8 + t3]
-                else:
-                    eps = jnp.where(rows < 4, eps_ref[after + t3], eps_ref[before + t3])
-                tiles.append(-forces[t3] / eps)
+                tiles.append(-forces[t3] / eps_ref[t * 8 + t3])
             tiles = transpose_granules(tiles, lane)
             first = 8 * (t + 1) % 24
             for z in range(8):
@@ -378,9 +394,9 @@
         odd_ref[:, :, at, :] = jnp.where(even, rows[:, :4], rows[:, depth - 4 :])
 
 
-def void_kernel(after_any, eps_ref, out_ref, tick_ref):
-    tick_ref[...] = jnp.zeros_like(tick_ref)
-    lane = lanes_iota()
+def void_kernel(place_ref, after_any, eps_ref, out_ref, near_ref):
+    lane, rows = lanes_iota(), rows_iota()
+    tiles_x = out_ref.shape[1] // 8
 
     def convert(number, carry):
         for k in range(4):
@@ -390,7 +406,12 @@
                 out_ref[z, pl.ds(pl.multiple_of(tx * 8, 8), 8), :] = tiles[z]
         return carry
 
-    lax.fori_loop(0, out_ref.shape[1] // 32, convert, 0)
+    lax.fori_loop(0, tiles_x // 4, convert, 0)
+    own = place_ref[1] * 2
+    near_ref[0:16] = eps_ref[pl.ds(own * 8, 16)]
+    after = eps_ref[pl.ds(jnp.minimum(own + 2, tiles_x - 1) * 8, 8)]
+    before = eps_ref[pl.ds(jnp.maximum(own - 1, 0) * 8, 8)]
+    near_ref[16:24] = jnp.where(rows[None] < 4, after, before)
 
 
 def edges(slab, sub, planes, width):
@@ -442,44 +463,83 @@
     lax.fori_loop(0, 7, plane, 0)
 
 
-def stencil_kernel(
-    place_ref, first_ref, own_ref, even_ref, odd_ref, out_ref, even, odd, source
-):
+def forced(old, new, source, z, keep, lane):
+    moved = unforced(old, z, lane)
+    inside = keep(z)
+    for c in range(3):
+        total = moved[c] + TIME_STEP * source[c, z - 1]
+        new[c, z] = jnp.where(inside, total, 0.0)
+
+
+def near_kernel(place_ref, first_ref, own_ref, even_ref, *refs):
+    keeps, last_ref, levels, source = refs[:3], refs[3], refs[4:8], refs[8]
     keep = edges(place_ref[0], place_ref[1], place_ref[2], place_ref[3])
     lane = lax.broadcasted_iota(jnp.int32, (32, LANES), 1)
     side = place_ref[0] % 2
-    parts = ((even_ref, pl.ds(11 - 11 * side, 3)), (own_ref, slice(3, 11)), (odd_ref, pl.ds(11 * side, 3)))
-    for part, planes in parts:
+
+    def plane(n):
+        return n + side * (15 - 2 * n)
+
+    for part, planes in ((own_ref, slice(3, 11)), (even_ref, pl.ds(11 - 11 * side, 3))):
         source[:, planes, 0:24, :] = part[...]
         source[:, planes, 24:32, :] = part[:, :, 0:8, :]
-
-    def first(number, carry):
-        for k in range(2):
-            z = number * 2 + k
-            inside = keep(z + 1)
+    for n in range(4, 15):
+        z = plane(n)
+        inside = keep(z)
+        for c in range(3):
+            moved = first_ref[c, z - 1] + TIME_STEP * source[c, z - 1]
+            levels[0][c, z] = jnp.where(inside, moved, 0.0)
+    for step in range(1, ITERS):
+
+        def run(n, carry, step=step):
+            forced(levels[step - 1], levels[step], source, plane(n), keep, lane)
+            return carry
+
+        lax.fori_loop(4 + step, 15 - step, run, 0)
+    for step in range(3):
+        for n in range(2):
             for c in range(3):
-                moved = first_ref[c, z] + TIME_STEP * source[c, z]
-                odd[c, z + 1] = jnp.where(inside, moved, 0.0)
-        return carry
-
-    lax.fori_loop(0, 7, first, 0)
-    buffers = (even, odd)
+                keeps[step][c, n] = levels[step][c, plane(4 + step + n)]
+    for n in range(5):
+        for c in range(3):
+            last_ref[c, n] = levels[3][c, plane(7 + n), 8:24, :]
+
+
+def far_kernel(place_ref, first_ref, own_ref, odd_ref, *refs):
+    keeps, last_ref, out_ref, levels, source = refs[:3], refs[3], refs[4], refs[5:9], refs[9]
+    keep = edges(place_ref[0], place_ref[1], place_ref[2], place_ref[3])
+    lane = lax.broadcasted_iota(jnp.int32, (32, LANES), 1)
+    side = place_ref[0] % 2
+
+    def plane(n):
+        return n + side * (15 - 2 * n)
+
+    for part, planes in ((own_ref, slice(3, 11)), (odd_ref, pl.ds(11 * side, 3))):
+        source[:, planes, 0:24, :] = part[...]
+        source[:, planes, 24:32, :] = part[:, :, 0:8, :]
+    for step in range(3):
+        for n in range(2):
+            for c in range(3):
+                levels[step][c, plane(4 + step + n)] = keeps[step][c, n]
+    for n in range(1, 4):
+        z = plane(n)
+        inside = keep(z)
+        for c in range(3):
+            moved = first_ref[c, z - 1] + TIME_STEP * source[c, z - 1]
+            levels[0][c, z] = jnp.where(inside, moved, 0.0)
     for step in range(1, ITERS):
-        old, new = buffers[step % 2], buffers[(step + 1) % 2]
-
-        def plane(number, carry, old=old, new=new, step=step):
-            for k in range(2):
-                z = number * 2 + k + step + 1
-                moved = unforced(old, z, lane)
-                inside = keep(z)
-                for c in range(3):
-                    forced = moved[c] + TIME_STEP * source[c, z - 1]
-                    new[c, z] = jnp.where(inside, forced, 0.0)
-            return carry
-
-        lax.fori_loop(0, 7 - step, plane, 0)
-    for j in range(out_ref.shape[0]):
-        out_ref[j] = even[:, 4:12, 8:24, :]
+        for n in range(1 + step, 4 + step):
+            forced(levels[step - 1], levels[step], source, plane(n), keep, lane)
+    for c in range(3):
+        for n in range(3):
+            z = plane(4 + n)
+            rows = levels[3][c, z, 8:24, :]
+            for j in range(out_ref.shape[0]):
+                out_ref[j, c, z - 4] = rows
+        for n in range(5):
+            rows = last_ref[c, n]
+            for j in range(out_ref.shape[0]):
+                out_ref[j, c, plane(7 + n) - 4] = rows
 
 
 def place_kernel(parts_ref, out_ref, sems):
@@ -535,26 +595,25 @@
         pltpu.VMEM((3, blocks * BLOCK), F32),
     ]
     row_vmem = pltpu.VMEM((blocks, BLOCK), F32)
-    (solid,) = call(
+    solid, solid_tick = call(
         solid_kernel,
-        [(tiles, 8, LANES)],
+        [(tiles, 8, LANES), (8, LANES)],
         [HBM] * 4,
         [pltpu.VMEM((tiles, 8, LANES), F32)]
         + particles_vmem
         + [row_vmem, pltpu.SemaphoreType.DMA((4,))],
-        outs=[HBM],
+        outs=[HBM, VMEM],
         us=5.0,
     )(*pinned(brick_of_block, base, fraction, pvol))
     solid_parts = lax.all_to_all(solid.reshape(subs, share, 8, LANES), "sub", 0, 0)
     half = blocks // 2
 
-    def slip_of(first, after, out):
+    def slip_of(first, after):
         (slip,) = call(
             functools.partial(slip_kernel, first, half),
             [(3, half * BLOCK)],
-            [HBM] * 8,
+            [ANY] + [HBM] * 7,
             [
-                pltpu.VMEM((3, half * BLOCK), F32),
                 pltpu.SMEM((blocks,), jnp.int32),
                 pltpu.VMEM((half, BLOCK), jnp.int32),
                 pltpu.VMEM((3, half * BLOCK), F32),
@@ -569,29 +628,28 @@
             )(after, brick_of_block, base, fraction, part_vel, coef, pvol, velocity)
         return slip
 
-    slip_a = slip_of(0, solid, HBM)
-    (eps_copies,) = call(
+    slip_a = slip_of(0, solid_tick)
+    eps_copies, eps_tick = call(
         eps_kernel,
-        [(subs, share, 8, LANES)],
+        [(subs, share, 8, LANES), (8, LANES)],
         [VMEM],
         [pltpu.VMEM((share, 8, LANES), F32), pltpu.SemaphoreType.DMA((subs,))],
-        outs=[HBM],
+        outs=[HBM, VMEM],
         us=0.5,
     )(solid_parts)
-    slip_b = slip_of(half, eps_copies, ANY)
+    slip_b = slip_of(half, eps_tick)
     eps = lax.all_to_all(eps_copies, "sub", 0, 0).reshape(tiles, 8, LANES)
     drag, force, tick = call(
         drag_kernel,
         [(3, blocks * BLOCK), (subs, 66, 8, LANES), (8, LANES)],
-        [SMEM, VMEM, VMEM, HBM, VMEM, VMEM],
+        [SMEM] + [VMEM] * 5,
         [
             pltpu.VMEM((subs, 66, 8, LANES), F32),
-            pltpu.VMEM((3, half * BLOCK), F32),
             pltpu.SemaphoreType.DMA((2 * subs,)),
         ],
         outs=[VMEM, HBM, VMEM],
         us=6.0,
-    )(brick_of_block, base, fraction, *pinned(slip_a), slip_b, eps)
+    )(brick_of_block, base, fraction, slip_a, slip_b, eps)
     forces = lax.all_to_all(force, "sub", 0, 0)
     planes = depth * lax.axis_size("slab")
     place = jnp.stack([slab, sub, jnp.int32(planes), jnp.int32(width_x)])
@@ -602,9 +660,9 @@
         [pltpu.SemaphoreType.DMA((4,))],
     )(place, tick, *pinned(velocity))
     even, odd = pair_up(even, 0), pair_up(odd, 1)
-    voidfraction, void_tick = call(
-        void_kernel, [(depth, width_x, LANES), (8, LANES)], [ANY, VMEM], us=2.0
-    )(tick, eps)
+    voidfraction, near = call(
+        void_kernel, [(depth, width_x, LANES), (24, 8, LANES)], [SMEM, ANY, VMEM], us=2.0
+    )(place, tick, eps)
     first, first_tick = call(
         first_kernel,
         [(3, 14, 32, LANES), (8, LANES)],
@@ -617,20 +675,20 @@
     own, even, odd = call(
         source_kernel,
         [(3, depth, 24, LANES), (3, 3, 24, LANES), (3, 3, 24, LANES)],
-        [SMEM, VMEM, VMEM, ANY, ANY],
-    )(place, forces, eps, first_tick, void_tick)
+        [SMEM, VMEM, VMEM, ANY],
+    )(place, forces, near, first_tick)
     even, odd = pair_up(even, 0), pair_up(odd, 1)
+    buffers = [pltpu.VMEM((3, 16, 32, LANES), F32)] * 4 + [pltpu.VMEM((3, 14, 32, LANES), F32)]
+    known = call(
+        near_kernel,
+        [(3, 2, 32, LANES)] * 3 + [(3, 5, rows, LANES)],
+        [SMEM] + [VMEM] * 3,
+        buffers,
+        us=2.0,
+    )(place, first, own, even)
     (moved,) = call(
-        stencil_kernel,
-        [(subs, 3, depth, rows, LANES)],
-        [SMEM] + [VMEM] * 4,
-        [
-            pltpu.VMEM((3, 16, 32, LANES), F32),
-            pltpu.VMEM((3, 16, 32, LANES), F32),
-            pltpu.VMEM((3, 14, 32, LANES), F32),
-        ],
-        us=4.0,
-    )(place, first, own, even, odd)
+        far_kernel, [(subs, 3, depth, rows, LANES)], [SMEM] + [VMEM] * 7, buffers, us=1.0
+    )(place, first, own, odd, *known)
     moved = lax.all_to_all(moved, "sub", 0, 0)
     (new_velocity,) = call(
         place_kernel,

time: 110 us -> 109 us (level)
  local copies, waits for them, and re-layouts: 2.79 us -> 0.03 us
  Pallas kernels: 34.1 us -> 35.9 us
    ppermute x4, waiting for transfers between devices: 14.7 us -> 11.3 us  [pair_up(): return lax.ppermute(x, 'slab', pairs + [(j, i) for i, j in pairs])]
    unnamed x20 -> x14, local copies, waits for them, and re-layouts: 2.79 us -> 0.03 us
    all_to_all x1, waiting for transfers between devices: 0.63 us -> 2.46 us  [body(): lax.all_to_all(solid.reshape(subs, share, 8, LANES), 'sub', 0, 0)]
    pallas_call x6 -> x7, Pallas kernels: 21.2 us -> 22.8 us  [the longest x2 10.5 us: slip_of(): call(functools.partial(slip_kernel, first, half), [(3, half * BLOCK)], [A...]
    all_to_all x1, waiting for transfers between devices: 1.32 us -> 2.54 us  [body(): eps = lax.all_to_all(eps_copies, 'sub', 0, 0).reshape(tiles, 8, LANES)]
  transfers between devices with their start and end apart: 7 -> 7, of which waited for: 5 -> 5; matrix products, arithmetic and copies ran while one was open for 0% -> 0% of each run, Pallas kernels for 14% -> 17%
where the time goes in v7:
time: 109 us; the launch traced here: 108 us
  Pallas kernels  35.9 us (33%)
  waiting for transfers between devices  27.9 us (26%)
  blocking collectives  22 us (20%)
  starting transfers between devices  21.6 us (20%)
    all_to_all x1, blocking collectives, body(): moved = lax.all_to_all(moved, 'sub', 0, 0)  22 us
    all_to_all x1, waiting for transfers between devices, body(): forces = lax.all_to_all(force, 'sub', 0, 0)  11.6 us
    ppermute x4, waiting for transfers between devices, pair_up(): return lax.ppermute(x, 'slab', pairs + [(j, i) for i, j in pairs])  11.3 us
    pallas_call x2, Pallas kernels, slip_of(): call(functools.partial(slip_kernel, first, half), [(3, half * BLOCK)], [A...  10.5 us
    pallas_call x1, Pallas kernels, body(): call(drag_kernel, [(3, blocks * BLOCK), (subs, 66, 8, LANES), (8, LANES)]...  7.72 us
    ppermute x4, starting transfers between devices, pair_up(): return lax.ppermute(x, 'slab', pairs + [(j, i) for i, j in pairs])  6.01 us
    all_to_all x1, starting transfers between devices, body(): eps = lax.all_to_all(eps_copies, 'sub', 0, 0).reshape(tiles, 8, LANES)  5.21 us
    all_to_all x1, starting transfers between devices, body(): forces = lax.all_to_all(force, 'sub', 0, 0)  5.21 us
  transfers between devices with their start and end apart: 7, of which 5 were waited for; matrix products, arithmetic and copies ran while one was open for 0% of the time, Pallas kernels for 17%

profile of v7, /device:TPU:225, one launch (start us, length us, event | category | flops | bytes accessed | tf_op | source)
XLA Modules:
  0.0 108.3 jit_solution(8227767189567279214)
XLA Ops:
  0.6 0.0 copy-start
  0.6 0.0 copy-start.1
  0.7 0.0 copy-start.2
  0.7 0.0 copy-start.3
  0.7 0.0 copy-start.4
  0.7 0.0 copy-start.5
  0.7 0.0 copy-start.6
  0.7 4.9 %shard_map.94 = (f32[128,8,128]{2,1,0:T(8,128)}, f32[8,128]{1,0:T(8,128)S(1)}) custom-call(s32[128]{0:T(128)} %brick_ref.1, s32[128,128]{1,0:T(8,128)} %bitcast.14, f32[3,16384]{1,0:T(4,128)} %frac_ref.1, f32[128,128]{1,0:T(8,128)} %bitcast.9), custom_call_target="tpu_custom_call" | custom-call | flops 5000000000 | bytes 18000000 | tf_op jit(solution)/shard_map/pallas_call | solution.py:598
  5.6 5.1 %all-to-all-start = ((f32[8,16,8,128]{3,2,1,0:T(8,128)}), f32[8,16,8,128]{3,2,1,0:T(8,128)S(1)}, u32[]{:S(2)}, u32[]{:S(2)}) async-start(f32[8,16,8,128]{3,2,1,0:T(8,128)} %bitcast.18), calls=%async_computation | async-start | bytes 1048576 | tf_op jit(solution)/shard_map/all_to_all | solution.py:608
  10.8 0.0 copy-done
  10.8 0.0 copy-done.1
  10.8 0.0 copy-done.2
  10.8 0.0 copy-done.3
  10.8 0.0 copy-done.4
  10.8 0.0 copy-done.5
  10.8 0.0 copy-done.6
  10.8 5.3 %shard_map.95.slip_a_ref = f32[3,8192]{1,0:T(4,128)S(1)} custom-call(f32[8,128]{1,0:T(8,128)S(1)} %get-tuple-element.24.after_any, s32[128]{0:T(128)S(1)} %copy-done.6, s32[128,128]{1,0:T(8,128)S(1)} %bitcast.15, f32[3,16384]{1,0:T(4,128)S(1)} %copy-done.2, f32[3,16384]{1,0:T(4,128)S(1)} %copy-done.1, f32[128,128]{1,0:T(8,128)S(1)} %bitcast.12, ...), custom_call_target="tpu_custom_call" | custom-call | flops 5000000000 | bytes 18000000 | tf_op jit(solution)/shard_map/pallas_call | solution.py:612
  16.1 2.5 %all-to-all-done.parts_ref = f32[8,16,8,128]{3,2,1,0:T(8,128)S(1)} async-done(((f32[8,16,8,128]{3,2,1,0:T(8,128)}), f32[8,16,8,128]{3,2,1,0:T(8,128)S(1)}, u32[]{:S(2)}, u32[]{:S(2)}) %all-to-all-start) | async-done | bytes 524320 | tf_op jit(solution)/shard_map/all_to_all | solution.py:608
  18.6 0.9 shard_map.96
  19.4 5.2 %all-to-all-start.1 = ((f32[8,16,8,128]{3,2,1,0:T(8,128)}), f32[8,16,8,128]{3,2,1,0:T(8,128)S(1)}, u32[]{:S(2)}, u32[]{:S(2)}) async-start(f32[8,16,8,128]{3,2,1,0:T(8,128)} %get-tuple-element.27), calls=%async_computation.1 | async-start | bytes 1048576 | tf_op jit(solution)/shard_map/all_to_all | solution.py:641
  24.7 5.3 %shard_map.97.slip_b_ref = f32[3,8192]{1,0:T(4,128)S(1)} custom-call(f32[8,128]{1,0:T(8,128)S(1)} %get-tuple-element.26.after_any, s32[128]{0:T(128)S(1)} %copy-done.6, s32[128,128]{1,0:T(8,128)S(1)} %bitcast.16, f32[3,16384]{1,0:T(4,128)S(1)} %copy-done.2, f32[3,16384]{1,0:T(4,128)S(1)} %copy-done.1, f32[128,128]{1,0:T(8,128)S(1)} %bitcast.13, ...), custom_call_target="tpu_custom_call" | custom-call | flops 5000000000 | bytes 18000000 | tf_op jit(solution)/shard_map/pallas_call | solution.py:612
  29.9 2.5 %all-to-all-done.1 = f32[8,16,8,128]{3,2,1,0:T(8,128)S(1)} async-done(((f32[8,16,8,128]{3,2,1,0:T(8,128)}), f32[8,16,8,128]{3,2,1,0:T(8,128)S(1)}, u32[]{:S(2)}, u32[]{:S(2)}) %all-to-all-start.1) | async-done | bytes 524320 | tf_op jit(solution)/shard_map/all_to_all | solution.py:641
  32.5 7.7 %shard_map.98 = (f32[3,16384]{1,0:T(4,128)}, f32[8,66,8,128]{3,2,1,0:T(8,128)}, f32[8,128]{1,0:T(8,128)S(1)}) custom-call(s32[128]{0:T(128)S(1)} %copy-done.6, s32[128,128]{1,0:T(8,128)S(1)} %bitcast.17, f32[3,16384]{1,0:T(4,128)S(1)} %copy-done.2, f32[3,8192]{1,0:T(4,128)S(1)} %shard_map.95.slip_a_ref, f32[3,8192]{1,0:T(4,128)S(1)} %shard_map.97.slip_b_ref, ...), custom_call_target="tpu_custom_call" | custom-call | flops 6000000000 | bytes 21600000 | tf_op jit(solution)/shard_map/pallas_call | solution.py:642
  40.2 5.2 %all-to-all-start.2 = ((f32[8,66,8,128]{3,2,1,0:T(8,128)}), f32[8,66,8,128]{3,2,1,0:T(8,128)S(1)}, u32[]{:S(2)}, u32[]{:S(2)}) async-start(f32[8,66,8,128]{3,2,1,0:T(8,128)} %get-tuple-element.33), calls=%async_computation.2 | async-start | bytes 4325376 | tf_op jit(solution)/shard_map/all_to_all | solution.py:653
  45.4 0.1 pad_add_fusion.place_ref
  45.5 1.7 %shard_map.99 = (f32[3,8,32,128]{3,2,1,0:T(8,128)S(1)}, f32[3,4,32,128]{3,2,1,0:T(8,128)S(1)}, f32[3,4,32,128]{3,2,1,0:T(8,128)S(1)}) custom-call(s32[4]{0:T(128)S(1)} %pad_add_fusion.place_ref, f32[8,128]{1,0:T(8,128)S(1)} %get-tuple-element.28.after_any, f32[3,8,128,128]{3,2,1,0:T(8,128)} %velocity_hbm.5), custom_call_target="tpu_custom_call" | custom-call | flops 1000000000 | bytes 3600000 | tf_op jit(solution)/shard_map/pallas_call | solution.py:656
  47.2 1.3 %collective-permute-start = (f32[3,4,32,128]{3,2,1,0:T(8,128)S(1)}, f32[3,4,32,128]{3,2,1,0:T(8,128)S(1)}, u32[]{:S(2)}, u32[]{:S(2)}) collective-permute-start(f32[3,4,32,128]{3,2,1,0:T(8,128)S(1)} %get-tuple-element.30), channel_id=1, source_target_pairs={{0,8},{16,24},{32,40},{48,56},{64,72},{80,88},{96,104},{112,120},{... | collective-permute-start | bytes 589832 | tf_op jit(solution)/shard_map/ppermute | solution.py:576
  48.4 1.9 %collective-permute-start.1 = (f32[3,4,32,128]{3,2,1,0:T(8,128)S(1)}, f32[3,4,32,128]{3,2,1,0:T(8,128)S(1)}, u32[]{:S(2)}, u32[]{:S(2)}) collective-permute-start(f32[3,4,32,128]{3,2,1,0:T(8,128)S(1)} %get-tuple-element.31), channel_id=1, source_target_pairs={{8,16},{24,32},{40,48},{56,64},{72,80},{88,96},{104,112},{120,128}... | collective-permute-start | bytes 589832 | tf_op jit(solution)/shard_map/ppermute | solution.py:576
  50.4 2.3 %shard_map.101 = (f32[8,128,128]{2,1,0:T(8,128)}, f32[24,8,128]{2,1,0:T(8,128)S(1)}) custom-call(s32[4]{0:T(128)S(1)} %pad_add_fusion.place_ref, f32[8,128]{1,0:T(8,128)S(1)} %get-tuple-element.28.after_any, f32[128,8,128]{2,1,0:T(8,128)S(1)} %bitcast.8), custom_call_target="tpu_custom_call" | custom-call | flops 2000000000 | bytes 7200000 | tf_op jit(solution)/shard_map/pallas_call | solution.py:663
  52.7 0.0 collective-permute-done.even_ref
  52.7 6.5 %collective-permute-done.1.odd_ref = f32[3,4,32,128]{3,2,1,0:T(8,128)S(1)} collective-permute-done((f32[3,4,32,128]{3,2,1,0:T(8,128)S(1)}, f32[3,4,32,128]{3,2,1,0:T(8,128)S(1)}, u32[]{:S(2)}, u32[]{:S(2)}) %collective-permute-start.1) | collective-permute-done | bytes 196640 | tf_op jit(solution)/shard_map/ppermute | solution.py:576
  59.1 1.5 %shard_map.100 = (f32[3,14,32,128]{3,2,1,0:T(8,128)S(1)}, f32[8,128]{1,0:T(8,128)S(1)}) custom-call(s32[4]{0:T(128)S(1)} %pad_add_fusion.place_ref, f32[3,8,32,128]{3,2,1,0:T(8,128)S(1)} %get-tuple-element.29.window_ref, f32[3,4,32,128]{3,2,1,0:T(8,128)S(1)} %collective-permute-done.even_ref, f32[3,4,32,128]{3,2,1,0:T(8,128)S(1)} %collective-permute-done.1.odd_ref), custom_call_target="tpu_custom_call" | custom-call | flops 1000000000 | bytes 3600000 | tf_op jit(solution)/shard_map/pallas_call | solution.py:666
  60.6 11.6 %all-to-all-done.2.parts_ref = f32[8,66,8,128]{3,2,1,0:T(8,128)S(1)} async-done(((f32[8,66,8,128]{3,2,1,0:T(8,128)}), f32[8,66,8,128]{3,2,1,0:T(8,128)S(1)}, u32[]{:S(2)}, u32[]{:S(2)}) %all-to-all-start.2) | async-done | bytes 2162720 | tf_op jit(solution)/shard_map/all_to_all | solution.py:653
  72.2 1.0 shard_map.102
  73.2 0.9 collective-permute-start.3
  74.2 1.9 %collective-permute-start.2 = (f32[3,3,24,128]{3,2,1,0:T(8,128)S(1)}, f32[3,3,24,128]{3,2,1,0:T(8,128)S(1)}, u32[]{:S(2)}, u32[]{:S(2)}) collective-permute-start(f32[3,3,24,128]{3,2,1,0:T(8,128)S(1)} %get-tuple-element.37), channel_id=1, source_target_pairs={{8,16},{24,32},{40,48},{56,64},{72,80},{88,96},{104,112},{120,128}... | collective-permute-start | bytes 331784 | tf_op jit(solution)/shard_map/ppermute | solution.py:576
  76.1 0.0 collective-permute-done.3.even_ref
  76.1 3.0 %shard_map.103 = (f32[3,2,32,128]{3,2,1,0:T(8,128)S(1)}, f32[3,2,32,128]{3,2,1,0:T(8,128)S(1)}, f32[3,2,32,128]{3,2,1,0:T(8,128)S(1)}, f32[3,5,16,128]{3,2,1,0:T(8,128)S(1)}) custom-call(s32[4]{0:T(128)S(1)} %pad_add_fusion.place_ref, f32[3,14,32,128]{3,2,1,0:T(8,128)S(1)} %get-tuple-element.32.first_ref, f32[3,8,24,128]{3,2,1,0:T(8,128)S(1)} %get-tuple-element.36.own_ref, ...), custom_call_target="tpu_custom_call" | custom-call | flops 2000000000 | bytes 7200000 | tf_op jit(solution)/shard_map/pallas_call | solution.py:682
  79.0 4.8 %collective-permute-done.2.odd_ref = f32[3,3,24,128]{3,2,1,0:T(8,128)S(1)} collective-permute-done((f32[3,3,24,128]{3,2,1,0:T(8,128)S(1)}, f32[3,3,24,128]{3,2,1,0:T(8,128)S(1)}, u32[]{:S(2)}, u32[]{:S(2)}) %collective-permute-start.2) | collective-permute-done | bytes 110624 | tf_op jit(solution)/shard_map/ppermute | solution.py:576
  83.8 1.2 %shard_map.104 = f32[8,3,8,16,128]{4,3,2,1,0:T(8,128)S(1)} custom-call(s32[4]{0:T(128)S(1)} %pad_add_fusion.place_ref, f32[3,14,32,128]{3,2,1,0:T(8,128)S(1)} %get-tuple-element.32.first_ref, f32[3,8,24,128]{3,2,1,0:T(8,128)S(1)} %get-tuple-element.36.own_ref, f32[3,3,24,128]{3,2,1,0:T(8,128)S(1)} %collective-permute-done.2.odd_ref, ...), custom_call_target="tpu_custom_call" | custom-call | flops 1000000000 | bytes 3600000 | tf_op jit(solution)/shard_map/pallas_call | solution.py:689
  85.1 22.0 %all_to_all.20.parts_ref = f32[8,3,8,16,128]{4,3,2,1,0:T(8,128)S(1)} all-to-all(f32[8,3,8,16,128]{4,3,2,1,0:T(8,128)S(1)} %shard_map.104), channel_id=1, replica_groups=mesh['slab'=32,'sub'=8] {'sub'}, dimensions={0} | all-to-all | bytes 3145728 | tf_op jit(solution)/shard_map/all_to_all | solution.py:692
  107.1 1.2 %shard_map.105 = f32[3,8,128,128]{3,2,1,0:T(8,128)} custom-call(f32[8,3,8,16,128]{4,3,2,1,0:T(8,128)S(1)} %all_to_all.20.parts_ref), custom_call_target="tpu_custom_call" | custom-call | flops 1000000000 | bytes 3600000 | tf_op jit(solution)/shard_map/pallas_call | solution.py:693
Async XLA Ops:
  0.6 10.1 %copy-start = (f32[3,8,128,128]{3,2,1,0:T(8,128)S(1)}, f32[3,8,128,128]{3,2,1,0:T(8,128)}, u32[]{:S(2)}) copy-start(f32[3,8,128,128]{3,2,1,0:T(8,128)} %velocity_hbm.5) | copy-start | bytes 4718596
  0.6 10.1 %copy-start.1 = (f32[3,16384]{1,0:T(4,128)S(1)}, f32[3,16384]{1,0:T(4,128)}, u32[]{:S(2)}) copy-start(f32[3,16384]{1,0:T(4,128)} %pvel_hbm.3) | copy-start | bytes 589828
  0.7 10.1 %copy-start.2 = (f32[3,16384]{1,0:T(4,128)S(1)}, f32[3,16384]{1,0:T(4,128)}, u32[]{:S(2)}) copy-start(f32[3,16384]{1,0:T(4,128)} %frac_ref.1) | copy-start | bytes 589828
  0.7 10.1 %copy-start.3 = (f32[16384]{0:T(1024)S(1)}, f32[16384]{0:T(1024)}, u32[]{:S(2)}) copy-start(f32[16384]{0:T(1024)} %param.12) | copy-start | bytes 196612
  0.7 10.1 %copy-start.4 = (f32[16384]{0:T(1024)S(1)}, f32[16384]{0:T(1024)}, u32[]{:S(2)}) copy-start(f32[16384]{0:T(1024)} %param.11) | copy-start | bytes 196612
  0.7 10.1 %copy-start.5 = (s32[16384]{0:T(1024)S(1)}, s32[16384]{0:T(1024)}, u32[]{:S(2)}) copy-start(s32[16384]{0:T(1024)} %param.10) | copy-start | bytes 196612
  0.7 10.1 %copy-start.6 = (s32[128]{0:T(128)S(1)}, s32[128]{0:T(128)}, u32[]{:S(2)}) copy-start(s32[128]{0:T(128)} %brick_ref.1) | copy-start | bytes 1540
  5.6 12.9 %all-to-all-start = ((f32[8,16,8,128]{3,2,1,0:T(8,128)}), f32[8,16,8,128]{3,2,1,0:T(8,128)S(1)}, u32[]{:S(2)}, u32[]{:S(2)}) async-start(f32[8,16,8,128]{3,2,1,0:T(8,128)} %bitcast.18), calls=%async_computation | async-start | bytes 1048576 | tf_op jit(solution)/shard_map/all_to_all | solution.py:608
  19.4 13.0 %all-to-all-start.1 = ((f32[8,16,8,128]{3,2,1,0:T(8,128)}), f32[8,16,8,128]{3,2,1,0:T(8,128)S(1)}, u32[]{:S(2)}, u32[]{:S(2)}) async-start(f32[8,16,8,128]{3,2,1,0:T(8,128)} %get-tuple-element.27), calls=%async_computation.1 | async-start | bytes 1048576 | tf_op jit(solution)/shard_map/all_to_all | solution.py:641
  40.2 32.0 %all-to-all-start.2 = ((f32[8,66,8,128]{3,2,1,0:T(8,128)}), f32[8,66,8,128]{3,2,1,0:T(8,128)S(1)}, u32[]{:S(2)}, u32[]{:S(2)}) async-start(f32[8,66,8,128]{3,2,1,0:T(8,128)} %get-tuple-element.33), calls=%async_computation.2 | async-start | bytes 4325376 | tf_op jit(solution)/shard_map/all_to_all | solution.py:653
  47.2 5.5 %collective-permute-start = (f32[3,4,32,128]{3,2,1,0:T(8,128)S(1)}, f32[3,4,32,128]{3,2,1,0:T(8,128)S(1)}, u32[]{:S(2)}, u32[]{:S(2)}) collective-permute-start(f32[3,4,32,128]{3,2,1,0:T(8,128)S(1)} %get-tuple-element.30), channel_id=1, source_target_pairs={{0,8},{16,24},{32,40},{48,56},{64,72},{80,88},{96,104},{112,120},{... | collective-permute-start | bytes 589832 | tf_op jit(solution)/shard_map/ppermute | solution.py:576
  48.4 10.7 %collective-permute-start.1 = (f32[3,4,32,128]{3,2,1,0:T(8,128)S(1)}, f32[3,4,32,128]{3,2,1,0:T(8,128)S(1)}, u32[]{:S(2)}, u32[]{:S(2)}) collective-permute-start(f32[3,4,32,128]{3,2,1,0:T(8,128)S(1)} %get-tuple-element.31), channel_id=1, source_target_pairs={{8,16},{24,32},{40,48},{56,64},{72,80},{88,96},{104,112},{120,128}... | collective-permute-start | bytes 589832 | tf_op jit(solution)/shard_map/ppermute | solution.py:576
  73.2 2.9 %collective-permute-start.3 = (f32[3,3,24,128]{3,2,1,0:T(8,128)S(1)}, f32[3,3,24,128]{3,2,1,0:T(8,128)S(1)}, u32[]{:S(2)}, u32[]{:S(2)}) collective-permute-start(f32[3,3,24,128]{3,2,1,0:T(8,128)S(1)} %get-tuple-element.38), channel_id=1, source_target_pairs={{0,8},{16,24},{32,40},{48,56},{64,72},{80,88},{96,104},{112,120},{... | collective-permute-start | bytes 331784 | tf_op jit(solution)/shard_map/ppermute | solution.py:576
  74.2 9.7 %collective-permute-start.2 = (f32[3,3,24,128]{3,2,1,0:T(8,128)S(1)}, f32[3,3,24,128]{3,2,1,0:T(8,128)S(1)}, u32[]{:S(2)}, u32[]{:S(2)}) collective-permute-start(f32[3,3,24,128]{3,2,1,0:T(8,128)S(1)} %get-tuple-element.37), channel_id=1, source_target_pairs={{8,16},{24,32},{40,48},{56,64},{72,80},{88,96},{104,112},{120,128}... | collective-permute-start | bytes 331784 | tf_op jit(solution)/shard_map/ppermute | solution.py:576

commit v8 on v7

--- a/solution.py
+++ b/solution.py
@@ -80,14 +80,20 @@
 
 def plane_weights(rows, zb, yb, fz, fy):
     ky = axis_weights(rows, yb, fy)
-    zero = jnp.zeros_like(fz)
-    at = [zb == z for z in range(7)]
+    number = zb.astype(F32)
+    offset = jnp.concatenate([number, number - 1.0], axis=0).astype(jnp.bfloat16)
+    zero = jnp.zeros((16, LANES), jnp.bfloat16)
+
+    def twice(value):
+        return jnp.concatenate([value, value], axis=0).astype(jnp.bfloat16)
+
     parts = []
     for here, above in zip(halves((1.0 - fz) * ky), halves(fz * ky)):
-        for z in range(8):
-            part = zero if z == 0 else jnp.where(at[z - 1], above, zero)
-            parts.append(part if z == 7 else jnp.where(at[z], here, part))
-    return jnp.concatenate(parts, axis=0).astype(jnp.bfloat16)
+        here, above = twice(here), twice(above)
+        for q in range(4):
+            upper = jnp.where(offset == 2 * q - 1, above, zero)
+            parts.append(jnp.where(offset == 2 * q, here, upper))
+    return jnp.concatenate(parts, axis=0)
 
 
 def split_rows(parts):
@@ -133,26 +139,6 @@
         term = weight * jnp.take_along_axis(tile, index, axis=1, mode="promise_in_bounds")
         total = term if total is None else total + term
     return jnp.sum(kx * total, axis=0, keepdims=True)
-
-
-def interpolate_pair(blocks):
-    lane = lanes_iota()
-    left = []
-    for n, (tile, t1, _, _) in enumerate(blocks):
-        brick = jnp.where((lane >> 6) == t1, tile, 0.0)
-        rows = split_rows([brick + pltpu.roll(brick, 64, 1)])
-        pair = [rows, jnp.zeros_like(rows)]
-        left.append(jnp.concatenate(pair if n == 0 else pair[::-1], axis=1))
-    both = jnp.dot(
-        jnp.concatenate(left, axis=0),
-        jnp.concatenate([weights for _, _, _, weights in blocks], axis=0),
-        preferred_element_type=F32,
-    )
-    found = []
-    for n, (_, _, kx, _) in enumerate(blocks):
-        total = both[16 * n : 16 * n + 8] + both[16 * n + 8 : 16 * n + 16]
-        found.append(jnp.sum(kx * total, axis=0, keepdims=True))
-    return found
 
 
 def brick_place(brick):
@@ -279,39 +265,36 @@
 
 
 def drag_kernel(
-    brick_ref, base_ref, frac_ref, slip_a_ref, slip_b_ref, eps_ref,
+    brick_hbm, base_ref, frac_ref, slip_a_ref, slip_b_ref, eps_ref,
     drag_ref, out_hbm, tick_ref,
-    force_ref, sems,
+    force_ref, brick_ref, sems,
 ):
     subs = force_ref.shape[0]
     rows, lane = rows_iota(), lanes_iota()
+    (copy,) = fetch([(brick_hbm, brick_ref)], sems)
     for j in range(subs):
         force_ref[j, 0:48] = jnp.zeros((48, 8, LANES), F32)
+    copy.wait()
 
     for slip_ref, start in ((slip_a_ref, 0), (slip_b_ref, slip_a_ref.shape[1] // BLOCK)):
 
         def step(number, carry, slip_ref=slip_ref, start=start):
-            known = []
-            for k in range(UNROLL):
-                block = number * UNROLL + k + start
-                _, zb, xb, yb, fz, fx, fy = particles(base_ref, frac_ref, block)
-                tx, t3, t1 = brick_place(brick_ref[block])
-                kx = axis_weights(rows, xb, fx)
-                known.append((eps_ref[tx * 8 + t3], t1, kx, plane_weights(rows, zb, yb, fz, fy)))
-            at_particles = sum((interpolate_pair(known[k : k + 2]) for k in range(0, UNROLL, 2)), [])
             found = []
             for k in range(UNROLL):
                 inner = number * UNROLL + k
+                block = inner + start
+                at, zb, xb, yb, fz, fx, fy = particles(base_ref, frac_ref, block)
                 inner_at = pl.ds(pl.multiple_of(inner * BLOCK, BLOCK), BLOCK)
-                at = pl.ds(pl.multiple_of((inner + start) * BLOCK, BLOCK), BLOCK)
-                _, _, kx, weights = known[k]
-                factor = jnp.exp(DRAG_POWER * jnp.log(at_particles[k]))
+                tx, t3, t1 = brick_place(brick_ref[block])
+                kx = axis_weights(rows, xb, fx)
+                eps = interpolate(eps_ref[tx * 8 + t3], kx, corner_terms(zb, yb, fz, fy, t1 * 64))
+                factor = jnp.exp(DRAG_POWER * jnp.log(eps))
                 parts = []
                 for c in range(3):
                     force = factor * slip_ref[c : c + 1, inner_at]
                     drag_ref[c : c + 1, at] = force
                     parts.append(kx * spread(force))
-                found.append((parts, weights))
+                found.append((parts, plane_weights(rows, zb, yb, fz, fy)))
             found = sum((deposit(found[k : k + 2]) for k in range(0, UNROLL, 2)), [])
             for k in range(UNROLL):
                 tx, t3, t1 = brick_place(brick_ref[number * UNROLL + k + start])
@@ -343,9 +326,9 @@
         copy.wait()
 
 
-def source_kernel(place_ref, parts_ref, eps_ref, first_any, own_ref, even_ref, odd_ref):
+def source_kernel(parts_ref, eps_ref, first_any, own_ref, even_ref, odd_ref):
     lane, rows = lanes_iota(), rows_iota()
-    even = place_ref[0] % 2 == 0
+    even = lax.axis_index("slab") % 2 == 0
 
     def summed(at):
         total = parts_ref[0, at]
@@ -374,13 +357,13 @@
                 odd_ref[c, n, at, :] = jnp.where(even, tiles[n], tiles[5 + n])
 
 
-def window_kernel(place_ref, after_any, velocity_hbm, out_ref, even_ref, odd_ref, sems):
-    even = place_ref[0] % 2 == 0
+def window_kernel(after_any, velocity_hbm, out_ref, even_ref, odd_ref, sems):
+    even = lax.axis_index("slab") % 2 == 0
     depth = velocity_hbm.shape[1]
     tiles_x = velocity_hbm.shape[2] // 8
     pairs, inside = [], []
     for r in range(4):
-        want = place_ref[1] * 2 + r - 1
+        want = lax.axis_index("sub") * 2 + r - 1
         inside.append(jnp.logical_and(want >= 0, want < tiles_x))
         at = pl.ds(pl.multiple_of(jnp.clip(want, 0, tiles_x - 1) * 8, 8), 8)
         pairs.append((velocity_hbm.at[:, :, at, :], out_ref.at[:, :, 8 * r : 8 * r + 8, :]))
@@ -394,7 +377,7 @@
         odd_ref[:, :, at, :] = jnp.where(even, rows[:, :4], rows[:, depth - 4 :])
 
 
-def void_kernel(place_ref, after_any, eps_ref, out_ref, near_ref):
+def void_kernel(after_any, eps_ref, out_ref, near_ref):
     lane, rows = lanes_iota(), rows_iota()
     tiles_x = out_ref.shape[1] // 8
 
@@ -407,14 +390,16 @@
         return carry
 
     lax.fori_loop(0, tiles_x // 4, convert, 0)
-    own = place_ref[1] * 2
+    own = lax.axis_index("sub") * 2
     near_ref[0:16] = eps_ref[pl.ds(own * 8, 16)]
     after = eps_ref[pl.ds(jnp.minimum(own + 2, tiles_x - 1) * 8, 8)]
     before = eps_ref[pl.ds(jnp.maximum(own - 1, 0) * 8, 8)]
     near_ref[16:24] = jnp.where(rows[None] < 4, after, before)
 
 
-def edges(slab, sub, planes, width):
+def edges():
+    slab, sub = lax.axis_index("slab"), lax.axis_index("sub")
+    planes, width = lax.axis_size("slab") * 8, lax.axis_size("sub") * 16
     row = lax.broadcasted_iota(jnp.int32, (32, LANES), 0) + sub * 16 - 8
     inside_x = jnp.logical_and(row >= 0, row < width)
 
@@ -444,9 +429,9 @@
     return [centres[c] + viscous * laps[c] for c in range(3)]
 
 
-def first_kernel(place_ref, window_ref, even_ref, odd_ref, out_ref, tick_ref, old):
+def first_kernel(window_ref, even_ref, odd_ref, out_ref, tick_ref, old):
     tick_ref[...] = jnp.zeros_like(tick_ref)
-    side = place_ref[0] % 2
+    side = lax.axis_index("slab") % 2
     old[:, pl.ds(12 - 12 * side, 4)] = even_ref[...]
     old[:, pl.ds(12 * side, 4)] = odd_ref[...]
     old[:, 4:12] = window_ref[...]
@@ -471,11 +456,11 @@
         new[c, z] = jnp.where(inside, total, 0.0)
 
 
-def near_kernel(place_ref, first_ref, own_ref, even_ref, *refs):
+def near_kernel(first_ref, own_ref, even_ref, *refs):
     keeps, last_ref, levels, source = refs[:3], refs[3], refs[4:8], refs[8]
-    keep = edges(place_ref[0], place_ref[1], place_ref[2], place_ref[3])
+    keep = edges()
     lane = lax.broadcasted_iota(jnp.int32, (32, LANES), 1)
-    side = place_ref[0] % 2
+    side = lax.axis_index("slab") % 2
 
     def plane(n):
         return n + side * (15 - 2 * n)
@@ -505,11 +490,11 @@
             last_ref[c, n] = levels[3][c, plane(7 + n), 8:24, :]
 
 
-def far_kernel(place_ref, first_ref, own_ref, odd_ref, *refs):
+def far_kernel(first_ref, own_ref, odd_ref, *refs):
     keeps, last_ref, out_ref, levels, source = refs[:3], refs[3], refs[4], refs[5:9], refs[9]
-    keep = edges(place_ref[0], place_ref[1], place_ref[2], place_ref[3])
+    keep = edges()
     lane = lax.broadcasted_iota(jnp.int32, (32, LANES), 1)
-    side = place_ref[0] % 2
+    side = lax.axis_index("slab") % 2
 
     def plane(n):
         return n + side * (15 - 2 * n)
@@ -580,8 +565,6 @@
     depth, width_x = velocity.shape[1], velocity.shape[2]
     blocks = brick_of_block.shape[0]
     subs = lax.axis_size("sub")
-    slab = lax.axis_index("slab").astype(jnp.int32)
-    sub = lax.axis_index("sub").astype(jnp.int32)
     tiles_x = width_x // 8
     tiles = tiles_x * 8
     share = tiles // subs
@@ -642,53 +625,52 @@
     drag, force, tick = call(
         drag_kernel,
         [(3, blocks * BLOCK), (subs, 66, 8, LANES), (8, LANES)],
-        [SMEM] + [VMEM] * 5,
+        [HBM] + [VMEM] * 5,
         [
             pltpu.VMEM((subs, 66, 8, LANES), F32),
+            pltpu.SMEM((blocks,), jnp.int32),
             pltpu.SemaphoreType.DMA((2 * subs,)),
         ],
         outs=[VMEM, HBM, VMEM],
         us=6.0,
-    )(brick_of_block, base, fraction, slip_a, slip_b, eps)
+    )(*pinned(brick_of_block), base, fraction, slip_a, slip_b, eps)
     forces = lax.all_to_all(force, "sub", 0, 0)
-    planes = depth * lax.axis_size("slab")
-    place = jnp.stack([slab, sub, jnp.int32(planes), jnp.int32(width_x)])
     window, even, odd = call(
         window_kernel,
         [(3, depth, 32, LANES), (3, 4, 32, LANES), (3, 4, 32, LANES)],
-        [SMEM, ANY, HBM],
+        [ANY, HBM],
         [pltpu.SemaphoreType.DMA((4,))],
-    )(place, tick, *pinned(velocity))
+    )(tick, *pinned(velocity))
     even, odd = pair_up(even, 0), pair_up(odd, 1)
     voidfraction, near = call(
-        void_kernel, [(depth, width_x, LANES), (24, 8, LANES)], [SMEM, ANY, VMEM], us=2.0
-    )(place, tick, eps)
+        void_kernel, [(depth, width_x, LANES), (24, 8, LANES)], [ANY, VMEM], us=2.0
+    )(tick, eps)
     first, first_tick = call(
         first_kernel,
         [(3, 14, 32, LANES), (8, LANES)],
-        [SMEM] + [VMEM] * 3,
+        [VMEM] * 3,
         [pltpu.VMEM((3, 16, 32, LANES), F32)],
         us=1.0,
-    )(place, window, even, odd)
+    )(window, even, odd)
 
     rows = width_x // subs
     own, even, odd = call(
         source_kernel,
         [(3, depth, 24, LANES), (3, 3, 24, LANES), (3, 3, 24, LANES)],
-        [SMEM, VMEM, VMEM, ANY],
-    )(place, forces, near, first_tick)
+        [VMEM, VMEM, ANY],
+    )(forces, near, first_tick)
     even, odd = pair_up(even, 0), pair_up(odd, 1)
     buffers = [pltpu.VMEM((3, 16, 32, LANES), F32)] * 4 + [pltpu.VMEM((3, 14, 32, LANES), F32)]
     known = call(
         near_kernel,
         [(3, 2, 32, LANES)] * 3 + [(3, 5, rows, LANES)],
-        [SMEM] + [VMEM] * 3,
+        [VMEM] * 3,
         buffers,
         us=2.0,
-    )(place, first, own, even)
+    )(first, own, even)
     (moved,) = call(
-        far_kernel, [(subs, 3, depth, rows, LANES)], [SMEM] + [VMEM] * 7, buffers, us=1.0
-    )(place, first, own, odd, *known)
+        far_kernel, [(subs, 3, depth, rows, LANES)], [VMEM] * 7, buffers, us=1.0
+    )(first, own, odd, *known)
     moved = lax.all_to_all(moved, "sub", 0, 0)
     (new_velocity,) = call(
         place_kernel,

time: 109 us -> 107 us (0.982)
  Pallas kernels: 35.9 us -> 31.7 us
  waiting for transfers between devices: 27.9 us -> 30.1 us
    pallas_call x4, Pallas kernels: 7.96 us -> 5.8 us  [the longest x1 2.4 us: body(): call(near_kernel, [(3, 2, 32, LANES)] * 3 + [(3, 5, rows, LANES)], [VMEM]...]
    all_to_all x1, waiting for transfers between devices: 11.6 us -> 12.7 us  [body(): forces = lax.all_to_all(force, 'sub', 0, 0)]
    ppermute x4, waiting for transfers between devices: 11.3 us -> 12.3 us  [pair_up(): return lax.ppermute(x, 'slab', pairs + [(j, i) for i, j in pairs])]
  transfers between devices with their start and end apart: 7 -> 7, of which waited for: 5 -> 5; matrix products, arithmetic and copies ran while one was open for 0% -> 0% of each run, Pallas kernels for 17% -> 16%
where the time goes in v8:
time: 107 us; the launch traced here: 106 us
  Pallas kernels  31.7 us (30%)
  waiting for transfers between devices  30.1 us (28%)
  blocking collectives  22 us (21%)
  starting transfers between devices  21.5 us (20%)
    all_to_all x1, blocking collectives, body(): moved = lax.all_to_all(moved, 'sub', 0, 0)  22 us
    all_to_all x1, waiting for transfers between devices, body(): forces = lax.all_to_all(force, 'sub', 0, 0)  12.7 us
    ppermute x4, waiting for transfers between devices, pair_up(): return lax.ppermute(x, 'slab', pairs + [(j, i) for i, j in pairs])  12.3 us
    pallas_call x2, Pallas kernels, slip_of(): call(functools.partial(slip_kernel, first, half), [(3, half * BLOCK)], [A...  10.5 us
    pallas_call x1, Pallas kernels, body(): call(drag_kernel, [(3, blocks * BLOCK), (subs, 66, 8, LANES), (8, LANES)]...  6.8 us
    ppermute x4, starting transfers between devices, pair_up(): return lax.ppermute(x, 'slab', pairs + [(j, i) for i, j in pairs])  6.03 us
    all_to_all x1, starting transfers between devices, body(): eps = lax.all_to_all(eps_copies, 'sub', 0, 0).reshape(tiles, 8, LANES)  5.19 us
    all_to_all x1, starting transfers between devices, body(): forces = lax.all_to_all(force, 'sub', 0, 0)  5.19 us
  transfers between devices with their start and end apart: 7, of which 5 were waited for; matrix products, arithmetic and copies ran while one was open for 0% of the time, Pallas kernels for 16%

profile of v8, /device:TPU:225, one launch (start us, length us, event | category | flops | bytes accessed | tf_op | source)
XLA Modules:
  0.0 106.3 jit_solution(2920560416963506576)
XLA Ops:
  0.6 0.0 copy-start
  0.6 0.0 copy-start.1
  0.7 0.0 copy-start.2
  0.7 0.0 copy-start.3
  0.7 0.0 copy-start.4
  0.7 0.0 copy-start.5
  0.7 0.0 copy-start.6
  0.7 4.9 %shard_map.94 = (f32[128,8,128]{2,1,0:T(8,128)}, f32[8,128]{1,0:T(8,128)S(1)}) custom-call(s32[128]{0:T(128)} %brick_hbm.7, s32[128,128]{1,0:T(8,128)} %bitcast.12, f32[3,16384]{1,0:T(4,128)} %frac_ref.1, f32[128,128]{1,0:T(8,128)} %bitcast.7), custom_call_target="tpu_custom_call" | custom-call | flops 5000000000 | bytes 18000000 | tf_op jit(solution)/shard_map/pallas_call | solution.py:581
  5.7 5.1 %all-to-all-start = ((f32[8,16,8,128]{3,2,1,0:T(8,128)}), f32[8,16,8,128]{3,2,1,0:T(8,128)S(1)}, u32[]{:S(2)}, u32[]{:S(2)}) async-start(f32[8,16,8,128]{3,2,1,0:T(8,128)} %bitcast.16), calls=%async_computation | async-start | bytes 1048576 | tf_op jit(solution)/shard_map/all_to_all | solution.py:591
  10.8 0.0 copy-done
  10.8 0.0 copy-done.1
  10.8 0.0 copy-done.2
  10.8 0.0 copy-done.3
  10.8 0.0 copy-done.4
  10.8 0.0 copy-done.5
  10.8 0.0 copy-done.6
  10.8 5.3 %shard_map.95.slip_a_ref = f32[3,8192]{1,0:T(4,128)S(1)} custom-call(f32[8,128]{1,0:T(8,128)S(1)} %get-tuple-element.24.after_any, s32[128]{0:T(128)S(1)} %copy-done.6, s32[128,128]{1,0:T(8,128)S(1)} %bitcast.13, f32[3,16384]{1,0:T(4,128)S(1)} %copy-done.2, f32[3,16384]{1,0:T(4,128)S(1)} %copy-done.1, f32[128,128]{1,0:T(8,128)S(1)} %bitcast.10, ...), custom_call_target="tpu_custom_call" | custom-call | flops 5000000000 | bytes 18000000 | tf_op jit(solution)/shard_map/pallas_call | solution.py:595
  16.1 2.5 %all-to-all-done.parts_ref = f32[8,16,8,128]{3,2,1,0:T(8,128)S(1)} async-done(((f32[8,16,8,128]{3,2,1,0:T(8,128)}), f32[8,16,8,128]{3,2,1,0:T(8,128)S(1)}, u32[]{:S(2)}, u32[]{:S(2)}) %all-to-all-start) | async-done | bytes 524320 | tf_op jit(solution)/shard_map/all_to_all | solution.py:591
  18.6 0.9 shard_map.96
  19.5 5.2 %all-to-all-start.1 = ((f32[8,16,8,128]{3,2,1,0:T(8,128)}), f32[8,16,8,128]{3,2,1,0:T(8,128)S(1)}, u32[]{:S(2)}, u32[]{:S(2)}) async-start(f32[8,16,8,128]{3,2,1,0:T(8,128)} %get-tuple-element.27), calls=%async_computation.1 | async-start | bytes 1048576 | tf_op jit(solution)/shard_map/all_to_all | solution.py:624
  24.7 5.3 %shard_map.97.slip_b_ref = f32[3,8192]{1,0:T(4,128)S(1)} custom-call(f32[8,128]{1,0:T(8,128)S(1)} %get-tuple-element.26.after_any, s32[128]{0:T(128)S(1)} %copy-done.6, s32[128,128]{1,0:T(8,128)S(1)} %bitcast.14, f32[3,16384]{1,0:T(4,128)S(1)} %copy-done.2, f32[3,16384]{1,0:T(4,128)S(1)} %copy-done.1, f32[128,128]{1,0:T(8,128)S(1)} %bitcast.11, ...), custom_call_target="tpu_custom_call" | custom-call | flops 5000000000 | bytes 18000000 | tf_op jit(solution)/shard_map/pallas_call | solution.py:595
  29.9 2.6 %all-to-all-done.1 = f32[8,16,8,128]{3,2,1,0:T(8,128)S(1)} async-done(((f32[8,16,8,128]{3,2,1,0:T(8,128)}), f32[8,16,8,128]{3,2,1,0:T(8,128)S(1)}, u32[]{:S(2)}, u32[]{:S(2)}) %all-to-all-start.1) | async-done | bytes 524320 | tf_op jit(solution)/shard_map/all_to_all | solution.py:624
  32.5 6.8 %shard_map.98 = (f32[3,16384]{1,0:T(4,128)}, f32[8,66,8,128]{3,2,1,0:T(8,128)}, f32[8,128]{1,0:T(8,128)S(1)}) custom-call(s32[128]{0:T(128)} %brick_hbm.7, s32[128,128]{1,0:T(8,128)S(1)} %bitcast.15, f32[3,16384]{1,0:T(4,128)S(1)} %copy-done.2, f32[3,8192]{1,0:T(4,128)S(1)} %shard_map.95.slip_a_ref, f32[3,8192]{1,0:T(4,128)S(1)} %shard_map.97.slip_b_ref, ...), custom_call_target="tpu_custom_call" | custom-call | flops 6000000000 | bytes 21600000 | tf_op jit(solution)/shard_map/pallas_call | solution.py:625
  39.3 5.2 %all-to-all-start.2 = ((f32[8,66,8,128]{3,2,1,0:T(8,128)}), f32[8,66,8,128]{3,2,1,0:T(8,128)S(1)}, u32[]{:S(2)}, u32[]{:S(2)}) async-start(f32[8,66,8,128]{3,2,1,0:T(8,128)} %get-tuple-element.33), calls=%async_computation.2 | async-start | bytes 4325376 | tf_op jit(solution)/shard_map/all_to_all | solution.py:637
  44.5 1.2 %shard_map.99 = (f32[3,8,32,128]{3,2,1,0:T(8,128)S(1)}, f32[3,4,32,128]{3,2,1,0:T(8,128)S(1)}, f32[3,4,32,128]{3,2,1,0:T(8,128)S(1)}) custom-call(f32[8,128]{1,0:T(8,128)S(1)} %get-tuple-element.28.after_any, f32[3,8,128,128]{3,2,1,0:T(8,128)} %velocity_hbm.5), custom_call_target="tpu_custom_call" | custom-call | flops 1000000000 | bytes 3600000 | tf_op jit(solution)/shard_map/pallas_call | solution.py:638
  45.7 1.3 %collective-permute-start = (f32[3,4,32,128]{3,2,1,0:T(8,128)S(1)}, f32[3,4,32,128]{3,2,1,0:T(8,128)S(1)}, u32[]{:S(2)}, u32[]{:S(2)}) collective-permute-start(f32[3,4,32,128]{3,2,1,0:T(8,128)S(1)} %get-tuple-element.30), channel_id=1, source_target_pairs={{0,8},{16,24},{32,40},{48,56},{64,72},{80,88},{96,104},{112,120},{... | collective-permute-start | bytes 589832 | tf_op jit(solution)/shard_map/ppermute | solution.py:561
  47.0 1.9 %collective-permute-start.1 = (f32[3,4,32,128]{3,2,1,0:T(8,128)S(1)}, f32[3,4,32,128]{3,2,1,0:T(8,128)S(1)}, u32[]{:S(2)}, u32[]{:S(2)}) collective-permute-start(f32[3,4,32,128]{3,2,1,0:T(8,128)S(1)} %get-tuple-element.31), channel_id=1, source_target_pairs={{8,16},{24,32},{40,48},{56,64},{72,80},{88,96},{104,112},{120,128}... | collective-permute-start | bytes 589832 | tf_op jit(solution)/shard_map/ppermute | solution.py:561
  48.9 1.8 %shard_map.101 = (f32[8,128,128]{2,1,0:T(8,128)}, f32[24,8,128]{2,1,0:T(8,128)S(1)}) custom-call(f32[8,128]{1,0:T(8,128)S(1)} %get-tuple-element.28.after_any, f32[128,8,128]{2,1,0:T(8,128)S(1)} %bitcast.6), custom_call_target="tpu_custom_call" | custom-call | flops 2000000000 | bytes 7200000 | tf_op jit(solution)/shard_map/pallas_call | solution.py:645
  50.6 0.0 collective-permute-done.even_ref
  50.6 7.0 %collective-permute-done.1.odd_ref = f32[3,4,32,128]{3,2,1,0:T(8,128)S(1)} collective-permute-done((f32[3,4,32,128]{3,2,1,0:T(8,128)S(1)}, f32[3,4,32,128]{3,2,1,0:T(8,128)S(1)}, u32[]{:S(2)}, u32[]{:S(2)}) %collective-permute-start.1) | collective-permute-done | bytes 196640 | tf_op jit(solution)/shard_map/ppermute | solution.py:561
  57.6 0.9 shard_map.100
  58.6 12.7 %all-to-all-done.2.parts_ref = f32[8,66,8,128]{3,2,1,0:T(8,128)S(1)} async-done(((f32[8,66,8,128]{3,2,1,0:T(8,128)}), f32[8,66,8,128]{3,2,1,0:T(8,128)S(1)}, u32[]{:S(2)}, u32[]{:S(2)}) %all-to-all-start.2) | async-done | bytes 2162720 | tf_op jit(solution)/shard_map/all_to_all | solution.py:637
  71.3 0.4 shard_map.102
  71.8 0.9 collective-permute-start.3
  72.7 1.9 %collective-permute-start.2 = (f32[3,3,24,128]{3,2,1,0:T(8,128)S(1)}, f32[3,3,24,128]{3,2,1,0:T(8,128)S(1)}, u32[]{:S(2)}, u32[]{:S(2)}) collective-permute-start(f32[3,3,24,128]{3,2,1,0:T(8,128)S(1)} %get-tuple-element.37), channel_id=1, source_target_pairs={{8,16},{24,32},{40,48},{56,64},{72,80},{88,96},{104,112},{120,128}... | collective-permute-start | bytes 331784 | tf_op jit(solution)/shard_map/ppermute | solution.py:561
  74.6 0.0 collective-permute-done.3.even_ref
  74.6 2.4 %shard_map.103 = (f32[3,2,32,128]{3,2,1,0:T(8,128)S(1)}, f32[3,2,32,128]{3,2,1,0:T(8,128)S(1)}, f32[3,2,32,128]{3,2,1,0:T(8,128)S(1)}, f32[3,5,16,128]{3,2,1,0:T(8,128)S(1)}) custom-call(f32[3,14,32,128]{3,2,1,0:T(8,128)S(1)} %get-tuple-element.32.first_ref, f32[3,8,24,128]{3,2,1,0:T(8,128)S(1)} %get-tuple-element.36.own_ref, ...), custom_call_target="tpu_custom_call" | custom-call | flops 2000000000 | bytes 7200000 | tf_op jit(solution)/shard_map/pallas_call | solution.py:664
  77.0 5.3 %collective-permute-done.2.odd_ref = f32[3,3,24,128]{3,2,1,0:T(8,128)S(1)} collective-permute-done((f32[3,3,24,128]{3,2,1,0:T(8,128)S(1)}, f32[3,3,24,128]{3,2,1,0:T(8,128)S(1)}, u32[]{:S(2)}, u32[]{:S(2)}) %collective-permute-start.2) | collective-permute-done | bytes 110624 | tf_op jit(solution)/shard_map/ppermute | solution.py:561
  82.4 0.7 shard_map.104
  83.1 22.0 %all_to_all.20.parts_ref = f32[8,3,8,16,128]{4,3,2,1,0:T(8,128)S(1)} all-to-all(f32[8,3,8,16,128]{4,3,2,1,0:T(8,128)S(1)} %shard_map.104), channel_id=1, replica_groups=mesh['slab'=32,'sub'=8] {'sub'}, dimensions={0} | all-to-all | bytes 3145728 | tf_op jit(solution)/shard_map/all_to_all | solution.py:674
  105.1 1.2 %shard_map.105 = f32[3,8,128,128]{3,2,1,0:T(8,128)} custom-call(f32[8,3,8,16,128]{4,3,2,1,0:T(8,128)S(1)} %all_to_all.20.parts_ref), custom_call_target="tpu_custom_call" | custom-call | flops 1000000000 | bytes 3600000 | tf_op jit(solution)/shard_map/pallas_call | solution.py:675
Async XLA Ops:
  0.6 10.2 %copy-start = (f32[3,8,128,128]{3,2,1,0:T(8,128)S(1)}, f32[3,8,128,128]{3,2,1,0:T(8,128)}, u32[]{:S(2)}) copy-start(f32[3,8,128,128]{3,2,1,0:T(8,128)} %velocity_hbm.5) | copy-start | bytes 4718596
  0.6 10.1 %copy-start.1 = (f32[3,16384]{1,0:T(4,128)S(1)}, f32[3,16384]{1,0:T(4,128)}, u32[]{:S(2)}) copy-start(f32[3,16384]{1,0:T(4,128)} %pvel_hbm.3) | copy-start | bytes 589828
  0.7 10.1 %copy-start.2 = (f32[3,16384]{1,0:T(4,128)S(1)}, f32[3,16384]{1,0:T(4,128)}, u32[]{:S(2)}) copy-start(f32[3,16384]{1,0:T(4,128)} %frac_ref.1) | copy-start | bytes 589828
  0.7 10.1 %copy-start.3 = (f32[16384]{0:T(1024)S(1)}, f32[16384]{0:T(1024)}, u32[]{:S(2)}) copy-start(f32[16384]{0:T(1024)} %param.12) | copy-start | bytes 196612
  0.7 10.1 %copy-start.4 = (f32[16384]{0:T(1024)S(1)}, f32[16384]{0:T(1024)}, u32[]{:S(2)}) copy-start(f32[16384]{0:T(1024)} %param.11) | copy-start | bytes 196612
  0.7 10.1 %copy-start.5 = (s32[16384]{0:T(1024)S(1)}, s32[16384]{0:T(1024)}, u32[]{:S(2)}) copy-start(s32[16384]{0:T(1024)} %param.10) | copy-start | bytes 196612
  0.7 10.1 %copy-start.6 = (s32[128]{0:T(128)S(1)}, s32[128]{0:T(128)}, u32[]{:S(2)}) copy-start(s32[128]{0:T(128)} %brick_hbm.7) | copy-start | bytes 1540
  5.7 12.9 %all-to-all-start = ((f32[8,16,8,128]{3,2,1,0:T(8,128)}), f32[8,16,8,128]{3,2,1,0:T(8,128)S(1)}, u32[]{:S(2)}, u32[]{:S(2)}) async-start(f32[8,16,8,128]{3,2,1,0:T(8,128)} %bitcast.16), calls=%async_computation | async-start | bytes 1048576 | tf_op jit(solution)/shard_map/all_to_all | solution.py:591
  19.5 13.0 %all-to-all-start.1 = ((f32[8,16,8,128]{3,2,1,0:T(8,128)}), f32[8,16,8,128]{3,2,1,0:T(8,128)S(1)}, u32[]{:S(2)}, u32[]{:S(2)}) async-start(f32[8,16,8,128]{3,2,1,0:T(8,128)} %get-tuple-element.27), calls=%async_computation.1 | async-start | bytes 1048576 | tf_op jit(solution)/shard_map/all_to_all | solution.py:624
  39.3 32.0 %all-to-all-start.2 = ((f32[8,66,8,128]{3,2,1,0:T(8,128)}), f32[8,66,8,128]{3,2,1,0:T(8,128)S(1)}, u32[]{:S(2)}, u32[]{:S(2)}) async-start(f32[8,66,8,128]{3,2,1,0:T(8,128)} %get-tuple-element.33), calls=%async_computation.2 | async-start | bytes 4325376 | tf_op jit(solution)/shard_map/all_to_all | solution.py:637
  45.7 5.0 %collective-permute-start = (f32[3,4,32,128]{3,2,1,0:T(8,128)S(1)}, f32[3,4,32,128]{3,2,1,0:T(8,128)S(1)}, u32[]{:S(2)}, u32[]{:S(2)}) collective-permute-start(f32[3,4,32,128]{3,2,1,0:T(8,128)S(1)} %get-tuple-element.30), channel_id=1, source_target_pairs={{0,8},{16,24},{32,40},{48,56},{64,72},{80,88},{96,104},{112,120},{... | collective-permute-start | bytes 589832 | tf_op jit(solution)/shard_map/ppermute | solution.py:561
  47.0 10.7 %collective-permute-start.1 = (f32[3,4,32,128]{3,2,1,0:T(8,128)S(1)}, f32[3,4,32,128]{3,2,1,0:T(8,128)S(1)}, u32[]{:S(2)}, u32[]{:S(2)}) collective-permute-start(f32[3,4,32,128]{3,2,1,0:T(8,128)S(1)} %get-tuple-element.31), channel_id=1, source_target_pairs={{8,16},{24,32},{40,48},{56,64},{72,80},{88,96},{104,112},{120,128}... | collective-permute-start | bytes 589832 | tf_op jit(solution)/shard_map/ppermute | solution.py:561
  71.8 2.9 %collective-permute-start.3 = (f32[3,3,24,128]{3,2,1,0:T(8,128)S(1)}, f32[3,3,24,128]{3,2,1,0:T(8,128)S(1)}, u32[]{:S(2)}, u32[]{:S(2)}) collective-permute-start(f32[3,3,24,128]{3,2,1,0:T(8,128)S(1)} %get-tuple-element.38), channel_id=1, source_target_pairs={{0,8},{16,24},{32,40},{48,56},{64,72},{80,88},{96,104},{112,120},{... | collective-permute-start | bytes 331784 | tf_op jit(solution)/shard_map/ppermute | solution.py:561
  72.7 9.7 %collective-permute-start.2 = (f32[3,3,24,128]{3,2,1,0:T(8,128)S(1)}, f32[3,3,24,128]{3,2,1,0:T(8,128)S(1)}, u32[]{:S(2)}, u32[]{:S(2)}) collective-permute-start(f32[3,3,24,128]{3,2,1,0:T(8,128)S(1)} %get-tuple-element.37), channel_id=1, source_target_pairs={{8,16},{24,32},{40,48},{56,64},{72,80},{88,96},{104,112},{120,128}... | collective-permute-start | bytes 331784 | tf_op jit(solution)/shard_map/ppermute | solution.py:561

commit v9 on v8

--- a/solution.py
+++ b/solution.py
@@ -16,6 +16,7 @@
 TIME_STEP = 0.05
 ITERS = 4
 UNROLL = 16
+LONG = 32
 F32 = jnp.float32
 PARAMS = pltpu.CompilerParams(vmem_limit_bytes=16 * 1024 * 1024)
 VMEM = pl.BlockSpec(memory_space=pltpu.VMEM)
@@ -147,7 +148,7 @@
 
 def solid_kernel(
     brick_hbm, base_hbm, frac_hbm, pvol_hbm, out_hbm, tick_ref,
-    out_ref, brick_ref, base_ref, frac_ref, pvol_ref, sems,
+    out_ref, late_ref, brick_ref, base_ref, frac_ref, pvol_ref, sems,
 ):
     copies = fetch(
         [(brick_hbm, brick_ref), (base_hbm, base_ref), (frac_hbm, frac_ref), (pvol_hbm, pvol_ref)],
@@ -157,22 +158,28 @@
     for copy in copies:
         copy.wait()
     rows, lane = rows_iota(), lanes_iota()
+    late_ref[...] = jnp.zeros_like(late_ref)
+
+    def add(number):
+        for k in range(LONG):
+            tx, t3, t1 = brick_place(brick_ref[number * LONG + k])
+            out_ref[tx * 8 + t3] += jnp.where((lane >> 6) == t1, late_ref[k], 0.0)
 
     def step(number, carry):
+        add(jnp.maximum(number - 1, 0))
         found = []
-        for k in range(UNROLL):
-            block = number * UNROLL + k
+        for k in range(LONG):
+            block = number * LONG + k
             _, zb, xb, yb, fz, fx, fy = particles(base_ref, frac_ref, block)
             kx = axis_weights(rows, xb, fx) * spread(pvol_ref[pl.ds(block, 1), :])
             found.append(([kx], plane_weights(rows, zb, yb, fz, fy)))
-        found = sum((deposit(found[k : k + 2]) for k in range(0, UNROLL, 2)), [])
-        for k in range(UNROLL):
-            tx, t3, t1 = brick_place(brick_ref[number * UNROLL + k])
-            tile = tx * 8 + t3
-            out_ref[tile] += jnp.where((lane >> 6) == t1, found[k], 0.0)
+            if k % 2:
+                late_ref[k - 1], late_ref[k] = deposit(found[-2:])
         return carry
 
-    lax.fori_loop(0, base_ref.shape[0] // UNROLL, step, 0)
+    steps = base_ref.shape[0] // LONG
+    lax.fori_loop(0, steps, step, 0)
+    add(steps - 1)
     (copy,) = fetch([(out_ref, out_hbm)], sems)
     tick_ref[...] = jnp.zeros_like(tick_ref)
     copy.wait()
@@ -267,7 +274,7 @@
 def drag_kernel(
     brick_hbm, base_ref, frac_ref, slip_a_ref, slip_b_ref, eps_ref,
     drag_ref, out_hbm, tick_ref,
-    force_ref, brick_ref, sems,
+    force_ref, late_ref, brick_ref, sems,
 ):
     subs = force_ref.shape[0]
     rows, lane = rows_iota(), lanes_iota()
@@ -276,13 +283,25 @@
         force_ref[j, 0:48] = jnp.zeros((48, 8, LANES), F32)
     copy.wait()
 
-    for slip_ref, start in ((slip_a_ref, 0), (slip_b_ref, slip_a_ref.shape[1] // BLOCK)):
+    late_ref[...] = jnp.zeros_like(late_ref)
+
+    def add(number):
+        for k in range(LONG):
+            tx, t3, t1 = brick_place(brick_ref[number * LONG + k])
+            mine = (lane >> 6) == t1
+            for c in range(3):
+                tile = (tx & 1) * 24 + c * 8 + t3
+                force_ref[tx >> 1, tile] += jnp.where(mine, late_ref[k, 8 * c : 8 * c + 8], 0.0)
+
+    steps = base_ref.shape[0] // LONG
+    for slip_ref, start in ((slip_a_ref, 0), (slip_b_ref, steps // 2)):
 
         def step(number, carry, slip_ref=slip_ref, start=start):
+            add(jnp.maximum(number - 1, 0))
             found = []
-            for k in range(UNROLL):
-                inner = number * UNROLL + k
-                block = inner + start
+            for k in range(LONG):
+                block = number * LONG + k
+                inner = block - start * LONG
                 at, zb, xb, yb, fz, fx, fy = particles(base_ref, frac_ref, block)
                 inner_at = pl.ds(pl.multiple_of(inner * BLOCK, BLOCK), BLOCK)
                 tx, t3, t1 = brick_place(brick_ref[block])
@@ -295,16 +314,12 @@
                     drag_ref[c : c + 1, at] = force
                     parts.append(kx * spread(force))
                 found.append((parts, plane_weights(rows, zb, yb, fz, fy)))
-            found = sum((deposit(found[k : k + 2]) for k in range(0, UNROLL, 2)), [])
-            for k in range(UNROLL):
-                tx, t3, t1 = brick_place(brick_ref[number * UNROLL + k + start])
-                mine = (lane >> 6) == t1
-                for c in range(3):
-                    tile = (tx & 1) * 24 + c * 8 + t3
-                    force_ref[tx >> 1, tile] += jnp.where(mine, found[k][8 * c : 8 * c + 8], 0.0)
+                if k % 2:
+                    late_ref[k - 1], late_ref[k] = deposit(found[-2:])
             return carry
 
-        lax.fori_loop(0, slip_ref.shape[1] // BLOCK // UNROLL, step, 0)
+        lax.fori_loop(start, start + steps // 2, step, 0)
+    add(steps - 1)
     copies = fetch([(force_ref.at[j, 0:48], out_hbm.at[j, 0:48]) for j in range(subs)], sems)
     zero = jnp.zeros((8, LANES), F32)
     tick_ref[...] = zero
@@ -582,7 +597,7 @@
         solid_kernel,
         [(tiles, 8, LANES), (8, LANES)],
         [HBM] * 4,
-        [pltpu.VMEM((tiles, 8, LANES), F32)]
+        [pltpu.VMEM((tiles, 8, LANES), F32), pltpu.VMEM((LONG, 8, LANES), F32)]
         + particles_vmem
         + [row_vmem, pltpu.SemaphoreType.DMA((4,))],
         outs=[HBM, VMEM],
@@ -628,6 +643,7 @@
         [HBM] + [VMEM] * 5,
         [
             pltpu.VMEM((subs, 66, 8, LANES), F32),
+            pltpu.VMEM((LONG, 24, LANES), F32),
             pltpu.SMEM((blocks,), jnp.int32),
             pltpu.SemaphoreType.DMA((2 * subs,)),
         ],

time: 107 us -> 106 us (level)
  no operation moved by 1% of the time
where the time goes in v9:
time: 106 us; the launch traced here: 105 us
  Pallas kernels  30.8 us (29%)
  waiting for transfers between devices  30.1 us (28%)
  blocking collectives  22 us (21%)
  starting transfers between devices  21.6 us (20%)
    all_to_all x1, blocking collectives, body(): moved = lax.all_to_all(moved, 'sub', 0, 0)  22 us
    all_to_all x1, waiting for transfers between devices, body(): forces = lax.all_to_all(force, 'sub', 0, 0)  12.7 us
    ppermute x4, waiting for transfers between devices, pair_up(): return lax.ppermute(x, 'slab', pairs + [(j, i) for i, j in pairs])  12.3 us
    pallas_call x2, Pallas kernels, slip_of(): call(functools.partial(slip_kernel, first, half), [(3, half * BLOCK)], [A...  10.5 us
    pallas_call x1, Pallas kernels, body(): call(drag_kernel, [(3, blocks * BLOCK), (subs, 66, 8, LANES), (8, LANES)]...  6.52 us
    ppermute x4, starting transfers between devices, pair_up(): return lax.ppermute(x, 'slab', pairs + [(j, i) for i, j in pairs])  6.03 us
    all_to_all x1, starting transfers between devices, body(): eps = lax.all_to_all(eps_copies, 'sub', 0, 0).reshape(tiles, 8, LANES)  5.22 us
    all_to_all x1, starting transfers between devices, body(): forces = lax.all_to_all(force, 'sub', 0, 0)  5.2 us
  transfers between devices with their start and end apart: 7, of which 5 were waited for; matrix products, arithmetic and copies ran while one was open for 0% of the time, Pallas kernels for 16%

profile of v9, /device:TPU:225, one launch (start us, length us, event | category | flops | bytes accessed | tf_op | source)
XLA Modules:
  0.0 105.3 jit_solution(884932561646118959)
XLA Ops:
  0.6 0.0 copy-start
  0.6 0.0 copy-start.1
  0.7 0.0 copy-start.2
  0.7 0.0 copy-start.3
  0.7 0.0 copy-start.4
  0.7 0.0 copy-start.5
  0.7 0.0 copy-start.6
  0.7 4.3 %shard_map.94 = (f32[128,8,128]{2,1,0:T(8,128)}, f32[8,128]{1,0:T(8,128)S(1)}) custom-call(s32[128]{0:T(128)} %brick_hbm.7, s32[128,128]{1,0:T(8,128)} %bitcast.12, f32[3,16384]{1,0:T(4,128)} %frac_ref.1, f32[128,128]{1,0:T(8,128)} %bitcast.7), custom_call_target="tpu_custom_call" | custom-call | flops 5000000000 | bytes 18000000 | tf_op jit(solution)/shard_map/pallas_call | solution.py:596
  5.0 5.1 %all-to-all-start = ((f32[8,16,8,128]{3,2,1,0:T(8,128)}), f32[8,16,8,128]{3,2,1,0:T(8,128)S(1)}, u32[]{:S(2)}, u32[]{:S(2)}) async-start(f32[8,16,8,128]{3,2,1,0:T(8,128)} %bitcast.16), calls=%async_computation | async-start | bytes 1048576 | tf_op jit(solution)/shard_map/all_to_all | solution.py:606
  10.1 0.0 copy-done
  10.1 0.0 copy-done.1
  10.1 0.0 copy-done.2
  10.1 0.0 copy-done.3
  10.1 0.0 copy-done.4
  10.2 0.0 copy-done.5
  10.2 0.0 copy-done.6
  10.2 5.3 %shard_map.95.slip_a_ref = f32[3,8192]{1,0:T(4,128)S(1)} custom-call(f32[8,128]{1,0:T(8,128)S(1)} %get-tuple-element.24.after_any, s32[128]{0:T(128)S(1)} %copy-done.6, s32[128,128]{1,0:T(8,128)S(1)} %bitcast.13, f32[3,16384]{1,0:T(4,128)S(1)} %copy-done.2, f32[3,16384]{1,0:T(4,128)S(1)} %copy-done.1, f32[128,128]{1,0:T(8,128)S(1)} %bitcast.10, ...), custom_call_target="tpu_custom_call" | custom-call | flops 5000000000 | bytes 18000000 | tf_op jit(solution)/shard_map/pallas_call | solution.py:610
  15.4 2.5 %all-to-all-done.parts_ref = f32[8,16,8,128]{3,2,1,0:T(8,128)S(1)} async-done(((f32[8,16,8,128]{3,2,1,0:T(8,128)}), f32[8,16,8,128]{3,2,1,0:T(8,128)S(1)}, u32[]{:S(2)}, u32[]{:S(2)}) %all-to-all-start) | async-done | bytes 524320 | tf_op jit(solution)/shard_map/all_to_all | solution.py:606
  17.9 0.9 shard_map.96
  18.8 5.2 %all-to-all-start.1 = ((f32[8,16,8,128]{3,2,1,0:T(8,128)}), f32[8,16,8,128]{3,2,1,0:T(8,128)S(1)}, u32[]{:S(2)}, u32[]{:S(2)}) async-start(f32[8,16,8,128]{3,2,1,0:T(8,128)} %get-tuple-element.27), calls=%async_computation.1 | async-start | bytes 1048576 | tf_op jit(solution)/shard_map/all_to_all | solution.py:639
  24.0 5.3 %shard_map.97.slip_b_ref = f32[3,8192]{1,0:T(4,128)S(1)} custom-call(f32[8,128]{1,0:T(8,128)S(1)} %get-tuple-element.26.after_any, s32[128]{0:T(128)S(1)} %copy-done.6, s32[128,128]{1,0:T(8,128)S(1)} %bitcast.14, f32[3,16384]{1,0:T(4,128)S(1)} %copy-done.2, f32[3,16384]{1,0:T(4,128)S(1)} %copy-done.1, f32[128,128]{1,0:T(8,128)S(1)} %bitcast.11, ...), custom_call_target="tpu_custom_call" | custom-call | flops 5000000000 | bytes 18000000 | tf_op jit(solution)/shard_map/pallas_call | solution.py:610
  29.3 2.5 %all-to-all-done.1 = f32[8,16,8,128]{3,2,1,0:T(8,128)S(1)} async-done(((f32[8,16,8,128]{3,2,1,0:T(8,128)}), f32[8,16,8,128]{3,2,1,0:T(8,128)S(1)}, u32[]{:S(2)}, u32[]{:S(2)}) %all-to-all-start.1) | async-done | bytes 524320 | tf_op jit(solution)/shard_map/all_to_all | solution.py:639
  31.8 6.5 %shard_map.98 = (f32[3,16384]{1,0:T(4,128)}, f32[8,66,8,128]{3,2,1,0:T(8,128)}, f32[8,128]{1,0:T(8,128)S(1)}) custom-call(s32[128]{0:T(128)} %brick_hbm.7, s32[128,128]{1,0:T(8,128)S(1)} %bitcast.15, f32[3,16384]{1,0:T(4,128)S(1)} %copy-done.2, f32[3,8192]{1,0:T(4,128)S(1)} %shard_map.95.slip_a_ref, f32[3,8192]{1,0:T(4,128)S(1)} %shard_map.97.slip_b_ref, ...), custom_call_target="tpu_custom_call" | custom-call | flops 6000000000 | bytes 21600000 | tf_op jit(solution)/shard_map/pallas_call | solution.py:640
  38.3 5.2 %all-to-all-start.2 = ((f32[8,66,8,128]{3,2,1,0:T(8,128)}), f32[8,66,8,128]{3,2,1,0:T(8,128)S(1)}, u32[]{:S(2)}, u32[]{:S(2)}) async-start(f32[8,66,8,128]{3,2,1,0:T(8,128)} %get-tuple-element.33), calls=%async_computation.2 | async-start | bytes 4325376 | tf_op jit(solution)/shard_map/all_to_all | solution.py:653
  43.5 1.2 %shard_map.99 = (f32[3,8,32,128]{3,2,1,0:T(8,128)S(1)}, f32[3,4,32,128]{3,2,1,0:T(8,128)S(1)}, f32[3,4,32,128]{3,2,1,0:T(8,128)S(1)}) custom-call(f32[8,128]{1,0:T(8,128)S(1)} %get-tuple-element.28.after_any, f32[3,8,128,128]{3,2,1,0:T(8,128)} %velocity_hbm.5), custom_call_target="tpu_custom_call" | custom-call | flops 1000000000 | bytes 3600000 | tf_op jit(solution)/shard_map/pallas_call | solution.py:654
  44.7 1.3 %collective-permute-start = (f32[3,4,32,128]{3,2,1,0:T(8,128)S(1)}, f32[3,4,32,128]{3,2,1,0:T(8,128)S(1)}, u32[]{:S(2)}, u32[]{:S(2)}) collective-permute-start(f32[3,4,32,128]{3,2,1,0:T(8,128)S(1)} %get-tuple-element.30), channel_id=1, source_target_pairs={{0,8},{16,24},{32,40},{48,56},{64,72},{80,88},{96,104},{112,120},{... | collective-permute-start | bytes 589832 | tf_op jit(solution)/shard_map/ppermute | solution.py:576
  46.0 1.9 %collective-permute-start.1 = (f32[3,4,32,128]{3,2,1,0:T(8,128)S(1)}, f32[3,4,32,128]{3,2,1,0:T(8,128)S(1)}, u32[]{:S(2)}, u32[]{:S(2)}) collective-permute-start(f32[3,4,32,128]{3,2,1,0:T(8,128)S(1)} %get-tuple-element.31), channel_id=1, source_target_pairs={{8,16},{24,32},{40,48},{56,64},{72,80},{88,96},{104,112},{120,128}... | collective-permute-start | bytes 589832 | tf_op jit(solution)/shard_map/ppermute | solution.py:576
  47.9 1.8 %shard_map.101 = (f32[8,128,128]{2,1,0:T(8,128)}, f32[24,8,128]{2,1,0:T(8,128)S(1)}) custom-call(f32[8,128]{1,0:T(8,128)S(1)} %get-tuple-element.28.after_any, f32[128,8,128]{2,1,0:T(8,128)S(1)} %bitcast.6), custom_call_target="tpu_custom_call" | custom-call | flops 2000000000 | bytes 7200000 | tf_op jit(solution)/shard_map/pallas_call | solution.py:661
  49.7 0.0 collective-permute-done.even_ref
  49.7 7.0 %collective-permute-done.1.odd_ref = f32[3,4,32,128]{3,2,1,0:T(8,128)S(1)} collective-permute-done((f32[3,4,32,128]{3,2,1,0:T(8,128)S(1)}, f32[3,4,32,128]{3,2,1,0:T(8,128)S(1)}, u32[]{:S(2)}, u32[]{:S(2)}) %collective-permute-start.1) | collective-permute-done | bytes 196640 | tf_op jit(solution)/shard_map/ppermute | solution.py:576
  56.7 0.9 shard_map.100
  57.6 12.7 %all-to-all-done.2.parts_ref = f32[8,66,8,128]{3,2,1,0:T(8,128)S(1)} async-done(((f32[8,66,8,128]{3,2,1,0:T(8,128)}), f32[8,66,8,128]{3,2,1,0:T(8,128)S(1)}, u32[]{:S(2)}, u32[]{:S(2)}) %all-to-all-start.2) | async-done | bytes 2162720 | tf_op jit(solution)/shard_map/all_to_all | solution.py:653
  70.4 0.4 shard_map.102
  70.8 0.9 collective-permute-start.3
  71.7 1.9 %collective-permute-start.2 = (f32[3,3,24,128]{3,2,1,0:T(8,128)S(1)}, f32[3,3,24,128]{3,2,1,0:T(8,128)S(1)}, u32[]{:S(2)}, u32[]{:S(2)}) collective-permute-start(f32[3,3,24,128]{3,2,1,0:T(8,128)S(1)} %get-tuple-element.37), channel_id=1, source_target_pairs={{8,16},{24,32},{40,48},{56,64},{72,80},{88,96},{104,112},{120,128}... | collective-permute-start | bytes 331784 | tf_op jit(solution)/shard_map/ppermute | solution.py:576
  73.7 0.0 collective-permute-done.3.even_ref
  73.7 2.4 %shard_map.103 = (f32[3,2,32,128]{3,2,1,0:T(8,128)S(1)}, f32[3,2,32,128]{3,2,1,0:T(8,128)S(1)}, f32[3,2,32,128]{3,2,1,0:T(8,128)S(1)}, f32[3,5,16,128]{3,2,1,0:T(8,128)S(1)}) custom-call(f32[3,14,32,128]{3,2,1,0:T(8,128)S(1)} %get-tuple-element.32.first_ref, f32[3,8,24,128]{3,2,1,0:T(8,128)S(1)} %get-tuple-element.36.own_ref, ...), custom_call_target="tpu_custom_call" | custom-call | flops 2000000000 | bytes 7200000 | tf_op jit(solution)/shard_map/pallas_call | solution.py:680
  76.1 5.3 %collective-permute-done.2.odd_ref = f32[3,3,24,128]{3,2,1,0:T(8,128)S(1)} collective-permute-done((f32[3,3,24,128]{3,2,1,0:T(8,128)S(1)}, f32[3,3,24,128]{3,2,1,0:T(8,128)S(1)}, u32[]{:S(2)}, u32[]{:S(2)}) %collective-permute-start.2) | collective-permute-done | bytes 110624 | tf_op jit(solution)/shard_map/ppermute | solution.py:576
  81.4 0.7 shard_map.104
  82.1 22.0 %all_to_all.20.parts_ref = f32[8,3,8,16,128]{4,3,2,1,0:T(8,128)S(1)} all-to-all(f32[8,3,8,16,128]{4,3,2,1,0:T(8,128)S(1)} %shard_map.104), channel_id=1, replica_groups=mesh['slab'=32,'sub'=8] {'sub'}, dimensions={0} | all-to-all | bytes 3145728 | tf_op jit(solution)/shard_map/all_to_all | solution.py:690
  104.1 1.2 %shard_map.105 = f32[3,8,128,128]{3,2,1,0:T(8,128)} custom-call(f32[8,3,8,16,128]{4,3,2,1,0:T(8,128)S(1)} %all_to_all.20.parts_ref), custom_call_target="tpu_custom_call" | custom-call | flops 1000000000 | bytes 3600000 | tf_op jit(solution)/shard_map/pallas_call | solution.py:691
Async XLA Ops:
  0.6 9.5 %copy-start = (f32[3,8,128,128]{3,2,1,0:T(8,128)S(1)}, f32[3,8,128,128]{3,2,1,0:T(8,128)}, u32[]{:S(2)}) copy-start(f32[3,8,128,128]{3,2,1,0:T(8,128)} %velocity_hbm.5) | copy-start | bytes 4718596
  0.6 9.5 %copy-start.1 = (f32[3,16384]{1,0:T(4,128)S(1)}, f32[3,16384]{1,0:T(4,128)}, u32[]{:S(2)}) copy-start(f32[3,16384]{1,0:T(4,128)} %pvel_hbm.3) | copy-start | bytes 589828
  0.7 9.5 %copy-start.2 = (f32[3,16384]{1,0:T(4,128)S(1)}, f32[3,16384]{1,0:T(4,128)}, u32[]{:S(2)}) copy-start(f32[3,16384]{1,0:T(4,128)} %frac_ref.1) | copy-start | bytes 589828
  0.7 9.5 %copy-start.3 = (f32[16384]{0:T(1024)S(1)}, f32[16384]{0:T(1024)}, u32[]{:S(2)}) copy-start(f32[16384]{0:T(1024)} %param.12) | copy-start | bytes 196612
  0.7 9.5 %copy-start.4 = (f32[16384]{0:T(1024)S(1)}, f32[16384]{0:T(1024)}, u32[]{:S(2)}) copy-start(f32[16384]{0:T(1024)} %param.11) | copy-start | bytes 196612
  0.7 9.5 %copy-start.5 = (s32[16384]{0:T(1024)S(1)}, s32[16384]{0:T(1024)}, u32[]{:S(2)}) copy-start(s32[16384]{0:T(1024)} %param.10) | copy-start | bytes 196612
  0.7 9.5 %copy-start.6 = (s32[128]{0:T(128)S(1)}, s32[128]{0:T(128)}, u32[]{:S(2)}) copy-start(s32[128]{0:T(128)} %brick_hbm.7) | copy-start | bytes 1540
  5.0 12.9 %all-to-all-start = ((f32[8,16,8,128]{3,2,1,0:T(8,128)}), f32[8,16,8,128]{3,2,1,0:T(8,128)S(1)}, u32[]{:S(2)}, u32[]{:S(2)}) async-start(f32[8,16,8,128]{3,2,1,0:T(8,128)} %bitcast.16), calls=%async_computation | async-start | bytes 1048576 | tf_op jit(solution)/shard_map/all_to_all | solution.py:606
  18.8 13.0 %all-to-all-start.1 = ((f32[8,16,8,128]{3,2,1,0:T(8,128)}), f32[8,16,8,128]{3,2,1,0:T(8,128)S(1)}, u32[]{:S(2)}, u32[]{:S(2)}) async-start(f32[8,16,8,128]{3,2,1,0:T(8,128)} %get-tuple-element.27), calls=%async_computation.1 | async-start | bytes 1048576 | tf_op jit(solution)/shard_map/all_to_all | solution.py:639
  38.3 32.0 %all-to-all-start.2 = ((f32[8,66,8,128]{3,2,1,0:T(8,128)}), f32[8,66,8,128]{3,2,1,0:T(8,128)S(1)}, u32[]{:S(2)}, u32[]{:S(2)}) async-start(f32[8,66,8,128]{3,2,1,0:T(8,128)} %get-tuple-element.33), calls=%async_computation.2 | async-start | bytes 4325376 | tf_op jit(solution)/shard_map/all_to_all | solution.py:653
  44.7 5.0 %collective-permute-start = (f32[3,4,32,128]{3,2,1,0:T(8,128)S(1)}, f32[3,4,32,128]{3,2,1,0:T(8,128)S(1)}, u32[]{:S(2)}, u32[]{:S(2)}) collective-permute-start(f32[3,4,32,128]{3,2,1,0:T(8,128)S(1)} %get-tuple-element.30), channel_id=1, source_target_pairs={{0,8},{16,24},{32,40},{48,56},{64,72},{80,88},{96,104},{112,120},{... | collective-permute-start | bytes 589832 | tf_op jit(solution)/shard_map/ppermute | solution.py:576
  46.0 10.7 %collective-permute-start.1 = (f32[3,4,32,128]{3,2,1,0:T(8,128)S(1)}, f32[3,4,32,128]{3,2,1,0:T(8,128)S(1)}, u32[]{:S(2)}, u32[]{:S(2)}) collective-permute-start(f32[3,4,32,128]{3,2,1,0:T(8,128)S(1)} %get-tuple-element.31), channel_id=1, source_target_pairs={{8,16},{24,32},{40,48},{56,64},{72,80},{88,96},{104,112},{120,128}... | collective-permute-start | bytes 589832 | tf_op jit(solution)/shard_map/ppermute | solution.py:576
  70.8 2.9 %collective-permute-start.3 = (f32[3,3,24,128]{3,2,1,0:T(8,128)S(1)}, f32[3,3,24,128]{3,2,1,0:T(8,128)S(1)}, u32[]{:S(2)}, u32[]{:S(2)}) collective-permute-start(f32[3,3,24,128]{3,2,1,0:T(8,128)S(1)} %get-tuple-element.38), channel_id=1, source_target_pairs={{0,8},{16,24},{32,40},{48,56},{64,72},{80,88},{96,104},{112,120},{... | collective-permute-start | bytes 331784 | tf_op jit(solution)/shard_map/ppermute | solution.py:576
  71.7 9.7 %collective-permute-start.2 = (f32[3,3,24,128]{3,2,1,0:T(8,128)S(1)}, f32[3,3,24,128]{3,2,1,0:T(8,128)S(1)}, u32[]{:S(2)}, u32[]{:S(2)}) collective-permute-start(f32[3,3,24,128]{3,2,1,0:T(8,128)S(1)} %get-tuple-element.37), channel_id=1, source_target_pairs={{8,16},{24,32},{40,48},{56,64},{72,80},{88,96},{104,112},{120,128}... | collective-permute-start | bytes 331784 | tf_op jit(solution)/shard_map/ppermute | solution.py:576

commit v10 on v9

--- a/solution.py
+++ b/solution.py
@@ -196,9 +196,9 @@
         copy.wait()
 
 
-def slip_kernel(
+def slip_work(
     first, count,
-    after_any, brick_hbm, base_hbm, frac_hbm, pvel_hbm, coef_hbm, pvol_hbm, velocity_hbm,
+    brick_hbm, base_hbm, frac_hbm, pvel_hbm, coef_hbm, pvol_hbm, velocity_hbm,
     out_ref,
     brick_ref, base_ref, frac_ref, pvel_ref, coef_ref, pvol_ref, velocity_ref, table_ref, sems,
 ):
@@ -269,6 +269,40 @@
     inner = jnp.where(rows == 2, pltpu.roll(b, 7, 0), pltpu.roll(b, 1, 0))
     d = jnp.where(rows < 2, pltpu.roll(a, 5, 0), jnp.where(rows > 5, pltpu.roll(c, 3, 0), inner))
     return a, b, c, d
+
+
+def slip_kernel(first, count, after_any, *refs):
+    slip_work(first, count, *refs)
+
+
+def even_slip_kernel(count, after_any, early_ref, *refs):
+    out_ref = refs[7]
+    odd = lax.axis_index("slab") % 2 == 1
+
+    @pl.when(odd)
+    def _():
+        out_ref[...] = early_ref[...]
+
+    @pl.when(jnp.logical_not(odd))
+    def _():
+        slip_work(0, count, *refs)
+
+
+def start_kernel(
+    count,
+    brick_hbm, base_hbm, frac_hbm, pvel_hbm, coef_hbm, pvol_hbm, velocity_hbm,
+    out_hbm, tick_ref, early_ref,
+    *scratch,
+):
+    @pl.when(lax.axis_index("slab") % 2 == 1)
+    def _():
+        slip_work(
+            0, count,
+            brick_hbm, base_hbm, frac_hbm, pvel_hbm, coef_hbm, pvol_hbm, velocity_hbm,
+            early_ref, *scratch[7:],
+        )
+
+    solid_kernel(brick_hbm, base_hbm, frac_hbm, pvol_hbm, out_hbm, tick_ref, *scratch[:7])
 
 
 def drag_kernel(
@@ -593,40 +627,38 @@
         pltpu.VMEM((3, blocks * BLOCK), F32),
     ]
     row_vmem = pltpu.VMEM((blocks, BLOCK), F32)
-    solid, solid_tick = call(
-        solid_kernel,
-        [(tiles, 8, LANES), (8, LANES)],
-        [HBM] * 4,
+    half = blocks // 2
+    slip_scratch = [
+        pltpu.SMEM((blocks,), jnp.int32),
+        pltpu.VMEM((half, BLOCK), jnp.int32),
+        pltpu.VMEM((3, half * BLOCK), F32),
+        pltpu.VMEM((3, half * BLOCK), F32),
+        pltpu.VMEM((half, BLOCK), F32),
+        pltpu.VMEM((half, BLOCK), F32),
+        pltpu.VMEM(velocity.shape, F32),
+        pltpu.VMEM((3 * tiles, 8, LANES), F32),
+        pltpu.SemaphoreType.DMA((7,)),
+    ]
+    particle_args = pinned(brick_of_block, base, fraction, part_vel, coef, pvol, velocity)
+    solid, solid_tick, early = call(
+        functools.partial(start_kernel, half),
+        [(tiles, 8, LANES), (8, LANES), (3, half * BLOCK)],
+        [HBM] * 7,
         [pltpu.VMEM((tiles, 8, LANES), F32), pltpu.VMEM((LONG, 8, LANES), F32)]
         + particles_vmem
-        + [row_vmem, pltpu.SemaphoreType.DMA((4,))],
-        outs=[HBM, VMEM],
+        + [row_vmem, pltpu.SemaphoreType.DMA((4,))]
+        + slip_scratch,
+        outs=[HBM, VMEM, VMEM],
         us=5.0,
-    )(*pinned(brick_of_block, base, fraction, pvol))
+    )(*particle_args)
     solid_parts = lax.all_to_all(solid.reshape(subs, share, 8, LANES), "sub", 0, 0)
-    half = blocks // 2
-
-    def slip_of(first, after):
-        (slip,) = call(
-            functools.partial(slip_kernel, first, half),
-            [(3, half * BLOCK)],
-            [ANY] + [HBM] * 7,
-            [
-                pltpu.SMEM((blocks,), jnp.int32),
-                pltpu.VMEM((half, BLOCK), jnp.int32),
-                pltpu.VMEM((3, half * BLOCK), F32),
-                pltpu.VMEM((3, half * BLOCK), F32),
-                pltpu.VMEM((half, BLOCK), F32),
-                pltpu.VMEM((half, BLOCK), F32),
-                pltpu.VMEM(velocity.shape, F32),
-                pltpu.VMEM((3 * tiles, 8, LANES), F32),
-                pltpu.SemaphoreType.DMA((7,)),
-            ],
-            us=5.0,
-            )(after, brick_of_block, base, fraction, part_vel, coef, pvol, velocity)
-        return slip
-
-    slip_a = slip_of(0, solid_tick)
+    (slip_a,) = call(
+        functools.partial(even_slip_kernel, half),
+        [(3, half * BLOCK)],
+        [ANY, VMEM] + [HBM] * 7,
+        slip_scratch,
+        us=5.0,
+    )(solid_tick, early, *particle_args)
     eps_copies, eps_tick = call(
         eps_kernel,
         [(subs, share, 8, LANES), (8, LANES)],
@@ -635,7 +667,13 @@
         outs=[HBM, VMEM],
         us=0.5,
     )(solid_parts)
-    slip_b = slip_of(half, eps_tick)
+    (slip_b,) = call(
+        functools.partial(slip_kernel, half, half),
+        [(3, half * BLOCK)],
+        [ANY] + [HBM] * 7,
+        slip_scratch,
+        us=5.0,
+    )(eps_tick, *particle_args)
     eps = lax.all_to_all(eps_copies, "sub", 0, 0).reshape(tiles, 8, LANES)
     drag, force, tick = call(
         drag_kernel,

time: 106 us -> 105 us (level)
  starting transfers between devices: 21.6 us -> 17.1 us
  waiting for transfers between devices: 30.1 us -> 31.8 us
  Pallas kernels: 30.8 us -> 32.4 us
    all_to_all x1, waiting for transfers between devices: 2.45 us -> 7.05 us  [body(): lax.all_to_all(solid.reshape(subs, share, 8, LANES), 'sub', 0, 0)]
    ppermute x4, starting transfers between devices: 6.03 us -> 4.24 us  [pair_up(): return lax.ppermute(x, 'slab', pairs + [(j, i) for i, j in pairs])]
    all_to_all x1, starting transfers between devices: 5.22 us -> 3.51 us  [body(): eps = lax.all_to_all(eps_copies, 'sub', 0, 0).reshape(tiles, 8, LANES)]
    pallas_call x3, Pallas kernels: 14.8 us -> 16.4 us  [the longest x1 10.2 us: body(): call(functools.partial(start_kernel, half), [(tiles, 8, LANES), (8, LANES...]
    all_to_all x1, waiting for transfers between devices: 2.54 us -> 0.88 us  [body(): eps = lax.all_to_all(eps_copies, 'sub', 0, 0).reshape(tiles, 8, LANES)]
    all_to_all x1, waiting for transfers between devices: 12.7 us -> 11.5 us  [body(): forces = lax.all_to_all(force, 'sub', 0, 0)]
  transfers between devices with their start and end apart: 7 -> 7, of which waited for: 5 -> 5; matrix products, arithmetic and copies ran while one was open for 0% -> 0% of each run, Pallas kernels for 16% -> 12%
where the time goes in v10:
time: 105 us
  Pallas kernels  32.4 us (31%)
  waiting for transfers between devices  31.8 us (30%)
  blocking collectives  22.5 us (21%)
  starting transfers between devices  17.1 us (16%)
    all_to_all x1, blocking collectives, body(): moved = lax.all_to_all(moved, 'sub', 0, 0)  22.5 us
    ppermute x4, waiting for transfers between devices, pair_up(): return lax.ppermute(x, 'slab', pairs + [(j, i) for i, j in pairs])  12.3 us
    all_to_all x1, waiting for transfers between devices, body(): forces = lax.all_to_all(force, 'sub', 0, 0)  11.5 us
    pallas_call x1, Pallas kernels, body(): call(functools.partial(start_kernel, half), [(tiles, 8, LANES), (8, LANES...  10.2 us
    all_to_all x1, waiting for transfers between devices, body(): lax.all_to_all(solid.reshape(subs, share, 8, LANES), 'sub', 0, 0)  7.05 us
    pallas_call x1, Pallas kernels, body(): call(drag_kernel, [(3, blocks * BLOCK), (subs, 66, 8, LANES), (8, LANES)]...  6.51 us
    pallas_call x1, Pallas kernels, body(): call(functools.partial(slip_kernel, half, half), [(3, half * BLOCK)], [AN...  6.15 us
    all_to_all x1, starting transfers between devices, body(): lax.all_to_all(solid.reshape(subs, share, 8, LANES), 'sub', 0, 0)  5.13 us
  transfers between devices with their start and end apart: 7, of which 5 were waited for; matrix products, arithmetic and copies ran while one was open for 0% of the time, Pallas kernels for 12%

profile of v10, /device:TPU:225, one launch (start us, length us, event | category | flops | bytes accessed | tf_op | source)
XLA Modules:
  0.0 104.5 jit_solution(11504577890735745329)
XLA Ops:
  0.6 10.2 %shard_map.94 = (f32[128,8,128]{2,1,0:T(8,128)}, f32[8,128]{1,0:T(8,128)S(1)}, f32[3,8192]{1,0:T(4,128)S(1)}) custom-call(s32[128]{0:T(128)} %brick_hbm.3, s32[128,128]{1,0:T(8,128)} %bitcast.7, f32[3,16384]{1,0:T(4,128)} %frac_ref.1, f32[3,16384]{1,0:T(4,128)} %refs_3_.3, f32[128,128]{1,0:T(8,128)} %bitcast.12, f32[128,128]{1,0:T(8,128)} %bitcast.15, ...), custom_call_target="tpu_custom_call" | custom-call | flops 5000000000 | bytes 18000000 | tf_op jit(solution)/shard_map/pallas_call | solution.py:643
  10.9 5.1 %all-to-all-start = ((f32[8,16,8,128]{3,2,1,0:T(8,128)}), f32[8,16,8,128]{3,2,1,0:T(8,128)S(1)}, u32[]{:S(2)}, u32[]{:S(2)}) async-start(f32[8,16,8,128]{3,2,1,0:T(8,128)} %bitcast.11), calls=%async_computation | async-start | bytes 1048576 | tf_op jit(solution)/shard_map/all_to_all | solution.py:654
  16.0 0.1 shard_map.95.slip_a_ref
  16.1 7.0 %all-to-all-done.parts_ref = f32[8,16,8,128]{3,2,1,0:T(8,128)S(1)} async-done(((f32[8,16,8,128]{3,2,1,0:T(8,128)}), f32[8,16,8,128]{3,2,1,0:T(8,128)S(1)}, u32[]{:S(2)}, u32[]{:S(2)}) %all-to-all-start) | async-done | bytes 524320 | tf_op jit(solution)/shard_map/all_to_all | solution.py:654
  23.1 0.9 shard_map.96
  24.0 3.5 %all-to-all-start.1 = ((f32[8,16,8,128]{3,2,1,0:T(8,128)}), f32[8,16,8,128]{3,2,1,0:T(8,128)S(1)}, u32[]{:S(2)}, u32[]{:S(2)}) async-start(f32[8,16,8,128]{3,2,1,0:T(8,128)} %get-tuple-element.29), calls=%async_computation.1 | async-start | bytes 1048576 | tf_op jit(solution)/shard_map/all_to_all | solution.py:677
  27.5 0.0 copy-start
  27.5 0.0 copy-start.1
  27.5 6.1 %shard_map.97.slip_b_ref = f32[3,8192]{1,0:T(4,128)S(1)} custom-call(f32[8,128]{1,0:T(8,128)S(1)} %get-tuple-element.28.after_any, s32[128]{0:T(128)} %brick_hbm.3, s32[128,128]{1,0:T(8,128)} %bitcast.9, f32[3,16384]{1,0:T(4,128)} %frac_ref.1, f32[3,16384]{1,0:T(4,128)} %refs_3_.3, f32[128,128]{1,0:T(8,128)} %bitcast.14, f32[128,128]{1,0:T(8,128)} %bitcast.17, ...), custom_call_target="tpu_custom_call" | custom-call | flops 5000000000 | bytes 18000000 | tf_op jit(solution)/shard_map/pallas_call | solution.py:670
  33.7 0.9 all-to-all-done.1
  34.6 0.0 copy-done
  34.6 0.0 copy-done.1
  34.6 6.5 %shard_map.98 = (f32[3,16384]{1,0:T(4,128)}, f32[8,66,8,128]{3,2,1,0:T(8,128)}, f32[8,128]{1,0:T(8,128)S(1)}) custom-call(s32[128]{0:T(128)} %brick_hbm.3, s32[128,128]{1,0:T(8,128)S(1)} %bitcast.10, f32[3,16384]{1,0:T(4,128)S(1)} %copy-done, f32[3,8192]{1,0:T(4,128)S(1)} %shard_map.95.slip_a_ref, f32[3,8192]{1,0:T(4,128)S(1)} %shard_map.97.slip_b_ref, ...), custom_call_target="tpu_custom_call" | custom-call | flops 6000000000 | bytes 21600000 | tf_op jit(solution)/shard_map/pallas_call | solution.py:678
  41.1 4.2 %all-to-all-start.2 = ((f32[8,66,8,128]{3,2,1,0:T(8,128)}), f32[8,66,8,128]{3,2,1,0:T(8,128)S(1)}, u32[]{:S(2)}, u32[]{:S(2)}) async-start(f32[8,66,8,128]{3,2,1,0:T(8,128)} %get-tuple-element.35), calls=%async_computation.2 | async-start | bytes 4325376 | tf_op jit(solution)/shard_map/all_to_all | solution.py:691
  45.3 1.2 %shard_map.99 = (f32[3,8,32,128]{3,2,1,0:T(8,128)S(1)}, f32[3,4,32,128]{3,2,1,0:T(8,128)S(1)}, f32[3,4,32,128]{3,2,1,0:T(8,128)S(1)}) custom-call(f32[8,128]{1,0:T(8,128)S(1)} %get-tuple-element.30.after_any, f32[3,8,128,128]{3,2,1,0:T(8,128)} %velocity_hbm.3), custom_call_target="tpu_custom_call" | custom-call | flops 1000000000 | bytes 3600000 | tf_op jit(solution)/shard_map/pallas_call | solution.py:692
  46.5 0.1 collective-permute-start
  46.6 1.9 %collective-permute-start.1 = (f32[3,4,32,128]{3,2,1,0:T(8,128)S(1)}, f32[3,4,32,128]{3,2,1,0:T(8,128)S(1)}, u32[]{:S(2)}, u32[]{:S(2)}) collective-permute-start(f32[3,4,32,128]{3,2,1,0:T(8,128)S(1)} %get-tuple-element.33), channel_id=1, source_target_pairs={{8,16},{24,32},{40,48},{56,64},{72,80},{88,96},{104,112},{120,128}... | collective-permute-start | bytes 589832 | tf_op jit(solution)/shard_map/ppermute | solution.py:610
  48.5 1.8 %shard_map.101 = (f32[8,128,128]{2,1,0:T(8,128)}, f32[24,8,128]{2,1,0:T(8,128)S(1)}) custom-call(f32[8,128]{1,0:T(8,128)S(1)} %get-tuple-element.30.after_any, f32[128,8,128]{2,1,0:T(8,128)S(1)} %bitcast.6), custom_call_target="tpu_custom_call" | custom-call | flops 2000000000 | bytes 7200000 | tf_op jit(solution)/shard_map/pallas_call | solution.py:699
  50.3 0.0 collective-permute-done.even_ref
  50.3 7.0 %collective-permute-done.1.odd_ref = f32[3,4,32,128]{3,2,1,0:T(8,128)S(1)} collective-permute-done((f32[3,4,32,128]{3,2,1,0:T(8,128)S(1)}, f32[3,4,32,128]{3,2,1,0:T(8,128)S(1)}, u32[]{:S(2)}, u32[]{:S(2)}) %collective-permute-start.1) | collective-permute-done | bytes 196640 | tf_op jit(solution)/shard_map/ppermute | solution.py:610
  57.3 0.9 shard_map.100
  58.2 11.5 %all-to-all-done.2.parts_ref = f32[8,66,8,128]{3,2,1,0:T(8,128)S(1)} async-done(((f32[8,66,8,128]{3,2,1,0:T(8,128)}), f32[8,66,8,128]{3,2,1,0:T(8,128)S(1)}, u32[]{:S(2)}, u32[]{:S(2)}) %all-to-all-start.2) | async-done | bytes 2162720 | tf_op jit(solution)/shard_map/all_to_all | solution.py:691
  69.7 0.4 shard_map.102
  70.2 0.3 collective-permute-start.3
  70.5 1.9 %collective-permute-start.2 = (f32[3,3,24,128]{3,2,1,0:T(8,128)S(1)}, f32[3,3,24,128]{3,2,1,0:T(8,128)S(1)}, u32[]{:S(2)}, u32[]{:S(2)}) collective-permute-start(f32[3,3,24,128]{3,2,1,0:T(8,128)S(1)} %get-tuple-element.39), channel_id=1, source_target_pairs={{8,16},{24,32},{40,48},{56,64},{72,80},{88,96},{104,112},{120,128}... | collective-permute-start | bytes 331784 | tf_op jit(solution)/shard_map/ppermute | solution.py:610
  72.4 0.0 collective-permute-done.3.even_ref
  72.4 2.4 %shard_map.103 = (f32[3,2,32,128]{3,2,1,0:T(8,128)S(1)}, f32[3,2,32,128]{3,2,1,0:T(8,128)S(1)}, f32[3,2,32,128]{3,2,1,0:T(8,128)S(1)}, f32[3,5,16,128]{3,2,1,0:T(8,128)S(1)}) custom-call(f32[3,14,32,128]{3,2,1,0:T(8,128)S(1)} %get-tuple-element.34.first_ref, f32[3,8,24,128]{3,2,1,0:T(8,128)S(1)} %get-tuple-element.38.own_ref, ...), custom_call_target="tpu_custom_call" | custom-call | flops 2000000000 | bytes 7200000 | tf_op jit(solution)/shard_map/pallas_call | solution.py:718
  74.8 5.3 %collective-permute-done.2.odd_ref = f32[3,3,24,128]{3,2,1,0:T(8,128)S(1)} collective-permute-done((f32[3,3,24,128]{3,2,1,0:T(8,128)S(1)}, f32[3,3,24,128]{3,2,1,0:T(8,128)S(1)}, u32[]{:S(2)}, u32[]{:S(2)}) %collective-permute-start.2) | collective-permute-done | bytes 110624 | tf_op jit(solution)/shard_map/ppermute | solution.py:610
  80.2 0.7 shard_map.104
  80.9 22.5 %all_to_all.20.parts_ref = f32[8,3,8,16,128]{4,3,2,1,0:T(8,128)S(1)} all-to-all(f32[8,3,8,16,128]{4,3,2,1,0:T(8,128)S(1)} %shard_map.104), channel_id=1, replica_groups=mesh['slab'=32,'sub'=8] {'sub'}, dimensions={0} | all-to-all | bytes 3145728 | tf_op jit(solution)/shard_map/all_to_all | solution.py:728
  103.3 1.2 %shard_map.105 = f32[3,8,128,128]{3,2,1,0:T(8,128)} custom-call(f32[8,3,8,16,128]{4,3,2,1,0:T(8,128)S(1)} %all_to_all.20.parts_ref), custom_call_target="tpu_custom_call" | custom-call | flops 1000000000 | bytes 3600000 | tf_op jit(solution)/shard_map/pallas_call | solution.py:729
Async XLA Ops:
  10.9 12.3 %all-to-all-start = ((f32[8,16,8,128]{3,2,1,0:T(8,128)}), f32[8,16,8,128]{3,2,1,0:T(8,128)S(1)}, u32[]{:S(2)}, u32[]{:S(2)}) async-start(f32[8,16,8,128]{3,2,1,0:T(8,128)} %bitcast.11), calls=%async_computation | async-start | bytes 1048576 | tf_op jit(solution)/shard_map/all_to_all | solution.py:654
  24.0 10.6 %all-to-all-start.1 = ((f32[8,16,8,128]{3,2,1,0:T(8,128)}), f32[8,16,8,128]{3,2,1,0:T(8,128)S(1)}, u32[]{:S(2)}, u32[]{:S(2)}) async-start(f32[8,16,8,128]{3,2,1,0:T(8,128)} %get-tuple-element.29), calls=%async_computation.1 | async-start | bytes 1048576 | tf_op jit(solution)/shard_map/all_to_all | solution.py:677
  27.5 7.1 %copy-start = (f32[3,16384]{1,0:T(4,128)S(1)}, f32[3,16384]{1,0:T(4,128)}, u32[]{:S(2)}) copy-start(f32[3,16384]{1,0:T(4,128)} %frac_ref.1) | copy-start | bytes 589828
  27.5 7.1 %copy-start.1 = (s32[16384]{0:T(1024)S(1)}, s32[16384]{0:T(1024)}, u32[]{:S(2)}) copy-start(s32[16384]{0:T(1024)} %param.10) | copy-start | bytes 196612
  41.1 28.7 %all-to-all-start.2 = ((f32[8,66,8,128]{3,2,1,0:T(8,128)}), f32[8,66,8,128]{3,2,1,0:T(8,128)S(1)}, u32[]{:S(2)}, u32[]{:S(2)}) async-start(f32[8,66,8,128]{3,2,1,0:T(8,128)} %get-tuple-element.35), calls=%async_computation.2 | async-start | bytes 4325376 | tf_op jit(solution)/shard_map/all_to_all | solution.py:691
  46.5 3.8 %collective-permute-start = (f32[3,4,32,128]{3,2,1,0:T(8,128)S(1)}, f32[3,4,32,128]{3,2,1,0:T(8,128)S(1)}, u32[]{:S(2)}, u32[]{:S(2)}) collective-permute-start(f32[3,4,32,128]{3,2,1,0:T(8,128)S(1)} %get-tuple-element.32), channel_id=1, source_target_pairs={{0,8},{16,24},{32,40},{48,56},{64,72},{80,88},{96,104},{112,120},{... | collective-permute-start | bytes 589832 | tf_op jit(solution)/shard_map/ppermute | solution.py:610
  46.6 10.7 %collective-permute-start.1 = (f32[3,4,32,128]{3,2,1,0:T(8,128)S(1)}, f32[3,4,32,128]{3,2,1,0:T(8,128)S(1)}, u32[]{:S(2)}, u32[]{:S(2)}) collective-permute-start(f32[3,4,32,128]{3,2,1,0:T(8,128)S(1)} %get-tuple-element.33), channel_id=1, source_target_pairs={{8,16},{24,32},{40,48},{56,64},{72,80},{88,96},{104,112},{120,128}... | collective-permute-start | bytes 589832 | tf_op jit(solution)/shard_map/ppermute | solution.py:610
  70.2 2.2 %collective-permute-start.3 = (f32[3,3,24,128]{3,2,1,0:T(8,128)S(1)}, f32[3,3,24,128]{3,2,1,0:T(8,128)S(1)}, u32[]{:S(2)}, u32[]{:S(2)}) collective-permute-start(f32[3,3,24,128]{3,2,1,0:T(8,128)S(1)} %get-tuple-element.40), channel_id=1, source_target_pairs={{0,8},{16,24},{32,40},{48,56},{64,72},{80,88},{96,104},{112,120},{... | collective-permute-start | bytes 331784 | tf_op jit(solution)/shard_map/ppermute | solution.py:610
  70.5 9.7 %collective-permute-start.2 = (f32[3,3,24,128]{3,2,1,0:T(8,128)S(1)}, f32[3,3,24,128]{3,2,1,0:T(8,128)S(1)}, u32[]{:S(2)}, u32[]{:S(2)}) collective-permute-start(f32[3,3,24,128]{3,2,1,0:T(8,128)S(1)} %get-tuple-element.39), channel_id=1, source_target_pairs={{8,16},{24,32},{40,48},{56,64},{72,80},{88,96},{104,112},{120,128}... | collective-permute-start | bytes 331784 | tf_op jit(solution)/shard_map/ppermute | solution.py:610

commit v11 on v10

--- a/solution.py
+++ b/solution.py
@@ -15,7 +15,6 @@
 VISCOSITY = 1.2
 TIME_STEP = 0.05
 ITERS = 4
-UNROLL = 16
 LONG = 32
 F32 = jnp.float32
 PARAMS = pltpu.CompilerParams(vmem_limit_bytes=16 * 1024 * 1024)
@@ -204,9 +203,11 @@
 ):
     some = pl.ds(first, count)
     wide = pl.ds(first * BLOCK, count * BLOCK)
+    middle = velocity_hbm.shape[2] // 2
+    sides = (slice(0, middle), slice(middle, 2 * middle))
     copies = fetch(
-        [
-            (velocity_hbm, velocity_ref),
+        [(velocity_hbm.at[:, :, side, :], velocity_ref.at[:, :, side, :]) for side in sides]
+        + [
             (brick_hbm, brick_ref),
             (base_hbm.at[some], base_ref),
             (frac_hbm.at[:, wide], frac_ref),
@@ -229,14 +230,15 @@
                     table_ref[(tx * 3 + c) * 8 + t3] = tiles[t3]
         return carry
 
-    copies[0].wait()
-    lax.fori_loop(0, tiles_x // 2, convert, 0)
-    for copy in copies[1:]:
+    for n in range(2):
+        copies[n].wait()
+        lax.fori_loop(n * tiles_x // 4, (n + 1) * tiles_x // 4, convert, 0)
+    for copy in copies[2:]:
         copy.wait()
 
     def step(number, carry):
-        for k in range(UNROLL):
-            block = number * UNROLL + k
+        for k in range(LONG):
+            block = number * LONG + k
             at, zb, xb, yb, fz, fx, fy = particles(base_ref, frac_ref, block)
             tx, t3, t1 = brick_place(brick_ref[first + block])
             kx = axis_weights(rows, xb, fx)
@@ -252,7 +254,7 @@
                 out_ref[c : c + 1, at] = factor * rel[c]
         return carry
 
-    lax.fori_loop(0, count // UNROLL, step, 0)
+    lax.fori_loop(0, count // LONG, step, 0)
 
 
 def pack_halo(rows, tiles):
@@ -637,7 +639,7 @@
         pltpu.VMEM((half, BLOCK), F32),
         pltpu.VMEM(velocity.shape, F32),
         pltpu.VMEM((3 * tiles, 8, LANES), F32),
-        pltpu.SemaphoreType.DMA((7,)),
+        pltpu.SemaphoreType.DMA((8,)),
     ]
     particle_args = pinned(brick_of_block, base, fraction, part_vel, coef, pvol, velocity)
     solid, solid_tick, early = call(

time: 105 us -> 105 us (level)
  no operation moved by 1% of the time
where the time goes in v11:
time: 105 us; the launch traced here: 104 us
  waiting for transfers between devices  32.8 us (31%)
  Pallas kernels  31.5 us (30%)
  blocking collectives  22.5 us (21%)
  starting transfers between devices  16.7 us (16%)
    all_to_all x1, blocking collectives, body(): moved = lax.all_to_all(moved, 'sub', 0, 0)  22.5 us
    ppermute x4, waiting for transfers between devices, pair_up(): return lax.ppermute(x, 'slab', pairs + [(j, i) for i, j in pairs])  12.3 us
    all_to_all x1, waiting for transfers between devices, body(): forces = lax.all_to_all(force, 'sub', 0, 0)  12.1 us
    pallas_call x1, Pallas kernels, body(): call(functools.partial(start_kernel, half), [(tiles, 8, LANES), (8, LANES...  9.77 us
    all_to_all x1, waiting for transfers between devices, body(): lax.all_to_all(solid.reshape(subs, share, 8, LANES), 'sub', 0, 0)  7.04 us
    pallas_call x1, Pallas kernels, body(): call(drag_kernel, [(3, blocks * BLOCK), (subs, 66, 8, LANES), (8, LANES)]...  6.5 us
    pallas_call x1, Pallas kernels, body(): call(functools.partial(slip_kernel, half, half), [(3, half * BLOCK)], [AN...  5.7 us
    all_to_all x1, starting transfers between devices, body(): lax.all_to_all(solid.reshape(subs, share, 8, LANES), 'sub', 0, 0)  5.13 us
  transfers between devices with their start and end apart: 7, of which 5 were waited for; matrix products, arithmetic and copies ran while one was open for 0% of the time, Pallas kernels for 12%

profile of v11, /device:TPU:225, one launch (start us, length us, event | category | flops | bytes accessed | tf_op | source)
XLA Modules:
  0.0 104.2 jit_solution(16139362651242264992)
XLA Ops:
  0.6 9.8 %shard_map.94 = (f32[128,8,128]{2,1,0:T(8,128)}, f32[8,128]{1,0:T(8,128)S(1)}, f32[3,8192]{1,0:T(4,128)S(1)}) custom-call(s32[128]{0:T(128)} %brick_hbm.3, s32[128,128]{1,0:T(8,128)} %bitcast.7, f32[3,16384]{1,0:T(4,128)} %frac_ref.1, f32[3,16384]{1,0:T(4,128)} %refs_3_.3, f32[128,128]{1,0:T(8,128)} %bitcast.12, f32[128,128]{1,0:T(8,128)} %bitcast.15, ...), custom_call_target="tpu_custom_call" | custom-call | flops 5000000000 | bytes 18000000 | tf_op jit(solution)/shard_map/pallas_call | solution.py:645
  10.4 5.1 %all-to-all-start = ((f32[8,16,8,128]{3,2,1,0:T(8,128)}), f32[8,16,8,128]{3,2,1,0:T(8,128)S(1)}, u32[]{:S(2)}, u32[]{:S(2)}) async-start(f32[8,16,8,128]{3,2,1,0:T(8,128)} %bitcast.11), calls=%async_computation | async-start | bytes 1048576 | tf_op jit(solution)/shard_map/all_to_all | solution.py:656
  15.5 0.1 shard_map.95.slip_a_ref
  15.6 7.0 %all-to-all-done.parts_ref = f32[8,16,8,128]{3,2,1,0:T(8,128)S(1)} async-done(((f32[8,16,8,128]{3,2,1,0:T(8,128)}), f32[8,16,8,128]{3,2,1,0:T(8,128)S(1)}, u32[]{:S(2)}, u32[]{:S(2)}) %all-to-all-start) | async-done | bytes 524320 | tf_op jit(solution)/shard_map/all_to_all | solution.py:656
  22.7 0.9 shard_map.96
  23.6 3.5 %all-to-all-start.1 = ((f32[8,16,8,128]{3,2,1,0:T(8,128)}), f32[8,16,8,128]{3,2,1,0:T(8,128)S(1)}, u32[]{:S(2)}, u32[]{:S(2)}) async-start(f32[8,16,8,128]{3,2,1,0:T(8,128)} %get-tuple-element.29), calls=%async_computation.1 | async-start | bytes 1048576 | tf_op jit(solution)/shard_map/all_to_all | solution.py:679
  27.1 0.0 copy-start
  27.1 0.0 copy-start.1
  27.1 5.7 %shard_map.97.slip_b_ref = f32[3,8192]{1,0:T(4,128)S(1)} custom-call(f32[8,128]{1,0:T(8,128)S(1)} %get-tuple-element.28.after_any, s32[128]{0:T(128)} %brick_hbm.3, s32[128,128]{1,0:T(8,128)} %bitcast.9, f32[3,16384]{1,0:T(4,128)} %frac_ref.1, f32[3,16384]{1,0:T(4,128)} %refs_3_.3, f32[128,128]{1,0:T(8,128)} %bitcast.14, f32[128,128]{1,0:T(8,128)} %bitcast.17, ...), custom_call_target="tpu_custom_call" | custom-call | flops 5000000000 | bytes 18000000 | tf_op jit(solution)/shard_map/pallas_call | solution.py:672
  32.8 1.3 %all-to-all-done.1 = f32[8,16,8,128]{3,2,1,0:T(8,128)S(1)} async-done(((f32[8,16,8,128]{3,2,1,0:T(8,128)}), f32[8,16,8,128]{3,2,1,0:T(8,128)S(1)}, u32[]{:S(2)}, u32[]{:S(2)}) %all-to-all-start.1) | async-done | bytes 524320 | tf_op jit(solution)/shard_map/all_to_all | solution.py:679
  34.1 0.0 copy-done
  34.1 0.0 copy-done.1
  34.1 6.5 %shard_map.98 = (f32[3,16384]{1,0:T(4,128)}, f32[8,66,8,128]{3,2,1,0:T(8,128)}, f32[8,128]{1,0:T(8,128)S(1)}) custom-call(s32[128]{0:T(128)} %brick_hbm.3, s32[128,128]{1,0:T(8,128)S(1)} %bitcast.10, f32[3,16384]{1,0:T(4,128)S(1)} %copy-done, f32[3,8192]{1,0:T(4,128)S(1)} %shard_map.95.slip_a_ref, f32[3,8192]{1,0:T(4,128)S(1)} %shard_map.97.slip_b_ref, ...), custom_call_target="tpu_custom_call" | custom-call | flops 6000000000 | bytes 21600000 | tf_op jit(solution)/shard_map/pallas_call | solution.py:680
  40.6 3.8 %all-to-all-start.2 = ((f32[8,66,8,128]{3,2,1,0:T(8,128)}), f32[8,66,8,128]{3,2,1,0:T(8,128)S(1)}, u32[]{:S(2)}, u32[]{:S(2)}) async-start(f32[8,66,8,128]{3,2,1,0:T(8,128)} %get-tuple-element.35), calls=%async_computation.2 | async-start | bytes 4325376 | tf_op jit(solution)/shard_map/all_to_all | solution.py:693
  44.4 1.2 %shard_map.99 = (f32[3,8,32,128]{3,2,1,0:T(8,128)S(1)}, f32[3,4,32,128]{3,2,1,0:T(8,128)S(1)}, f32[3,4,32,128]{3,2,1,0:T(8,128)S(1)}) custom-call(f32[8,128]{1,0:T(8,128)S(1)} %get-tuple-element.30.after_any, f32[3,8,128,128]{3,2,1,0:T(8,128)} %velocity_hbm.3), custom_call_target="tpu_custom_call" | custom-call | flops 1000000000 | bytes 3600000 | tf_op jit(solution)/shard_map/pallas_call | solution.py:694
  45.6 0.1 collective-permute-start
  45.7 1.9 %collective-permute-start.1 = (f32[3,4,32,128]{3,2,1,0:T(8,128)S(1)}, f32[3,4,32,128]{3,2,1,0:T(8,128)S(1)}, u32[]{:S(2)}, u32[]{:S(2)}) collective-permute-start(f32[3,4,32,128]{3,2,1,0:T(8,128)S(1)} %get-tuple-element.33), channel_id=1, source_target_pairs={{8,16},{24,32},{40,48},{56,64},{72,80},{88,96},{104,112},{120,128}... | collective-permute-start | bytes 589832 | tf_op jit(solution)/shard_map/ppermute | solution.py:612
  47.6 1.8 %shard_map.101 = (f32[8,128,128]{2,1,0:T(8,128)}, f32[24,8,128]{2,1,0:T(8,128)S(1)}) custom-call(f32[8,128]{1,0:T(8,128)S(1)} %get-tuple-element.30.after_any, f32[128,8,128]{2,1,0:T(8,128)S(1)} %bitcast.6), custom_call_target="tpu_custom_call" | custom-call | flops 2000000000 | bytes 7200000 | tf_op jit(solution)/shard_map/pallas_call | solution.py:701
  49.4 0.0 collective-permute-done.even_ref
  49.4 7.0 %collective-permute-done.1.odd_ref = f32[3,4,32,128]{3,2,1,0:T(8,128)S(1)} collective-permute-done((f32[3,4,32,128]{3,2,1,0:T(8,128)S(1)}, f32[3,4,32,128]{3,2,1,0:T(8,128)S(1)}, u32[]{:S(2)}, u32[]{:S(2)}) %collective-permute-start.1) | collective-permute-done | bytes 196640 | tf_op jit(solution)/shard_map/ppermute | solution.py:612
  56.4 0.9 shard_map.100
  57.4 12.1 %all-to-all-done.2.parts_ref = f32[8,66,8,128]{3,2,1,0:T(8,128)S(1)} async-done(((f32[8,66,8,128]{3,2,1,0:T(8,128)}), f32[8,66,8,128]{3,2,1,0:T(8,128)S(1)}, u32[]{:S(2)}, u32[]{:S(2)}) %all-to-all-start.2) | async-done | bytes 2162720 | tf_op jit(solution)/shard_map/all_to_all | solution.py:693
  69.5 0.4 shard_map.102
  69.9 0.3 collective-permute-start.3
  70.2 1.9 %collective-permute-start.2 = (f32[3,3,24,128]{3,2,1,0:T(8,128)S(1)}, f32[3,3,24,128]{3,2,1,0:T(8,128)S(1)}, u32[]{:S(2)}, u32[]{:S(2)}) collective-permute-start(f32[3,3,24,128]{3,2,1,0:T(8,128)S(1)} %get-tuple-element.39), channel_id=1, source_target_pairs={{8,16},{24,32},{40,48},{56,64},{72,80},{88,96},{104,112},{120,128}... | collective-permute-start | bytes 331784 | tf_op jit(solution)/shard_map/ppermute | solution.py:612
  72.1 0.0 collective-permute-done.3.even_ref
  72.1 2.4 %shard_map.103 = (f32[3,2,32,128]{3,2,1,0:T(8,128)S(1)}, f32[3,2,32,128]{3,2,1,0:T(8,128)S(1)}, f32[3,2,32,128]{3,2,1,0:T(8,128)S(1)}, f32[3,5,16,128]{3,2,1,0:T(8,128)S(1)}) custom-call(f32[3,14,32,128]{3,2,1,0:T(8,128)S(1)} %get-tuple-element.34.first_ref, f32[3,8,24,128]{3,2,1,0:T(8,128)S(1)} %get-tuple-element.38.own_ref, ...), custom_call_target="tpu_custom_call" | custom-call | flops 2000000000 | bytes 7200000 | tf_op jit(solution)/shard_map/pallas_call | solution.py:720
  74.6 5.3 %collective-permute-done.2.odd_ref = f32[3,3,24,128]{3,2,1,0:T(8,128)S(1)} collective-permute-done((f32[3,3,24,128]{3,2,1,0:T(8,128)S(1)}, f32[3,3,24,128]{3,2,1,0:T(8,128)S(1)}, u32[]{:S(2)}, u32[]{:S(2)}) %collective-permute-start.2) | collective-permute-done | bytes 110624 | tf_op jit(solution)/shard_map/ppermute | solution.py:612
  79.9 0.7 shard_map.104
  80.6 22.5 %all_to_all.20.parts_ref = f32[8,3,8,16,128]{4,3,2,1,0:T(8,128)S(1)} all-to-all(f32[8,3,8,16,128]{4,3,2,1,0:T(8,128)S(1)} %shard_map.104), channel_id=1, replica_groups=mesh['slab'=32,'sub'=8] {'sub'}, dimensions={0} | all-to-all | bytes 3145728 | tf_op jit(solution)/shard_map/all_to_all | solution.py:730
  103.0 1.2 %shard_map.105 = f32[3,8,128,128]{3,2,1,0:T(8,128)} custom-call(f32[8,3,8,16,128]{4,3,2,1,0:T(8,128)S(1)} %all_to_all.20.parts_ref), custom_call_target="tpu_custom_call" | custom-call | flops 1000000000 | bytes 3600000 | tf_op jit(solution)/shard_map/pallas_call | solution.py:731
Async XLA Ops:
  10.4 12.3 %all-to-all-start = ((f32[8,16,8,128]{3,2,1,0:T(8,128)}), f32[8,16,8,128]{3,2,1,0:T(8,128)S(1)}, u32[]{:S(2)}, u32[]{:S(2)}) async-start(f32[8,16,8,128]{3,2,1,0:T(8,128)} %bitcast.11), calls=%async_computation | async-start | bytes 1048576 | tf_op jit(solution)/shard_map/all_to_all | solution.py:656
  23.6 10.6 %all-to-all-start.1 = ((f32[8,16,8,128]{3,2,1,0:T(8,128)}), f32[8,16,8,128]{3,2,1,0:T(8,128)S(1)}, u32[]{:S(2)}, u32[]{:S(2)}) async-start(f32[8,16,8,128]{3,2,1,0:T(8,128)} %get-tuple-element.29), calls=%async_computation.1 | async-start | bytes 1048576 | tf_op jit(solution)/shard_map/all_to_all | solution.py:679
  27.1 7.1 %copy-start = (f32[3,16384]{1,0:T(4,128)S(1)}, f32[3,16384]{1,0:T(4,128)}, u32[]{:S(2)}) copy-start(f32[3,16384]{1,0:T(4,128)} %frac_ref.1) | copy-start | bytes 589828
  27.1 7.1 %copy-start.1 = (s32[16384]{0:T(1024)S(1)}, s32[16384]{0:T(1024)}, u32[]{:S(2)}) copy-start(s32[16384]{0:T(1024)} %param.10) | copy-start | bytes 196612
  40.6 28.8 %all-to-all-start.2 = ((f32[8,66,8,128]{3,2,1,0:T(8,128)}), f32[8,66,8,128]{3,2,1,0:T(8,128)S(1)}, u32[]{:S(2)}, u32[]{:S(2)}) async-start(f32[8,66,8,128]{3,2,1,0:T(8,128)} %get-tuple-element.35), calls=%async_computation.2 | async-start | bytes 4325376 | tf_op jit(solution)/shard_map/all_to_all | solution.py:693
  45.6 3.8 %collective-permute-start = (f32[3,4,32,128]{3,2,1,0:T(8,128)S(1)}, f32[3,4,32,128]{3,2,1,0:T(8,128)S(1)}, u32[]{:S(2)}, u32[]{:S(2)}) collective-permute-start(f32[3,4,32,128]{3,2,1,0:T(8,128)S(1)} %get-tuple-element.32), channel_id=1, source_target_pairs={{0,8},{16,24},{32,40},{48,56},{64,72},{80,88},{96,104},{112,120},{... | collective-permute-start | bytes 589832 | tf_op jit(solution)/shard_map/ppermute | solution.py:612
  45.7 10.7 %collective-permute-start.1 = (f32[3,4,32,128]{3,2,1,0:T(8,128)S(1)}, f32[3,4,32,128]{3,2,1,0:T(8,128)S(1)}, u32[]{:S(2)}, u32[]{:S(2)}) collective-permute-start(f32[3,4,32,128]{3,2,1,0:T(8,128)S(1)} %get-tuple-element.33), channel_id=1, source_target_pairs={{8,16},{24,32},{40,48},{56,64},{72,80},{88,96},{104,112},{120,128}... | collective-permute-start | bytes 589832 | tf_op jit(solution)/shard_map/ppermute | solution.py:612
  69.9 2.2 %collective-permute-start.3 = (f32[3,3,24,128]{3,2,1,0:T(8,128)S(1)}, f32[3,3,24,128]{3,2,1,0:T(8,128)S(1)}, u32[]{:S(2)}, u32[]{:S(2)}) collective-permute-start(f32[3,3,24,128]{3,2,1,0:T(8,128)S(1)} %get-tuple-element.40), channel_id=1, source_target_pairs={{0,8},{16,24},{32,40},{48,56},{64,72},{80,88},{96,104},{112,120},{... | collective-permute-start | bytes 331784 | tf_op jit(solution)/shard_map/ppermute | solution.py:612
  70.2 9.7 %collective-permute-start.2 = (f32[3,3,24,128]{3,2,1,0:T(8,128)S(1)}, f32[3,3,24,128]{3,2,1,0:T(8,128)S(1)}, u32[]{:S(2)}, u32[]{:S(2)}) collective-permute-start(f32[3,3,24,128]{3,2,1,0:T(8,128)S(1)} %get-tuple-element.39), channel_id=1, source_target_pairs={{8,16},{24,32},{40,48},{56,64},{72,80},{88,96},{104,112},{120,128}... | collective-permute-start | bytes 331784 | tf_op jit(solution)/shard_map/ppermute | solution.py:612
